TPU v7x, 32 devices: a whole 2x2x4 slice. The times are simulated.
32 devices in a mesh: dp: 4 (over y, x), vocab: 8 (over z, core).
Axes of the slice: x: 2, y: 2, z: 4, core: 2. Of those that a mesh axis runs over, the one named last changes fastest.
Arguments:
- hidden: bfloat16 [4096, 5120], P('dp', 'vocab'), may hold values from -6 to 6
- logit_grad: bfloat16 [4096, 384], P('dp', 'vocab'), may hold values from -0.3984375 to 0.3984375
- predict_mask: int32 [4096], P('dp'), may hold values 0 or 1
- slot_grads: bfloat16 [32, 8, 6, 5120], P(('dp', 'vocab')), may hold values from -6 to 6
- slot_rows: int32 [32, 8, 6], P(('dp', 'vocab')), may hold values from 0 to 47
- slot_counts: int32 [32, 8], P(('dp', 'vocab')), may hold values from 0 to 6, as said below
- master: float32 [384, 5120], P(('vocab', 'dp')), may hold values from -0.1 to 0.1
- first_moment: float32 [384, 5120], P(('vocab', 'dp')), may hold values from -2 to 2
- second_moment: float32 [384, 5120], P(('vocab', 'dp')), may hold values from 0.5 to 8
Outputs:
- master_new: float32 [384, 5120], P(('vocab', 'dp'))
- first_new: float32 [384, 5120], P(('vocab', 'dp'))
- second_new: float32 [384, 5120], P(('vocab', 'dp'))
- table_new: bfloat16 [384, 5120], P('vocab')
Inputs may be any that keep to these rules, and one draw needn't show every extreme that they name: `slot_counts`: some owner receives 6 live slots from every sender, in every draw.
All inputs are finite; a program needn't handle non-finite values. No bound on the sum of `predict_mask` on one device may be relied on, other than what follows from the above.
Results may differ from a plain program's by a relative error of at most 0.0004.
Values may be sent and summed in bfloat16 or wider, within the bound.
No kernel may reach another device: no remote copies, remote signals or barrier semaphores. Data moves between devices by JAX's collectives and lax.ppermute only.
A program may use at most 64 MiB of HBM per device.

v0:
```python
import jax
import jax.numpy as jnp
from jax import lax
from jax.sharding import PartitionSpec as P

STEP = 8


def local(
    hidden,
    logit_grad,
    predict_mask,
    slot_grads,
    slot_rows,
    slot_counts,
    master,
    first_moment,
    second_moment,
):
    masked = logit_grad * predict_mask.astype(jnp.bfloat16)[:, None]
    rows_block = logit_grad.shape[1]
    width = slot_grads.shape[3]
    contract = (((0,), (0,)), ((), ()))
    head_part = lax.dot_general(
        masked,
        lax.all_gather(hidden, "vocab", axis=1, tiled=True),
        contract,
        preferred_element_type=jnp.float32,
    )
    slot_index = jnp.arange(slot_grads.shape[2], dtype=jnp.int32)[None, None, :]
    alive_slot = slot_index < slot_counts[:, :, None]
    slot_ids = jnp.where(alive_slot, slot_rows, -1).astype(jnp.bfloat16)
    arrived, arrived_ids = (
        lax.all_to_all(slot_grads, "vocab", split_axis=1, concat_axis=0, tiled=True),
        lax.all_to_all(slot_ids, "vocab", split_axis=1, concat_axis=0, tiled=True),
    )
    arrived = arrived.reshape(-1, width)
    arrived_ids = arrived_ids.reshape(-1).astype(jnp.float32)
    row_labels = jnp.arange(rows_block, dtype=jnp.float32)[:, None]
    picked = (row_labels == arrived_ids[None, :]).astype(jnp.bfloat16)
    embed_part = jnp.dot(picked, arrived, preferred_element_type=jnp.float32)
    head_shard = lax.psum_scatter(head_part, "dp", scatter_dimension=0, tiled=True)
    embed_shard = lax.psum_scatter(embed_part, "dp", scatter_dimension=0, tiled=True)
    gradient = head_shard + embed_shard
    first_new = 0.9 * first_moment + 0.1 * gradient
    second_new = 0.95 * second_moment + 0.05 * gradient * gradient
    first_hat = first_new / (1.0 - 0.9**STEP)
    second_hat = second_new / (1.0 - 0.95**STEP)
    master_new = master - 0.05 * (first_hat / (jnp.sqrt(second_hat) + 1e-08) + 0.1 * master)
    table_new = lax.all_gather(master_new.astype(jnp.bfloat16), "dp", axis=0, tiled=True)
    return (master_new, first_new, second_new, table_new)


def solution(mesh):
    in_specs = (
        P("dp", "vocab"),
        P("dp", "vocab"),
        P("dp"),
        P(("dp", "vocab"), None, None, None),
        P(("dp", "vocab"), None, None),
        P(("dp", "vocab"), None),
        P(("vocab", "dp"), None),
        P(("vocab", "dp"), None),
        P(("vocab", "dp"), None),
    )
    out_specs = (
        P(("vocab", "dp"), None),
        P(("vocab", "dp"), None),
        P(("vocab", "dp"), None),
        P("vocab", None),
    )
    return jax.shard_map(local, mesh=mesh, in_specs=in_specs, out_specs=out_specs, check_vma=False)
```

profile of v0, /device:TPU:0, one launch (start us, length us, event | category | flops | bytes accessed | tf_op | source)
XLA Modules:
  0.0 190.2 jit_solution(8278356498829274427)
XLA Ops:
  7.2 0.0 all-gather.3.cloned.1.call-start
  7.2 0.7 all-gather.3.cloned.1.call-update
  7.9 0.8 copy.18
  8.7 1.3 fusion.6
  10.0 6.3 %all-to-all-start = ((bf16[1,8,6]{2,0,1:T(2,128)(2,1)}), bf16[1,8,6]{2,0,1:T(2,128)(2,1)S(1)}, u32[]{:S(2)}, u32[]{:S(2)}) async-start(bf16[1,8,6]{2,0,1:T(2,128)(2,1)} %fusion.6), calls=%async_computation | async-start | bytes 8192 | tf_op jit(solution)/shard_map/all_to_all | solution.py:35
  16.3 2.2 %copy.19 = bf16[1,8,6,5120]{3,2,0,1:T(8,128)(2,1)} copy(bf16[1,8,6,5120]{3,1,2,0:T(8,128)(2,1)} %param.12) | data formatting | bytes 983040 | tf_op args[3]
  18.5 3.3 %all-to-all-done = bf16[1,8,6]{2,0,1:T(2,128)(2,1)S(1)} async-done(((bf16[1,8,6]{2,0,1:T(2,128)(2,1)}), bf16[1,8,6]{2,0,1:T(2,128)(2,1)S(1)}, u32[]{:S(2)}, u32[]{:S(2)}) %all-to-all-start) | async-done | bytes 128 | tf_op jit(solution)/shard_map/all_to_all | solution.py:35
  21.8 3.5 %all-to-all-start.1 = ((bf16[1,8,6,5120]{3,2,0,1:T(8,128)(2,1)}), bf16[1,8,6,5120]{3,2,0,1:T(8,128)(2,1)S(1)}, u32[]{:S(2)}, u32[]{:S(2)}) async-start(bf16[1,8,6,5120]{3,2,0,1:T(8,128)(2,1)} %copy.19), calls=%async_computation.1 | async-start | bytes 1310720 | tf_op jit(solution)/shard_map/all_to_all | solution.py:34
  25.3 0.7 convert_element_type.20
  26.1 0.1 reshape.68
  26.1 31.8 %all-to-all-done.1 = bf16[1,8,6,5120]{3,2,0,1:T(8,128)(2,1)S(1)} async-done(((bf16[1,8,6,5120]{3,2,0,1:T(8,128)(2,1)}), bf16[1,8,6,5120]{3,2,0,1:T(8,128)(2,1)S(1)}, u32[]{:S(2)}, u32[]{:S(2)}) %all-to-all-start.1) | async-done | bytes 491552 | tf_op jit(solution)/shard_map/all_to_all | solution.py:34
  57.9 0.2 reshape.67
  58.1 0.0 copy-start.3
  58.1 0.3 fusion.4
  58.4 0.0 copy-start
  58.4 0.0 copy-start.1
  58.4 0.0 copy-start.2
  58.4 67.2 %all-gather.3.cloned.1.call-done = bf16[1024,5120]{1,0:T(8,128)(2,1)} async-done(((bf16[1024,640]{1,0:T(8,128)(2,1)}), bf16[1024,5120]{1,0:T(8,128)(2,1)}) %all-gather.3.cloned.1.call-update) | async-done | bytes 10485776 | tf_op jit(solution)/shard_map/all_gather | solution.py:26
  125.6 6.0 %convolution_add_fusion = f32[48,5120]{1,0:T(8,128)S(1)} fusion(f32[48,5120]{1,0:T(8,128)S(1)} %fusion.4, bf16[1024,5120]{1,0:T(8,128)(2,1)} %all-gather.3.cloned.1.call-done, bf16[1024,48]{0,1:T(8,128)(2,1)} %param.10, bf16[1024]{0:T(1024)(128)(2,1)S(1)} %convert_element_type.20), kind=kOutput, calls=%fused_computation | convolution fusion | flops 503611392 | bytes 12552192 | tf_op jit(solution)/shard_map/dot_general | solution.py:24
  131.6 28.4 %fusion = f32[16,5120]{1,0:T(8,128)S(1)} fusion(f32[48,5120]{1,0:T(8,128)S(1)} %convolution_add_fusion), kind=kCustom, calls=%all-reduce-scatter | all-reduce-scatter fusion | flops 327681 | bytes 1311232
  160.0 2.5 %collective-permute-start = (f32[12,5120]{1,0:T(8,128)S(1)}, f32[12,5120]{1,0:T(8,128)S(1)}, u32[]{:S(2)}, u32[]{:S(2)}) collective-permute-start(f32[12,5120]{1,0:T(8,128)S(1)} %slice), channel_id=1, source_target_pairs={{0,8},{8,16},{16,24},{1,9},{9,17},{17,25},{2,10},{10,18},{18,26},{... | collective-permute-start | bytes 737288
  162.5 0.0 copy-done.3
  162.5 0.6 dynamic-slice.4
  163.8 4.2 %collective-permute-done = f32[12,5120]{1,0:T(8,128)S(1)} collective-permute-done((f32[12,5120]{1,0:T(8,128)S(1)}, f32[12,5120]{1,0:T(8,128)S(1)}, u32[]{:S(2)}, u32[]{:S(2)}) %collective-permute-start) | collective-permute-done | bytes 245792
  168.0 0.5 concatenate
  168.5 0.0 copy-done
  168.5 0.0 copy-done.1
  168.5 0.0 copy-done.2
  168.5 1.1 convert_bitcast_fusion
  169.6 12.8 %all-gather = bf16[4,12,5120]{2,1,0:T(8,128)(2,1)S(1)} all-gather(bf16[1,12,5120]{2,1,0:T(8,128)(2,1)S(1)} %get-tuple-element.4), channel_id=1, replica_groups=mesh['dp'=4,'vocab'=8] {'dp'}, dimensions={0}, use_global_device_ids=true | all-gather | bytes 614400 | tf_op jit(solution)/shard_map/all_gather | solution.py:50
  182.4 0.9 reshape.70
  (2 shorter events, 0.0 us)
Async XLA Ops:
  7.2 118.4 %all-gather.3.cloned.1.call-start = ((), (), s32[]{:S(2)}) async-start(), calls=%async_computation.2 | async-start | bytes 11796480 | tf_op jit(solution)/shard_map/all_gather | solution.py:26
  10.0 11.8 %all-to-all-start = ((bf16[1,8,6]{2,0,1:T(2,128)(2,1)}), bf16[1,8,6]{2,0,1:T(2,128)(2,1)S(1)}, u32[]{:S(2)}, u32[]{:S(2)}) async-start(bf16[1,8,6]{2,0,1:T(2,128)(2,1)} %fusion.6), calls=%async_computation | async-start | bytes 8192 | tf_op jit(solution)/shard_map/all_to_all | solution.py:35
  21.8 36.1 %all-to-all-start.1 = ((bf16[1,8,6,5120]{3,2,0,1:T(8,128)(2,1)}), bf16[1,8,6,5120]{3,2,0,1:T(8,128)(2,1)S(1)}, u32[]{:S(2)}, u32[]{:S(2)}) async-start(bf16[1,8,6,5120]{3,2,0,1:T(8,128)(2,1)} %copy.19), calls=%async_computation.1 | async-start | bytes 1310720 | tf_op jit(solution)/shard_map/all_to_all | solution.py:34
  58.1 104.4 %copy-start.3 = (u32[32]{0:T(128)S(1)}, u32[32]{0:T(128)}, u32[]{:S(2)}) copy-start(u32[32]{0:T(128)} %constant.26) | copy-start | bytes 388
  58.4 110.1 %copy-start = (f32[12,5120]{1,0:T(8,128)S(1)}, f32[12,5120]{1,0:T(8,128)}, u32[]{:S(2)}) copy-start(f32[12,5120]{1,0:T(8,128)} %param.15) | copy-start | bytes 737284
  58.4 110.1 %copy-start.1 = (f32[12,5120]{1,0:T(8,128)S(1)}, f32[12,5120]{1,0:T(8,128)}, u32[]{:S(2)}) copy-start(f32[12,5120]{1,0:T(8,128)} %param.16) | copy-start | bytes 737284
  58.4 110.1 %copy-start.2 = (f32[12,5120]{1,0:T(8,128)S(1)}, f32[12,5120]{1,0:T(8,128)}, u32[]{:S(2)}) copy-start(f32[12,5120]{1,0:T(8,128)} %param.17) | copy-start | bytes 737284
  160.0 8.0 %collective-permute-start = (f32[12,5120]{1,0:T(8,128)S(1)}, f32[12,5120]{1,0:T(8,128)S(1)}, u32[]{:S(2)}, u32[]{:S(2)}) collective-permute-start(f32[12,5120]{1,0:T(8,128)S(1)} %slice), channel_id=1, source_target_pairs={{0,8},{8,16},{16,24},{1,9},{9,17},{17,25},{2,10},{10,18},{18,26},{... | collective-permute-start | bytes 737288
Sparse Core Ops, SparseCore 0:
  9.6 115.9 all-gather.2
where the time goes:
time: 191 us; the launch traced here: 190 us
  waiting for transfers between devices  107 us (56%)
  blocking collectives  41.2 us (22%)
  between operations  14.8 us (8%)
  starting transfers between devices  12.4 us (6%)
  matrix products  6.24 us (3%)
  local copies, waits for them, and re-layouts  5.18 us (3%)
  other arithmetic  3.15 us (2%)
    all_gather x1, waiting for transfers between devices, local(): lax.all_gather(hidden, 'vocab', axis=1, tiled=True)  67.2 us
    all_to_all x1, waiting for transfers between devices, local(): lax.all_to_all(slot_grads, 'vocab', split_axis=1, concat_axis=0, tiled=True)  31.8 us
    unnamed x1, blocking collectives  28.4 us
    all_gather x1, blocking collectives, local(): lax.all_gather(master_new.astype(jnp.bfloat16), 'dp', axis=0, tiled=True)  12.8 us
    all_to_all x1, starting transfers between devices, local(): lax.all_to_all(slot_ids, 'vocab', split_axis=1, concat_axis=0, tiled=True)  6.33 us
    dot_general x1, matrix products, local(): lax.dot_general(masked, lax.all_gather(hidden, 'vocab', axis=1, tiled=Tru...  5.97 us
    unnamed x14, local copies, waits for them, and re-layouts  4.93 us
    unnamed x2, waiting for transfers between devices  4.93 us
  transfers between devices with their start and end apart: 4, of which 4 were waited for; matrix products, arithmetic and copies ran while one was open for 3% of the time, Pallas kernels for 0%

commit v1 on v0

v1 whole, which is shorter than its diff:
```python
import jax
import jax.numpy as jnp
from jax import lax
from jax.sharding import PartitionSpec as P

STEP = 8


def local(
    hidden,
    logit_grad,
    predict_mask,
    slot_grads,
    slot_rows,
    slot_counts,
    master,
    first_moment,
    second_moment,
):
    vocab = lax.axis_size("vocab")
    dp = lax.axis_size("dp")
    rows = logit_grad.shape[1]
    shard = master.shape[0]
    cols = hidden.shape[1]
    owners, cap, width = slot_grads.shape[1:]
    masked = (logit_grad * predict_mask.astype(jnp.bfloat16)[:, None]).T
    masked_all = lax.all_gather(masked, "vocab", axis=0, tiled=True)
    slot_index = jnp.arange(cap, dtype=jnp.int32)[None, :]
    ids = jnp.where(slot_index < slot_counts[0][:, None], slot_rows[0], -1)
    ids_all = lax.all_gather(ids, "vocab", axis=0, tiled=False)
    outgoing = slot_grads.reshape(owners * cap, vocab, cols).transpose(1, 0, 2)
    arrived = lax.all_to_all(outgoing, "vocab", split_axis=0, concat_axis=0, tiled=True)
    arrived = arrived.reshape(vocab, owners, cap, cols).transpose(1, 0, 2, 3).reshape(owners, vocab * cap, cols)
    ids_all = ids_all.transpose(1, 0, 2).reshape(owners, 1, vocab * cap)
    picked = (jnp.arange(rows, dtype=jnp.int32)[None, :, None] == ids_all).astype(jnp.bfloat16)
    head = jnp.dot(masked_all, hidden, preferred_element_type=jnp.float32)
    embed = lax.dot_general(picked, arrived, (((2,), (1,)), ((0,), (0,))), preferred_element_type=jnp.float32)
    part = head.reshape(vocab, dp, shard, cols) + embed.reshape(vocab, dp, shard, cols)
    part = part.transpose(1, 0, 2, 3).reshape(dp, vocab * shard, cols)
    part = lax.all_to_all(part, "dp", split_axis=0, concat_axis=0, tiled=True)
    total = part.sum(axis=0).reshape(vocab, shard, cols)
    total = lax.all_to_all(total, "vocab", split_axis=0, concat_axis=0, tiled=True)
    gradient = total.transpose(1, 0, 2).reshape(shard, width)
    first_new = 0.9 * first_moment + 0.1 * gradient
    second_new = 0.95 * second_moment + 0.05 * gradient * gradient
    first_hat = first_new / (1.0 - 0.9**STEP)
    second_hat = second_new / (1.0 - 0.95**STEP)
    master_new = master - 0.05 * (first_hat / (jnp.sqrt(second_hat) + 1e-08) + 0.1 * master)
    table_new = lax.all_gather(master_new.astype(jnp.bfloat16), "dp", axis=0, tiled=True)
    return (master_new, first_new, second_new, table_new)


def solution(mesh):
    in_specs = (
        P("dp", "vocab"),
        P("dp", "vocab"),
        P("dp"),
        P(("dp", "vocab"), None, None, None),
        P(("dp", "vocab"), None, None),
        P(("dp", "vocab"), None),
        P(("vocab", "dp"), None),
        P(("vocab", "dp"), None),
        P(("vocab", "dp"), None),
    )
    out_specs = (
        P(("vocab", "dp"), None),
        P(("vocab", "dp"), None),
        P(("vocab", "dp"), None),
        P("vocab", None),
    )
    return jax.shard_map(local, mesh=mesh, in_specs=in_specs, out_specs=out_specs, check_vma=False)
```

time: 191 us -> 96.5 us (0.51)
  waiting for transfers between devices: 107 us -> 0.01 us
  blocking collectives: 41.2 us -> 79 us
  between operations: 14.8 us -> 0.85 us
  starting transfers between devices: 12.4 us -> 6.33 us
  matrix products: 6.24 us -> 2 us
    all_gather x1 -> x0, waiting for transfers between devices: 67.2 us -> none  [local(): lax.all_gather(hidden, 'vocab', axis=1, tiled=True)]
    all_gather x0 -> x2, blocking collectives: none -> 36.4 us  [the longest x1 20.9 us: local(): ids_all = lax.all_gather(ids, 'vocab', axis=0, tiled=False)]
    all_to_all x2 -> x1, waiting for transfers between devices: 35.1 us -> 0.01 us  [local(): lax.all_to_all(outgoing, 'vocab', split_axis=0, concat_axis=0, tiled=True)]
    all_to_all x0 -> x2, blocking collectives: none -> 32.8 us  [the longest x1 17.6 us: local(): part = lax.all_to_all(part, 'dp', split_axis=0, concat_axis=0, tiled=True)]
    unnamed x1 -> x0, blocking collectives: 28.4 us -> none
    unnamed x2 -> x0, waiting for transfers between devices: 4.93 us -> none
    dot_general x2, matrix products: 6.24 us -> 2 us  [the longest x1 1.71 us: local(): head = jnp.dot(masked_all, hidden, preferred_element_type=jnp.float32)]
    all_to_all x2 -> x1, starting transfers between devices: 9.87 us -> 6.33 us  [local(): lax.all_to_all(outgoing, 'vocab', split_axis=0, concat_axis=0, tiled=True)]
  transfers between devices with their start and end apart: 4 -> 1, of which waited for: 4 -> 0; matrix products, arithmetic and copies ran while one was open for 3% -> 3% of each run, Pallas kernels for 0% -> 0%
where the time goes in v1:
time: 96.5 us; the launch traced here: 96.1 us
  blocking collectives  79 us (82%)
  local copies, waits for them, and re-layouts  6.46 us (7%)
  starting transfers between devices  6.33 us (7%)
  matrix products  2 us (2%)
  other arithmetic  1.49 us (2%)
    all_gather x1, blocking collectives, local(): ids_all = lax.all_gather(ids, 'vocab', axis=0, tiled=False)  20.9 us
    all_to_all x1, blocking collectives, local(): part = lax.all_to_all(part, 'dp', split_axis=0, concat_axis=0, tiled=True)  17.6 us
    all_gather x1, blocking collectives, local(): masked_all = lax.all_gather(masked, 'vocab', axis=0, tiled=True)  15.5 us
    all_to_all x1, blocking collectives, local(): lax.all_to_all(total, 'vocab', split_axis=0, concat_axis=0, tiled=True)  15.1 us
    all_gather x1, blocking collectives, local(): lax.all_gather(master_new.astype(jnp.bfloat16), 'dp', axis=0, tiled=True)  9.79 us
    all_to_all x1, starting transfers between devices, local(): lax.all_to_all(outgoing, 'vocab', split_axis=0, concat_axis=0, tiled=True)  6.33 us
    unnamed x21, local copies, waits for them, and re-layouts  2.53 us
  transfers between devices with their start and end apart: 1, of which 0 were waited for; matrix products, arithmetic and copies ran while one was open for 3% of the time, Pallas kernels for 0%

profile of v1, /device:TPU:0, one launch (start us, length us, event | category | flops | bytes accessed | tf_op | source)
XLA Modules:
  0.0 96.1 jit_solution(5863417995825983882)
XLA Ops:
  0.6 0.0 copy-start
  0.6 1.4 %copy.30 = bf16[1,8,6,5120]{3,2,1,0:T(8,128)(2,1)S(1)} copy(bf16[1,8,6,5120]{3,1,2,0:T(8,128)(2,1)} %param.12) | data formatting | bytes 983040 | tf_op args[3]
  2.1 0.0 copy-start.5
  2.1 0.0 copy-start.6
  2.1 0.0 copy-start.7
  2.1 0.6 reshape.71
  2.7 0.0 copy-start.4
  2.7 0.8 copy.31
  3.6 6.3 %all-to-all-start = ((bf16[8,48,640]{2,1,0:T(8,128)(2,1)}), bf16[8,48,640]{2,1,0:T(8,128)(2,1)S(1)}, u32[]{:S(2)}, u32[]{:S(2)}) async-start(bf16[8,48,640]{2,1,0:T(8,128)(2,1)} %copy.31), calls=%async_computation | async-start | bytes 983040 | tf_op jit(solution)/shard_map/all_to_all | solution.py:32
  9.9 0.0 copy-done.5
  9.9 0.0 copy-done.6
  9.9 0.1 copy.28
  10.0 0.0 copy-done.7
  10.0 0.1 fusion.5
  10.1 20.9 %all_gather.11 = s32[8,8,6]{2,1,0:T(8,128)S(1)} all-gather(s32[1,8,6]{2,1,0:T(8,128)S(1)} %fusion.5), channel_id=1, replica_groups=mesh['dp'=4,'vocab'=8] {'vocab'}, dimensions={0}, use_global_device_ids=true | all-gather | bytes 1728 | tf_op jit(solution)/shard_map/all_gather | solution.py:30
  31.0 0.1 eq.16
  31.0 0.0 copy-done.4
  31.1 15.5 %all_gather.10 = bf16[384,1024]{1,0:T(8,128)(2,1)S(1)} all-gather(bf16[48,1024]{1,0:T(8,128)(2,1)S(1)} %multiply_bitcast_fusion), channel_id=1, replica_groups=mesh['dp'=4,'vocab'=8] {'vocab'}, dimensions={0}, use_global_device_ids=true | all-gather | bytes 884736 | tf_op jit(solution)/shard_map/all_gather | solution.py:27
  46.6 0.0 copy-done
  46.6 1.7 %fusion.7 = f32[384,640]{1,0:T(8,128)} fusion(bf16[384,1024]{1,0:T(8,128)(2,1)S(1)} %all_gather.10, bf16[1024,640]{1,0:T(8,128)(2,1)S(1)} %copy-done), kind=kOutput, calls=%fused_computation.14 | convolution fusion | flops 503316480 | bytes 3080192 | tf_op jit(solution)/shard_map/dot_general | solution.py:36
  48.3 1.3 %reshape.70 = f32[8,4,12,640]{3,2,1,0:T(8,128)S(1)} reshape(f32[384,640]{1,0:T(8,128)} %fusion.7) | data formatting | bytes 1966080 | tf_op jit(solution)/shard_map/reshape | solution.py:38
  49.7 0.0 all-to-all-done
  49.7 0.1 copy.32
  49.8 0.1 copy.33
  49.9 0.3 fusion.1
  50.2 0.3 copy.35
  50.5 0.2 fusion
  50.7 0.4 copy.37
  51.1 0.1 copy.38
  51.2 17.6 %all_to_all.15 = f32[4,96,640]{2,1,0:T(8,128)S(1)} all-to-all(f32[4,96,640]{2,1,0:T(8,128)S(1)} %copy.38), channel_id=1, replica_groups=mesh['dp'=4,'vocab'=8] {'dp'}, dimensions={0} | all-to-all | bytes 1966080 | tf_op jit(solution)/shard_map/all_to_all | solution.py:40
  68.8 0.1 reduce_sum.9
  68.9 0.0 copy-start.1
  69.0 0.0 copy-start.2
  69.0 0.0 copy-start.3
  69.0 15.1 %all_to_all.16 = f32[8,12,640]{2,1,0:T(8,128)S(1)} all-to-all(f32[8,12,640]{2,1,0:T(8,128)S(1)} %reshape.76), channel_id=1, replica_groups=mesh['dp'=4,'vocab'=8] {'vocab'}, dimensions={0} | all-to-all | bytes 491520 | tf_op jit(solution)/shard_map/all_to_all | solution.py:42
  84.1 0.1 copy.39
  84.2 0.1 copy.40
  84.3 0.0 copy-done.1
  84.3 0.0 copy-done.2
  84.3 0.0 copy-done.3
  84.3 1.1 %convert_bitcast_fusion = (bf16[1,12,5120]{2,1,0:T(8,128)(2,1)S(1)}, f32[12,5120]{1,0:T(8,128)}, f32[12,5120]{1,0:T(8,128)}, f32[12,5120]{1,0:T(8,128)}) fusion(f32[12,5120]{1,0:T(8,128)S(1)} %copy-done.1, f32[12,5120]{1,0:T(8,128)S(1)} %bitcast.26, f32[12,5120]{1,0:T(8,128)S(1)} %copy-done.2, f32[12,5120]{1,0:T(8,128)S(1)} %copy-done.3), kind=kLoop, calls=%fused_computation.9 | loop fusion | flops 983040 | bytes 1843200
  85.4 9.8 %all-gather = bf16[4,12,5120]{2,1,0:T(8,128)(2,1)S(1)} all-gather(bf16[1,12,5120]{2,1,0:T(8,128)(2,1)S(1)} %get-tuple-element.4), channel_id=1, replica_groups=mesh['dp'=4,'vocab'=8] {'dp'}, dimensions={0}, use_global_device_ids=true | all-gather | bytes 614400 | tf_op jit(solution)/shard_map/all_gather | solution.py:49
  95.2 0.9 reshape.79
  (5 shorter events, 0.1 us)
Async XLA Ops:
  0.6 46.0 %copy-start = (bf16[1024,640]{1,0:T(8,128)(2,1)S(1)}, bf16[1024,640]{1,0:T(8,128)(2,1)}, u32[]{:S(2)}) copy-start(bf16[1024,640]{1,0:T(8,128)(2,1)} %param.9) | copy-start | bytes 3932164
  2.1 7.8 %copy-start.5 = (s32[1024]{0:T(1024)S(1)}, s32[1024]{0:T(1024)}, u32[]{:S(2)}) copy-start(s32[1024]{0:T(1024)} %param.11) | copy-start | bytes 12292
  2.1 7.8 %copy-start.6 = (s32[1,8,6]{1,0,2:T(1,128)S(1)}, s32[1,8,6]{1,0,2:T(1,128)}, u32[]{:S(2)}) copy-start(s32[1,8,6]{1,0,2:T(1,128)} %param.13) | copy-start | bytes 580
  2.1 7.9 %copy-start.7 = (s32[1,8]{1,0:T(1,128)S(1)}, s32[1,8]{1,0:T(1,128)}, u32[]{:S(2)}) copy-start(s32[1,8]{1,0:T(1,128)} %param.14) | copy-start | bytes 100
  2.7 28.3 %copy-start.4 = (bf16[1024,48]{0,1:T(8,128)(2,1)S(1)}, bf16[1024,48]{0,1:T(8,128)(2,1)}, u32[]{:S(2)}) copy-start(bf16[1024,48]{0,1:T(8,128)(2,1)} %param.10) | copy-start | bytes 294916
  3.6 46.1 %all-to-all-start = ((bf16[8,48,640]{2,1,0:T(8,128)(2,1)}), bf16[8,48,640]{2,1,0:T(8,128)(2,1)S(1)}, u32[]{:S(2)}, u32[]{:S(2)}) async-start(bf16[8,48,640]{2,1,0:T(8,128)(2,1)} %copy.31), calls=%async_computation | async-start | bytes 983040 | tf_op jit(solution)/shard_map/all_to_all | solution.py:32
  68.9 15.4 %copy-start.1 = (f32[12,5120]{1,0:T(8,128)S(1)}, f32[12,5120]{1,0:T(8,128)}, u32[]{:S(2)}) copy-start(f32[12,5120]{1,0:T(8,128)} %param.15) | copy-start | bytes 737284
  69.0 15.4 %copy-start.2 = (f32[12,5120]{1,0:T(8,128)S(1)}, f32[12,5120]{1,0:T(8,128)}, u32[]{:S(2)}) copy-start(f32[12,5120]{1,0:T(8,128)} %param.16) | copy-start | bytes 737284
  69.0 15.4 %copy-start.3 = (f32[12,5120]{1,0:T(8,128)S(1)}, f32[12,5120]{1,0:T(8,128)}, u32[]{:S(2)}) copy-start(f32[12,5120]{1,0:T(8,128)} %param.17) | copy-start | bytes 737284

commit v2 on v1

v2 whole, which is shorter than its diff:
```python
import jax
import jax.numpy as jnp
from jax import lax
from jax.sharding import PartitionSpec as P

STEP = 8
CORES = 2
LANES = 128


def local(
    hidden,
    logit_grad,
    predict_mask,
    slot_grads,
    slot_rows,
    slot_counts,
    master,
    first_moment,
    second_moment,
):
    vocab = lax.axis_size("vocab")
    dp = lax.axis_size("dp")
    chips = vocab // CORES
    rows = logit_grad.shape[1]
    shard = master.shape[0]
    cols = hidden.shape[1] * CORES
    owners, cap, width = slot_grads.shape[1:]
    here = lax.axis_index("vocab")
    core = here % CORES
    z = here // CORES
    d = lax.axis_index("dp")

    def to_core(x):
        return lax.ppermute(x, "vocab", [(v, v ^ 1) for v in range(vocab)])

    def to_chip(x, s):
        return lax.ppermute(x, "vocab", [(v, v ^ (s * CORES)) for v in range(vocab)])

    def to_dp(x, t):
        return lax.ppermute(x, "dp", [(i, i ^ t) for i in range(dp)])

    label = jnp.arange(rows, dtype=jnp.int32)
    source = ((label // shard) ^ d) * shard + label % shard
    reorder = (source[:, None] == label[None, :]).astype(jnp.bfloat16)
    masked = logit_grad * predict_mask.astype(jnp.bfloat16)[:, None]
    masked = lax.dot_general(reorder, masked, (((1,), (1,)), ((), ())), preferred_element_type=jnp.bfloat16)

    slot_index = jnp.arange(cap, dtype=jnp.int32)[None, :]
    ids = ((slot_rows[0] // shard) ^ d) * shard + slot_rows[0] % shard
    ids = jnp.where(slot_index < slot_counts[0][:, None], ids, -1).astype(jnp.bfloat16)
    ids = jnp.broadcast_to(ids[:, :, None, None], (owners, cap, chips, LANES))
    slots = slot_grads[0].reshape(owners, cap, chips, cols)
    slots = jnp.concatenate([slots, ids], axis=3).reshape(chips, CORES, cap, chips, cols + LANES)
    mine = lax.dynamic_index_in_dim(slots, core, 1, keepdims=False)
    other = lax.dynamic_index_in_dim(slots, 1 - core, 1, keepdims=False)
    hidden_other = to_core(hidden)
    other = to_core(other)
    masked = [masked] + [to_chip(masked, s) for s in range(1, chips)]
    both = jnp.stack([mine, other]).reshape(CORES * chips * cap, chips, cols + LANES)
    slots = [lax.dynamic_index_in_dim(both, z ^ s, 1, keepdims=False) for s in range(chips)]
    slots = [slots[0]] + [to_chip(slots[s], s) for s in range(1, chips)]

    swap = core == 1
    low = jnp.where(swap, hidden_other, hidden)
    high = jnp.where(swap, hidden, hidden_other)
    wide = jnp.concatenate([low, high], axis=1)
    slots = jnp.concatenate(slots, axis=0)
    owner = (jnp.arange(slots.shape[0], dtype=jnp.int32) // cap) % chips
    ids = slots[:, cols].astype(jnp.int32)
    ids = jnp.where(ids < 0, -1, (owner ^ z) * rows + ids)
    picked = (jnp.arange(chips * rows, dtype=jnp.int32)[:, None] == ids[None, :]).astype(jnp.bfloat16)
    part = jnp.dot(jnp.concatenate(masked, axis=0), wide, preferred_element_type=jnp.float32)
    part = part + jnp.dot(picked, slots[:, :cols], preferred_element_type=jnp.float32)
    part = part.reshape(chips, dp, shard, cols)
    part = [part[:, t].reshape(chips * shard, cols) for t in range(dp)]
    total = part[0]
    for t in range(1, dp):
        total = total + to_dp(part[t], t)
    total = total.reshape(chips, shard, CORES, cols // CORES).transpose(0, 2, 1, 3)
    total = total.reshape(chips, CORES * shard, cols // CORES)
    pieces = [total[0]] + [to_chip(total[s], s) for s in range(1, chips)]
    pieces = jnp.stack(pieces).reshape(chips, CORES, shard, cols // CORES).transpose(0, 2, 1, 3)
    pieces = pieces.reshape(chips, shard, cols)
    gradient = jnp.concatenate([lax.dynamic_index_in_dim(pieces, z ^ s, 0, keepdims=False) for s in range(chips)], axis=1)
    first_new = 0.9 * first_moment + 0.1 * gradient
    second_new = 0.95 * second_moment + 0.05 * gradient * gradient
    first_hat = first_new / (1.0 - 0.9**STEP)
    second_hat = second_new / (1.0 - 0.95**STEP)
    master_new = master - 0.05 * (first_hat / (jnp.sqrt(second_hat) + 1e-08) + 0.1 * master)
    table = master_new.astype(jnp.bfloat16)
    table = table.reshape(shard, chips, cols).transpose(1, 0, 2).reshape(chips * shard, cols)
    table = jnp.stack([table] + [to_dp(table, t) for t in range(1, dp)])
    table = jnp.stack([lax.dynamic_index_in_dim(table, d ^ t, 0, keepdims=False) for t in range(dp)])
    table = table.reshape(dp, chips, shard, cols).transpose(0, 2, 1, 3).reshape(rows, width)
    return (master_new, first_new, second_new, table)


def solution(mesh):
    in_specs = (
        P("dp", "vocab"),
        P("dp", "vocab"),
        P("dp"),
        P(("dp", "vocab"), None, None, None),
        P(("dp", "vocab"), None, None),
        P(("dp", "vocab"), None),
        P(("vocab", "dp"), None),
        P(("vocab", "dp"), None),
        P(("vocab", "dp"), None),
    )
    out_specs = (
        P(("vocab", "dp"), None),
        P(("vocab", "dp"), None),
        P(("vocab", "dp"), None),
        P("vocab", None),
    )
    return jax.shard_map(local, mesh=mesh, in_specs=in_specs, out_specs=out_specs, check_vma=False)
```

time: 96.5 us -> 73.8 us (0.76)
  blocking collectives: 79 us -> 0 us
  waiting for transfers between devices: 0.01 us -> 26 us
  starting transfers between devices: 6.33 us -> 27.9 us
  other arithmetic: 1.49 us -> 6.15 us
  local copies, waits for them, and re-layouts: 6.46 us -> 8.47 us
  matrix products: 2 us -> 3.81 us
    all_gather x3 -> x0, blocking collectives: 46.2 us -> none  [the longest x1 20.9 us: local(): ids_all = lax.all_gather(ids, 'vocab', axis=0, tiled=False)]
    all_to_all x2 -> x0, blocking collectives: 32.8 us -> none  [the longest x1 17.6 us: local(): part = lax.all_to_all(part, 'dp', split_axis=0, concat_axis=0, tiled=True)]
    ppermute x0 -> x17, starting transfers between devices: none -> 27.9 us  [the longest x9 20.1 us: to_chip(): return lax.ppermute(x, 'vocab', [(v, v ^ s * CORES) for v in range(vocab)])]
    ppermute x0 -> x17, waiting for transfers between devices: none -> 26 us  [the longest x9 13.3 us: to_chip(): return lax.ppermute(x, 'vocab', [(v, v ^ s * CORES) for v in range(vocab)])]
    all_to_all x1 -> x0, starting transfers between devices: 6.33 us -> none  [local(): lax.all_to_all(outgoing, 'vocab', split_axis=0, concat_axis=0, tiled=True)]
    dynamic_slice x0 -> x5, local copies, waits for them, and re-layouts: none -> 2.28 us  [the longest x1 1.12 us: local(): lax.dynamic_index_in_dim(both, z ^ s, 1, keepdims=False)]
    convert_element_type x1 -> x4, other arithmetic: 0.01 us -> 2.04 us  [the longest x1 1.1 us: local(): table = master_new.astype(jnp.bfloat16)]
    dot_general x2 -> x3, matrix products: 2 us -> 3.81 us  [the longest x1 1.63 us: local(): jnp.dot(jnp.concatenate(masked, axis=0), wide, preferred_element_type=jnp...]
  transfers between devices with their start and end apart: 1 -> 17, of which waited for: 0 -> 11; matrix products, arithmetic and copies ran while one was open for 3% -> 8% of each run, Pallas kernels for 0% -> 0%
where the time goes in v2:
time: 73.8 us; the launch traced here: 73.4 us
  starting transfers between devices  27.9 us (38%)
  waiting for transfers between devices  26 us (35%)
  local copies, waits for them, and re-layouts  8.47 us (11%)
  other arithmetic  6.15 us (8%)
  matrix products  3.81 us (5%)
  between operations  1.08 us (1%)
    ppermute x9, starting transfers between devices, to_chip(): return lax.ppermute(x, 'vocab', [(v, v ^ s * CORES) for v in range(vocab)])  20.1 us
    ppermute x9, waiting for transfers between devices, to_chip(): return lax.ppermute(x, 'vocab', [(v, v ^ s * CORES) for v in range(vocab)])  13.3 us
    ppermute x6, waiting for transfers between devices, to_dp(): return lax.ppermute(x, 'dp', [(i, i ^ t) for i in range(dp)])  11.4 us
    ppermute x6, starting transfers between devices, to_dp(): return lax.ppermute(x, 'dp', [(i, i ^ t) for i in range(dp)])  7.24 us
    unnamed x21, local copies, waits for them, and re-layouts  2.68 us
    dot_general x1, matrix products, local(): jnp.dot(jnp.concatenate(masked, axis=0), wide, preferred_element_type=jnp...  1.63 us
    concatenate x1, local copies, waits for them, and re-layouts, local(): jnp.concatenate([slots, ids], axis=3)  1.5 us
  transfers between devices with their start and end apart: 17, of which 11 were waited for; matrix products, arithmetic and copies ran while one was open for 8% of the time, Pallas kernels for 0%

profile of v2, /device:TPU:0, one launch (start us, length us, event | category | flops | bytes accessed | tf_op | source)
XLA Modules:
  0.0 73.4 jit_solution(8932523654193334432)
XLA Ops:
  0.6 0.8 %copy.28 = s32[1,8,6]{2,1,0:T(8,128)S(1)} copy(s32[1,8,6]{1,0,2:T(1,128)} %param.13) | data formatting | bytes 384 | tf_op args[4]
  1.4 0.7 sign_compare_fusion
  2.2 0.5 broadcast.194
  2.8 1.3 %reduce.5 = s32[8]{0:T(128)S(1)} reduce(s32[1,8]{1,0:T(1,128)} %param.14, s32[]{:T(128)} %broadcast.194), dimensions={0}, to_apply=%param.14.reduce_sub_computation.3 | reduce | bytes 68 | tf_op args[5]
  4.4 1.5 %concatenate.21 = bf16[4,2,6,4,1280]{4,3,1,0,2:T(4,128)(2,1)S(1)} reshape(bf16[1,8,6,5120]{3,1,2,0:T(8,128)(2,1)} %param.12) | data formatting | bytes 983040 | tf_op jit(solution)/shard_map/concatenate | solution.py:54
  6.0 0.3 fusion.14
  6.3 0.8 %copy.60 = bf16[4,1,6,4,1408]{4,3,2,0,1:T(4,128)(2,1)} copy(bf16[4,1,6,4,1408]{4,3,1,0,2:T(4,128)(2,1)S(1)} %get-tuple-element.19) | data formatting | bytes 540672 | tf_op jit(solution)/shard_map/jit(dynamic_index_in_dim)/dynamic_slice | solution.py:56
  7.1 0.5 collective-permute-start.4
  7.8 1.3 %collective-permute-done.4 = bf16[4,6,4,1408]{3,2,1,0:T(4,128)(2,1)} collective-permute-done((bf16[4,6,4,1408]{3,2,1,0:T(4,128)(2,1)}, bf16[4,6,4,1408]{3,2,1,0:T(4,128)(2,1)}, u32[]{:S(2)}, u32[]{:S(2)}) %collective-permute-start.4) | collective-permute-done | bytes 270368 | tf_op jit(solution)/shard_map/ppermute | solution.py:35
  9.0 1.4 %pad_maximum_fusion = bf16[2,4,6,4,1408]{4,3,2,1,0:T(4,128)(2,1)S(1)} fusion(bf16[1,4,6,4,1408]{4,3,2,1,0:T(4,128)(2,1)} %bitcast.4, bf16[1,4,6,4,1408]{4,3,2,1,0:T(4,128)(2,1)S(1)} %bitcast.59), kind=kLoop, calls=%fused_computation.8 | loop fusion | flops 270336 | bytes 1081344 | tf_op jit(solution)/shard_map/stack | solution.py:60
  10.4 1.1 %constant_dynamic-slice_fusion.11 = (bf16[48,1,1408]{2,1,0:T(2,128)(2,1)S(1)}, bf16[48,1,1408]{2,1,0:T(2,128)(2,1)S(1)}, bf16[48,1,1408]{2,1,0:T(2,128)(2,1)S(1)}, bf16[48,1,1408]{2,1,0:T(2,128)(2,1)S(1)}) fusion(bf16[48,4,1408]{2,1,0:T(4,128)(2,1)S(1)} %bitcast.53, s32[]{:T(128)S(6)} %select_n.146, s32[]{:T(128)S(6)} %select_n.149, s32[]{:T(128)S(6)} %select_n.148, ...), kind=kLoop, calls=%fused_computation.72 | loop fusion | bytes 1081360 | tf_op jit(solution)/shard_map/jit(dynamic_index_in_dim)/dynamic_slice | solution.py:61
  11.6 3.3 %collective-permute-start.5 = (bf16[48,1408]{1,0:T(8,128)(2,1)S(1)}, bf16[48,1408]{1,0:T(8,128)(2,1)}, u32[]{:S(2)}, u32[]{:S(2)}) collective-permute-start(bf16[48,1408]{1,0:T(8,128)(2,1)S(1)} %bitcast.65), channel_id=1, source_target_pairs={{0,2},{1,3},{2,0},{3,1},{4,6},{5,7},{6,4},{7,5},{8,10},{9,11},{10,... | collective-permute-start | bytes 405512 | tf_op jit(solution)/shard_map/ppermute | solution.py:38
  14.9 2.7 %collective-permute-start.6 = (bf16[48,1408]{1,0:T(8,128)(2,1)S(1)}, bf16[48,1408]{1,0:T(8,128)(2,1)}, u32[]{:S(2)}, u32[]{:S(2)}) collective-permute-start(bf16[48,1408]{1,0:T(8,128)(2,1)S(1)} %bitcast.64), channel_id=1, source_target_pairs={{0,4},{1,5},{2,6},{3,7},{4,0},{5,1},{6,2},{7,3},{8,12},{9,13},{10,... | collective-permute-start | bytes 405512 | tf_op jit(solution)/shard_map/ppermute | solution.py:38
  17.7 0.9 %fusion.16 = bf16[48,1024]{1,0:T(8,128)(2,1)} fusion(bf16[1024,48]{0,1:T(8,128)(2,1)S(1)} %copy-done.4, bf16[1024]{0:T(1024)(128)(2,1)S(1)} %convert_element_type.25, s32[48]{0:T(128)S(1)} %fusion.28), kind=kOutput, calls=%fused_computation.45 | convolution fusion | flops 4770048 | bytes 198848 | tf_op jit(solution)/shard_map/dot_general | solution.py:47
  18.6 0.9 %collective-permute-start = (bf16[48,1024]{1,0:T(8,128)(2,1)}, bf16[48,1024]{1,0:T(8,128)(2,1)}, u32[]{:S(2)}, u32[]{:S(2)}) collective-permute-start(bf16[48,1024]{1,0:T(8,128)(2,1)} %fusion.16), channel_id=1, source_target_pairs={{0,2},{1,3},{2,0},{3,1},{4,6},{5,7},{6,4},{7,5},{8,10},{9,11},{10,... | collective-permute-start | bytes 294920 | tf_op jit(solution)/shard_map/ppermute | solution.py:38
  19.5 1.4 %collective-permute-done.5 = bf16[48,1408]{1,0:T(8,128)(2,1)} collective-permute-done((bf16[48,1408]{1,0:T(8,128)(2,1)S(1)}, bf16[48,1408]{1,0:T(8,128)(2,1)}, u32[]{:S(2)}, u32[]{:S(2)}) %collective-permute-start.5) | collective-permute-done | bytes 135200 | tf_op jit(solution)/shard_map/ppermute | solution.py:38
  20.8 2.2 %collective-permute-start.1 = (bf16[48,1024]{1,0:T(8,128)(2,1)}, bf16[48,1024]{1,0:T(8,128)(2,1)S(1)}, u32[]{:S(2)}, u32[]{:S(2)}) collective-permute-start(bf16[48,1024]{1,0:T(8,128)(2,1)} %fusion.16), channel_id=1, source_target_pairs={{0,4},{1,5},{2,6},{3,7},{4,0},{5,1},{6,2},{7,3},{8,12},{9,13},{10,... | collective-permute-start | bytes 294920 | tf_op jit(solution)/shard_map/ppermute | solution.py:38
  23.0 5.3 %collective-permute-done.6 = bf16[48,1408]{1,0:T(8,128)(2,1)} collective-permute-done((bf16[48,1408]{1,0:T(8,128)(2,1)S(1)}, bf16[48,1408]{1,0:T(8,128)(2,1)}, u32[]{:S(2)}, u32[]{:S(2)}) %collective-permute-start.6) | collective-permute-done | bytes 135200 | tf_op jit(solution)/shard_map/ppermute | solution.py:38
  28.3 4.6 %collective-permute-start.2 = (bf16[48,1024]{1,0:T(8,128)(2,1)}, bf16[48,1024]{1,0:T(8,128)(2,1)S(1)}, u32[]{:S(2)}, u32[]{:S(2)}) collective-permute-start(bf16[48,1024]{1,0:T(8,128)(2,1)} %fusion.16), channel_id=1, source_target_pairs={{0,6},{1,7},{2,4},{3,5},{4,2},{5,3},{6,0},{7,1},{8,14},{9,15},{10,... | collective-permute-start | bytes 294920 | tf_op jit(solution)/shard_map/ppermute | solution.py:38
  32.9 0.9 %convert_reduce_fusion = s32[192]{0:T(256)S(1)} fusion(bf16[48,1408]{1,0:T(8,128)(2,1)} %collective-permute-done.7, bf16[48,1408]{1,0:T(8,128)(2,1)} %collective-permute-done.6, bf16[48,1408]{1,0:T(8,128)(2,1)} %collective-permute-done.5, bf16[48,1408]{1,0:T(8,128)(2,1)S(1)} %bitcast.60), kind=kLoop, calls=%fused_computation.43 | loop fusion | flops 1536 | bytes 541440 | tf_op jit(solution)/shard_map/convert_element_type | solution.py:70
  33.8 1.3 %fusion.3 = f32[192,1280]{1,0:T(8,128)S(1)} fusion(bf16[48,1408]{1,0:T(8,128)(2,1)} %collective-permute-done.7, bf16[48,1408]{1,0:T(8,128)(2,1)} %collective-permute-done.6, bf16[48,1408]{1,0:T(8,128)(2,1)} %collective-permute-done.5, bf16[48,1408]{1,0:T(8,128)(2,1)S(1)} %bitcast.61, s32[192]{0:T(256)S(1)} %compare_select_fusion.3), kind=kOutput, calls=%fused_computation.10 | convolution fusion | flops 96374784 | bytes 1524480 | tf_op jit(solution)/shard_map/dot_general | solution.py:74
  35.1 0.2 broadcast_select_fusion.1
  35.3 2.0 %collective-permute-done.1 = bf16[48,1024]{1,0:T(8,128)(2,1)S(1)} collective-permute-done((bf16[48,1024]{1,0:T(8,128)(2,1)}, bf16[48,1024]{1,0:T(8,128)(2,1)S(1)}, u32[]{:S(2)}, u32[]{:S(2)}) %collective-permute-start.1) | collective-permute-done | bytes 98336 | tf_op jit(solution)/shard_map/ppermute | solution.py:38
  37.4 1.6 %convolution_add_fusion = f32[192,1280]{1,0:T(8,128)S(1)} fusion(f32[192,1280]{1,0:T(8,128)S(1)} %fusion.3, bf16[1024,640]{1,0:T(8,128)(2,1)S(1)} %get-tuple-element.9, bf16[1024,640]{1,0:T(8,128)(2,1)S(1)} %get-tuple-element.8, bf16[48,1024]{1,0:T(8,128)(2,1)S(1)} %collective-permute-done.2, bf16[48,1024]{1,0:T(8,128)(2,1)S(1)} %collective-permute-done.1, ...), kind=kOutput, calls=%fused_computation | convolution fusion | flops 510377984 | bytes 4980736 | tf_op jit(solution)/shard_map/dot_general | solution.py:73
  39.2 2.5 %collective-permute-start.10 = (f32[48,1280]{1,0:T(8,128)S(1)}, f32[48,1280]{1,0:T(8,128)S(1)}, u32[]{:S(2)}, u32[]{:S(2)}) collective-permute-start(f32[48,1280]{1,0:T(8,128)S(1)} %reshape_squeeze.16), channel_id=1, source_target_pairs={{0,24},{8,16},{16,8},{24,0},{1,25},{9,17},{17,9},{25,1},{2,26},{10... | collective-permute-start | bytes 737288 | tf_op jit(solution)/shard_map/ppermute | solution.py:41
  41.8 0.6 collective-permute-start.8
  42.4 0.6 collective-permute-start.9
  43.0 4.4 %collective-permute-done.10 = f32[48,1280]{1,0:T(8,128)S(1)} collective-permute-done((f32[48,1280]{1,0:T(8,128)S(1)}, f32[48,1280]{1,0:T(8,128)S(1)}, u32[]{:S(2)}, u32[]{:S(2)}) %collective-permute-start.10) | collective-permute-done | bytes 245792 | tf_op jit(solution)/shard_map/ppermute | solution.py:41
  47.4 2.7 %collective-permute-done.8 = f32[48,1280]{1,0:T(8,128)S(1)} collective-permute-done((f32[48,1280]{1,0:T(8,128)S(1)}, f32[48,1280]{1,0:T(8,128)S(1)}, u32[]{:S(2)}, u32[]{:S(2)}) %collective-permute-start.8) | collective-permute-done | bytes 245792 | tf_op jit(solution)/shard_map/ppermute | solution.py:41
  50.2 0.1 reshape.173
  50.4 3.7 %collective-permute-start.11 = (f32[24,640]{1,0:T(8,128)S(1)}, f32[24,640]{1,0:T(8,128)S(1)}, u32[]{:S(2)}, u32[]{:S(2)}) collective-permute-start(f32[24,640]{1,0:T(8,128)S(1)} %squeeze.53), channel_id=1, source_target_pairs={{0,2},{1,3},{2,0},{3,1},{4,6},{5,7},{6,4},{7,5},{8,10},{9,11},{10,... | collective-permute-start | bytes 184328 | tf_op jit(solution)/shard_map/ppermute | solution.py:38
  54.1 1.2 %collective-permute-start.12 = (f32[24,640]{1,0:T(8,128)S(1)}, f32[24,640]{1,0:T(8,128)S(1)}, u32[]{:S(2)}, u32[]{:S(2)}) collective-permute-start(f32[24,640]{1,0:T(8,128)S(1)} %squeeze.54), channel_id=1, source_target_pairs={{0,4},{1,5},{2,6},{3,7},{4,0},{5,1},{6,2},{7,3},{8,12},{9,13},{10,... | collective-permute-start | bytes 184328 | tf_op jit(solution)/shard_map/ppermute | solution.py:38
  55.3 1.5 %collective-permute-start.13 = (f32[24,640]{1,0:T(8,128)S(1)}, f32[24,640]{1,0:T(8,128)S(1)}, u32[]{:S(2)}, u32[]{:S(2)}) collective-permute-start(f32[24,640]{1,0:T(8,128)S(1)} %squeeze.55), channel_id=1, source_target_pairs={{0,6},{1,7},{2,4},{3,5},{4,2},{5,3},{6,0},{7,1},{8,14},{9,15},{10,... | collective-permute-start | bytes 184328 | tf_op jit(solution)/shard_map/ppermute | solution.py:38
  56.9 3.8 %collective-permute-done.12 = f32[24,640]{1,0:T(8,128)S(1)} collective-permute-done((f32[24,640]{1,0:T(8,128)S(1)}, f32[24,640]{1,0:T(8,128)S(1)}, u32[]{:S(2)}, u32[]{:S(2)}) %collective-permute-start.12) | collective-permute-done | bytes 61472 | tf_op jit(solution)/shard_map/ppermute | solution.py:38
  60.7 0.8 %collective-permute-done.13 = f32[24,640]{1,0:T(8,128)S(1)} collective-permute-done((f32[24,640]{1,0:T(8,128)S(1)}, f32[24,640]{1,0:T(8,128)S(1)}, u32[]{:S(2)}, u32[]{:S(2)}) %collective-permute-start.13) | collective-permute-done | bytes 61472 | tf_op jit(solution)/shard_map/ppermute | solution.py:38
  61.7 0.2 reshape.174
  62.0 0.2 constant_dynamic-slice_fusion.7
  62.2 0.2 copy-done.1
  62.7 1.1 %fusion.33 = (bf16[12,5120]{1,0:T(8,128)(2,1)S(1)}, f32[12,5120]{1,0:T(8,128)}, f32[12,5120]{1,0:T(8,128)}, f32[12,5120]{1,0:T(8,128)}) fusion(f32[12,5120]{1,0:T(8,128)S(1)} %copy-done.1, f32[12,1280]{1,0:T(8,128)S(1)} %get-tuple-element.34, f32[12,1280]{1,0:T(8,128)S(1)} %get-tuple-element.35, f32[12,1280]{1,0:T(8,128)S(1)} %get-tuple-element.36, ...), kind=kLoop, calls=%fused_computation.98 | loop fusion | flops 1167360 | bytes 1843200 | tf_op jit(solution)/shard_map/convert_element_type | solution.py:91
  63.9 1.9 %collective-permute-start.15 = (bf16[48,1280]{1,0:T(8,128)(2,1)S(1)}, bf16[48,1280]{1,0:T(8,128)(2,1)S(1)}, u32[]{:S(2)}, u32[]{:S(2)}) collective-permute-start(bf16[48,1280]{1,0:T(8,128)(2,1)S(1)} %reshape.176), channel_id=1, source_target_pairs={{0,16},{8,24},{16,0},{24,8},{1,17},{9,25},{17,1},{25,9},{2,18},{10... | collective-permute-start | bytes 368648 | tf_op jit(solution)/shard_map/ppermute | solution.py:41
  65.9 1.1 %collective-permute-start.16 = (bf16[48,1280]{1,0:T(8,128)(2,1)S(1)}, bf16[48,1280]{1,0:T(8,128)(2,1)S(1)}, u32[]{:S(2)}, u32[]{:S(2)}) collective-permute-start(bf16[48,1280]{1,0:T(8,128)(2,1)S(1)} %reshape.176), channel_id=1, source_target_pairs={{0,24},{8,16},{16,8},{24,0},{1,25},{9,17},{17,9},{25,1},{2,26},{10... | collective-permute-start | bytes 368648 | tf_op jit(solution)/shard_map/ppermute | solution.py:41
  67.0 0.5 collective-permute-start.14
  67.5 2.5 %collective-permute-done.15 = bf16[48,1280]{1,0:T(8,128)(2,1)S(1)} collective-permute-done((bf16[48,1280]{1,0:T(8,128)(2,1)S(1)}, bf16[48,1280]{1,0:T(8,128)(2,1)S(1)}, u32[]{:S(2)}, u32[]{:S(2)}) %collective-permute-start.15) | collective-permute-done | bytes 122912 | tf_op jit(solution)/shard_map/ppermute | solution.py:41
  70.0 1.6 %collective-permute-done.16 = bf16[48,1280]{1,0:T(8,128)(2,1)S(1)} collective-permute-done((bf16[48,1280]{1,0:T(8,128)(2,1)S(1)}, bf16[48,1280]{1,0:T(8,128)(2,1)S(1)}, u32[]{:S(2)}, u32[]{:S(2)}) %collective-permute-start.16) | collective-permute-done | bytes 122912 | tf_op jit(solution)/shard_map/ppermute | solution.py:41
  71.6 0.2 collective-permute-done.14
  72.0 0.3 copy.36
  72.3 0.3 copy.37
  72.6 0.8 %copy.46 = bf16[6,8,4,1280]{3,1,2,0:T(8,128)(2,1)} copy(bf16[6,8,4,1280]{3,2,1,0:T(4,128)(2,1)S(1)} %bitcast.55) | data formatting | bytes 983040
  (60 shorter events, 2.1 us)
Async XLA Ops:
  4.4 3.2 %copy-start = (bf16[1024,640]{1,0:T(8,128)(2,1)S(1)}, bf16[1024,640]{1,0:T(8,128)(2,1)}, u32[]{:S(2)}) copy-start(bf16[1024,640]{1,0:T(8,128)(2,1)} %param.9) | copy-start | bytes 3932164
  5.9 1.8 %copy-start.5 = (s32[1024]{0:T(1024)S(1)}, s32[1024]{0:T(1024)}, u32[]{:S(2)}) copy-start(s32[1024]{0:T(1024)} %param.11) | copy-start | bytes 12292
  7.1 2.0 %collective-permute-start.4 = (bf16[4,6,4,1408]{3,2,1,0:T(4,128)(2,1)}, bf16[4,6,4,1408]{3,2,1,0:T(4,128)(2,1)}, u32[]{:S(2)}, u32[]{:S(2)}) collective-permute-start(bf16[4,6,4,1408]{3,2,1,0:T(4,128)(2,1)} %bitcast.46), channel_id=1, source_target_pairs={{0,1},{1,0},{2,3},{3,2},{4,5},{5,4},{6,7},{7,6},{8,9},{9,8},{10,11... | collective-permute-start | bytes 811016 | tf_op jit(solution)/shard_map/ppermute | solution.py:35
  7.5 27.5 %collective-permute-start.3 = (bf16[1024,640]{1,0:T(8,128)(2,1)S(1)}, bf16[1024,640]{1,0:T(8,128)(2,1)S(1)}, u32[]{:S(2)}, u32[]{:S(2)}) collective-permute-start(bf16[1024,640]{1,0:T(8,128)(2,1)S(1)} %copy-done), channel_id=1, source_target_pairs={{0,1},{1,0},{2,3},{3,2},{4,5},{5,4},{6,7},{7,6},{8,9},{9,8},{10,11... | collective-permute-start | bytes 3932168 | tf_op jit(solution)/shard_map/ppermute | solution.py:35
  10.4 7.3 %copy-start.4 = (bf16[1024,48]{0,1:T(8,128)(2,1)S(1)}, bf16[1024,48]{0,1:T(8,128)(2,1)}, u32[]{:S(2)}) copy-start(bf16[1024,48]{0,1:T(8,128)(2,1)} %param.10) | copy-start | bytes 294916
  11.6 9.3 %collective-permute-start.5 = (bf16[48,1408]{1,0:T(8,128)(2,1)S(1)}, bf16[48,1408]{1,0:T(8,128)(2,1)}, u32[]{:S(2)}, u32[]{:S(2)}) collective-permute-start(bf16[48,1408]{1,0:T(8,128)(2,1)S(1)} %bitcast.65), channel_id=1, source_target_pairs={{0,2},{1,3},{2,0},{3,1},{4,6},{5,7},{6,4},{7,5},{8,10},{9,11},{10,... | collective-permute-start | bytes 405512 | tf_op jit(solution)/shard_map/ppermute | solution.py:38
  14.9 13.4 %collective-permute-start.6 = (bf16[48,1408]{1,0:T(8,128)(2,1)S(1)}, bf16[48,1408]{1,0:T(8,128)(2,1)}, u32[]{:S(2)}, u32[]{:S(2)}) collective-permute-start(bf16[48,1408]{1,0:T(8,128)(2,1)S(1)} %bitcast.64), channel_id=1, source_target_pairs={{0,4},{1,5},{2,6},{3,7},{4,0},{5,1},{6,2},{7,3},{8,12},{9,13},{10,... | collective-permute-start | bytes 405512 | tf_op jit(solution)/shard_map/ppermute | solution.py:38
  17.6 15.3 %collective-permute-start.7 = (bf16[48,1408]{1,0:T(8,128)(2,1)S(1)}, bf16[48,1408]{1,0:T(8,128)(2,1)}, u32[]{:S(2)}, u32[]{:S(2)}) collective-permute-start(bf16[48,1408]{1,0:T(8,128)(2,1)S(1)} %bitcast.63), channel_id=1, source_target_pairs={{0,6},{1,7},{2,4},{3,5},{4,2},{5,3},{6,0},{7,1},{8,14},{9,15},{10,... | collective-permute-start | bytes 405512 | tf_op jit(solution)/shard_map/ppermute | solution.py:38
  18.6 16.8 %collective-permute-start = (bf16[48,1024]{1,0:T(8,128)(2,1)}, bf16[48,1024]{1,0:T(8,128)(2,1)}, u32[]{:S(2)}, u32[]{:S(2)}) collective-permute-start(bf16[48,1024]{1,0:T(8,128)(2,1)} %fusion.16), channel_id=1, source_target_pairs={{0,2},{1,3},{2,0},{3,1},{4,6},{5,7},{6,4},{7,5},{8,10},{9,11},{10,... | collective-permute-start | bytes 294920 | tf_op jit(solution)/shard_map/ppermute | solution.py:38
  20.8 16.5 %collective-permute-start.1 = (bf16[48,1024]{1,0:T(8,128)(2,1)}, bf16[48,1024]{1,0:T(8,128)(2,1)S(1)}, u32[]{:S(2)}, u32[]{:S(2)}) collective-permute-start(bf16[48,1024]{1,0:T(8,128)(2,1)} %fusion.16), channel_id=1, source_target_pairs={{0,4},{1,5},{2,6},{3,7},{4,0},{5,1},{6,2},{7,3},{8,12},{9,13},{10,... | collective-permute-start | bytes 294920 | tf_op jit(solution)/shard_map/ppermute | solution.py:38
  28.3 9.1 %collective-permute-start.2 = (bf16[48,1024]{1,0:T(8,128)(2,1)}, bf16[48,1024]{1,0:T(8,128)(2,1)S(1)}, u32[]{:S(2)}, u32[]{:S(2)}) collective-permute-start(bf16[48,1024]{1,0:T(8,128)(2,1)} %fusion.16), channel_id=1, source_target_pairs={{0,6},{1,7},{2,4},{3,5},{4,2},{5,3},{6,0},{7,1},{8,14},{9,15},{10,... | collective-permute-start | bytes 294920 | tf_op jit(solution)/shard_map/ppermute | solution.py:38
  39.2 8.2 %collective-permute-start.10 = (f32[48,1280]{1,0:T(8,128)S(1)}, f32[48,1280]{1,0:T(8,128)S(1)}, u32[]{:S(2)}, u32[]{:S(2)}) collective-permute-start(f32[48,1280]{1,0:T(8,128)S(1)} %reshape_squeeze.16), channel_id=1, source_target_pairs={{0,24},{8,16},{16,8},{24,0},{1,25},{9,17},{17,9},{25,1},{2,26},{10... | collective-permute-start | bytes 737288 | tf_op jit(solution)/shard_map/ppermute | solution.py:41
  41.8 8.3 %collective-permute-start.8 = (f32[48,1280]{1,0:T(8,128)S(1)}, f32[48,1280]{1,0:T(8,128)S(1)}, u32[]{:S(2)}, u32[]{:S(2)}) collective-permute-start(f32[48,1280]{1,0:T(8,128)S(1)} %reshape_squeeze.14), channel_id=1, source_target_pairs={{0,8},{8,0},{16,24},{24,16},{1,9},{9,1},{17,25},{25,17},{2,10},{10... | collective-permute-start | bytes 737288 | tf_op jit(solution)/shard_map/ppermute | solution.py:41
  42.4 7.7 %collective-permute-start.9 = (f32[48,1280]{1,0:T(8,128)S(1)}, f32[48,1280]{1,0:T(8,128)S(1)}, u32[]{:S(2)}, u32[]{:S(2)}) collective-permute-start(f32[48,1280]{1,0:T(8,128)S(1)} %reshape_squeeze.15), channel_id=1, source_target_pairs={{0,16},{8,24},{16,0},{24,8},{1,17},{9,25},{17,1},{25,9},{2,18},{10... | collective-permute-start | bytes 737288 | tf_op jit(solution)/shard_map/ppermute | solution.py:41
  50.4 6.5 %collective-permute-start.11 = (f32[24,640]{1,0:T(8,128)S(1)}, f32[24,640]{1,0:T(8,128)S(1)}, u32[]{:S(2)}, u32[]{:S(2)}) collective-permute-start(f32[24,640]{1,0:T(8,128)S(1)} %squeeze.53), channel_id=1, source_target_pairs={{0,2},{1,3},{2,0},{3,1},{4,6},{5,7},{6,4},{7,5},{8,10},{9,11},{10,... | collective-permute-start | bytes 184328 | tf_op jit(solution)/shard_map/ppermute | solution.py:38
  54.1 6.5 %collective-permute-start.12 = (f32[24,640]{1,0:T(8,128)S(1)}, f32[24,640]{1,0:T(8,128)S(1)}, u32[]{:S(2)}, u32[]{:S(2)}) collective-permute-start(f32[24,640]{1,0:T(8,128)S(1)} %squeeze.54), channel_id=1, source_target_pairs={{0,4},{1,5},{2,6},{3,7},{4,0},{5,1},{6,2},{7,3},{8,12},{9,13},{10,... | collective-permute-start | bytes 184328 | tf_op jit(solution)/shard_map/ppermute | solution.py:38
  55.3 6.2 %collective-permute-start.13 = (f32[24,640]{1,0:T(8,128)S(1)}, f32[24,640]{1,0:T(8,128)S(1)}, u32[]{:S(2)}, u32[]{:S(2)}) collective-permute-start(f32[24,640]{1,0:T(8,128)S(1)} %squeeze.55), channel_id=1, source_target_pairs={{0,6},{1,7},{2,4},{3,5},{4,2},{5,3},{6,0},{7,1},{8,14},{9,15},{10,... | collective-permute-start | bytes 184328 | tf_op jit(solution)/shard_map/ppermute | solution.py:38
  61.5 1.0 %copy-start.1 = (f32[12,5120]{1,0:T(8,128)S(1)}, f32[12,5120]{1,0:T(8,128)}, u32[]{:S(2)}) copy-start(f32[12,5120]{1,0:T(8,128)} %param.15) | copy-start | bytes 737284
  61.5 1.1 %copy-start.2 = (f32[12,5120]{1,0:T(8,128)S(1)}, f32[12,5120]{1,0:T(8,128)}, u32[]{:S(2)}) copy-start(f32[12,5120]{1,0:T(8,128)} %param.16) | copy-start | bytes 737284
  61.5 1.2 %copy-start.3 = (f32[12,5120]{1,0:T(8,128)S(1)}, f32[12,5120]{1,0:T(8,128)}, u32[]{:S(2)}) copy-start(f32[12,5120]{1,0:T(8,128)} %param.17) | copy-start | bytes 737284
  63.9 6.1 %collective-permute-start.15 = (bf16[48,1280]{1,0:T(8,128)(2,1)S(1)}, bf16[48,1280]{1,0:T(8,128)(2,1)S(1)}, u32[]{:S(2)}, u32[]{:S(2)}) collective-permute-start(bf16[48,1280]{1,0:T(8,128)(2,1)S(1)} %reshape.176), channel_id=1, source_target_pairs={{0,16},{8,24},{16,0},{24,8},{1,17},{9,25},{17,1},{25,9},{2,18},{10... | collective-permute-start | bytes 368648 | tf_op jit(solution)/shard_map/ppermute | solution.py:41
  65.9 5.8 %collective-permute-start.16 = (bf16[48,1280]{1,0:T(8,128)(2,1)S(1)}, bf16[48,1280]{1,0:T(8,128)(2,1)S(1)}, u32[]{:S(2)}, u32[]{:S(2)}) collective-permute-start(bf16[48,1280]{1,0:T(8,128)(2,1)S(1)} %reshape.176), channel_id=1, source_target_pairs={{0,24},{8,16},{16,8},{24,0},{1,25},{9,17},{17,9},{25,1},{2,26},{10... | collective-permute-start | bytes 368648 | tf_op jit(solution)/shard_map/ppermute | solution.py:41
  67.0 4.9 %collective-permute-start.14 = (bf16[48,1280]{1,0:T(8,128)(2,1)S(1)}, bf16[48,1280]{1,0:T(8,128)(2,1)S(1)}, u32[]{:S(2)}, u32[]{:S(2)}) collective-permute-start(bf16[48,1280]{1,0:T(8,128)(2,1)S(1)} %reshape.176), channel_id=1, source_target_pairs={{0,8},{8,0},{16,24},{24,16},{1,9},{9,1},{17,25},{25,17},{2,10},{10... | collective-permute-start | bytes 368648 | tf_op jit(solution)/shard_map/ppermute | solution.py:41

commit v3 on v2

--- a/solution.py
+++ b/solution.py
@@ -1,14 +1,251 @@
+import functools
+
 import jax
 import jax.numpy as jnp
 from jax import lax
+from jax.experimental import pallas as pl
+from jax.experimental.pallas import tpu as pltpu
 from jax.sharding import PartitionSpec as P
 
 STEP = 8
 CORES = 2
 LANES = 128
-
-
-def local(
+VMEM_LIMIT = 24 * 1024 * 1024
+
+
+def place():
+    here = lax.axis_index("vocab")
+    return lax.axis_index("dp"), lax.shift_right_logical(here, 1), here & 1
+
+
+def iota(shape, axis):
+    return lax.broadcasted_iota(jnp.int32, shape, axis)
+
+
+def over(x, n):
+    return ((x.astype(jnp.float32) + 0.5) * (1.0 / n)).astype(jnp.int32)
+
+
+def one_hot(flag):
+    return jnp.where(flag, 1.0, 0.0).astype(jnp.bfloat16)
+
+
+def exact(left, right):
+    return jnp.dot(left, right, preferred_element_type=jnp.float32)
+
+
+def slots_kernel(chips, dp, shard, slots_ref, rows_ref, counts_ref, *out_refs):
+    d, z, core = place()
+    cap, owners = rows_ref.shape[0], rows_ref.shape[2]
+    count = cap * owners
+    group = cap * chips
+    width = slots_ref.shape[1] // chips
+    own_lane = iota((count, owners), 1) == iota((count, owners), 0) % owners
+    rows = jnp.broadcast_to(rows_ref[...], (cap, owners, owners)).reshape(count, owners)
+    rows = jnp.sum(jnp.where(own_lane, rows, 0), axis=1, keepdims=True)
+    live = jnp.broadcast_to(counts_ref[...], (count, owners))
+    live = jnp.sum(jnp.where(own_lane, live, 0), axis=1, keepdims=True)
+    block = over(rows, shard)
+    ids = (block ^ d) * shard + rows - block * shard
+    ids = jnp.where(over(iota((count, 1), 0), owners) < live, ids, -1)
+    ids = jnp.broadcast_to(ids, (count, LANES)).astype(jnp.bfloat16)
+    for away in range(CORES):
+        q = iota((group, count), 0)
+        slot = over(q, chips)
+        wanted = slot * owners + (q - slot * chips) * CORES + (core ^ away)
+        pick = one_hot(iota((group, count), 1) == wanted)
+        picked_ids = exact(pick, ids).astype(jnp.bfloat16)
+        for s in range(chips):
+            start = pl.multiple_of((z ^ s) * width, LANES)
+            out_ref = out_refs[away * chips + s]
+            out_ref[:, :width] = exact(pick, slots_ref[:, pl.ds(start, width)]).astype(jnp.bfloat16)
+            out_ref[:, width:] = picked_ids
+
+
+def head_kernel(chips, dp, shard, mask_ref, own_ref, other_ref, *refs):
+    d, z, core = place()
+    parts, out_ref = refs[:-1], refs[-1]
+    rows = dp * shard
+    total = chips * rows
+    cols = own_ref.shape[1]
+    mask = mask_ref[...].astype(jnp.float32).astype(jnp.bfloat16)
+    columns = jnp.concatenate([part[...] for part in parts], axis=0) * mask
+    r = iota((total, total), 0)
+    t = over(r, chips * shard)
+    s = over(r - t * (chips * shard), shard)
+    i = r - t * (chips * shard) - s * shard
+    order = one_hot(iota((total, total), 1) == s * rows + (t ^ d) * shard + i)
+    columns = exact(order, columns).astype(jnp.bfloat16)
+    out_ref[:, pl.ds(pl.multiple_of(core * cols, LANES), cols)] = exact(columns, own_ref[...])
+    out_ref[:, pl.ds(pl.multiple_of((1 - core) * cols, LANES), cols)] = exact(columns, other_ref[...])
+
+
+def embed_kernel(chips, dp, shard, head_ref, *refs):
+    d, z, core = place()
+    slot_refs, out_refs = refs[:-dp], refs[-dp:]
+    total, cols = head_ref.shape
+    count = len(slot_refs) * slot_refs[0].shape[0]
+    ids = jnp.concatenate([ref[:, cols:].astype(jnp.float32) for ref in slot_refs], axis=0)
+    ids = ids[:, :1].astype(jnp.int32)
+    values = jnp.concatenate([ref[:, :cols].astype(jnp.float32) for ref in slot_refs], axis=0)
+    values = values.astype(jnp.bfloat16)
+    block = over(jnp.maximum(ids, 0), shard)
+    owner = (iota((count, 1), 0) % chips) ^ z
+    target = (block * chips + owner) * shard + ids - block * shard
+    target = jnp.where(ids < 0, -1, target)
+    picked = one_hot(iota((count, total), 1) == target)
+    embed = lax.dot_general(picked, values, (((0,), (0,)), ((), ())), preferred_element_type=jnp.float32)
+    part = head_ref[...] + embed
+    size = chips * shard
+    for t, out_ref in enumerate(out_refs):
+        out_ref[...] = part[t * size : (t + 1) * size]
+
+
+def sum_kernel(chips, shard, *refs):
+    dp = len(refs) - chips
+    total = refs[0][...]
+    for t in range(1, dp):
+        total = total + refs[t][...]
+    half = total.shape[1] // CORES
+    for s, out_ref in enumerate(refs[dp:]):
+        rows = total[s * shard : (s + 1) * shard]
+        out_ref[...] = jnp.concatenate([rows[:, :half], rows[:, half:]], axis=0)
+
+
+def adam_kernel(chips, shard, master_ref, first_ref, second_ref, *refs):
+    d, z, core = place()
+    pieces, (master_out, first_out, second_out, table_ref) = refs[:chips], refs[chips:]
+    half = pieces[0].shape[1]
+    table = []
+    for s, piece in enumerate(pieces):
+        piece = piece[...]
+        gradient = jnp.concatenate([piece[:shard], piece[shard:]], axis=1)
+        spot = pl.ds(pl.multiple_of((z ^ s) * (CORES * half), LANES), CORES * half)
+        master = master_ref[:, spot]
+        first_new = 0.9 * first_ref[:, spot] + 0.1 * gradient
+        second_new = 0.95 * second_ref[:, spot] + 0.05 * gradient * gradient
+        first_hat = first_new / (1.0 - 0.9**STEP)
+        second_hat = second_new / (1.0 - 0.95**STEP)
+        master_new = master - 0.05 * (first_hat / (jnp.sqrt(second_hat) + 1e-08) + 0.1 * master)
+        master_out[:, spot] = master_new
+        first_out[:, spot] = first_new
+        second_out[:, spot] = second_new
+        table.append(master_new)
+    table_ref[...] = jnp.concatenate(table, axis=0).astype(jnp.bfloat16)
+
+
+def table_kernel(chips, shard, *refs):
+    d, z, core = place()
+    parts, out_ref = refs[:-1], refs[-1]
+    dp = len(parts)
+    cols = parts[0].shape[1]
+    rows = dp * shard
+    total = chips * rows
+    values = jnp.concatenate([part[...] for part in parts], axis=0)
+    r = iota((total, total), 0)
+    s = over(r, rows)
+    e = over(r - s * rows, shard)
+    i = r - s * rows - e * shard
+    order = one_hot(iota((total, total), 1) == ((e ^ d) * chips + s) * shard + i)
+    values = exact(order, values).astype(jnp.bfloat16)
+    for s in range(chips):
+        spot = pl.ds(pl.multiple_of((z ^ s) * cols, LANES), cols)
+        out_ref[:, spot] = values[s * rows : (s + 1) * rows]
+
+
+def shaped(shape, kind):
+    return jax.ShapeDtypeStruct(shape, kind)
+
+
+def run(kernel, outs, *args, flops=0):
+    moved = sum(x.size * x.dtype.itemsize for x in (*args, *jax.tree.leaves(outs)))
+    return pl.pallas_call(
+        kernel,
+        out_shape=outs,
+        cost_estimate=pl.CostEstimate(flops=flops, bytes_accessed=moved, transcendentals=0),
+        compiler_params=pltpu.CompilerParams(vmem_limit_bytes=VMEM_LIMIT),
+    )(*args)
+
+
+def aligned(
+    hidden,
+    logit_grad,
+    predict_mask,
+    slot_grads,
+    slot_rows,
+    slot_counts,
+    master,
+    first_moment,
+    second_moment,
+):
+    vocab = lax.axis_size("vocab")
+    dp = lax.axis_size("dp")
+    chips = vocab // CORES
+    rows = logit_grad.shape[1]
+    shard = master.shape[0]
+    cols = hidden.shape[1] * CORES
+    depth = hidden.shape[0]
+    owners, cap, width = slot_grads.shape[1:]
+    sizes = (chips, dp, shard)
+    bf16, f32 = jnp.bfloat16, jnp.float32
+
+    def send(x, s, away=0):
+        move = s * CORES + away
+        return lax.ppermute(x, "vocab", [(v, v ^ move) for v in range(vocab)]) if move else x
+
+    def send_dp(x, t):
+        return lax.ppermute(x, "dp", [(i, i ^ t) for i in range(dp)]) if t else x
+
+    columns = logit_grad.T
+    columns = [send(columns, s) for s in range(chips)]
+    hidden_other = send(hidden, 0, 1)
+    messages = run(
+        functools.partial(slots_kernel, *sizes),
+        [shaped((cap * chips, cols + LANES), bf16)] * (CORES * chips),
+        slot_grads[0].transpose(1, 0, 2).reshape(cap * owners, width),
+        slot_rows.transpose(2, 0, 1),
+        slot_counts,
+    )
+    arrived = [send(messages[away * chips + s], s, away) for s in range(chips) for away in range(CORES)]
+    head = run(
+        functools.partial(head_kernel, *sizes),
+        shaped((chips * rows, cols), f32),
+        predict_mask[None, :],
+        hidden,
+        hidden_other,
+        *columns,
+        flops=2 * chips * rows * depth * cols,
+    )
+    parts = run(
+        functools.partial(embed_kernel, *sizes),
+        [shaped((chips * shard, cols), f32)] * dp,
+        head,
+        *arrived,
+    )
+    parts = [send_dp(parts[t], t) for t in range(dp)]
+    pieces = run(
+        functools.partial(sum_kernel, chips, shard),
+        [shaped((CORES * shard, cols // CORES), f32)] * chips,
+        *parts,
+    )
+    pieces = [send(pieces[s], s) for s in range(chips)]
+    master_new, first_new, second_new, table = run(
+        functools.partial(adam_kernel, chips, shard),
+        [shaped(master.shape, f32)] * 3 + [shaped((chips * shard, cols), bf16)],
+        master,
+        first_moment,
+        second_moment,
+        *pieces,
+    )
+    table = run(
+        functools.partial(table_kernel, chips, shard),
+        shaped((rows, width), bf16),
+        *[send_dp(table, t) for t in range(dp)],
+    )
+    return (master_new, first_new, second_new, table)
+
+
+def plain(
     hidden,
     logit_grad,
     predict_mask,
@@ -96,6 +333,14 @@
     return (master_new, first_new, second_new, table)
 
 
+def local(hidden, logit_grad, predict_mask, slot_grads, *rest):
+    vocab = lax.axis_size("vocab")
+    fits = hidden.shape[1] % LANES == 0 and logit_grad.shape[1] % 16 == 0
+    fits = fits and (vocab // CORES * slot_grads.shape[2]) % 8 == 0
+    step = aligned if fits else plain
+    return step(hidden, logit_grad, predict_mask, slot_grads, *rest)
+
+
 def solution(mesh):
     in_specs = (
         P("dp", "vocab"),

time: 73.8 us -> 63.1 us (0.86)
  other arithmetic: 6.15 us -> 0 us
  Pallas kernels: 0 us -> 4.26 us
  matrix products: 3.81 us -> 0 us
  starting transfers between devices: 27.9 us -> 24.7 us
  local copies, waits for them, and re-layouts: 8.47 us -> 5.28 us
  waiting for transfers between devices: 26 us -> 27.8 us
    pallas_call x0 -> x6, Pallas kernels: none -> 4.26 us  [run(): pl.pallas_call(kernel, out_shape=outs, cost_estimate=pl.CostEstimate(flop...]
    dot_general x3 -> x0, matrix products: 3.81 us -> none  [the longest x1 1.63 us: local(): jnp.dot(jnp.concatenate(masked, axis=0), wide, preferred_element_type=jnp...]
    ppermute x17 -> x20, starting transfers between devices: 27.9 us -> 24.7 us  [the longest x14 17.7 us: send(): lax.ppermute(x, 'vocab', [(v, v ^ move) for v in range(vocab)])]
    unnamed x21 -> x18, local copies, waits for them, and re-layouts: 2.68 us -> 5.28 us
    dynamic_slice x5 -> x0, local copies, waits for them, and re-layouts: 2.28 us -> none  [the longest x1 1.12 us: local(): lax.dynamic_index_in_dim(both, z ^ s, 1, keepdims=False)]
    convert_element_type x4 -> x0, other arithmetic: 2.04 us -> none  [the longest x1 1.1 us: local(): table = master_new.astype(jnp.bfloat16)]
    ppermute x17 -> x20, waiting for transfers between devices: 26 us -> 27.8 us  [the longest x6 16.3 us: send_dp(): return lax.ppermute(x, 'dp', [(i, i ^ t) for i in range(dp)]) if t else x]
    concatenate x1 -> x0, local copies, waits for them, and re-layouts: 1.5 us -> none  [local(): jnp.concatenate([slots, ids], axis=3)]
  transfers between devices with their start and end apart: 17 -> 20, of which waited for: 11 -> 10; matrix products, arithmetic and copies ran while one was open for 8% -> 0% of each run, Pallas kernels for 0% -> 2%
where the time goes in v3:
time: 63.1 us; the launch traced here: 62.8 us
  waiting for transfers between devices  27.8 us (44%)
  starting transfers between devices  24.7 us (39%)
  local copies, waits for them, and re-layouts  5.28 us (8%)
  Pallas kernels  4.26 us (7%)
  between operations  0.75 us (1%)
    ppermute x14, starting transfers between devices, send(): lax.ppermute(x, 'vocab', [(v, v ^ move) for v in range(vocab)])  17.7 us
    ppermute x6, waiting for transfers between devices, send_dp(): return lax.ppermute(x, 'dp', [(i, i ^ t) for i in range(dp)]) if t else x  16.3 us
    ppermute x14, waiting for transfers between devices, send(): lax.ppermute(x, 'vocab', [(v, v ^ move) for v in range(vocab)])  11.5 us
    ppermute x6, starting transfers between devices, send_dp(): return lax.ppermute(x, 'dp', [(i, i ^ t) for i in range(dp)]) if t else x  7.04 us
    unnamed x18, local copies, waits for them, and re-layouts  5.28 us
    pallas_call x6, Pallas kernels, run(): pl.pallas_call(kernel, out_shape=outs, cost_estimate=pl.CostEstimate(flop...  4.26 us
  transfers between devices with their start and end apart: 20, of which 10 were waited for; matrix products, arithmetic and copies ran while one was open for 0% of the time, Pallas kernels for 2%

profile of v3, /device:TPU:0, one launch (start us, length us, event | category | flops | bytes accessed | tf_op | source)
XLA Modules:
  0.0 62.8 jit_solution(13692190921176753998)
XLA Ops:
  0.6 0.5 collective-permute-start
  1.2 1.0 %copy-done.1 = bf16[1,8,6,5120]{3,1,2,0:T(8,128)(2,1)S(1)} copy-done((bf16[1,8,6,5120]{3,1,2,0:T(8,128)(2,1)S(1)}, bf16[1,8,6,5120]{3,1,2,0:T(8,128)(2,1)}, u32[]{:S(2)}) %copy-start.1) | copy-done | bytes 491544
  2.2 0.7 %copy-done.7 = s32[1,8,6]{1,0,2:T(1,128)S(1)} copy-done((s32[1,8,6]{1,0,2:T(1,128)S(1)}, s32[1,8,6]{1,0,2:T(1,128)}, u32[]{:S(2)}) %copy-start.7) | copy-done | bytes 216
  2.9 0.7 %copy-done.8 = s32[1,8]{1,0:T(1,128)S(1)} copy-done((s32[1,8]{1,0:T(1,128)S(1)}, s32[1,8]{1,0:T(1,128)}, u32[]{:S(2)}) %copy-start.8) | copy-done | bytes 56
  3.5 0.4 shard_map.121
  3.9 4.8 %collective-permute-start.10 = (bf16[24,1408]{1,0:T(8,128)(2,1)S(1)}, bf16[24,1408]{1,0:T(8,128)(2,1)S(1)}, u32[]{:S(2)}, u32[]{:S(2)}) collective-permute-start(bf16[24,1408]{1,0:T(8,128)(2,1)S(1)} %get-tuple-element.31), channel_id=1, source_target_pairs={{0,7},{1,6},{2,5},{3,4},{4,3},{5,2},{6,1},{7,0},{8,15},{9,14},{10,... | collective-permute-start | bytes 202760 | tf_op jit(solution)/shard_map/ppermute | solution.py:194
  8.7 0.0 collective-permute-start.1
  8.7 0.5 collective-permute-start.2
  9.3 3.8 %collective-permute-start.3 = (bf16[48,1024]{1,0:T(8,128)(2,1)}, bf16[48,1024]{1,0:T(8,128)(2,1)S(1)}, u32[]{:S(2)}, u32[]{:S(2)}) collective-permute-start(bf16[48,1024]{1,0:T(8,128)(2,1)} %bitcast.11), channel_id=1, source_target_pairs={{0,6},{1,7},{2,4},{3,5},{4,2},{5,3},{6,0},{7,1},{8,14},{9,15},{10,... | collective-permute-start | bytes 294920 | tf_op jit(solution)/shard_map/ppermute | solution.py:194
  13.1 0.0 collective-permute-done.10.refs_7_
  13.1 0.0 collective-permute-start.4
  13.1 1.3 %collective-permute-done.4.refs_1_ = bf16[24,1408]{1,0:T(8,128)(2,1)S(1)} collective-permute-done((bf16[24,1408]{1,0:T(8,128)(2,1)S(1)}, bf16[24,1408]{1,0:T(8,128)(2,1)S(1)}, u32[]{:S(2)}, u32[]{:S(2)}) %collective-permute-start.4) | collective-permute-done | bytes 67616 | tf_op jit(solution)/shard_map/ppermute | solution.py:194
  14.4 0.8 %collective-permute-done.1.refs_1_ = bf16[48,1024]{1,0:T(8,128)(2,1)S(1)} collective-permute-done((bf16[48,1024]{1,0:T(8,128)(2,1)}, bf16[48,1024]{1,0:T(8,128)(2,1)S(1)}, u32[]{:S(2)}, u32[]{:S(2)}) %collective-permute-start.1) | collective-permute-done | bytes 98336 | tf_op jit(solution)/shard_map/ppermute | solution.py:194
  15.2 0.7 %collective-permute-start.6 = (bf16[24,1408]{1,0:T(8,128)(2,1)S(1)}, bf16[24,1408]{1,0:T(8,128)(2,1)S(1)}, u32[]{:S(2)}, u32[]{:S(2)}) collective-permute-start(bf16[24,1408]{1,0:T(8,128)(2,1)S(1)} %get-tuple-element.27), channel_id=1, source_target_pairs={{0,3},{1,2},{2,1},{3,0},{4,7},{5,6},{6,5},{7,4},{8,11},{9,10},{10,... | collective-permute-start | bytes 202760 | tf_op jit(solution)/shard_map/ppermute | solution.py:194
  15.9 3.9 %collective-permute-done.2.refs_2_ = bf16[48,1024]{1,0:T(8,128)(2,1)S(1)} collective-permute-done((bf16[48,1024]{1,0:T(8,128)(2,1)}, bf16[48,1024]{1,0:T(8,128)(2,1)S(1)}, u32[]{:S(2)}, u32[]{:S(2)}) %collective-permute-start.2) | collective-permute-done | bytes 98336 | tf_op jit(solution)/shard_map/ppermute | solution.py:194
  19.8 2.1 %collective-permute-start.8 = (bf16[24,1408]{1,0:T(8,128)(2,1)S(1)}, bf16[24,1408]{1,0:T(8,128)(2,1)S(1)}, u32[]{:S(2)}, u32[]{:S(2)}) collective-permute-start(bf16[24,1408]{1,0:T(8,128)(2,1)S(1)} %get-tuple-element.29), channel_id=1, source_target_pairs={{0,5},{1,4},{2,7},{3,6},{4,1},{5,0},{6,3},{7,2},{8,13},{9,12},{10,... | collective-permute-start | bytes 202760 | tf_op jit(solution)/shard_map/ppermute | solution.py:194
  21.9 0.0 collective-permute-done.other_ref
  21.9 0.7 %collective-permute-start.9 = (bf16[24,1408]{1,0:T(8,128)(2,1)S(1)}, bf16[24,1408]{1,0:T(8,128)(2,1)S(1)}, u32[]{:S(2)}, u32[]{:S(2)}) collective-permute-start(bf16[24,1408]{1,0:T(8,128)(2,1)S(1)} %get-tuple-element.30), channel_id=1, source_target_pairs={{0,6},{1,7},{2,4},{3,5},{4,2},{5,3},{6,0},{7,1},{8,14},{9,15},{10,... | collective-permute-start | bytes 202760 | tf_op jit(solution)/shard_map/ppermute | solution.py:194
  22.6 1.3 %copy-done = bf16[1024,640]{1,0:T(8,128)(2,1)S(1)} copy-done((bf16[1024,640]{1,0:T(8,128)(2,1)S(1)}, bf16[1024,640]{1,0:T(8,128)(2,1)}, u32[]{:S(2)}) %copy-start) | copy-done | bytes 1310744
  23.9 0.9 %copy-done.5 = bf16[1024,48]{0,1:T(8,128)(2,1)S(1)} copy-done((bf16[1024,48]{0,1:T(8,128)(2,1)S(1)}, bf16[1024,48]{0,1:T(8,128)(2,1)}, u32[]{:S(2)}) %copy-start.5) | copy-done | bytes 98328
  24.8 0.7 %copy-done.6 = s32[1024]{0:T(1024)S(1)} copy-done((s32[1024]{0:T(1024)S(1)}, s32[1024]{0:T(1024)}, u32[]{:S(2)}) %copy-start.6) | copy-done | bytes 4120
  25.5 0.9 %shard_map.120.head_ref = f32[192,1280]{1,0:T(8,128)S(1)} custom-call(s32[1,1024]{1,0:T(1,128)S(1)} %bitcast.13, bf16[1024,640]{1,0:T(8,128)(2,1)S(1)} %copy-done, bf16[1024,640]{1,0:T(8,128)(2,1)S(1)} %collective-permute-done.other_ref, bf16[48,1024]{1,0:T(8,128)(2,1)S(1)} %bitcast.12, bf16[48,1024]{1,0:T(8,128)(2,1)S(1)} %collective-permute-done.1.refs_1_, ...), custom_call_target="tpu_custom_call" | custom-call | flops 503316480 | bytes 4001792 | tf_op jit(solution)/shard_map/pallas_call | solution.py:162
  26.5 0.0 copy-start.2
  26.5 0.0 copy-start.3
  26.5 0.0 copy-start.4
  26.5 0.0 collective-permute-done.5.refs_2_
  26.5 0.0 collective-permute-done.8.refs_5_
  26.5 2.0 %collective-permute-done.9.refs_6_ = bf16[24,1408]{1,0:T(8,128)(2,1)S(1)} collective-permute-done((bf16[24,1408]{1,0:T(8,128)(2,1)S(1)}, bf16[24,1408]{1,0:T(8,128)(2,1)S(1)}, u32[]{:S(2)}, u32[]{:S(2)}) %collective-permute-start.9) | collective-permute-done | bytes 67616 | tf_op jit(solution)/shard_map/ppermute | solution.py:194
  28.6 0.4 shard_map.122
  29.0 1.6 %collective-permute-start.11 = (f32[48,1280]{1,0:T(8,128)S(1)}, f32[48,1280]{1,0:T(8,128)S(1)}, u32[]{:S(2)}, u32[]{:S(2)}) collective-permute-start(f32[48,1280]{1,0:T(8,128)S(1)} %get-tuple-element.33), channel_id=1, source_target_pairs={{0,8},{8,0},{16,24},{24,16},{1,9},{9,1},{17,25},{25,17},{2,10},{10... | collective-permute-start | bytes 737288 | tf_op jit(solution)/shard_map/ppermute | solution.py:197
  30.6 1.5 %collective-permute-start.12 = (f32[48,1280]{1,0:T(8,128)S(1)}, f32[48,1280]{1,0:T(8,128)S(1)}, u32[]{:S(2)}, u32[]{:S(2)}) collective-permute-start(f32[48,1280]{1,0:T(8,128)S(1)} %get-tuple-element.34), channel_id=1, source_target_pairs={{0,16},{8,24},{16,0},{24,8},{1,17},{9,25},{17,1},{25,9},{2,18},{10... | collective-permute-start | bytes 737288 | tf_op jit(solution)/shard_map/ppermute | solution.py:197
  32.1 0.5 collective-permute-start.13
  32.6 5.3 %collective-permute-done.11.refs_1_ = f32[48,1280]{1,0:T(8,128)S(1)} collective-permute-done((f32[48,1280]{1,0:T(8,128)S(1)}, f32[48,1280]{1,0:T(8,128)S(1)}, u32[]{:S(2)}, u32[]{:S(2)}) %collective-permute-start.11) | collective-permute-done | bytes 245792 | tf_op jit(solution)/shard_map/ppermute | solution.py:197
  37.9 6.2 %collective-permute-done.12.refs_2_ = f32[48,1280]{1,0:T(8,128)S(1)} collective-permute-done((f32[48,1280]{1,0:T(8,128)S(1)}, f32[48,1280]{1,0:T(8,128)S(1)}, u32[]{:S(2)}, u32[]{:S(2)}) %collective-permute-start.12) | collective-permute-done | bytes 245792 | tf_op jit(solution)/shard_map/ppermute | solution.py:197
  44.2 0.0 collective-permute-done.13.refs_3_
  44.2 0.1 collective-permute-start.14
  44.4 1.3 %collective-permute-start.15 = (f32[24,640]{1,0:T(8,128)S(1)}, f32[24,640]{1,0:T(8,128)S(1)}, u32[]{:S(2)}, u32[]{:S(2)}) collective-permute-start(f32[24,640]{1,0:T(8,128)S(1)} %get-tuple-element.38), channel_id=1, source_target_pairs={{0,4},{1,5},{2,6},{3,7},{4,0},{5,1},{6,2},{7,3},{8,12},{9,13},{10,... | collective-permute-start | bytes 184328 | tf_op jit(solution)/shard_map/ppermute | solution.py:194
  45.6 3.0 %collective-permute-start.16 = (f32[24,640]{1,0:T(8,128)S(1)}, f32[24,640]{1,0:T(8,128)S(1)}, u32[]{:S(2)}, u32[]{:S(2)}) collective-permute-start(f32[24,640]{1,0:T(8,128)S(1)} %get-tuple-element.39), channel_id=1, source_target_pairs={{0,6},{1,7},{2,4},{3,5},{4,2},{5,3},{6,0},{7,1},{8,14},{9,15},{10,... | collective-permute-start | bytes 184328 | tf_op jit(solution)/shard_map/ppermute | solution.py:194
  48.7 0.2 collective-permute-done.14.refs_1_
  48.8 3.3 %collective-permute-done.15.refs_2_ = f32[24,640]{1,0:T(8,128)S(1)} collective-permute-done((f32[24,640]{1,0:T(8,128)S(1)}, f32[24,640]{1,0:T(8,128)S(1)}, u32[]{:S(2)}, u32[]{:S(2)}) %collective-permute-start.15) | collective-permute-done | bytes 61472 | tf_op jit(solution)/shard_map/ppermute | solution.py:194
  52.1 0.0 collective-permute-done.16.refs_3_
  52.1 1.3 %shard_map.124 = (f32[12,5120]{1,0:T(8,128)}, f32[12,5120]{1,0:T(8,128)}, f32[12,5120]{1,0:T(8,128)}, bf16[48,1280]{1,0:T(8,128)(2,1)S(1)}) custom-call(f32[12,5120]{1,0:T(8,128)S(1)} %copy-done.2, f32[12,5120]{1,0:T(8,128)S(1)} %copy-done.3, f32[12,5120]{1,0:T(8,128)S(1)} %copy-done.4, f32[24,640]{1,0:T(8,128)S(1)} %get-tuple-element.36.refs_0_, ...), custom_call_target="tpu_custom_call" | custom-call | bytes 1843200 | tf_op jit(solution)/shard_map/pallas_call | solution.py:162
  53.5 1.4 %collective-permute-start.17 = (bf16[48,1280]{1,0:T(8,128)(2,1)S(1)}, bf16[48,1280]{1,0:T(8,128)(2,1)S(1)}, u32[]{:S(2)}, u32[]{:S(2)}) collective-permute-start(bf16[48,1280]{1,0:T(8,128)(2,1)S(1)} %get-tuple-element.43.refs_0_), channel_id=1, source_target_pairs={{0,8},{8,0},{16,24},{24,16},{1,9},{9,1},{17,25},{25,17},{2,10},{10... | collective-permute-start | bytes 368648 | tf_op jit(solution)/shard_map/ppermute | solution.py:197
  54.9 0.6 %collective-permute-start.18 = (bf16[48,1280]{1,0:T(8,128)(2,1)S(1)}, bf16[48,1280]{1,0:T(8,128)(2,1)S(1)}, u32[]{:S(2)}, u32[]{:S(2)}) collective-permute-start(bf16[48,1280]{1,0:T(8,128)(2,1)S(1)} %get-tuple-element.43.refs_0_), channel_id=1, source_target_pairs={{0,16},{8,24},{16,0},{24,8},{1,17},{9,25},{17,1},{25,9},{2,18},{10... | collective-permute-start | bytes 368648 | tf_op jit(solution)/shard_map/ppermute | solution.py:197
  55.5 1.4 %collective-permute-start.19 = (bf16[48,1280]{1,0:T(8,128)(2,1)S(1)}, bf16[48,1280]{1,0:T(8,128)(2,1)S(1)}, u32[]{:S(2)}, u32[]{:S(2)}) collective-permute-start(bf16[48,1280]{1,0:T(8,128)(2,1)S(1)} %get-tuple-element.43.refs_0_), channel_id=1, source_target_pairs={{0,24},{8,16},{16,8},{24,0},{1,25},{9,17},{17,9},{25,1},{2,26},{10... | collective-permute-start | bytes 368648 | tf_op jit(solution)/shard_map/ppermute | solution.py:197
  56.9 2.4 %collective-permute-done.17.refs_1_ = bf16[48,1280]{1,0:T(8,128)(2,1)S(1)} collective-permute-done((bf16[48,1280]{1,0:T(8,128)(2,1)S(1)}, bf16[48,1280]{1,0:T(8,128)(2,1)S(1)}, u32[]{:S(2)}, u32[]{:S(2)}) %collective-permute-start.17) | collective-permute-done | bytes 122912 | tf_op jit(solution)/shard_map/ppermute | solution.py:197
  59.4 2.3 %collective-permute-done.18.refs_2_ = bf16[48,1280]{1,0:T(8,128)(2,1)S(1)} collective-permute-done((bf16[48,1280]{1,0:T(8,128)(2,1)S(1)}, bf16[48,1280]{1,0:T(8,128)(2,1)S(1)}, u32[]{:S(2)}, u32[]{:S(2)}) %collective-permute-start.18) | collective-permute-done | bytes 122912 | tf_op jit(solution)/shard_map/ppermute | solution.py:197
  61.7 1.1 %shard_map.125 = bf16[48,5120]{1,0:T(8,128)(2,1)} custom-call(bf16[48,1280]{1,0:T(8,128)(2,1)S(1)} %get-tuple-element.43.refs_0_, bf16[48,1280]{1,0:T(8,128)(2,1)S(1)} %collective-permute-done.17.refs_1_, bf16[48,1280]{1,0:T(8,128)(2,1)S(1)} %collective-permute-done.18.refs_2_, bf16[48,1280]{1,0:T(8,128)(2,1)S(1)} %collective-permute-done.19.refs_3_), custom_call_target="tpu_custom_call" | custom-call | bytes 983040 | tf_op jit(solution)/shard_map/pallas_call | solution.py:162
  (16 shorter events, 0.1 us)
Async XLA Ops:
  0.6 21.3 %collective-permute-start = (bf16[1024,640]{1,0:T(8,128)(2,1)}, bf16[1024,640]{1,0:T(8,128)(2,1)S(1)}, u32[]{:S(2)}, u32[]{:S(2)}) collective-permute-start(bf16[1024,640]{1,0:T(8,128)(2,1)} %own_ref.1), channel_id=1, source_target_pairs={{0,1},{1,0},{2,3},{3,2},{4,5},{5,4},{6,7},{7,6},{8,9},{9,8},{10,11... | collective-permute-start | bytes 3932168 | tf_op jit(solution)/shard_map/ppermute | solution.py:194
  1.1 1.0 %copy-start.1 = (bf16[1,8,6,5120]{3,1,2,0:T(8,128)(2,1)S(1)}, bf16[1,8,6,5120]{3,1,2,0:T(8,128)(2,1)}, u32[]{:S(2)}) copy-start(bf16[1,8,6,5120]{3,1,2,0:T(8,128)(2,1)} %param.12) | copy-start | bytes 1474564
  2.2 0.7 %copy-start.7 = (s32[1,8,6]{1,0,2:T(1,128)S(1)}, s32[1,8,6]{1,0,2:T(1,128)}, u32[]{:S(2)}) copy-start(s32[1,8,6]{1,0,2:T(1,128)} %param.13) | copy-start | bytes 580
  2.9 0.7 %copy-start.8 = (s32[1,8]{1,0:T(1,128)S(1)}, s32[1,8]{1,0:T(1,128)}, u32[]{:S(2)}) copy-start(s32[1,8]{1,0:T(1,128)} %counts_ref.1) | copy-start | bytes 100
  3.9 9.2 %collective-permute-start.10 = (bf16[24,1408]{1,0:T(8,128)(2,1)S(1)}, bf16[24,1408]{1,0:T(8,128)(2,1)S(1)}, u32[]{:S(2)}, u32[]{:S(2)}) collective-permute-start(bf16[24,1408]{1,0:T(8,128)(2,1)S(1)} %get-tuple-element.31), channel_id=1, source_target_pairs={{0,7},{1,6},{2,5},{3,4},{4,3},{5,2},{6,1},{7,0},{8,15},{9,14},{10,... | collective-permute-start | bytes 202760 | tf_op jit(solution)/shard_map/ppermute | solution.py:194
  8.7 6.5 %collective-permute-start.1 = (bf16[48,1024]{1,0:T(8,128)(2,1)}, bf16[48,1024]{1,0:T(8,128)(2,1)S(1)}, u32[]{:S(2)}, u32[]{:S(2)}) collective-permute-start(bf16[48,1024]{1,0:T(8,128)(2,1)} %bitcast.9), channel_id=1, source_target_pairs={{0,2},{1,3},{2,0},{3,1},{4,6},{5,7},{6,4},{7,5},{8,10},{9,11},{10,... | collective-permute-start | bytes 294920 | tf_op jit(solution)/shard_map/ppermute | solution.py:194
  8.7 11.0 %collective-permute-start.2 = (bf16[48,1024]{1,0:T(8,128)(2,1)}, bf16[48,1024]{1,0:T(8,128)(2,1)S(1)}, u32[]{:S(2)}, u32[]{:S(2)}) collective-permute-start(bf16[48,1024]{1,0:T(8,128)(2,1)} %bitcast.10), channel_id=1, source_target_pairs={{0,4},{1,5},{2,6},{3,7},{4,0},{5,1},{6,2},{7,3},{8,12},{9,13},{10,... | collective-permute-start | bytes 294920 | tf_op jit(solution)/shard_map/ppermute | solution.py:194
  9.3 10.5 %collective-permute-start.3 = (bf16[48,1024]{1,0:T(8,128)(2,1)}, bf16[48,1024]{1,0:T(8,128)(2,1)S(1)}, u32[]{:S(2)}, u32[]{:S(2)}) collective-permute-start(bf16[48,1024]{1,0:T(8,128)(2,1)} %bitcast.11), channel_id=1, source_target_pairs={{0,6},{1,7},{2,4},{3,5},{4,2},{5,3},{6,0},{7,1},{8,14},{9,15},{10,... | collective-permute-start | bytes 294920 | tf_op jit(solution)/shard_map/ppermute | solution.py:194
  13.1 1.3 %collective-permute-start.4 = (bf16[24,1408]{1,0:T(8,128)(2,1)S(1)}, bf16[24,1408]{1,0:T(8,128)(2,1)S(1)}, u32[]{:S(2)}, u32[]{:S(2)}) collective-permute-start(bf16[24,1408]{1,0:T(8,128)(2,1)S(1)} %get-tuple-element.25), channel_id=1, source_target_pairs={{0,1},{1,0},{2,3},{3,2},{4,5},{5,4},{6,7},{7,6},{8,9},{9,8},{10,11... | collective-permute-start | bytes 202760 | tf_op jit(solution)/shard_map/ppermute | solution.py:194
  14.4 12.1 %collective-permute-start.5 = (bf16[24,1408]{1,0:T(8,128)(2,1)S(1)}, bf16[24,1408]{1,0:T(8,128)(2,1)S(1)}, u32[]{:S(2)}, u32[]{:S(2)}) collective-permute-start(bf16[24,1408]{1,0:T(8,128)(2,1)S(1)} %get-tuple-element.26), channel_id=1, source_target_pairs={{0,2},{1,3},{2,0},{3,1},{4,6},{5,7},{6,4},{7,5},{8,10},{9,11},{10,... | collective-permute-start | bytes 202760 | tf_op jit(solution)/shard_map/ppermute | solution.py:194
  15.2 11.3 %collective-permute-start.6 = (bf16[24,1408]{1,0:T(8,128)(2,1)S(1)}, bf16[24,1408]{1,0:T(8,128)(2,1)S(1)}, u32[]{:S(2)}, u32[]{:S(2)}) collective-permute-start(bf16[24,1408]{1,0:T(8,128)(2,1)S(1)} %get-tuple-element.27), channel_id=1, source_target_pairs={{0,3},{1,2},{2,1},{3,0},{4,7},{5,6},{6,5},{7,4},{8,11},{9,10},{10,... | collective-permute-start | bytes 202760 | tf_op jit(solution)/shard_map/ppermute | solution.py:194
  19.8 6.8 %collective-permute-start.7 = (bf16[24,1408]{1,0:T(8,128)(2,1)S(1)}, bf16[24,1408]{1,0:T(8,128)(2,1)S(1)}, u32[]{:S(2)}, u32[]{:S(2)}) collective-permute-start(bf16[24,1408]{1,0:T(8,128)(2,1)S(1)} %get-tuple-element.28), channel_id=1, source_target_pairs={{0,4},{1,5},{2,6},{3,7},{4,0},{5,1},{6,2},{7,3},{8,12},{9,13},{10,... | collective-permute-start | bytes 202760 | tf_op jit(solution)/shard_map/ppermute | solution.py:194
  19.8 6.8 %collective-permute-start.8 = (bf16[24,1408]{1,0:T(8,128)(2,1)S(1)}, bf16[24,1408]{1,0:T(8,128)(2,1)S(1)}, u32[]{:S(2)}, u32[]{:S(2)}) collective-permute-start(bf16[24,1408]{1,0:T(8,128)(2,1)S(1)} %get-tuple-element.29), channel_id=1, source_target_pairs={{0,5},{1,4},{2,7},{3,6},{4,1},{5,0},{6,3},{7,2},{8,13},{9,12},{10,... | collective-permute-start | bytes 202760 | tf_op jit(solution)/shard_map/ppermute | solution.py:194
  21.9 6.7 %collective-permute-start.9 = (bf16[24,1408]{1,0:T(8,128)(2,1)S(1)}, bf16[24,1408]{1,0:T(8,128)(2,1)S(1)}, u32[]{:S(2)}, u32[]{:S(2)}) collective-permute-start(bf16[24,1408]{1,0:T(8,128)(2,1)S(1)} %get-tuple-element.30), channel_id=1, source_target_pairs={{0,6},{1,7},{2,4},{3,5},{4,2},{5,3},{6,0},{7,1},{8,14},{9,15},{10,... | collective-permute-start | bytes 202760 | tf_op jit(solution)/shard_map/ppermute | solution.py:194
  22.6 1.3 %copy-start = (bf16[1024,640]{1,0:T(8,128)(2,1)S(1)}, bf16[1024,640]{1,0:T(8,128)(2,1)}, u32[]{:S(2)}) copy-start(bf16[1024,640]{1,0:T(8,128)(2,1)} %own_ref.1) | copy-start | bytes 3932164
  23.9 0.9 %copy-start.5 = (bf16[1024,48]{0,1:T(8,128)(2,1)S(1)}, bf16[1024,48]{0,1:T(8,128)(2,1)}, u32[]{:S(2)}) copy-start(bf16[1024,48]{0,1:T(8,128)(2,1)} %param.10) | copy-start | bytes 294916
  24.8 0.7 %copy-start.6 = (s32[1024]{0:T(1024)S(1)}, s32[1024]{0:T(1024)}, u32[]{:S(2)}) copy-start(s32[1024]{0:T(1024)} %param.11) | copy-start | bytes 12292
  26.5 25.7 %copy-start.2 = (f32[12,5120]{1,0:T(8,128)S(1)}, f32[12,5120]{1,0:T(8,128)}, u32[]{:S(2)}) copy-start(f32[12,5120]{1,0:T(8,128)} %master_ref.1) | copy-start | bytes 737284
  26.5 25.7 %copy-start.3 = (f32[12,5120]{1,0:T(8,128)S(1)}, f32[12,5120]{1,0:T(8,128)}, u32[]{:S(2)}) copy-start(f32[12,5120]{1,0:T(8,128)} %first_ref.1) | copy-start | bytes 737284
  26.5 25.6 %copy-start.4 = (f32[12,5120]{1,0:T(8,128)S(1)}, f32[12,5120]{1,0:T(8,128)}, u32[]{:S(2)}) copy-start(f32[12,5120]{1,0:T(8,128)} %second_ref.1) | copy-start | bytes 737284
  29.0 8.9 %collective-permute-start.11 = (f32[48,1280]{1,0:T(8,128)S(1)}, f32[48,1280]{1,0:T(8,128)S(1)}, u32[]{:S(2)}, u32[]{:S(2)}) collective-permute-start(f32[48,1280]{1,0:T(8,128)S(1)} %get-tuple-element.33), channel_id=1, source_target_pairs={{0,8},{8,0},{16,24},{24,16},{1,9},{9,1},{17,25},{25,17},{2,10},{10... | collective-permute-start | bytes 737288 | tf_op jit(solution)/shard_map/ppermute | solution.py:197
  30.6 13.6 %collective-permute-start.12 = (f32[48,1280]{1,0:T(8,128)S(1)}, f32[48,1280]{1,0:T(8,128)S(1)}, u32[]{:S(2)}, u32[]{:S(2)}) collective-permute-start(f32[48,1280]{1,0:T(8,128)S(1)} %get-tuple-element.34), channel_id=1, source_target_pairs={{0,16},{8,24},{16,0},{24,8},{1,17},{9,25},{17,1},{25,9},{2,18},{10... | collective-permute-start | bytes 737288 | tf_op jit(solution)/shard_map/ppermute | solution.py:197
  32.1 12.0 %collective-permute-start.13 = (f32[48,1280]{1,0:T(8,128)S(1)}, f32[48,1280]{1,0:T(8,128)S(1)}, u32[]{:S(2)}, u32[]{:S(2)}) collective-permute-start(f32[48,1280]{1,0:T(8,128)S(1)} %get-tuple-element.35), channel_id=1, source_target_pairs={{0,24},{8,16},{16,8},{24,0},{1,25},{9,17},{17,9},{25,1},{2,26},{10... | collective-permute-start | bytes 737288 | tf_op jit(solution)/shard_map/ppermute | solution.py:197
  44.2 4.6 %collective-permute-start.14 = (f32[24,640]{1,0:T(8,128)S(1)}, f32[24,640]{1,0:T(8,128)S(1)}, u32[]{:S(2)}, u32[]{:S(2)}) collective-permute-start(f32[24,640]{1,0:T(8,128)S(1)} %get-tuple-element.37), channel_id=1, source_target_pairs={{0,2},{1,3},{2,0},{3,1},{4,6},{5,7},{6,4},{7,5},{8,10},{9,11},{10,... | collective-permute-start | bytes 184328 | tf_op jit(solution)/shard_map/ppermute | solution.py:194
  44.4 7.8 %collective-permute-start.15 = (f32[24,640]{1,0:T(8,128)S(1)}, f32[24,640]{1,0:T(8,128)S(1)}, u32[]{:S(2)}, u32[]{:S(2)}) collective-permute-start(f32[24,640]{1,0:T(8,128)S(1)} %get-tuple-element.38), channel_id=1, source_target_pairs={{0,4},{1,5},{2,6},{3,7},{4,0},{5,1},{6,2},{7,3},{8,12},{9,13},{10,... | collective-permute-start | bytes 184328 | tf_op jit(solution)/shard_map/ppermute | solution.py:194
  45.6 6.5 %collective-permute-start.16 = (f32[24,640]{1,0:T(8,128)S(1)}, f32[24,640]{1,0:T(8,128)S(1)}, u32[]{:S(2)}, u32[]{:S(2)}) collective-permute-start(f32[24,640]{1,0:T(8,128)S(1)} %get-tuple-element.39), channel_id=1, source_target_pairs={{0,6},{1,7},{2,4},{3,5},{4,2},{5,3},{6,0},{7,1},{8,14},{9,15},{10,... | collective-permute-start | bytes 184328 | tf_op jit(solution)/shard_map/ppermute | solution.py:194
  53.5 5.9 %collective-permute-start.17 = (bf16[48,1280]{1,0:T(8,128)(2,1)S(1)}, bf16[48,1280]{1,0:T(8,128)(2,1)S(1)}, u32[]{:S(2)}, u32[]{:S(2)}) collective-permute-start(bf16[48,1280]{1,0:T(8,128)(2,1)S(1)} %get-tuple-element.43.refs_0_), channel_id=1, source_target_pairs={{0,8},{8,0},{16,24},{24,16},{1,9},{9,1},{17,25},{25,17},{2,10},{10... | collective-permute-start | bytes 368648 | tf_op jit(solution)/shard_map/ppermute | solution.py:197
  54.9 6.8 %collective-permute-start.18 = (bf16[48,1280]{1,0:T(8,128)(2,1)S(1)}, bf16[48,1280]{1,0:T(8,128)(2,1)S(1)}, u32[]{:S(2)}, u32[]{:S(2)}) collective-permute-start(bf16[48,1280]{1,0:T(8,128)(2,1)S(1)} %get-tuple-element.43.refs_0_), channel_id=1, source_target_pairs={{0,16},{8,24},{16,0},{24,8},{1,17},{9,25},{17,1},{25,9},{2,18},{10... | collective-permute-start | bytes 368648 | tf_op jit(solution)/shard_map/ppermute | solution.py:197
  55.5 6.2 %collective-permute-start.19 = (bf16[48,1280]{1,0:T(8,128)(2,1)S(1)}, bf16[48,1280]{1,0:T(8,128)(2,1)S(1)}, u32[]{:S(2)}, u32[]{:S(2)}) collective-permute-start(bf16[48,1280]{1,0:T(8,128)(2,1)S(1)} %get-tuple-element.43.refs_0_), channel_id=1, source_target_pairs={{0,24},{8,16},{16,8},{24,0},{1,25},{9,17},{17,9},{25,1},{2,26},{10... | collective-permute-start | bytes 368648 | tf_op jit(solution)/shard_map/ppermute | solution.py:197

commit v4 on v3

--- a/solution.py
+++ b/solution.py
@@ -34,12 +34,22 @@
     return jnp.dot(left, right, preferred_element_type=jnp.float32)
 
 
-def slots_kernel(chips, dp, shard, slots_ref, rows_ref, counts_ref, *out_refs):
+def slots_kernel(chips, dp, shard, slots_hbm, rows_hbm, counts_hbm, own_out, other_out, slots_ref, rows_ref, counts_ref, sems):
     d, z, core = place()
+    copies = [
+        pltpu.make_async_copy(rows_hbm, rows_ref, sems.at[0]),
+        pltpu.make_async_copy(counts_hbm, counts_ref, sems.at[1]),
+        pltpu.make_async_copy(slots_hbm, slots_ref, sems.at[2]),
+    ]
+    for copy in copies:
+        copy.start()
+    for copy in copies:
+        copy.wait()
     cap, owners = rows_ref.shape[0], rows_ref.shape[2]
     count = cap * owners
     group = cap * chips
     width = slots_ref.shape[1] // chips
+    half = chips // 2
     own_lane = iota((count, owners), 1) == iota((count, owners), 0) % owners
     rows = jnp.broadcast_to(rows_ref[...], (cap, owners, owners)).reshape(count, owners)
     rows = jnp.sum(jnp.where(own_lane, rows, 0), axis=1, keepdims=True)
@@ -49,40 +59,74 @@
     ids = (block ^ d) * shard + rows - block * shard
     ids = jnp.where(over(iota((count, 1), 0), owners) < live, ids, -1)
     ids = jnp.broadcast_to(ids, (count, LANES)).astype(jnp.bfloat16)
-    for away in range(CORES):
-        q = iota((group, count), 0)
-        slot = over(q, chips)
-        wanted = slot * owners + (q - slot * chips) * CORES + (core ^ away)
-        pick = one_hot(iota((group, count), 1) == wanted)
+    q = iota((CORES * group, count), 0)
+    away = jnp.where(q >= group, 1, 0)
+    q = q - away * group
+    near = jnp.where(q >= group // 2, 1, 0)
+    q = q - near * (group // 2)
+    slot = over(q, half)
+    owner = q - slot * half + (1 - near) * half
+    for s in range(chips):
+        wanted = slot * owners + (owner ^ z ^ s) * CORES + (away ^ core)
+        pick = one_hot(iota((CORES * group, count), 1) == wanted)
+        start = pl.multiple_of((z ^ s) * width, LANES)
+        values = exact(pick, slots_ref[:, pl.ds(start, width)]).astype(jnp.bfloat16)
         picked_ids = exact(pick, ids).astype(jnp.bfloat16)
-        for s in range(chips):
-            start = pl.multiple_of((z ^ s) * width, LANES)
-            out_ref = out_refs[away * chips + s]
-            out_ref[:, :width] = exact(pick, slots_ref[:, pl.ds(start, width)]).astype(jnp.bfloat16)
-            out_ref[:, width:] = picked_ids
-
-
-def head_kernel(chips, dp, shard, mask_ref, own_ref, other_ref, *refs):
+        first = s * (width + LANES)
+        for out_ref, spot in ((own_out, slice(0, group)), (other_out, slice(group, CORES * group))):
+            out_ref[:, first : first + width] = values[spot]
+            out_ref[:, first + width : first + width + LANES] = picked_ids[spot]
+
+
+def merge_kernel(chips, own_ref, other_ref, *out_refs):
+    size = own_ref.shape[1] // chips
+    part = own_ref.shape[0] // 2
+    for s in range(chips):
+        own = own_ref[:, s * size : (s + 1) * size].astype(jnp.float32)
+        other = other_ref[:, s * size : (s + 1) * size].astype(jnp.float32)
+        for h in range(2):
+            spot = slice(h * part, (h + 1) * part)
+            both = jnp.concatenate([own[spot], other[spot]], axis=0)
+            out_refs[h * chips + s][...] = both.astype(jnp.bfloat16)
+
+
+def head_kernel(chips, dp, shard, mask_hbm, hidden_hbm, columns_hbm, other_ref, *refs):
     d, z, core = place()
-    parts, out_ref = refs[:-1], refs[-1]
+    parts, outs = refs[: chips - 1], refs[chips - 1 : chips + 1]
+    mask_ref, own_ref, columns_ref, sems = refs[chips + 1 :]
+    copies = [
+        pltpu.make_async_copy(mask_hbm, mask_ref, sems.at[0]),
+        pltpu.make_async_copy(columns_hbm, columns_ref, sems.at[1]),
+        pltpu.make_async_copy(hidden_hbm, own_ref, sems.at[2]),
+    ]
+    for copy in copies:
+        copy.start()
+    for copy in copies:
+        copy.wait()
     rows = dp * shard
     total = chips * rows
     cols = own_ref.shape[1]
+    half = chips // 2
     mask = mask_ref[...].astype(jnp.float32).astype(jnp.bfloat16)
-    columns = jnp.concatenate([part[...] for part in parts], axis=0) * mask
+    columns = jnp.concatenate([part[...] for part in (columns_ref, *parts)], axis=0) * mask
     r = iota((total, total), 0)
-    t = over(r, chips * shard)
-    s = over(r - t * (chips * shard), shard)
-    i = r - t * (chips * shard) - s * shard
-    order = one_hot(iota((total, total), 1) == s * rows + (t ^ d) * shard + i)
+    near = jnp.where(r >= total // 2, 1, 0)
+    r = r - near * (total // 2)
+    t = over(r, half * shard)
+    j = over(r - t * (half * shard), shard)
+    i = r - t * (half * shard) - j * shard
+    order = one_hot(iota((total, total), 1) == (j + (1 - near) * half) * rows + (t ^ d) * shard + i)
     columns = exact(order, columns).astype(jnp.bfloat16)
-    out_ref[:, pl.ds(pl.multiple_of(core * cols, LANES), cols)] = exact(columns, own_ref[...])
-    out_ref[:, pl.ds(pl.multiple_of((1 - core) * cols, LANES), cols)] = exact(columns, other_ref[...])
+    for at, ref in ((core, own_ref), (1 - core, other_ref)):
+        head = exact(columns, ref[...])
+        spot = pl.ds(pl.multiple_of(at * cols, LANES), cols)
+        for h in range(2):
+            outs[h][:, spot] = head[h * (total // 2) : (h + 1) * (total // 2)]
 
 
 def embed_kernel(chips, dp, shard, head_ref, *refs):
-    d, z, core = place()
     slot_refs, out_refs = refs[:-dp], refs[-dp:]
+    half = chips // 2
     total, cols = head_ref.shape
     count = len(slot_refs) * slot_refs[0].shape[0]
     ids = jnp.concatenate([ref[:, cols:].astype(jnp.float32) for ref in slot_refs], axis=0)
@@ -90,63 +134,75 @@
     values = jnp.concatenate([ref[:, :cols].astype(jnp.float32) for ref in slot_refs], axis=0)
     values = values.astype(jnp.bfloat16)
     block = over(jnp.maximum(ids, 0), shard)
-    owner = (iota((count, 1), 0) % chips) ^ z
-    target = (block * chips + owner) * shard + ids - block * shard
+    target = (block * half + iota((count, 1), 0) % half) * shard + ids - block * shard
     target = jnp.where(ids < 0, -1, target)
     picked = one_hot(iota((count, total), 1) == target)
     embed = lax.dot_general(picked, values, (((0,), (0,)), ((), ())), preferred_element_type=jnp.float32)
     part = head_ref[...] + embed
-    size = chips * shard
+    size = half * shard
     for t, out_ref in enumerate(out_refs):
         out_ref[...] = part[t * size : (t + 1) * size]
 
 
-def sum_kernel(chips, shard, *refs):
-    dp = len(refs) - chips
+def sum_kernel(half, shard, *refs):
+    dp = len(refs) - half
     total = refs[0][...]
     for t in range(1, dp):
         total = total + refs[t][...]
-    half = total.shape[1] // CORES
-    for s, out_ref in enumerate(refs[dp:]):
-        rows = total[s * shard : (s + 1) * shard]
-        out_ref[...] = jnp.concatenate([rows[:, :half], rows[:, half:]], axis=0)
-
-
-def adam_kernel(chips, shard, master_ref, first_ref, second_ref, *refs):
+    cut = total.shape[1] // CORES
+    for j, out_ref in enumerate(refs[dp:]):
+        rows = total[j * shard : (j + 1) * shard]
+        out_ref[...] = jnp.concatenate([rows[:, :cut], rows[:, cut:]], axis=0)
+
+
+def step(shard, spot, piece_ref, master_ref, first_ref, second_ref):
+    piece = piece_ref[...]
+    gradient = jnp.concatenate([piece[:shard], piece[shard:]], axis=1)
+    master = master_ref[:, spot]
+    first_new = 0.9 * first_ref[:, spot] + 0.1 * gradient
+    second_new = 0.95 * second_ref[:, spot] + 0.05 * gradient * gradient
+    first_hat = first_new / (1.0 - 0.9**STEP)
+    second_hat = second_new / (1.0 - 0.95**STEP)
+    master_new = master - 0.05 * (first_hat / (jnp.sqrt(second_hat) + 1e-08) + 0.1 * master)
+    return master_new, first_new, second_new
+
+
+def chip_spot(z, s, piece_ref):
+    cols = piece_ref.shape[1] * CORES
+    return pl.ds(pl.multiple_of((z ^ s) * cols, LANES), cols)
+
+
+def rows_kernel(members, shard, *refs):
     d, z, core = place()
-    pieces, (master_out, first_out, second_out, table_ref) = refs[:chips], refs[chips:]
-    half = pieces[0].shape[1]
-    table = []
+    state, pieces, out_ref = refs[:3], refs[3:-1], refs[-1]
+    table = [step(shard, chip_spot(z, s, piece), piece, *state)[0] for s, piece in zip(members, pieces)]
+    out_ref[...] = jnp.concatenate(table, axis=0).astype(jnp.bfloat16)
+
+
+def adam_kernel(shard, *refs):
+    d, z, core = place()
+    state, pieces, outs = refs[:3], refs[3:-3], refs[-3:]
     for s, piece in enumerate(pieces):
-        piece = piece[...]
-        gradient = jnp.concatenate([piece[:shard], piece[shard:]], axis=1)
-        spot = pl.ds(pl.multiple_of((z ^ s) * (CORES * half), LANES), CORES * half)
-        master = master_ref[:, spot]
-        first_new = 0.9 * first_ref[:, spot] + 0.1 * gradient
-        second_new = 0.95 * second_ref[:, spot] + 0.05 * gradient * gradient
-        first_hat = first_new / (1.0 - 0.9**STEP)
-        second_hat = second_new / (1.0 - 0.95**STEP)
-        master_new = master - 0.05 * (first_hat / (jnp.sqrt(second_hat) + 1e-08) + 0.1 * master)
-        master_out[:, spot] = master_new
-        first_out[:, spot] = first_new
-        second_out[:, spot] = second_new
-        table.append(master_new)
-    table_ref[...] = jnp.concatenate(table, axis=0).astype(jnp.bfloat16)
-
-
-def table_kernel(chips, shard, *refs):
+        spot = chip_spot(z, s, piece)
+        for out_ref, value in zip(outs, step(shard, spot, piece, *state)):
+            out_ref[:, spot] = value
+
+
+def table_kernel(chips, dp, shard, *refs):
     d, z, core = place()
     parts, out_ref = refs[:-1], refs[-1]
-    dp = len(parts)
     cols = parts[0].shape[1]
     rows = dp * shard
     total = chips * rows
-    values = jnp.concatenate([part[...] for part in parts], axis=0)
+    half = chips // 2
+    values = jnp.concatenate([part[...].astype(jnp.float32) for part in parts], axis=0).astype(jnp.bfloat16)
     r = iota((total, total), 0)
     s = over(r, rows)
     e = over(r - s * rows, shard)
     i = r - s * rows - e * shard
-    order = one_hot(iota((total, total), 1) == ((e ^ d) * chips + s) * shard + i)
+    far = jnp.where(s >= half, 1, 0)
+    j = s - far * half
+    order = one_hot(iota((total, total), 1) == ((far * dp + (e ^ d)) * half + j) * shard + i)
     values = exact(order, values).astype(jnp.bfloat16)
     for s in range(chips):
         spot = pl.ds(pl.multiple_of((z ^ s) * cols, LANES), cols)
@@ -157,14 +213,23 @@
     return jax.ShapeDtypeStruct(shape, kind)
 
 
-def run(kernel, outs, *args, flops=0):
+def run(kernel, outs, *args, flops=0, hbm=0, scratch=()):
     moved = sum(x.size * x.dtype.itemsize for x in (*args, *jax.tree.leaves(outs)))
+    vmem = pl.BlockSpec(memory_space=pltpu.VMEM)
+    args = [pltpu.with_memory_space_constraint(x, pltpu.HBM) if n < hbm else x for n, x in enumerate(args)]
     return pl.pallas_call(
         kernel,
         out_shape=outs,
+        in_specs=[pl.BlockSpec(memory_space=pltpu.HBM)] * hbm + [vmem] * (len(args) - hbm),
+        out_specs=jax.tree.map(lambda _: vmem, outs),
+        scratch_shapes=list(scratch),
         cost_estimate=pl.CostEstimate(flops=flops, bytes_accessed=moved, transcendentals=0),
         compiler_params=pltpu.CompilerParams(vmem_limit_bytes=VMEM_LIMIT),
     )(*args)
+
+
+def local_copies(*args):
+    return [pltpu.VMEM(x.shape, x.dtype) for x in args] + [pltpu.SemaphoreType.DMA((len(args),))]
 
 
 def aligned(
@@ -181,6 +246,7 @@
     vocab = lax.axis_size("vocab")
     dp = lax.axis_size("dp")
     chips = vocab // CORES
+    half = chips // 2
     rows = logit_grad.shape[1]
     shard = master.shape[0]
     cols = hidden.shape[1] * CORES
@@ -188,6 +254,7 @@
     owners, cap, width = slot_grads.shape[1:]
     sizes = (chips, dp, shard)
     bf16, f32 = jnp.bfloat16, jnp.float32
+    far, near = range(half, chips), range(half)
 
     def send(x, s, away=0):
         move = s * CORES + away
@@ -196,52 +263,75 @@
     def send_dp(x, t):
         return lax.ppermute(x, "dp", [(i, i ^ t) for i in range(dp)]) if t else x
 
-    columns = logit_grad.T
-    columns = [send(columns, s) for s in range(chips)]
+    columns = [logit_grad.T]
+    for s in range(1, chips):
+        columns.append(send(columns[s - 1], 1) if s % 2 else send(columns[0], s))
     hidden_other = send(hidden, 0, 1)
-    messages = run(
-        functools.partial(slots_kernel, *sizes),
-        [shaped((cap * chips, cols + LANES), bf16)] * (CORES * chips),
+    slots_in = (
         slot_grads[0].transpose(1, 0, 2).reshape(cap * owners, width),
         slot_rows.transpose(2, 0, 1),
         slot_counts,
     )
-    arrived = [send(messages[away * chips + s], s, away) for s in range(chips) for away in range(CORES)]
+    slots_own, slots_other = run(
+        functools.partial(slots_kernel, *sizes),
+        [shaped((cap * chips, chips * (cols + LANES)), bf16)] * CORES,
+        *slots_in,
+        hbm=3,
+        scratch=local_copies(*slots_in),
+    )
+    messages = run(
+        functools.partial(merge_kernel, chips),
+        [shaped((cap * half * CORES, cols + LANES), bf16)] * (2 * chips),
+        slots_own,
+        send(slots_other, 0, 1),
+    )
+    head_in = (predict_mask[None, :], hidden, columns[0])
     head = run(
         functools.partial(head_kernel, *sizes),
-        shaped((chips * rows, cols), f32),
-        predict_mask[None, :],
-        hidden,
+        [shaped((half * rows, cols), f32)] * 2,
+        *head_in,
         hidden_other,
-        *columns,
+        *columns[1:],
         flops=2 * chips * rows * depth * cols,
-    )
-    parts = run(
-        functools.partial(embed_kernel, *sizes),
-        [shaped((chips * shard, cols), f32)] * dp,
-        head,
-        *arrived,
-    )
-    parts = [send_dp(parts[t], t) for t in range(dp)]
-    pieces = run(
-        functools.partial(sum_kernel, chips, shard),
-        [shaped((CORES * shard, cols // CORES), f32)] * chips,
-        *parts,
-    )
-    pieces = [send(pieces[s], s) for s in range(chips)]
-    master_new, first_new, second_new, table = run(
-        functools.partial(adam_kernel, chips, shard),
-        [shaped(master.shape, f32)] * 3 + [shaped((chips * shard, cols), bf16)],
-        master,
-        first_moment,
-        second_moment,
-        *pieces,
-    )
-    table = run(
-        functools.partial(table_kernel, chips, shard),
-        shaped((rows, width), bf16),
-        *[send_dp(table, t) for t in range(dp)],
-    )
+        hbm=3,
+        scratch=local_copies(*head_in),
+    )
+    state = (master, first_moment, second_moment)
+    messages = [messages[:chips], messages[chips:]]
+    pieces, table = {}, []
+    for h, members in enumerate((far, near)):
+        start = head[h]
+        if h:
+            messages[h], _ = lax.optimization_barrier((messages[h], arrived[1]))
+            start, _ = lax.optimization_barrier((start, parts[0]))
+        arrived = [send(messages[h][s], s) for s in range(chips)]
+        parts = run(
+            functools.partial(embed_kernel, *sizes),
+            [shaped((half * shard, cols), f32)] * dp,
+            start,
+            *arrived,
+        )
+        sums = run(
+            functools.partial(sum_kernel, half, shard),
+            [shaped((CORES * shard, cols // CORES), f32)] * half,
+            *[send_dp(part, t) for t, part in enumerate(parts)],
+        )
+        for s, total in zip(members, sums):
+            pieces[s] = send(total, s)
+        table_rows = run(
+            functools.partial(rows_kernel, tuple(members), shard),
+            shaped((half * shard, cols), bf16),
+            *state,
+            *[pieces[s] for s in members],
+        )
+        table = [send_dp(table_rows, t) for t in range(dp)] + table
+    master_new, first_new, second_new = run(
+        functools.partial(adam_kernel, shard),
+        [shaped(master.shape, f32)] * 3,
+        *state,
+        *[pieces[s] for s in range(chips)],
+    )
+    table = run(functools.partial(table_kernel, *sizes), shaped((rows, width), bf16), *table)
     return (master_new, first_new, second_new, table)
 
 

time: 63.1 us -> 58.8 us (0.932)
  waiting for transfers between devices: 27.8 us -> 14.3 us
  starting transfers between devices: 24.7 us -> 36.2 us
  local copies, waits for them, and re-layouts: 5.28 us -> 0.02 us
  Pallas kernels: 4.26 us -> 7.41 us
    ppermute x6 -> x12, waiting for transfers between devices: 16.3 us -> 5.01 us  [send_dp(): return lax.ppermute(x, 'dp', [(i, i ^ t) for i in range(dp)]) if t else x]
    ppermute x6 -> x12, starting transfers between devices: 7.04 us -> 14.2 us  [send_dp(): return lax.ppermute(x, 'dp', [(i, i ^ t) for i in range(dp)]) if t else x]
    unnamed x18 -> x6, local copies, waits for them, and re-layouts: 5.28 us -> 0.02 us
    ppermute x14, starting transfers between devices: 17.7 us -> 22 us  [send(): lax.ppermute(x, 'vocab', [(v, v ^ move) for v in range(vocab)])]
    pallas_call x6 -> x11, Pallas kernels: 4.26 us -> 7.41 us  [run(): pl.pallas_call(kernel, out_shape=outs, in_specs=[pl.BlockSpec(memory_spac...]
    ppermute x14, waiting for transfers between devices: 11.5 us -> 9.25 us  [send(): lax.ppermute(x, 'vocab', [(v, v ^ move) for v in range(vocab)])]
  transfers between devices with their start and end apart: 20 -> 26, of which waited for: 10 -> 7; matrix products, arithmetic and copies ran while one was open for 0% -> 0% of each run, Pallas kernels for 2% -> 11%
where the time goes in v4:
time: 58.8 us; the launch traced here: 58.6 us
  starting transfers between devices  36.2 us (62%)
  waiting for transfers between devices  14.3 us (24%)
  Pallas kernels  7.41 us (13%)
  between operations  0.76 us (1%)
    ppermute x14, starting transfers between devices, send(): lax.ppermute(x, 'vocab', [(v, v ^ move) for v in range(vocab)])  22 us
    ppermute x12, starting transfers between devices, send_dp(): return lax.ppermute(x, 'dp', [(i, i ^ t) for i in range(dp)]) if t else x  14.2 us
    ppermute x14, waiting for transfers between devices, send(): lax.ppermute(x, 'vocab', [(v, v ^ move) for v in range(vocab)])  9.25 us
    pallas_call x11, Pallas kernels, run(): pl.pallas_call(kernel, out_shape=outs, in_specs=[pl.BlockSpec(memory_spac...  7.41 us
    ppermute x12, waiting for transfers between devices, send_dp(): return lax.ppermute(x, 'dp', [(i, i ^ t) for i in range(dp)]) if t else x  5.01 us
  transfers between devices with their start and end apart: 26, of which 7 were waited for; matrix products, arithmetic and copies ran while one was open for 0% of the time, Pallas kernels for 11%

profile of v4, /device:TPU:0, one launch (start us, length us, event | category | flops | bytes accessed | tf_op | source)
XLA Modules:
  0.0 58.6 jit_solution(10825662565565582281)
XLA Ops:
  0.6 0.5 collective-permute-start
  1.1 1.5 %shard_map.121 = (bf16[24,5632]{1,0:T(8,128)(2,1)S(1)}, bf16[24,5632]{1,0:T(8,128)(2,1)S(1)}) custom-call(bf16[48,5120]{1,0:T(8,128)(2,1)} %bitcast.8, s32[6,1,8]{2,1,0:T(1,128)} %bitcast.13, s32[1,8]{1,0:T(1,128)} %counts_hbm.1), custom_call_target="tpu_custom_call" | custom-call | bytes 1032416 | tf_op jit(solution)/shard_map/pallas_call | solution.py:220
  2.6 0.1 collective-permute-start.4
  2.7 4.0 %collective-permute-start.2 = (bf16[48,1024]{1,0:T(8,128)(2,1)}, bf16[48,1024]{1,0:T(8,128)(2,1)S(1)}, u32[]{:S(2)}, u32[]{:S(2)}) collective-permute-start(bf16[48,1024]{1,0:T(8,128)(2,1)} %bitcast.9), channel_id=1, source_target_pairs={{0,4},{1,5},{2,6},{3,7},{4,0},{5,1},{6,2},{7,3},{8,12},{9,13},{10,... | collective-permute-start | bytes 294920 | tf_op jit(solution)/shard_map/ppermute | solution.py:261
  6.8 1.6 %collective-permute-start.1 = (bf16[48,1024]{1,0:T(8,128)(2,1)}, bf16[48,1024]{1,0:T(8,128)(2,1)S(1)}, u32[]{:S(2)}, u32[]{:S(2)}) collective-permute-start(bf16[48,1024]{1,0:T(8,128)(2,1)} %bitcast.10), channel_id=1, source_target_pairs={{0,2},{1,3},{2,0},{3,1},{4,6},{5,7},{6,4},{7,5},{8,10},{9,11},{10,... | collective-permute-start | bytes 294920 | tf_op jit(solution)/shard_map/ppermute | solution.py:261
  8.4 3.9 %collective-permute-done.2.refs_1_ = bf16[48,1024]{1,0:T(8,128)(2,1)S(1)} collective-permute-done((bf16[48,1024]{1,0:T(8,128)(2,1)}, bf16[48,1024]{1,0:T(8,128)(2,1)S(1)}, u32[]{:S(2)}, u32[]{:S(2)}) %collective-permute-start.2) | collective-permute-done | bytes 98336 | tf_op jit(solution)/shard_map/ppermute | solution.py:261
  12.2 0.7 %collective-permute-start.3 = (bf16[48,1024]{1,0:T(8,128)(2,1)S(1)}, bf16[48,1024]{1,0:T(8,128)(2,1)S(1)}, u32[]{:S(2)}, u32[]{:S(2)}) collective-permute-start(bf16[48,1024]{1,0:T(8,128)(2,1)S(1)} %collective-permute-done.2.refs_1_), channel_id=1, source_target_pairs={{0,2},{1,3},{2,0},{3,1},{4,6},{5,7},{6,4},{7,5},{8,10},{9,11},{10,... | collective-permute-start | bytes 294920 | tf_op jit(solution)/shard_map/ppermute | solution.py:261
  13.0 0.1 shard_map.122
  13.1 1.4 %collective-permute-start.5 = (bf16[24,1408]{1,0:T(8,128)(2,1)S(1)}, bf16[24,1408]{1,0:T(8,128)(2,1)S(1)}, u32[]{:S(2)}, u32[]{:S(2)}) collective-permute-start(bf16[24,1408]{1,0:T(8,128)(2,1)S(1)} %get-tuple-element.41), channel_id=1, source_target_pairs={{0,2},{1,3},{2,0},{3,1},{4,6},{5,7},{6,4},{7,5},{8,10},{9,11},{10,... | collective-permute-start | bytes 202760 | tf_op jit(solution)/shard_map/ppermute | solution.py:261
  14.4 2.0 %collective-permute-start.6 = (bf16[24,1408]{1,0:T(8,128)(2,1)S(1)}, bf16[24,1408]{1,0:T(8,128)(2,1)S(1)}, u32[]{:S(2)}, u32[]{:S(2)}) collective-permute-start(bf16[24,1408]{1,0:T(8,128)(2,1)S(1)} %get-tuple-element.42), channel_id=1, source_target_pairs={{0,4},{1,5},{2,6},{3,7},{4,0},{5,1},{6,2},{7,3},{8,12},{9,13},{10,... | collective-permute-start | bytes 202760 | tf_op jit(solution)/shard_map/ppermute | solution.py:261
  16.5 2.2 %collective-permute-done.5.refs_1_ = bf16[24,1408]{1,0:T(8,128)(2,1)S(1)} collective-permute-done((bf16[24,1408]{1,0:T(8,128)(2,1)S(1)}, bf16[24,1408]{1,0:T(8,128)(2,1)S(1)}, u32[]{:S(2)}, u32[]{:S(2)}) %collective-permute-start.5) | collective-permute-done | bytes 67616 | tf_op jit(solution)/shard_map/ppermute | solution.py:261
  18.7 3.5 %collective-permute-start.7 = (bf16[24,1408]{1,0:T(8,128)(2,1)S(1)}, bf16[24,1408]{1,0:T(8,128)(2,1)S(1)}, u32[]{:S(2)}, u32[]{:S(2)}) collective-permute-start(bf16[24,1408]{1,0:T(8,128)(2,1)S(1)} %get-tuple-element.43), channel_id=1, source_target_pairs={{0,6},{1,7},{2,4},{3,5},{4,2},{5,3},{6,0},{7,1},{8,14},{9,15},{10,... | collective-permute-start | bytes 202760 | tf_op jit(solution)/shard_map/ppermute | solution.py:261
  22.2 0.0 collective-permute-done.1.refs_0_
  22.2 0.3 collective-permute-start.10
  22.5 0.0 collective-permute-done.3.refs_2_
  22.5 2.4 %shard_map.120 = (f32[96,1280]{1,0:T(8,128)S(1)}, f32[96,1280]{1,0:T(8,128)S(1)}) custom-call(s32[1,1024]{1,0:T(1,128)} %bitcast.12, bf16[1024,640]{1,0:T(8,128)(2,1)} %hidden_hbm.1, bf16[48,1024]{1,0:T(8,128)(2,1)} %bitcast.11, bf16[1024,640]{1,0:T(8,128)(2,1)S(1)} %collective-permute-done.other_ref, bf16[48,1024]{1,0:T(8,128)(2,1)S(1)} %collective-permute-done.1.refs_0_, ...), custom_call_target="tpu_custom_call" | custom-call | flops 503316480 | bytes 4001792 | tf_op jit(solution)/shard_map/pallas_call | solution.py:220
  24.9 0.0 copy-start
  24.9 0.0 copy-start.1
  24.9 0.0 copy-start.2
  24.9 0.0 collective-permute-done.6.refs_2_
  24.9 0.4 shard_map.123
  25.3 1.6 %collective-permute-start.15 = (f32[24,1280]{1,0:T(8,128)S(1)}, f32[24,1280]{1,0:T(8,128)S(1)}, u32[]{:S(2)}, u32[]{:S(2)}) collective-permute-start(f32[24,1280]{1,0:T(8,128)S(1)} %get-tuple-element.60), channel_id=1, source_target_pairs={{0,8},{8,0},{16,24},{24,16},{1,9},{9,1},{17,25},{25,17},{2,10},{10... | collective-permute-start | bytes 368648 | tf_op jit(solution)/shard_map/ppermute | solution.py:264
  26.9 0.7 %collective-permute-start.8 = (bf16[24,1408]{1,0:T(8,128)(2,1)S(1)}, bf16[24,1408]{1,0:T(8,128)(2,1)S(1)}, u32[]{:S(2)}, u32[]{:S(2)}) collective-permute-start(bf16[24,1408]{1,0:T(8,128)(2,1)S(1)} %get-tuple-element.51), channel_id=1, source_target_pairs={{0,2},{1,3},{2,0},{3,1},{4,6},{5,7},{6,4},{7,5},{8,10},{9,11},{10,... | collective-permute-start | bytes 202760 | tf_op jit(solution)/shard_map/ppermute | solution.py:261
  27.5 3.4 %collective-permute-start.9 = (bf16[24,1408]{1,0:T(8,128)(2,1)S(1)}, bf16[24,1408]{1,0:T(8,128)(2,1)S(1)}, u32[]{:S(2)}, u32[]{:S(2)}) collective-permute-start(bf16[24,1408]{1,0:T(8,128)(2,1)S(1)} %get-tuple-element.52), channel_id=1, source_target_pairs={{0,4},{1,5},{2,6},{3,7},{4,0},{5,1},{6,2},{7,3},{8,12},{9,13},{10,... | collective-permute-start | bytes 202760 | tf_op jit(solution)/shard_map/ppermute | solution.py:261
  30.9 1.5 %collective-permute-start.16 = (f32[24,1280]{1,0:T(8,128)S(1)}, f32[24,1280]{1,0:T(8,128)S(1)}, u32[]{:S(2)}, u32[]{:S(2)}) collective-permute-start(f32[24,1280]{1,0:T(8,128)S(1)} %get-tuple-element.61), channel_id=1, source_target_pairs={{0,16},{8,24},{16,0},{24,8},{1,17},{9,25},{17,1},{25,9},{2,18},{10... | collective-permute-start | bytes 368648 | tf_op jit(solution)/shard_map/ppermute | solution.py:264
  32.5 0.5 collective-permute-start.17
  33.0 0.3 collective-permute-done.9.refs_2_
  33.2 0.3 shard_map.124
  33.6 1.3 %collective-permute-start.11 = (f32[24,1280]{1,0:T(8,128)S(1)}, f32[24,1280]{1,0:T(8,128)S(1)}, u32[]{:S(2)}, u32[]{:S(2)}) collective-permute-start(f32[24,1280]{1,0:T(8,128)S(1)} %get-tuple-element.55), channel_id=1, source_target_pairs={{0,8},{8,0},{16,24},{24,16},{1,9},{9,1},{17,25},{25,17},{2,10},{10... | collective-permute-start | bytes 368648 | tf_op jit(solution)/shard_map/ppermute | solution.py:264
  34.9 1.5 %collective-permute-start.12 = (f32[24,1280]{1,0:T(8,128)S(1)}, f32[24,1280]{1,0:T(8,128)S(1)}, u32[]{:S(2)}, u32[]{:S(2)}) collective-permute-start(f32[24,1280]{1,0:T(8,128)S(1)} %get-tuple-element.56), channel_id=1, source_target_pairs={{0,16},{8,24},{16,0},{24,8},{1,17},{9,25},{17,1},{25,9},{2,18},{10... | collective-permute-start | bytes 368648 | tf_op jit(solution)/shard_map/ppermute | solution.py:264
  36.4 0.7 %collective-permute-start.13 = (f32[24,1280]{1,0:T(8,128)S(1)}, f32[24,1280]{1,0:T(8,128)S(1)}, u32[]{:S(2)}, u32[]{:S(2)}) collective-permute-start(f32[24,1280]{1,0:T(8,128)S(1)} %get-tuple-element.57), channel_id=1, source_target_pairs={{0,24},{8,16},{16,8},{24,0},{1,25},{9,17},{17,9},{25,1},{2,26},{10... | collective-permute-start | bytes 368648 | tf_op jit(solution)/shard_map/ppermute | solution.py:264
  37.1 2.7 %collective-permute-done.16.refs_2_ = f32[24,1280]{1,0:T(8,128)S(1)} collective-permute-done((f32[24,1280]{1,0:T(8,128)S(1)}, f32[24,1280]{1,0:T(8,128)S(1)}, u32[]{:S(2)}, u32[]{:S(2)}) %collective-permute-start.16) | collective-permute-done | bytes 122912 | tf_op jit(solution)/shard_map/ppermute | solution.py:264
  39.8 0.4 collective-permute-start.18
  40.3 2.3 %collective-permute-start.19 = (f32[24,640]{1,0:T(8,128)S(1)}, f32[24,640]{1,0:T(8,128)S(1)}, u32[]{:S(2)}, u32[]{:S(2)}) collective-permute-start(f32[24,640]{1,0:T(8,128)S(1)} %get-tuple-element.64), channel_id=1, source_target_pairs={{0,6},{1,7},{2,4},{3,5},{4,2},{5,3},{6,0},{7,1},{8,14},{9,15},{10,... | collective-permute-start | bytes 184328 | tf_op jit(solution)/shard_map/ppermute | solution.py:261
  42.6 0.9 %collective-permute-start.14 = (f32[24,640]{1,0:T(8,128)S(1)}, f32[24,640]{1,0:T(8,128)S(1)}, u32[]{:S(2)}, u32[]{:S(2)}) collective-permute-start(f32[24,640]{1,0:T(8,128)S(1)} %get-tuple-element.59), channel_id=1, source_target_pairs={{0,2},{1,3},{2,0},{3,1},{4,6},{5,7},{6,4},{7,5},{8,10},{9,11},{10,... | collective-permute-start | bytes 184328 | tf_op jit(solution)/shard_map/ppermute | solution.py:261
  43.5 1.9 %collective-permute-done.18.refs_5_.refs_3_ = f32[24,640]{1,0:T(8,128)S(1)} collective-permute-done((f32[24,640]{1,0:T(8,128)S(1)}, f32[24,640]{1,0:T(8,128)S(1)}, u32[]{:S(2)}, u32[]{:S(2)}) %collective-permute-start.18) | collective-permute-done | bytes 61472 | tf_op jit(solution)/shard_map/ppermute | solution.py:261
  45.4 1.0 %collective-permute-done.19.refs_6_.refs_4_ = f32[24,640]{1,0:T(8,128)S(1)} collective-permute-done((f32[24,640]{1,0:T(8,128)S(1)}, f32[24,640]{1,0:T(8,128)S(1)}, u32[]{:S(2)}, u32[]{:S(2)}) %collective-permute-start.19) | collective-permute-done | bytes 61472 | tf_op jit(solution)/shard_map/ppermute | solution.py:261
  46.4 0.2 shard_map.129.refs_4_
  46.6 0.6 collective-permute-start.23
  47.1 1.5 %collective-permute-start.24 = (bf16[24,1280]{1,0:T(8,128)(2,1)S(1)}, bf16[24,1280]{1,0:T(8,128)(2,1)S(1)}, u32[]{:S(2)}, u32[]{:S(2)}) collective-permute-start(bf16[24,1280]{1,0:T(8,128)(2,1)S(1)} %shard_map.129.refs_4_), channel_id=1, source_target_pairs={{0,16},{8,24},{16,0},{24,8},{1,17},{9,25},{17,1},{25,9},{2,18},{10... | collective-permute-start | bytes 184328 | tf_op jit(solution)/shard_map/ppermute | solution.py:264
  48.6 1.5 %collective-permute-start.25 = (bf16[24,1280]{1,0:T(8,128)(2,1)S(1)}, bf16[24,1280]{1,0:T(8,128)(2,1)S(1)}, u32[]{:S(2)}, u32[]{:S(2)}) collective-permute-start(bf16[24,1280]{1,0:T(8,128)(2,1)S(1)} %shard_map.129.refs_4_), channel_id=1, source_target_pairs={{0,24},{8,16},{16,8},{24,0},{1,25},{9,17},{17,9},{25,1},{2,26},{10... | collective-permute-start | bytes 184328 | tf_op jit(solution)/shard_map/ppermute | solution.py:264
  50.1 0.2 shard_map.128.refs_0_
  50.3 0.6 collective-permute-start.20
  50.8 1.5 %collective-permute-start.21 = (bf16[24,1280]{1,0:T(8,128)(2,1)S(1)}, bf16[24,1280]{1,0:T(8,128)(2,1)S(1)}, u32[]{:S(2)}, u32[]{:S(2)}) collective-permute-start(bf16[24,1280]{1,0:T(8,128)(2,1)S(1)} %shard_map.128.refs_0_), channel_id=1, source_target_pairs={{0,16},{8,24},{16,0},{24,8},{1,17},{9,25},{17,1},{25,9},{2,18},{10... | collective-permute-start | bytes 184328 | tf_op jit(solution)/shard_map/ppermute | solution.py:264
  52.4 1.5 %collective-permute-start.22 = (bf16[24,1280]{1,0:T(8,128)(2,1)S(1)}, bf16[24,1280]{1,0:T(8,128)(2,1)S(1)}, u32[]{:S(2)}, u32[]{:S(2)}) collective-permute-start(bf16[24,1280]{1,0:T(8,128)(2,1)S(1)} %shard_map.128.refs_0_), channel_id=1, source_target_pairs={{0,24},{8,16},{16,8},{24,0},{1,25},{9,17},{17,9},{25,1},{2,26},{10... | collective-permute-start | bytes 184328 | tf_op jit(solution)/shard_map/ppermute | solution.py:264
  53.9 1.3 %shard_map.127 = (f32[12,5120]{1,0:T(8,128)}, f32[12,5120]{1,0:T(8,128)}, f32[12,5120]{1,0:T(8,128)}) custom-call(f32[12,5120]{1,0:T(8,128)S(1)} %copy-done, f32[12,5120]{1,0:T(8,128)S(1)} %copy-done.1, f32[12,5120]{1,0:T(8,128)S(1)} %copy-done.2, f32[24,640]{1,0:T(8,128)S(1)} %get-tuple-element.58.refs_3_, f32[24,640]{1,0:T(8,128)S(1)} %collective-permute-done.14.refs_4_, ...), custom_call_target="tpu_custom_call" | custom-call | bytes 1720320 | tf_op jit(solution)/shard_map/pallas_call | solution.py:220
  55.2 2.3 %collective-permute-done.22.refs_3_ = bf16[24,1280]{1,0:T(8,128)(2,1)S(1)} collective-permute-done((bf16[24,1280]{1,0:T(8,128)(2,1)S(1)}, bf16[24,1280]{1,0:T(8,128)(2,1)S(1)}, u32[]{:S(2)}, u32[]{:S(2)}) %collective-permute-start.22) | collective-permute-done | bytes 61472 | tf_op jit(solution)/shard_map/ppermute | solution.py:264
  57.5 1.1 %shard_map.130 = bf16[48,5120]{1,0:T(8,128)(2,1)} custom-call(bf16[24,1280]{1,0:T(8,128)(2,1)S(1)} %shard_map.128.refs_0_, bf16[24,1280]{1,0:T(8,128)(2,1)S(1)} %collective-permute-done.20.refs_1_, bf16[24,1280]{1,0:T(8,128)(2,1)S(1)} %collective-permute-done.21.refs_2_, bf16[24,1280]{1,0:T(8,128)(2,1)S(1)} %collective-permute-done.22.refs_3_, ...), custom_call_target="tpu_custom_call" | custom-call | bytes 983040 | tf_op jit(solution)/shard_map/pallas_call | solution.py:220
  (21 shorter events, 0.1 us)
Async XLA Ops:
  0.6 21.9 %collective-permute-start = (bf16[1024,640]{1,0:T(8,128)(2,1)}, bf16[1024,640]{1,0:T(8,128)(2,1)S(1)}, u32[]{:S(2)}, u32[]{:S(2)}) collective-permute-start(bf16[1024,640]{1,0:T(8,128)(2,1)} %hidden_hbm.1), channel_id=1, source_target_pairs={{0,1},{1,0},{2,3},{3,2},{4,5},{5,4},{6,7},{7,6},{8,9},{9,8},{10,11... | collective-permute-start | bytes 3932168 | tf_op jit(solution)/shard_map/ppermute | solution.py:261
  2.6 10.3 %collective-permute-start.4 = (bf16[24,5632]{1,0:T(8,128)(2,1)S(1)}, bf16[24,5632]{1,0:T(8,128)(2,1)S(1)}, u32[]{:S(2)}, u32[]{:S(2)}) collective-permute-start(bf16[24,5632]{1,0:T(8,128)(2,1)S(1)} %get-tuple-element.39), channel_id=1, source_target_pairs={{0,1},{1,0},{2,3},{3,2},{4,5},{5,4},{6,7},{7,6},{8,9},{9,8},{10,11... | collective-permute-start | bytes 811016 | tf_op jit(solution)/shard_map/ppermute | solution.py:261
  2.7 9.5 %collective-permute-start.2 = (bf16[48,1024]{1,0:T(8,128)(2,1)}, bf16[48,1024]{1,0:T(8,128)(2,1)S(1)}, u32[]{:S(2)}, u32[]{:S(2)}) collective-permute-start(bf16[48,1024]{1,0:T(8,128)(2,1)} %bitcast.9), channel_id=1, source_target_pairs={{0,4},{1,5},{2,6},{3,7},{4,0},{5,1},{6,2},{7,3},{8,12},{9,13},{10,... | collective-permute-start | bytes 294920 | tf_op jit(solution)/shard_map/ppermute | solution.py:261
  6.8 15.4 %collective-permute-start.1 = (bf16[48,1024]{1,0:T(8,128)(2,1)}, bf16[48,1024]{1,0:T(8,128)(2,1)S(1)}, u32[]{:S(2)}, u32[]{:S(2)}) collective-permute-start(bf16[48,1024]{1,0:T(8,128)(2,1)} %bitcast.10), channel_id=1, source_target_pairs={{0,2},{1,3},{2,0},{3,1},{4,6},{5,7},{6,4},{7,5},{8,10},{9,11},{10,... | collective-permute-start | bytes 294920 | tf_op jit(solution)/shard_map/ppermute | solution.py:261
  12.2 10.3 %collective-permute-start.3 = (bf16[48,1024]{1,0:T(8,128)(2,1)S(1)}, bf16[48,1024]{1,0:T(8,128)(2,1)S(1)}, u32[]{:S(2)}, u32[]{:S(2)}) collective-permute-start(bf16[48,1024]{1,0:T(8,128)(2,1)S(1)} %collective-permute-done.2.refs_1_), channel_id=1, source_target_pairs={{0,2},{1,3},{2,0},{3,1},{4,6},{5,7},{6,4},{7,5},{8,10},{9,11},{10,... | collective-permute-start | bytes 294920 | tf_op jit(solution)/shard_map/ppermute | solution.py:261
  13.1 5.6 %collective-permute-start.5 = (bf16[24,1408]{1,0:T(8,128)(2,1)S(1)}, bf16[24,1408]{1,0:T(8,128)(2,1)S(1)}, u32[]{:S(2)}, u32[]{:S(2)}) collective-permute-start(bf16[24,1408]{1,0:T(8,128)(2,1)S(1)} %get-tuple-element.41), channel_id=1, source_target_pairs={{0,2},{1,3},{2,0},{3,1},{4,6},{5,7},{6,4},{7,5},{8,10},{9,11},{10,... | collective-permute-start | bytes 202760 | tf_op jit(solution)/shard_map/ppermute | solution.py:261
  14.4 10.5 %collective-permute-start.6 = (bf16[24,1408]{1,0:T(8,128)(2,1)S(1)}, bf16[24,1408]{1,0:T(8,128)(2,1)S(1)}, u32[]{:S(2)}, u32[]{:S(2)}) collective-permute-start(bf16[24,1408]{1,0:T(8,128)(2,1)S(1)} %get-tuple-element.42), channel_id=1, source_target_pairs={{0,4},{1,5},{2,6},{3,7},{4,0},{5,1},{6,2},{7,3},{8,12},{9,13},{10,... | collective-permute-start | bytes 202760 | tf_op jit(solution)/shard_map/ppermute | solution.py:261
  18.7 6.3 %collective-permute-start.7 = (bf16[24,1408]{1,0:T(8,128)(2,1)S(1)}, bf16[24,1408]{1,0:T(8,128)(2,1)S(1)}, u32[]{:S(2)}, u32[]{:S(2)}) collective-permute-start(bf16[24,1408]{1,0:T(8,128)(2,1)S(1)} %get-tuple-element.43), channel_id=1, source_target_pairs={{0,6},{1,7},{2,4},{3,5},{4,2},{5,3},{6,0},{7,1},{8,14},{9,15},{10,... | collective-permute-start | bytes 202760 | tf_op jit(solution)/shard_map/ppermute | solution.py:261
  22.2 10.3 %collective-permute-start.10 = (bf16[24,1408]{1,0:T(8,128)(2,1)S(1)}, bf16[24,1408]{1,0:T(8,128)(2,1)S(1)}, u32[]{:S(2)}, u32[]{:S(2)}) collective-permute-start(bf16[24,1408]{1,0:T(8,128)(2,1)S(1)} %get-tuple-element.53), channel_id=1, source_target_pairs={{0,6},{1,7},{2,4},{3,5},{4,2},{5,3},{6,0},{7,1},{8,14},{9,15},{10,... | collective-permute-start | bytes 202760 | tf_op jit(solution)/shard_map/ppermute | solution.py:261
  24.9 21.5 %copy-start = (f32[12,5120]{1,0:T(8,128)S(1)}, f32[12,5120]{1,0:T(8,128)}, u32[]{:S(2)}) copy-start(f32[12,5120]{1,0:T(8,128)} %refs_0_.5) | copy-start | bytes 737284
  24.9 21.5 %copy-start.1 = (f32[12,5120]{1,0:T(8,128)S(1)}, f32[12,5120]{1,0:T(8,128)}, u32[]{:S(2)}) copy-start(f32[12,5120]{1,0:T(8,128)} %refs_1_.5) | copy-start | bytes 737284
  24.9 21.5 %copy-start.2 = (f32[12,5120]{1,0:T(8,128)S(1)}, f32[12,5120]{1,0:T(8,128)}, u32[]{:S(2)}) copy-start(f32[12,5120]{1,0:T(8,128)} %refs_2_.5) | copy-start | bytes 737284
  25.3 11.1 %collective-permute-start.15 = (f32[24,1280]{1,0:T(8,128)S(1)}, f32[24,1280]{1,0:T(8,128)S(1)}, u32[]{:S(2)}, u32[]{:S(2)}) collective-permute-start(f32[24,1280]{1,0:T(8,128)S(1)} %get-tuple-element.60), channel_id=1, source_target_pairs={{0,8},{8,0},{16,24},{24,16},{1,9},{9,1},{17,25},{25,17},{2,10},{10... | collective-permute-start | bytes 368648 | tf_op jit(solution)/shard_map/ppermute | solution.py:264
  26.9 6.1 %collective-permute-start.8 = (bf16[24,1408]{1,0:T(8,128)(2,1)S(1)}, bf16[24,1408]{1,0:T(8,128)(2,1)S(1)}, u32[]{:S(2)}, u32[]{:S(2)}) collective-permute-start(bf16[24,1408]{1,0:T(8,128)(2,1)S(1)} %get-tuple-element.51), channel_id=1, source_target_pairs={{0,2},{1,3},{2,0},{3,1},{4,6},{5,7},{6,4},{7,5},{8,10},{9,11},{10,... | collective-permute-start | bytes 202760 | tf_op jit(solution)/shard_map/ppermute | solution.py:261
  27.5 5.7 %collective-permute-start.9 = (bf16[24,1408]{1,0:T(8,128)(2,1)S(1)}, bf16[24,1408]{1,0:T(8,128)(2,1)S(1)}, u32[]{:S(2)}, u32[]{:S(2)}) collective-permute-start(bf16[24,1408]{1,0:T(8,128)(2,1)S(1)} %get-tuple-element.52), channel_id=1, source_target_pairs={{0,4},{1,5},{2,6},{3,7},{4,0},{5,1},{6,2},{7,3},{8,12},{9,13},{10,... | collective-permute-start | bytes 202760 | tf_op jit(solution)/shard_map/ppermute | solution.py:261
  30.9 8.8 %collective-permute-start.16 = (f32[24,1280]{1,0:T(8,128)S(1)}, f32[24,1280]{1,0:T(8,128)S(1)}, u32[]{:S(2)}, u32[]{:S(2)}) collective-permute-start(f32[24,1280]{1,0:T(8,128)S(1)} %get-tuple-element.61), channel_id=1, source_target_pairs={{0,16},{8,24},{16,0},{24,8},{1,17},{9,25},{17,1},{25,9},{2,18},{10... | collective-permute-start | bytes 368648 | tf_op jit(solution)/shard_map/ppermute | solution.py:264
  32.5 7.3 %collective-permute-start.17 = (f32[24,1280]{1,0:T(8,128)S(1)}, f32[24,1280]{1,0:T(8,128)S(1)}, u32[]{:S(2)}, u32[]{:S(2)}) collective-permute-start(f32[24,1280]{1,0:T(8,128)S(1)} %get-tuple-element.62), channel_id=1, source_target_pairs={{0,24},{8,16},{16,8},{24,0},{1,25},{9,17},{17,9},{25,1},{2,26},{10... | collective-permute-start | bytes 368648 | tf_op jit(solution)/shard_map/ppermute | solution.py:264
  33.6 9.0 %collective-permute-start.11 = (f32[24,1280]{1,0:T(8,128)S(1)}, f32[24,1280]{1,0:T(8,128)S(1)}, u32[]{:S(2)}, u32[]{:S(2)}) collective-permute-start(f32[24,1280]{1,0:T(8,128)S(1)} %get-tuple-element.55), channel_id=1, source_target_pairs={{0,8},{8,0},{16,24},{24,16},{1,9},{9,1},{17,25},{25,17},{2,10},{10... | collective-permute-start | bytes 368648 | tf_op jit(solution)/shard_map/ppermute | solution.py:264
  34.9 7.7 %collective-permute-start.12 = (f32[24,1280]{1,0:T(8,128)S(1)}, f32[24,1280]{1,0:T(8,128)S(1)}, u32[]{:S(2)}, u32[]{:S(2)}) collective-permute-start(f32[24,1280]{1,0:T(8,128)S(1)} %get-tuple-element.56), channel_id=1, source_target_pairs={{0,16},{8,24},{16,0},{24,8},{1,17},{9,25},{17,1},{25,9},{2,18},{10... | collective-permute-start | bytes 368648 | tf_op jit(solution)/shard_map/ppermute | solution.py:264
  36.4 6.1 %collective-permute-start.13 = (f32[24,1280]{1,0:T(8,128)S(1)}, f32[24,1280]{1,0:T(8,128)S(1)}, u32[]{:S(2)}, u32[]{:S(2)}) collective-permute-start(f32[24,1280]{1,0:T(8,128)S(1)} %get-tuple-element.57), channel_id=1, source_target_pairs={{0,24},{8,16},{16,8},{24,0},{1,25},{9,17},{17,9},{25,1},{2,26},{10... | collective-permute-start | bytes 368648 | tf_op jit(solution)/shard_map/ppermute | solution.py:264
  39.8 5.6 %collective-permute-start.18 = (f32[24,640]{1,0:T(8,128)S(1)}, f32[24,640]{1,0:T(8,128)S(1)}, u32[]{:S(2)}, u32[]{:S(2)}) collective-permute-start(f32[24,640]{1,0:T(8,128)S(1)} %get-tuple-element.63), channel_id=1, source_target_pairs={{0,4},{1,5},{2,6},{3,7},{4,0},{5,1},{6,2},{7,3},{8,12},{9,13},{10,... | collective-permute-start | bytes 184328 | tf_op jit(solution)/shard_map/ppermute | solution.py:261
  40.3 6.1 %collective-permute-start.19 = (f32[24,640]{1,0:T(8,128)S(1)}, f32[24,640]{1,0:T(8,128)S(1)}, u32[]{:S(2)}, u32[]{:S(2)}) collective-permute-start(f32[24,640]{1,0:T(8,128)S(1)} %get-tuple-element.64), channel_id=1, source_target_pairs={{0,6},{1,7},{2,4},{3,5},{4,2},{5,3},{6,0},{7,1},{8,14},{9,15},{10,... | collective-permute-start | bytes 184328 | tf_op jit(solution)/shard_map/ppermute | solution.py:261
  42.6 7.5 %collective-permute-start.14 = (f32[24,640]{1,0:T(8,128)S(1)}, f32[24,640]{1,0:T(8,128)S(1)}, u32[]{:S(2)}, u32[]{:S(2)}) collective-permute-start(f32[24,640]{1,0:T(8,128)S(1)} %get-tuple-element.59), channel_id=1, source_target_pairs={{0,2},{1,3},{2,0},{3,1},{4,6},{5,7},{6,4},{7,5},{8,10},{9,11},{10,... | collective-permute-start | bytes 184328 | tf_op jit(solution)/shard_map/ppermute | solution.py:261
  46.6 5.8 %collective-permute-start.23 = (bf16[24,1280]{1,0:T(8,128)(2,1)S(1)}, bf16[24,1280]{1,0:T(8,128)(2,1)S(1)}, u32[]{:S(2)}, u32[]{:S(2)}) collective-permute-start(bf16[24,1280]{1,0:T(8,128)(2,1)S(1)} %shard_map.129.refs_4_), channel_id=1, source_target_pairs={{0,8},{8,0},{16,24},{24,16},{1,9},{9,1},{17,25},{25,17},{2,10},{10... | collective-permute-start | bytes 184328 | tf_op jit(solution)/shard_map/ppermute | solution.py:264
  47.1 8.0 %collective-permute-start.24 = (bf16[24,1280]{1,0:T(8,128)(2,1)S(1)}, bf16[24,1280]{1,0:T(8,128)(2,1)S(1)}, u32[]{:S(2)}, u32[]{:S(2)}) collective-permute-start(bf16[24,1280]{1,0:T(8,128)(2,1)S(1)} %shard_map.129.refs_4_), channel_id=1, source_target_pairs={{0,16},{8,24},{16,0},{24,8},{1,17},{9,25},{17,1},{25,9},{2,18},{10... | collective-permute-start | bytes 184328 | tf_op jit(solution)/shard_map/ppermute | solution.py:264
  48.6 6.5 %collective-permute-start.25 = (bf16[24,1280]{1,0:T(8,128)(2,1)S(1)}, bf16[24,1280]{1,0:T(8,128)(2,1)S(1)}, u32[]{:S(2)}, u32[]{:S(2)}) collective-permute-start(bf16[24,1280]{1,0:T(8,128)(2,1)S(1)} %shard_map.129.refs_4_), channel_id=1, source_target_pairs={{0,24},{8,16},{16,8},{24,0},{1,25},{9,17},{17,9},{25,1},{2,26},{10... | collective-permute-start | bytes 184328 | tf_op jit(solution)/shard_map/ppermute | solution.py:264
  50.3 4.9 %collective-permute-start.20 = (bf16[24,1280]{1,0:T(8,128)(2,1)S(1)}, bf16[24,1280]{1,0:T(8,128)(2,1)S(1)}, u32[]{:S(2)}, u32[]{:S(2)}) collective-permute-start(bf16[24,1280]{1,0:T(8,128)(2,1)S(1)} %shard_map.128.refs_0_), channel_id=1, source_target_pairs={{0,8},{8,0},{16,24},{24,16},{1,9},{9,1},{17,25},{25,17},{2,10},{10... | collective-permute-start | bytes 184328 | tf_op jit(solution)/shard_map/ppermute | solution.py:264
  50.8 4.3 %collective-permute-start.21 = (bf16[24,1280]{1,0:T(8,128)(2,1)S(1)}, bf16[24,1280]{1,0:T(8,128)(2,1)S(1)}, u32[]{:S(2)}, u32[]{:S(2)}) collective-permute-start(bf16[24,1280]{1,0:T(8,128)(2,1)S(1)} %shard_map.128.refs_0_), channel_id=1, source_target_pairs={{0,16},{8,24},{16,0},{24,8},{1,17},{9,25},{17,1},{25,9},{2,18},{10... | collective-permute-start | bytes 184328 | tf_op jit(solution)/shard_map/ppermute | solution.py:264
  52.4 5.1 %collective-permute-start.22 = (bf16[24,1280]{1,0:T(8,128)(2,1)S(1)}, bf16[24,1280]{1,0:T(8,128)(2,1)S(1)}, u32[]{:S(2)}, u32[]{:S(2)}) collective-permute-start(bf16[24,1280]{1,0:T(8,128)(2,1)S(1)} %shard_map.128.refs_0_), channel_id=1, source_target_pairs={{0,24},{8,16},{16,8},{24,0},{1,25},{9,17},{17,9},{25,1},{2,26},{10... | collective-permute-start | bytes 184328 | tf_op jit(solution)/shard_map/ppermute | solution.py:264

commit v5 on v4

--- a/solution.py
+++ b/solution.py
@@ -70,30 +70,25 @@
         wanted = slot * owners + (owner ^ z ^ s) * CORES + (away ^ core)
         pick = one_hot(iota((CORES * group, count), 1) == wanted)
         start = pl.multiple_of((z ^ s) * width, LANES)
-        values = exact(pick, slots_ref[:, pl.ds(start, width)]).astype(jnp.bfloat16)
-        picked_ids = exact(pick, ids).astype(jnp.bfloat16)
+        values = exact(pick, slots_ref[:, pl.ds(start, width)])
+        picked_ids = exact(pick, ids)
         first = s * (width + LANES)
         for out_ref, spot in ((own_out, slice(0, group)), (other_out, slice(group, CORES * group))):
-            out_ref[:, first : first + width] = values[spot]
-            out_ref[:, first + width : first + width + LANES] = picked_ids[spot]
+            out_ref[:, first : first + width] = values[spot].astype(jnp.bfloat16)
+            out_ref[:, first + width : first + width + LANES] = picked_ids[spot].astype(jnp.bfloat16)
 
 
 def merge_kernel(chips, own_ref, other_ref, *out_refs):
     size = own_ref.shape[1] // chips
-    part = own_ref.shape[0] // 2
-    for s in range(chips):
-        own = own_ref[:, s * size : (s + 1) * size].astype(jnp.float32)
-        other = other_ref[:, s * size : (s + 1) * size].astype(jnp.float32)
-        for h in range(2):
-            spot = slice(h * part, (h + 1) * part)
-            both = jnp.concatenate([own[spot], other[spot]], axis=0)
-            out_refs[h * chips + s][...] = both.astype(jnp.bfloat16)
+    for s, out_ref in enumerate(out_refs):
+        parts = [ref[:, s * size : (s + 1) * size].astype(jnp.float32) for ref in (own_ref, other_ref)]
+        out_ref[...] = jnp.concatenate(parts, axis=0).astype(jnp.bfloat16)
 
 
 def head_kernel(chips, dp, shard, mask_hbm, hidden_hbm, columns_hbm, other_ref, *refs):
     d, z, core = place()
-    parts, outs = refs[: chips - 1], refs[chips - 1 : chips + 1]
-    mask_ref, own_ref, columns_ref, sems = refs[chips + 1 :]
+    parts, out_ref = refs[: chips - 1], refs[chips - 1]
+    mask_ref, own_ref, columns_ref, sems = refs[chips:]
     copies = [
         pltpu.make_async_copy(mask_hbm, mask_ref, sems.at[0]),
         pltpu.make_async_copy(columns_hbm, columns_ref, sems.at[1]),
@@ -118,30 +113,29 @@
     order = one_hot(iota((total, total), 1) == (j + (1 - near) * half) * rows + (t ^ d) * shard + i)
     columns = exact(order, columns).astype(jnp.bfloat16)
     for at, ref in ((core, own_ref), (1 - core, other_ref)):
-        head = exact(columns, ref[...])
-        spot = pl.ds(pl.multiple_of(at * cols, LANES), cols)
-        for h in range(2):
-            outs[h][:, spot] = head[h * (total // 2) : (h + 1) * (total // 2)]
+        out_ref[:, pl.ds(pl.multiple_of(at * cols, LANES), cols)] = exact(columns, ref[...])
 
 
 def embed_kernel(chips, dp, shard, head_ref, *refs):
-    slot_refs, out_refs = refs[:-dp], refs[-dp:]
+    slot_refs, out_refs = refs[: -2 * dp], refs[-2 * dp :]
     half = chips // 2
     total, cols = head_ref.shape
-    count = len(slot_refs) * slot_refs[0].shape[0]
-    ids = jnp.concatenate([ref[:, cols:].astype(jnp.float32) for ref in slot_refs], axis=0)
-    ids = ids[:, :1].astype(jnp.int32)
-    values = jnp.concatenate([ref[:, :cols].astype(jnp.float32) for ref in slot_refs], axis=0)
-    values = values.astype(jnp.bfloat16)
+    size = half * shard
+    count = sum(ref.shape[0] for ref in slot_refs)
+    ids = jnp.concatenate([ref[:, cols:] for ref in slot_refs], axis=0)
+    ids = ids.astype(jnp.float32)[:, :1].astype(jnp.int32)
+    values = jnp.concatenate([ref[:, :cols] for ref in slot_refs], axis=0)
     block = over(jnp.maximum(ids, 0), shard)
-    target = (block * half + iota((count, 1), 0) % half) * shard + ids - block * shard
+    group = slot_refs[0].shape[0] // CORES
+    place_in = iota((count, 1), 0) % group
+    near = jnp.where(place_in >= group // 2, 1, 0)
+    target = near * (total // 2) + (block * half + place_in % half) * shard + ids - block * shard
     target = jnp.where(ids < 0, -1, target)
     picked = one_hot(iota((count, total), 1) == target)
     embed = lax.dot_general(picked, values, (((0,), (0,)), ((), ())), preferred_element_type=jnp.float32)
-    part = head_ref[...] + embed
-    size = half * shard
-    for t, out_ref in enumerate(out_refs):
-        out_ref[...] = part[t * size : (t + 1) * size]
+    for n, out_ref in enumerate(out_refs):
+        spot = slice(n * size, (n + 1) * size)
+        out_ref[...] = head_ref[spot] + embed[spot]
 
 
 def sum_kernel(half, shard, *refs):
@@ -172,10 +166,10 @@
     return pl.ds(pl.multiple_of((z ^ s) * cols, LANES), cols)
 
 
-def rows_kernel(members, shard, *refs):
+def rows_kernel(shard, *refs):
     d, z, core = place()
     state, pieces, out_ref = refs[:3], refs[3:-1], refs[-1]
-    table = [step(shard, chip_spot(z, s, piece), piece, *state)[0] for s, piece in zip(members, pieces)]
+    table = [step(shard, chip_spot(z, s, piece), piece, *state)[0] for s, piece in enumerate(pieces)]
     out_ref[...] = jnp.concatenate(table, axis=0).astype(jnp.bfloat16)
 
 
@@ -194,15 +188,12 @@
     cols = parts[0].shape[1]
     rows = dp * shard
     total = chips * rows
-    half = chips // 2
-    values = jnp.concatenate([part[...].astype(jnp.float32) for part in parts], axis=0).astype(jnp.bfloat16)
+    values = jnp.concatenate([part[...] for part in parts], axis=0)
     r = iota((total, total), 0)
     s = over(r, rows)
     e = over(r - s * rows, shard)
     i = r - s * rows - e * shard
-    far = jnp.where(s >= half, 1, 0)
-    j = s - far * half
-    order = one_hot(iota((total, total), 1) == ((far * dp + (e ^ d)) * half + j) * shard + i)
+    order = one_hot(iota((total, total), 1) == ((e ^ d) * chips + s) * shard + i)
     values = exact(order, values).astype(jnp.bfloat16)
     for s in range(chips):
         spot = pl.ds(pl.multiple_of((z ^ s) * cols, LANES), cols)
@@ -281,14 +272,14 @@
     )
     messages = run(
         functools.partial(merge_kernel, chips),
-        [shaped((cap * half * CORES, cols + LANES), bf16)] * (2 * chips),
+        [shaped((cap * chips * CORES, cols + LANES), bf16)] * chips,
         slots_own,
         send(slots_other, 0, 1),
     )
     head_in = (predict_mask[None, :], hidden, columns[0])
     head = run(
         functools.partial(head_kernel, *sizes),
-        [shaped((half * rows, cols), f32)] * 2,
+        shaped((chips * rows, cols), f32),
         *head_in,
         hidden_other,
         *columns[1:],
@@ -297,41 +288,39 @@
         scratch=local_copies(*head_in),
     )
     state = (master, first_moment, second_moment)
-    messages = [messages[:chips], messages[chips:]]
-    pieces, table = {}, []
+    parts = run(
+        functools.partial(embed_kernel, *sizes),
+        [shaped((half * shard, cols), f32)] * (2 * dp),
+        head,
+        *[send(message, s) for s, message in enumerate(messages)],
+    )
+    pieces = {}
     for h, members in enumerate((far, near)):
-        start = head[h]
-        if h:
-            messages[h], _ = lax.optimization_barrier((messages[h], arrived[1]))
-            start, _ = lax.optimization_barrier((start, parts[0]))
-        arrived = [send(messages[h][s], s) for s in range(chips)]
-        parts = run(
-            functools.partial(embed_kernel, *sizes),
-            [shaped((half * shard, cols), f32)] * dp,
-            start,
-            *arrived,
-        )
         sums = run(
             functools.partial(sum_kernel, half, shard),
             [shaped((CORES * shard, cols // CORES), f32)] * half,
-            *[send_dp(part, t) for t, part in enumerate(parts)],
+            *[send_dp(parts[h * dp + t], t) for t in range(dp)],
         )
         for s, total in zip(members, sums):
             pieces[s] = send(total, s)
-        table_rows = run(
-            functools.partial(rows_kernel, tuple(members), shard),
-            shaped((half * shard, cols), bf16),
-            *state,
-            *[pieces[s] for s in members],
-        )
-        table = [send_dp(table_rows, t) for t in range(dp)] + table
+    pieces = [pieces[s] for s in range(chips)]
+    table = run(
+        functools.partial(rows_kernel, shard),
+        shaped((chips * shard, cols), bf16),
+        *state,
+        *pieces,
+    )
     master_new, first_new, second_new = run(
         functools.partial(adam_kernel, shard),
         [shaped(master.shape, f32)] * 3,
         *state,
-        *[pieces[s] for s in range(chips)],
-    )
-    table = run(functools.partial(table_kernel, *sizes), shaped((rows, width), bf16), *table)
+        *pieces,
+    )
+    table = run(
+        functools.partial(table_kernel, *sizes),
+        shaped((rows, width), bf16),
+        *[send_dp(table, t) for t in range(dp)],
+    )
     return (master_new, first_new, second_new, table)
 
 

time: 58.8 us -> 59.3 us (level)
  waiting for transfers between devices: 14.3 us -> 23.3 us
  starting transfers between devices: 36.2 us -> 27.9 us
    ppermute x14 -> x11, waiting for transfers between devices: 9.25 us -> 15.8 us  [send(): lax.ppermute(x, 'vocab', [(v, v ^ move) for v in range(vocab)])]
    ppermute x14 -> x11, starting transfers between devices: 22 us -> 16.9 us  [send(): lax.ppermute(x, 'vocab', [(v, v ^ move) for v in range(vocab)])]
    ppermute x12 -> x9, starting transfers between devices: 14.2 us -> 11 us  [send_dp(): return lax.ppermute(x, 'dp', [(i, i ^ t) for i in range(dp)]) if t else x]
    ppermute x12 -> x9, waiting for transfers between devices: 5.01 us -> 7.46 us  [send_dp(): return lax.ppermute(x, 'dp', [(i, i ^ t) for i in range(dp)]) if t else x]
    pallas_call x11 -> x9, Pallas kernels: 7.41 us -> 7.15 us  [run(): pl.pallas_call(kernel, out_shape=outs, in_specs=[pl.BlockSpec(memory_spac...]
  transfers between devices with their start and end apart: 26 -> 20, of which waited for: 7 -> 8; matrix products, arithmetic and copies ran while one was open for 0% -> 0% of each run, Pallas kernels for 11% -> 9%
where the time goes in v5:
time: 59.3 us; the launch traced here: 59.1 us
  starting transfers between devices  27.9 us (47%)
  waiting for transfers between devices  23.3 us (39%)
  Pallas kernels  7.15 us (12%)
  between operations  0.74 us (1%)
    ppermute x11, starting transfers between devices, send(): lax.ppermute(x, 'vocab', [(v, v ^ move) for v in range(vocab)])  16.9 us
    ppermute x11, waiting for transfers between devices, send(): lax.ppermute(x, 'vocab', [(v, v ^ move) for v in range(vocab)])  15.8 us
    ppermute x9, starting transfers between devices, send_dp(): return lax.ppermute(x, 'dp', [(i, i ^ t) for i in range(dp)]) if t else x  11 us
    ppermute x9, waiting for transfers between devices, send_dp(): return lax.ppermute(x, 'dp', [(i, i ^ t) for i in range(dp)]) if t else x  7.46 us
    pallas_call x9, Pallas kernels, run(): pl.pallas_call(kernel, out_shape=outs, in_specs=[pl.BlockSpec(memory_spac...  7.15 us
  transfers between devices with their start and end apart: 20, of which 8 were waited for; matrix products, arithmetic and copies ran while one was open for 0% of the time, Pallas kernels for 9%

profile of v5, /device:TPU:0, one launch (start us, length us, event | category | flops | bytes accessed | tf_op | source)
XLA Modules:
  0.0 59.1 jit_solution(10109114616610089949)
XLA Ops:
  0.6 0.5 collective-permute-start
  1.1 1.5 %shard_map.121 = (bf16[24,5632]{1,0:T(8,128)(2,1)S(1)}, bf16[24,5632]{1,0:T(8,128)(2,1)S(1)}) custom-call(bf16[48,5120]{1,0:T(8,128)(2,1)} %bitcast.8, s32[6,1,8]{2,1,0:T(1,128)} %bitcast.13, s32[1,8]{1,0:T(1,128)} %counts_hbm.1), custom_call_target="tpu_custom_call" | custom-call | bytes 1032416 | tf_op jit(solution)/shard_map/pallas_call | solution.py:211
  2.6 0.1 collective-permute-start.4
  2.7 4.0 %collective-permute-start.2 = (bf16[48,1024]{1,0:T(8,128)(2,1)}, bf16[48,1024]{1,0:T(8,128)(2,1)S(1)}, u32[]{:S(2)}, u32[]{:S(2)}) collective-permute-start(bf16[48,1024]{1,0:T(8,128)(2,1)} %bitcast.9), channel_id=1, source_target_pairs={{0,4},{1,5},{2,6},{3,7},{4,0},{5,1},{6,2},{7,3},{8,12},{9,13},{10,... | collective-permute-start | bytes 294920 | tf_op jit(solution)/shard_map/ppermute | solution.py:252
  6.8 1.6 %collective-permute-start.1 = (bf16[48,1024]{1,0:T(8,128)(2,1)}, bf16[48,1024]{1,0:T(8,128)(2,1)S(1)}, u32[]{:S(2)}, u32[]{:S(2)}) collective-permute-start(bf16[48,1024]{1,0:T(8,128)(2,1)} %bitcast.10), channel_id=1, source_target_pairs={{0,2},{1,3},{2,0},{3,1},{4,6},{5,7},{6,4},{7,5},{8,10},{9,11},{10,... | collective-permute-start | bytes 294920 | tf_op jit(solution)/shard_map/ppermute | solution.py:252
  8.4 3.9 %collective-permute-done.2.refs_1_ = bf16[48,1024]{1,0:T(8,128)(2,1)S(1)} collective-permute-done((bf16[48,1024]{1,0:T(8,128)(2,1)}, bf16[48,1024]{1,0:T(8,128)(2,1)S(1)}, u32[]{:S(2)}, u32[]{:S(2)}) %collective-permute-start.2) | collective-permute-done | bytes 98336 | tf_op jit(solution)/shard_map/ppermute | solution.py:252
  12.2 0.7 %collective-permute-start.3 = (bf16[48,1024]{1,0:T(8,128)(2,1)S(1)}, bf16[48,1024]{1,0:T(8,128)(2,1)S(1)}, u32[]{:S(2)}, u32[]{:S(2)}) collective-permute-start(bf16[48,1024]{1,0:T(8,128)(2,1)S(1)} %collective-permute-done.2.refs_1_), channel_id=1, source_target_pairs={{0,2},{1,3},{2,0},{3,1},{4,6},{5,7},{6,4},{7,5},{8,10},{9,11},{10,... | collective-permute-start | bytes 294920 | tf_op jit(solution)/shard_map/ppermute | solution.py:252
  13.0 0.0 collective-permute-done.4.other_ref
  13.0 1.4 %collective-permute-start.5 = (bf16[48,1408]{1,0:T(8,128)(2,1)S(1)}, bf16[48,1408]{1,0:T(8,128)(2,1)S(1)}, u32[]{:S(2)}, u32[]{:S(2)}) collective-permute-start(bf16[48,1408]{1,0:T(8,128)(2,1)S(1)} %get-tuple-element.28), channel_id=1, source_target_pairs={{0,2},{1,3},{2,0},{3,1},{4,6},{5,7},{6,4},{7,5},{8,10},{9,11},{10,... | collective-permute-start | bytes 405512 | tf_op jit(solution)/shard_map/ppermute | solution.py:252
  14.4 2.0 %collective-permute-start.6 = (bf16[48,1408]{1,0:T(8,128)(2,1)S(1)}, bf16[48,1408]{1,0:T(8,128)(2,1)S(1)}, u32[]{:S(2)}, u32[]{:S(2)}) collective-permute-start(bf16[48,1408]{1,0:T(8,128)(2,1)S(1)} %get-tuple-element.29), channel_id=1, source_target_pairs={{0,4},{1,5},{2,6},{3,7},{4,0},{5,1},{6,2},{7,3},{8,12},{9,13},{10,... | collective-permute-start | bytes 405512 | tf_op jit(solution)/shard_map/ppermute | solution.py:252
  16.4 0.0 collective-permute-done.1.refs_0_
  16.4 1.4 %collective-permute-start.7 = (bf16[48,1408]{1,0:T(8,128)(2,1)S(1)}, bf16[48,1408]{1,0:T(8,128)(2,1)S(1)}, u32[]{:S(2)}, u32[]{:S(2)}) collective-permute-start(bf16[48,1408]{1,0:T(8,128)(2,1)S(1)} %get-tuple-element.30), channel_id=1, source_target_pairs={{0,6},{1,7},{2,4},{3,5},{4,2},{5,3},{6,0},{7,1},{8,14},{9,15},{10,... | collective-permute-start | bytes 405512 | tf_op jit(solution)/shard_map/ppermute | solution.py:252
  17.8 2.6 %collective-permute-done.3.refs_2_ = bf16[48,1024]{1,0:T(8,128)(2,1)S(1)} collective-permute-done((bf16[48,1024]{1,0:T(8,128)(2,1)S(1)}, bf16[48,1024]{1,0:T(8,128)(2,1)S(1)}, u32[]{:S(2)}, u32[]{:S(2)}) %collective-permute-start.3) | collective-permute-done | bytes 98336 | tf_op jit(solution)/shard_map/ppermute | solution.py:252
  20.4 0.0 collective-permute-done.other_ref
  20.4 2.4 %shard_map.120.head_ref = f32[192,1280]{1,0:T(8,128)S(1)} custom-call(s32[1,1024]{1,0:T(1,128)} %bitcast.12, bf16[1024,640]{1,0:T(8,128)(2,1)} %hidden_hbm.1, bf16[48,1024]{1,0:T(8,128)(2,1)} %bitcast.11, bf16[1024,640]{1,0:T(8,128)(2,1)S(1)} %collective-permute-done.other_ref, bf16[48,1024]{1,0:T(8,128)(2,1)S(1)} %collective-permute-done.1.refs_0_, ...), custom_call_target="tpu_custom_call" | custom-call | flops 503316480 | bytes 4001792 | tf_op jit(solution)/shard_map/pallas_call | solution.py:211
  22.8 0.0 copy-start
  22.8 0.0 copy-start.1
  22.8 0.0 copy-start.2
  22.8 0.0 collective-permute-done.5.refs_1_
  22.8 0.0 collective-permute-done.6.refs_2_
  22.8 4.6 %collective-permute-done.7.refs_3_ = bf16[48,1408]{1,0:T(8,128)(2,1)S(1)} collective-permute-done((bf16[48,1408]{1,0:T(8,128)(2,1)S(1)}, bf16[48,1408]{1,0:T(8,128)(2,1)S(1)}, u32[]{:S(2)}, u32[]{:S(2)}) %collective-permute-start.7) | collective-permute-done | bytes 135200 | tf_op jit(solution)/shard_map/ppermute | solution.py:252
  27.5 0.5 shard_map.123
  28.0 1.6 %collective-permute-start.12 = (f32[24,1280]{1,0:T(8,128)S(1)}, f32[24,1280]{1,0:T(8,128)S(1)}, u32[]{:S(2)}, u32[]{:S(2)}) collective-permute-start(f32[24,1280]{1,0:T(8,128)S(1)} %get-tuple-element.38), channel_id=1, source_target_pairs={{0,8},{8,0},{16,24},{24,16},{1,9},{9,1},{17,25},{25,17},{2,10},{10... | collective-permute-start | bytes 368648 | tf_op jit(solution)/shard_map/ppermute | solution.py:255
  29.5 1.5 %collective-permute-start.13 = (f32[24,1280]{1,0:T(8,128)S(1)}, f32[24,1280]{1,0:T(8,128)S(1)}, u32[]{:S(2)}, u32[]{:S(2)}) collective-permute-start(f32[24,1280]{1,0:T(8,128)S(1)} %get-tuple-element.39), channel_id=1, source_target_pairs={{0,16},{8,24},{16,0},{24,8},{1,17},{9,25},{17,1},{25,9},{2,18},{10... | collective-permute-start | bytes 368648 | tf_op jit(solution)/shard_map/ppermute | solution.py:255
  31.1 0.5 collective-permute-start.14
  31.5 2.4 %collective-permute-start.10 = (f32[24,1280]{1,0:T(8,128)S(1)}, f32[24,1280]{1,0:T(8,128)S(1)}, u32[]{:S(2)}, u32[]{:S(2)}) collective-permute-start(f32[24,1280]{1,0:T(8,128)S(1)} %get-tuple-element.34), channel_id=1, source_target_pairs={{0,24},{8,16},{16,8},{24,0},{1,25},{9,17},{17,9},{25,1},{2,26},{10... | collective-permute-start | bytes 368648 | tf_op jit(solution)/shard_map/ppermute | solution.py:255
  34.0 0.5 collective-permute-start.8
  34.5 0.0 collective-permute-done.12.refs_1_
  34.5 0.5 collective-permute-start.9
  35.0 4.3 %collective-permute-done.13.refs_2_ = f32[24,1280]{1,0:T(8,128)S(1)} collective-permute-done((f32[24,1280]{1,0:T(8,128)S(1)}, f32[24,1280]{1,0:T(8,128)S(1)}, u32[]{:S(2)}, u32[]{:S(2)}) %collective-permute-start.13) | collective-permute-done | bytes 122912 | tf_op jit(solution)/shard_map/ppermute | solution.py:255
  39.4 0.0 collective-permute-done.14.refs_3_
  39.4 3.8 %collective-permute-start.15 = (f32[24,640]{1,0:T(8,128)S(1)}, f32[24,640]{1,0:T(8,128)S(1)}, u32[]{:S(2)}, u32[]{:S(2)}) collective-permute-start(f32[24,640]{1,0:T(8,128)S(1)} %get-tuple-element.41), channel_id=1, source_target_pairs={{0,4},{1,5},{2,6},{3,7},{4,0},{5,1},{6,2},{7,3},{8,12},{9,13},{10,... | collective-permute-start | bytes 184328 | tf_op jit(solution)/shard_map/ppermute | solution.py:252
  43.3 0.8 %collective-permute-start.16 = (f32[24,640]{1,0:T(8,128)S(1)}, f32[24,640]{1,0:T(8,128)S(1)}, u32[]{:S(2)}, u32[]{:S(2)}) collective-permute-start(f32[24,640]{1,0:T(8,128)S(1)} %get-tuple-element.42), channel_id=1, source_target_pairs={{0,6},{1,7},{2,4},{3,5},{4,2},{5,3},{6,0},{7,1},{8,14},{9,15},{10,... | collective-permute-start | bytes 184328 | tf_op jit(solution)/shard_map/ppermute | solution.py:252
  44.0 0.0 collective-permute-done.10.refs_3_
  44.0 0.0 collective-permute-done.9.refs_2_
  44.1 0.5 collective-permute-start.11
  44.6 1.1 %collective-permute-done.15.refs_5_ = f32[24,640]{1,0:T(8,128)S(1)} collective-permute-done((f32[24,640]{1,0:T(8,128)S(1)}, f32[24,640]{1,0:T(8,128)S(1)}, u32[]{:S(2)}, u32[]{:S(2)}) %collective-permute-start.15) | collective-permute-done | bytes 61472 | tf_op jit(solution)/shard_map/ppermute | solution.py:252
  45.6 3.6 %collective-permute-done.16.refs_6_ = f32[24,640]{1,0:T(8,128)S(1)} collective-permute-done((f32[24,640]{1,0:T(8,128)S(1)}, f32[24,640]{1,0:T(8,128)S(1)}, u32[]{:S(2)}, u32[]{:S(2)}) %collective-permute-start.16) | collective-permute-done | bytes 61472 | tf_op jit(solution)/shard_map/ppermute | solution.py:252
  49.3 0.0 collective-permute-done.11.refs_4_
  49.3 0.3 shard_map.127.refs_0_
  49.6 0.3 collective-permute-start.17
  49.9 2.3 %collective-permute-start.18 = (bf16[48,1280]{1,0:T(8,128)(2,1)S(1)}, bf16[48,1280]{1,0:T(8,128)(2,1)S(1)}, u32[]{:S(2)}, u32[]{:S(2)}) collective-permute-start(bf16[48,1280]{1,0:T(8,128)(2,1)S(1)} %shard_map.127.refs_0_), channel_id=1, source_target_pairs={{0,16},{8,24},{16,0},{24,8},{1,17},{9,25},{17,1},{25,9},{2,18},{10... | collective-permute-start | bytes 368648 | tf_op jit(solution)/shard_map/ppermute | solution.py:255
  52.2 1.4 %collective-permute-start.19 = (bf16[48,1280]{1,0:T(8,128)(2,1)S(1)}, bf16[48,1280]{1,0:T(8,128)(2,1)S(1)}, u32[]{:S(2)}, u32[]{:S(2)}) collective-permute-start(bf16[48,1280]{1,0:T(8,128)(2,1)S(1)} %shard_map.127.refs_0_), channel_id=1, source_target_pairs={{0,24},{8,16},{16,8},{24,0},{1,25},{9,17},{17,9},{25,1},{2,26},{10... | collective-permute-start | bytes 368648 | tf_op jit(solution)/shard_map/ppermute | solution.py:255
  53.6 1.3 %shard_map.126 = (f32[12,5120]{1,0:T(8,128)}, f32[12,5120]{1,0:T(8,128)}, f32[12,5120]{1,0:T(8,128)}) custom-call(f32[12,5120]{1,0:T(8,128)S(1)} %copy-done, f32[12,5120]{1,0:T(8,128)S(1)} %copy-done.1, f32[12,5120]{1,0:T(8,128)S(1)} %copy-done.2, f32[24,640]{1,0:T(8,128)S(1)} %get-tuple-element.35.refs_3_, f32[24,640]{1,0:T(8,128)S(1)} %collective-permute-done.11.refs_4_, ...), custom_call_target="tpu_custom_call" | custom-call | bytes 1720320 | tf_op jit(solution)/shard_map/pallas_call | solution.py:211
  54.9 0.0 collective-permute-done.17.refs_1_
  54.9 0.2 collective-permute-done.18.refs_2_
  55.1 2.9 %collective-permute-done.19.refs_3_ = bf16[48,1280]{1,0:T(8,128)(2,1)S(1)} collective-permute-done((bf16[48,1280]{1,0:T(8,128)(2,1)S(1)}, bf16[48,1280]{1,0:T(8,128)(2,1)S(1)}, u32[]{:S(2)}, u32[]{:S(2)}) %collective-permute-start.19) | collective-permute-done | bytes 122912 | tf_op jit(solution)/shard_map/ppermute | solution.py:255
  58.0 1.1 %shard_map.128 = bf16[48,5120]{1,0:T(8,128)(2,1)} custom-call(bf16[48,1280]{1,0:T(8,128)(2,1)S(1)} %shard_map.127.refs_0_, bf16[48,1280]{1,0:T(8,128)(2,1)S(1)} %collective-permute-done.17.refs_1_, bf16[48,1280]{1,0:T(8,128)(2,1)S(1)} %collective-permute-done.18.refs_2_, bf16[48,1280]{1,0:T(8,128)(2,1)S(1)} %collective-permute-done.19.refs_3_), custom_call_target="tpu_custom_call" | custom-call | bytes 983040 | tf_op jit(solution)/shard_map/pallas_call | solution.py:211
  (7 shorter events, 0.1 us)
Async XLA Ops:
  0.6 19.8 %collective-permute-start = (bf16[1024,640]{1,0:T(8,128)(2,1)}, bf16[1024,640]{1,0:T(8,128)(2,1)S(1)}, u32[]{:S(2)}, u32[]{:S(2)}) collective-permute-start(bf16[1024,640]{1,0:T(8,128)(2,1)} %hidden_hbm.1), channel_id=1, source_target_pairs={{0,1},{1,0},{2,3},{3,2},{4,5},{5,4},{6,7},{7,6},{8,9},{9,8},{10,11... | collective-permute-start | bytes 3932168 | tf_op jit(solution)/shard_map/ppermute | solution.py:252
  2.6 10.3 %collective-permute-start.4 = (bf16[24,5632]{1,0:T(8,128)(2,1)S(1)}, bf16[24,5632]{1,0:T(8,128)(2,1)S(1)}, u32[]{:S(2)}, u32[]{:S(2)}) collective-permute-start(bf16[24,5632]{1,0:T(8,128)(2,1)S(1)} %get-tuple-element.26), channel_id=1, source_target_pairs={{0,1},{1,0},{2,3},{3,2},{4,5},{5,4},{6,7},{7,6},{8,9},{9,8},{10,11... | collective-permute-start | bytes 811016 | tf_op jit(solution)/shard_map/ppermute | solution.py:252
  2.7 9.5 %collective-permute-start.2 = (bf16[48,1024]{1,0:T(8,128)(2,1)}, bf16[48,1024]{1,0:T(8,128)(2,1)S(1)}, u32[]{:S(2)}, u32[]{:S(2)}) collective-permute-start(bf16[48,1024]{1,0:T(8,128)(2,1)} %bitcast.9), channel_id=1, source_target_pairs={{0,4},{1,5},{2,6},{3,7},{4,0},{5,1},{6,2},{7,3},{8,12},{9,13},{10,... | collective-permute-start | bytes 294920 | tf_op jit(solution)/shard_map/ppermute | solution.py:252
  6.8 9.7 %collective-permute-start.1 = (bf16[48,1024]{1,0:T(8,128)(2,1)}, bf16[48,1024]{1,0:T(8,128)(2,1)S(1)}, u32[]{:S(2)}, u32[]{:S(2)}) collective-permute-start(bf16[48,1024]{1,0:T(8,128)(2,1)} %bitcast.10), channel_id=1, source_target_pairs={{0,2},{1,3},{2,0},{3,1},{4,6},{5,7},{6,4},{7,5},{8,10},{9,11},{10,... | collective-permute-start | bytes 294920 | tf_op jit(solution)/shard_map/ppermute | solution.py:252
  12.2 8.2 %collective-permute-start.3 = (bf16[48,1024]{1,0:T(8,128)(2,1)S(1)}, bf16[48,1024]{1,0:T(8,128)(2,1)S(1)}, u32[]{:S(2)}, u32[]{:S(2)}) collective-permute-start(bf16[48,1024]{1,0:T(8,128)(2,1)S(1)} %collective-permute-done.2.refs_1_), channel_id=1, source_target_pairs={{0,2},{1,3},{2,0},{3,1},{4,6},{5,7},{6,4},{7,5},{8,10},{9,11},{10,... | collective-permute-start | bytes 294920 | tf_op jit(solution)/shard_map/ppermute | solution.py:252
  13.0 9.8 %collective-permute-start.5 = (bf16[48,1408]{1,0:T(8,128)(2,1)S(1)}, bf16[48,1408]{1,0:T(8,128)(2,1)S(1)}, u32[]{:S(2)}, u32[]{:S(2)}) collective-permute-start(bf16[48,1408]{1,0:T(8,128)(2,1)S(1)} %get-tuple-element.28), channel_id=1, source_target_pairs={{0,2},{1,3},{2,0},{3,1},{4,6},{5,7},{6,4},{7,5},{8,10},{9,11},{10,... | collective-permute-start | bytes 405512 | tf_op jit(solution)/shard_map/ppermute | solution.py:252
  14.4 8.4 %collective-permute-start.6 = (bf16[48,1408]{1,0:T(8,128)(2,1)S(1)}, bf16[48,1408]{1,0:T(8,128)(2,1)S(1)}, u32[]{:S(2)}, u32[]{:S(2)}) collective-permute-start(bf16[48,1408]{1,0:T(8,128)(2,1)S(1)} %get-tuple-element.29), channel_id=1, source_target_pairs={{0,4},{1,5},{2,6},{3,7},{4,0},{5,1},{6,2},{7,3},{8,12},{9,13},{10,... | collective-permute-start | bytes 405512 | tf_op jit(solution)/shard_map/ppermute | solution.py:252
  16.4 11.0 %collective-permute-start.7 = (bf16[48,1408]{1,0:T(8,128)(2,1)S(1)}, bf16[48,1408]{1,0:T(8,128)(2,1)S(1)}, u32[]{:S(2)}, u32[]{:S(2)}) collective-permute-start(bf16[48,1408]{1,0:T(8,128)(2,1)S(1)} %get-tuple-element.30), channel_id=1, source_target_pairs={{0,6},{1,7},{2,4},{3,5},{4,2},{5,3},{6,0},{7,1},{8,14},{9,15},{10,... | collective-permute-start | bytes 405512 | tf_op jit(solution)/shard_map/ppermute | solution.py:252
  22.8 26.5 %copy-start = (f32[12,5120]{1,0:T(8,128)S(1)}, f32[12,5120]{1,0:T(8,128)}, u32[]{:S(2)}) copy-start(f32[12,5120]{1,0:T(8,128)} %refs_0_.3) | copy-start | bytes 737284
  22.8 26.5 %copy-start.1 = (f32[12,5120]{1,0:T(8,128)S(1)}, f32[12,5120]{1,0:T(8,128)}, u32[]{:S(2)}) copy-start(f32[12,5120]{1,0:T(8,128)} %refs_1_.3) | copy-start | bytes 737284
  22.8 26.5 %copy-start.2 = (f32[12,5120]{1,0:T(8,128)S(1)}, f32[12,5120]{1,0:T(8,128)}, u32[]{:S(2)}) copy-start(f32[12,5120]{1,0:T(8,128)} %refs_2_.3) | copy-start | bytes 737284
  28.0 6.5 %collective-permute-start.12 = (f32[24,1280]{1,0:T(8,128)S(1)}, f32[24,1280]{1,0:T(8,128)S(1)}, u32[]{:S(2)}, u32[]{:S(2)}) collective-permute-start(f32[24,1280]{1,0:T(8,128)S(1)} %get-tuple-element.38), channel_id=1, source_target_pairs={{0,8},{8,0},{16,24},{24,16},{1,9},{9,1},{17,25},{25,17},{2,10},{10... | collective-permute-start | bytes 368648 | tf_op jit(solution)/shard_map/ppermute | solution.py:255
  29.5 9.9 %collective-permute-start.13 = (f32[24,1280]{1,0:T(8,128)S(1)}, f32[24,1280]{1,0:T(8,128)S(1)}, u32[]{:S(2)}, u32[]{:S(2)}) collective-permute-start(f32[24,1280]{1,0:T(8,128)S(1)} %get-tuple-element.39), channel_id=1, source_target_pairs={{0,16},{8,24},{16,0},{24,8},{1,17},{9,25},{17,1},{25,9},{2,18},{10... | collective-permute-start | bytes 368648 | tf_op jit(solution)/shard_map/ppermute | solution.py:255
  31.1 8.3 %collective-permute-start.14 = (f32[24,1280]{1,0:T(8,128)S(1)}, f32[24,1280]{1,0:T(8,128)S(1)}, u32[]{:S(2)}, u32[]{:S(2)}) collective-permute-start(f32[24,1280]{1,0:T(8,128)S(1)} %get-tuple-element.40), channel_id=1, source_target_pairs={{0,24},{8,16},{16,8},{24,0},{1,25},{9,17},{17,9},{25,1},{2,26},{10... | collective-permute-start | bytes 368648 | tf_op jit(solution)/shard_map/ppermute | solution.py:255
  31.5 12.5 %collective-permute-start.10 = (f32[24,1280]{1,0:T(8,128)S(1)}, f32[24,1280]{1,0:T(8,128)S(1)}, u32[]{:S(2)}, u32[]{:S(2)}) collective-permute-start(f32[24,1280]{1,0:T(8,128)S(1)} %get-tuple-element.34), channel_id=1, source_target_pairs={{0,24},{8,16},{16,8},{24,0},{1,25},{9,17},{17,9},{25,1},{2,26},{10... | collective-permute-start | bytes 368648 | tf_op jit(solution)/shard_map/ppermute | solution.py:255
  34.0 10.1 %collective-permute-start.8 = (f32[24,1280]{1,0:T(8,128)S(1)}, f32[24,1280]{1,0:T(8,128)S(1)}, u32[]{:S(2)}, u32[]{:S(2)}) collective-permute-start(f32[24,1280]{1,0:T(8,128)S(1)} %get-tuple-element.32), channel_id=1, source_target_pairs={{0,8},{8,0},{16,24},{24,16},{1,9},{9,1},{17,25},{25,17},{2,10},{10... | collective-permute-start | bytes 368648 | tf_op jit(solution)/shard_map/ppermute | solution.py:255
  34.5 9.5 %collective-permute-start.9 = (f32[24,1280]{1,0:T(8,128)S(1)}, f32[24,1280]{1,0:T(8,128)S(1)}, u32[]{:S(2)}, u32[]{:S(2)}) collective-permute-start(f32[24,1280]{1,0:T(8,128)S(1)} %get-tuple-element.33), channel_id=1, source_target_pairs={{0,16},{8,24},{16,0},{24,8},{1,17},{9,25},{17,1},{25,9},{2,18},{10... | collective-permute-start | bytes 368648 | tf_op jit(solution)/shard_map/ppermute | solution.py:255
  39.4 6.2 %collective-permute-start.15 = (f32[24,640]{1,0:T(8,128)S(1)}, f32[24,640]{1,0:T(8,128)S(1)}, u32[]{:S(2)}, u32[]{:S(2)}) collective-permute-start(f32[24,640]{1,0:T(8,128)S(1)} %get-tuple-element.41), channel_id=1, source_target_pairs={{0,4},{1,5},{2,6},{3,7},{4,0},{5,1},{6,2},{7,3},{8,12},{9,13},{10,... | collective-permute-start | bytes 184328 | tf_op jit(solution)/shard_map/ppermute | solution.py:252
  43.3 6.0 %collective-permute-start.16 = (f32[24,640]{1,0:T(8,128)S(1)}, f32[24,640]{1,0:T(8,128)S(1)}, u32[]{:S(2)}, u32[]{:S(2)}) collective-permute-start(f32[24,640]{1,0:T(8,128)S(1)} %get-tuple-element.42), channel_id=1, source_target_pairs={{0,6},{1,7},{2,4},{3,5},{4,2},{5,3},{6,0},{7,1},{8,14},{9,15},{10,... | collective-permute-start | bytes 184328 | tf_op jit(solution)/shard_map/ppermute | solution.py:252
  44.1 5.2 %collective-permute-start.11 = (f32[24,640]{1,0:T(8,128)S(1)}, f32[24,640]{1,0:T(8,128)S(1)}, u32[]{:S(2)}, u32[]{:S(2)}) collective-permute-start(f32[24,640]{1,0:T(8,128)S(1)} %get-tuple-element.36), channel_id=1, source_target_pairs={{0,2},{1,3},{2,0},{3,1},{4,6},{5,7},{6,4},{7,5},{8,10},{9,11},{10,... | collective-permute-start | bytes 184328 | tf_op jit(solution)/shard_map/ppermute | solution.py:252
  49.6 5.3 %collective-permute-start.17 = (bf16[48,1280]{1,0:T(8,128)(2,1)S(1)}, bf16[48,1280]{1,0:T(8,128)(2,1)S(1)}, u32[]{:S(2)}, u32[]{:S(2)}) collective-permute-start(bf16[48,1280]{1,0:T(8,128)(2,1)S(1)} %shard_map.127.refs_0_), channel_id=1, source_target_pairs={{0,8},{8,0},{16,24},{24,16},{1,9},{9,1},{17,25},{25,17},{2,10},{10... | collective-permute-start | bytes 368648 | tf_op jit(solution)/shard_map/ppermute | solution.py:255
  49.9 5.2 %collective-permute-start.18 = (bf16[48,1280]{1,0:T(8,128)(2,1)S(1)}, bf16[48,1280]{1,0:T(8,128)(2,1)S(1)}, u32[]{:S(2)}, u32[]{:S(2)}) collective-permute-start(bf16[48,1280]{1,0:T(8,128)(2,1)S(1)} %shard_map.127.refs_0_), channel_id=1, source_target_pairs={{0,16},{8,24},{16,0},{24,8},{1,17},{9,25},{17,1},{25,9},{2,18},{10... | collective-permute-start | bytes 368648 | tf_op jit(solution)/shard_map/ppermute | solution.py:255
  52.2 5.8 %collective-permute-start.19 = (bf16[48,1280]{1,0:T(8,128)(2,1)S(1)}, bf16[48,1280]{1,0:T(8,128)(2,1)S(1)}, u32[]{:S(2)}, u32[]{:S(2)}) collective-permute-start(bf16[48,1280]{1,0:T(8,128)(2,1)S(1)} %shard_map.127.refs_0_), channel_id=1, source_target_pairs={{0,24},{8,16},{16,8},{24,0},{1,25},{9,17},{17,9},{25,1},{2,26},{10... | collective-permute-start | bytes 368648 | tf_op jit(solution)/shard_map/ppermute | solution.py:255

commit v6 on v5

--- a/solution.py
+++ b/solution.py
@@ -85,10 +85,10 @@
         out_ref[...] = jnp.concatenate(parts, axis=0).astype(jnp.bfloat16)
 
 
-def head_kernel(chips, dp, shard, mask_hbm, hidden_hbm, columns_hbm, other_ref, *refs):
+def head_kernel(chips, dp, shard, mask_hbm, columns_hbm, hidden_hbm, other_ref, *refs):
     d, z, core = place()
     parts, out_ref = refs[: chips - 1], refs[chips - 1]
-    mask_ref, own_ref, columns_ref, sems = refs[chips:]
+    mask_ref, columns_ref, own_ref, sems = refs[chips:]
     copies = [
         pltpu.make_async_copy(mask_hbm, mask_ref, sems.at[0]),
         pltpu.make_async_copy(columns_hbm, columns_ref, sems.at[1]),
@@ -96,14 +96,10 @@
     ]
     for copy in copies:
         copy.start()
-    for copy in copies:
-        copy.wait()
     rows = dp * shard
     total = chips * rows
-    cols = own_ref.shape[1]
+    cols = other_ref.shape[1]
     half = chips // 2
-    mask = mask_ref[...].astype(jnp.float32).astype(jnp.bfloat16)
-    columns = jnp.concatenate([part[...] for part in (columns_ref, *parts)], axis=0) * mask
     r = iota((total, total), 0)
     near = jnp.where(r >= total // 2, 1, 0)
     r = r - near * (total // 2)
@@ -111,9 +107,14 @@
     j = over(r - t * (half * shard), shard)
     i = r - t * (half * shard) - j * shard
     order = one_hot(iota((total, total), 1) == (j + (1 - near) * half) * rows + (t ^ d) * shard + i)
+    for copy in copies[:2]:
+        copy.wait()
+    mask = mask_ref[...].astype(jnp.float32).astype(jnp.bfloat16)
+    columns = jnp.concatenate([part[...] for part in (columns_ref, *parts)], axis=0) * mask
     columns = exact(order, columns).astype(jnp.bfloat16)
-    for at, ref in ((core, own_ref), (1 - core, other_ref)):
-        out_ref[:, pl.ds(pl.multiple_of(at * cols, LANES), cols)] = exact(columns, ref[...])
+    out_ref[:, pl.ds(pl.multiple_of((1 - core) * cols, LANES), cols)] = exact(columns, other_ref[...])
+    copies[2].wait()
+    out_ref[:, pl.ds(pl.multiple_of(core * cols, LANES), cols)] = exact(columns, own_ref[...])
 
 
 def embed_kernel(chips, dp, shard, head_ref, *refs):
@@ -204,7 +205,7 @@
     return jax.ShapeDtypeStruct(shape, kind)
 
 
-def run(kernel, outs, *args, flops=0, hbm=0, scratch=()):
+def run(kernel, outs, *args, cost=1, hbm=0, scratch=()):
     moved = sum(x.size * x.dtype.itemsize for x in (*args, *jax.tree.leaves(outs)))
     vmem = pl.BlockSpec(memory_space=pltpu.VMEM)
     args = [pltpu.with_memory_space_constraint(x, pltpu.HBM) if n < hbm else x for n, x in enumerate(args)]
@@ -214,7 +215,7 @@
         in_specs=[pl.BlockSpec(memory_space=pltpu.HBM)] * hbm + [vmem] * (len(args) - hbm),
         out_specs=jax.tree.map(lambda _: vmem, outs),
         scratch_shapes=list(scratch),
-        cost_estimate=pl.CostEstimate(flops=flops, bytes_accessed=moved, transcendentals=0),
+        cost_estimate=pl.CostEstimate(flops=0, bytes_accessed=moved * cost, transcendentals=0),
         compiler_params=pltpu.CompilerParams(vmem_limit_bytes=VMEM_LIMIT),
     )(*args)
 
@@ -241,7 +242,6 @@
     rows = logit_grad.shape[1]
     shard = master.shape[0]
     cols = hidden.shape[1] * CORES
-    depth = hidden.shape[0]
     owners, cap, width = slot_grads.shape[1:]
     sizes = (chips, dp, shard)
     bf16, f32 = jnp.bfloat16, jnp.float32
@@ -254,9 +254,6 @@
     def send_dp(x, t):
         return lax.ppermute(x, "dp", [(i, i ^ t) for i in range(dp)]) if t else x
 
-    columns = [logit_grad.T]
-    for s in range(1, chips):
-        columns.append(send(columns[s - 1], 1) if s % 2 else send(columns[0], s))
     hidden_other = send(hidden, 0, 1)
     slots_in = (
         slot_grads[0].transpose(1, 0, 2).reshape(cap * owners, width),
@@ -270,20 +267,30 @@
         hbm=3,
         scratch=local_copies(*slots_in),
     )
+    slots_other = send(slots_other, 0, 1)
+    slots_other, hidden_other = lax.optimization_barrier((slots_other, hidden_other))
     messages = run(
         functools.partial(merge_kernel, chips),
         [shaped((cap * chips * CORES, cols + LANES), bf16)] * chips,
         slots_own,
-        send(slots_other, 0, 1),
-    )
-    head_in = (predict_mask[None, :], hidden, columns[0])
+        slots_other,
+    )
+    columns = [logit_grad.T]
+    for s in range(1, chips):
+        if s % 2 and s > 1:
+            late = columns[s - 1]
+            late, _ = lax.optimization_barrier((late, messages[0]))
+            columns.append(send(late, 1))
+        else:
+            columns.append(send(columns[0], s))
+    head_in = (predict_mask[None, :], columns[0], hidden)
     head = run(
         functools.partial(head_kernel, *sizes),
         shaped((chips * rows, cols), f32),
         *head_in,
         hidden_other,
         *columns[1:],
-        flops=2 * chips * rows * depth * cols,
+        cost=0,
         hbm=3,
         scratch=local_copies(*head_in),
     )
@@ -292,14 +299,17 @@
         functools.partial(embed_kernel, *sizes),
         [shaped((half * shard, cols), f32)] * (2 * dp),
         head,
-        *[send(message, s) for s, message in enumerate(messages)],
+        *[send(messages[s], s) for s in reversed(range(chips))],
     )
     pieces = {}
     for h, members in enumerate((far, near)):
+        heard = [send_dp(parts[h * dp + t], t) for t in range(dp)]
+        if h:
+            heard[0], _ = lax.optimization_barrier((heard[0], sums[0]))
         sums = run(
             functools.partial(sum_kernel, half, shard),
             [shaped((CORES * shard, cols // CORES), f32)] * half,
-            *[send_dp(parts[h * dp + t], t) for t in range(dp)],
+            *heard,
         )
         for s, total in zip(members, sums):
             pieces[s] = send(total, s)

time: 59.3 us -> 56.9 us (0.960)
  waiting for transfers between devices: 23.3 us -> 22 us
  starting transfers between devices: 27.9 us -> 27.2 us
    ppermute x9, waiting for transfers between devices: 7.46 us -> 5.07 us  [send_dp(): return lax.ppermute(x, 'dp', [(i, i ^ t) for i in range(dp)]) if t else x]
    ppermute x11, starting transfers between devices: 16.9 us -> 14.5 us  [send(): lax.ppermute(x, 'vocab', [(v, v ^ move) for v in range(vocab)])]
    ppermute x9, starting transfers between devices: 11 us -> 12.6 us  [send_dp(): return lax.ppermute(x, 'dp', [(i, i ^ t) for i in range(dp)]) if t else x]
    ppermute x11, waiting for transfers between devices: 15.8 us -> 16.9 us  [send(): lax.ppermute(x, 'vocab', [(v, v ^ move) for v in range(vocab)])]
  transfers between devices with their start and end apart: 20 -> 20, of which waited for: 8 -> 9; matrix products, arithmetic and copies ran while one was open for 0% -> 0% of each run, Pallas kernels for 9% -> 9%
where the time goes in v6:
time: 56.9 us; the launch traced here: 56.7 us
  starting transfers between devices  27.2 us (48%)
  waiting for transfers between devices  22 us (39%)
  Pallas kernels  6.82 us (12%)
  between operations  0.74 us (1%)
    ppermute x11, waiting for transfers between devices, send(): lax.ppermute(x, 'vocab', [(v, v ^ move) for v in range(vocab)])  16.9 us
    ppermute x11, starting transfers between devices, send(): lax.ppermute(x, 'vocab', [(v, v ^ move) for v in range(vocab)])  14.5 us
    ppermute x9, starting transfers between devices, send_dp(): return lax.ppermute(x, 'dp', [(i, i ^ t) for i in range(dp)]) if t else x  12.6 us
    pallas_call x9, Pallas kernels, run(): pl.pallas_call(kernel, out_shape=outs, in_specs=[pl.BlockSpec(memory_spac...  6.82 us
    ppermute x9, waiting for transfers between devices, send_dp(): return lax.ppermute(x, 'dp', [(i, i ^ t) for i in range(dp)]) if t else x  5.07 us
  transfers between devices with their start and end apart: 20, of which 9 were waited for; matrix products, arithmetic and copies ran while one was open for 0% of the time, Pallas kernels for 9%

profile of v6, /device:TPU:0, one launch (start us, length us, event | category | flops | bytes accessed | tf_op | source)
XLA Modules:
  0.0 56.7 jit_solution(6093141503878668915)
XLA Ops:
  0.6 0.5 collective-permute-start.1
  1.1 1.5 %shard_map.120 = (bf16[24,5632]{1,0:T(8,128)(2,1)S(1)}, bf16[24,5632]{1,0:T(8,128)(2,1)S(1)}) custom-call(bf16[48,5120]{1,0:T(8,128)(2,1)} %bitcast.8, s32[6,1,8]{2,1,0:T(1,128)} %bitcast.13, s32[1,8]{1,0:T(1,128)} %counts_hbm.1), custom_call_target="tpu_custom_call" | custom-call | bytes 1032416 | tf_op jit(solution)/shard_map/pallas_call | solution.py:212
  2.6 0.1 collective-permute-start
  2.7 4.0 %collective-permute-start.3 = (bf16[48,1024]{1,0:T(8,128)(2,1)}, bf16[48,1024]{1,0:T(8,128)(2,1)S(1)}, u32[]{:S(2)}, u32[]{:S(2)}) collective-permute-start(bf16[48,1024]{1,0:T(8,128)(2,1)} %bitcast.9), channel_id=1, source_target_pairs={{0,4},{1,5},{2,6},{3,7},{4,0},{5,1},{6,2},{7,3},{8,12},{9,13},{10,... | collective-permute-start | bytes 294920 | tf_op jit(solution)/shard_map/ppermute | solution.py:252
  6.8 0.0 collective-permute-done.other_ref
  6.8 0.0 collective-permute-done.1.other_ref
  6.8 2.5 %collective-permute-start.5 = (bf16[48,1408]{1,0:T(8,128)(2,1)S(1)}, bf16[48,1408]{1,0:T(8,128)(2,1)S(1)}, u32[]{:S(2)}, u32[]{:S(2)}) collective-permute-start(bf16[48,1408]{1,0:T(8,128)(2,1)S(1)} %get-tuple-element.35), channel_id=1, source_target_pairs={{0,6},{1,7},{2,4},{3,5},{4,2},{5,3},{6,0},{7,1},{8,14},{9,15},{10,... | collective-permute-start | bytes 405512 | tf_op jit(solution)/shard_map/ppermute | solution.py:252
  9.3 0.7 %collective-permute-start.6 = (bf16[48,1408]{1,0:T(8,128)(2,1)S(1)}, bf16[48,1408]{1,0:T(8,128)(2,1)S(1)}, u32[]{:S(2)}, u32[]{:S(2)}) collective-permute-start(bf16[48,1408]{1,0:T(8,128)(2,1)S(1)} %get-tuple-element.36), channel_id=1, source_target_pairs={{0,4},{1,5},{2,6},{3,7},{4,0},{5,1},{6,2},{7,3},{8,12},{9,13},{10,... | collective-permute-start | bytes 405512 | tf_op jit(solution)/shard_map/ppermute | solution.py:252
  9.9 1.3 %collective-permute-start.7 = (bf16[48,1408]{1,0:T(8,128)(2,1)S(1)}, bf16[48,1408]{1,0:T(8,128)(2,1)S(1)}, u32[]{:S(2)}, u32[]{:S(2)}) collective-permute-start(bf16[48,1408]{1,0:T(8,128)(2,1)S(1)} %get-tuple-element.37), channel_id=1, source_target_pairs={{0,2},{1,3},{2,0},{3,1},{4,6},{5,7},{6,4},{7,5},{8,10},{9,11},{10,... | collective-permute-start | bytes 405512 | tf_op jit(solution)/shard_map/ppermute | solution.py:252
  11.3 0.7 %collective-permute-start.2 = (bf16[48,1024]{1,0:T(8,128)(2,1)}, bf16[48,1024]{1,0:T(8,128)(2,1)S(1)}, u32[]{:S(2)}, u32[]{:S(2)}) collective-permute-start(bf16[48,1024]{1,0:T(8,128)(2,1)} %bitcast.10), channel_id=1, source_target_pairs={{0,2},{1,3},{2,0},{3,1},{4,6},{5,7},{6,4},{7,5},{8,10},{9,11},{10,... | collective-permute-start | bytes 294920 | tf_op jit(solution)/shard_map/ppermute | solution.py:252
  12.0 6.5 %collective-permute-done.3.refs_1_ = bf16[48,1024]{1,0:T(8,128)(2,1)S(1)} collective-permute-done((bf16[48,1024]{1,0:T(8,128)(2,1)}, bf16[48,1024]{1,0:T(8,128)(2,1)S(1)}, u32[]{:S(2)}, u32[]{:S(2)}) %collective-permute-start.3) | collective-permute-done | bytes 98336 | tf_op jit(solution)/shard_map/ppermute | solution.py:252
  18.5 0.4 collective-permute-start.4
  18.9 2.3 %collective-permute-done.2.refs_0_ = bf16[48,1024]{1,0:T(8,128)(2,1)S(1)} collective-permute-done((bf16[48,1024]{1,0:T(8,128)(2,1)}, bf16[48,1024]{1,0:T(8,128)(2,1)S(1)}, u32[]{:S(2)}, u32[]{:S(2)}) %collective-permute-start.2) | collective-permute-done | bytes 98336 | tf_op jit(solution)/shard_map/ppermute | solution.py:252
  21.2 3.8 %collective-permute-done.4.refs_2_ = bf16[48,1024]{1,0:T(8,128)(2,1)S(1)} collective-permute-done((bf16[48,1024]{1,0:T(8,128)(2,1)S(1)}, bf16[48,1024]{1,0:T(8,128)(2,1)S(1)}, u32[]{:S(2)}, u32[]{:S(2)}) %collective-permute-start.4) | collective-permute-done | bytes 98336 | tf_op jit(solution)/shard_map/ppermute | solution.py:252
  25.0 2.0 %shard_map.122.head_ref = f32[192,1280]{1,0:T(8,128)S(1)} custom-call(s32[1,1024]{1,0:T(1,128)} %bitcast.12, bf16[48,1024]{1,0:T(8,128)(2,1)} %bitcast.11, bf16[1024,640]{1,0:T(8,128)(2,1)} %hidden_hbm.1, bf16[1024,640]{1,0:T(8,128)(2,1)S(1)} %collective-permute-done.1.other_ref, bf16[48,1024]{1,0:T(8,128)(2,1)S(1)} %collective-permute-done.2.refs_0_, ...), custom_call_target="tpu_custom_call" | custom-call | tf_op jit(solution)/shard_map/pallas_call | solution.py:212
  27.1 0.0 copy-start
  27.1 0.0 copy-start.1
  27.1 0.0 copy-start.2
  27.1 0.0 collective-permute-done.5.refs_0_
  27.1 0.0 collective-permute-done.6.refs_1_
  27.1 0.0 collective-permute-done.7.refs_2_
  27.1 0.5 shard_map.123
  27.7 1.6 %collective-permute-start.8 = (f32[24,1280]{1,0:T(8,128)S(1)}, f32[24,1280]{1,0:T(8,128)S(1)}, u32[]{:S(2)}, u32[]{:S(2)}) collective-permute-start(f32[24,1280]{1,0:T(8,128)S(1)} %get-tuple-element.40), channel_id=1, source_target_pairs={{0,8},{8,0},{16,24},{24,16},{1,9},{9,1},{17,25},{25,17},{2,10},{10... | collective-permute-start | bytes 368648 | tf_op jit(solution)/shard_map/ppermute | solution.py:255
  29.3 1.5 %collective-permute-start.9 = (f32[24,1280]{1,0:T(8,128)S(1)}, f32[24,1280]{1,0:T(8,128)S(1)}, u32[]{:S(2)}, u32[]{:S(2)}) collective-permute-start(f32[24,1280]{1,0:T(8,128)S(1)} %get-tuple-element.41), channel_id=1, source_target_pairs={{0,16},{8,24},{16,0},{24,8},{1,17},{9,25},{17,1},{25,9},{2,18},{10... | collective-permute-start | bytes 368648 | tf_op jit(solution)/shard_map/ppermute | solution.py:255
  30.8 0.4 collective-permute-start.10
  31.2 1.5 %collective-permute-start.11 = (f32[24,1280]{1,0:T(8,128)S(1)}, f32[24,1280]{1,0:T(8,128)S(1)}, u32[]{:S(2)}, u32[]{:S(2)}) collective-permute-start(f32[24,1280]{1,0:T(8,128)S(1)} %get-tuple-element.45), channel_id=1, source_target_pairs={{0,8},{8,0},{16,24},{24,16},{1,9},{9,1},{17,25},{25,17},{2,10},{10... | collective-permute-start | bytes 368648 | tf_op jit(solution)/shard_map/ppermute | solution.py:255
  32.8 1.5 %collective-permute-start.12 = (f32[24,1280]{1,0:T(8,128)S(1)}, f32[24,1280]{1,0:T(8,128)S(1)}, u32[]{:S(2)}, u32[]{:S(2)}) collective-permute-start(f32[24,1280]{1,0:T(8,128)S(1)} %get-tuple-element.46), channel_id=1, source_target_pairs={{0,16},{8,24},{16,0},{24,8},{1,17},{9,25},{17,1},{25,9},{2,18},{10... | collective-permute-start | bytes 368648 | tf_op jit(solution)/shard_map/ppermute | solution.py:255
  34.3 0.0 collective-permute-done.8.refs_1_
  34.3 2.0 %collective-permute-start.13 = (f32[24,1280]{1,0:T(8,128)S(1)}, f32[24,1280]{1,0:T(8,128)S(1)}, u32[]{:S(2)}, u32[]{:S(2)}) collective-permute-start(f32[24,1280]{1,0:T(8,128)S(1)} %get-tuple-element.47), channel_id=1, source_target_pairs={{0,24},{8,16},{16,8},{24,0},{1,25},{9,17},{17,9},{25,1},{2,26},{10... | collective-permute-start | bytes 368648 | tf_op jit(solution)/shard_map/ppermute | solution.py:255
  36.3 2.1 %collective-permute-done.9.refs_2_ = f32[24,1280]{1,0:T(8,128)S(1)} collective-permute-done((f32[24,1280]{1,0:T(8,128)S(1)}, f32[24,1280]{1,0:T(8,128)S(1)}, u32[]{:S(2)}, u32[]{:S(2)}) %collective-permute-start.9) | collective-permute-done | bytes 122912 | tf_op jit(solution)/shard_map/ppermute | solution.py:255
  38.5 0.0 collective-permute-done.10.refs_3_
  38.5 1.7 %collective-permute-start.15 = (f32[24,640]{1,0:T(8,128)S(1)}, f32[24,640]{1,0:T(8,128)S(1)}, u32[]{:S(2)}, u32[]{:S(2)}) collective-permute-start(f32[24,640]{1,0:T(8,128)S(1)} %get-tuple-element.43), channel_id=1, source_target_pairs={{0,4},{1,5},{2,6},{3,7},{4,0},{5,1},{6,2},{7,3},{8,12},{9,13},{10,... | collective-permute-start | bytes 184328 | tf_op jit(solution)/shard_map/ppermute | solution.py:252
  40.3 2.0 %collective-permute-start.16 = (f32[24,640]{1,0:T(8,128)S(1)}, f32[24,640]{1,0:T(8,128)S(1)}, u32[]{:S(2)}, u32[]{:S(2)}) collective-permute-start(f32[24,640]{1,0:T(8,128)S(1)} %get-tuple-element.50), channel_id=1, source_target_pairs={{0,6},{1,7},{2,4},{3,5},{4,2},{5,3},{6,0},{7,1},{8,14},{9,15},{10,... | collective-permute-start | bytes 184328 | tf_op jit(solution)/shard_map/ppermute | solution.py:252
  42.3 0.0 collective-permute-done.11.refs_1_
  42.3 0.0 collective-permute-done.12.refs_2_
  42.3 0.0 collective-permute-done.13.refs_3_
  42.3 0.6 collective-permute-start.14
  42.9 4.1 %collective-permute-done.16.refs_6_ = f32[24,640]{1,0:T(8,128)S(1)} collective-permute-done((f32[24,640]{1,0:T(8,128)S(1)}, f32[24,640]{1,0:T(8,128)S(1)}, u32[]{:S(2)}, u32[]{:S(2)}) %collective-permute-start.16) | collective-permute-done | bytes 61472 | tf_op jit(solution)/shard_map/ppermute | solution.py:252
  47.0 0.1 collective-permute-done.14.refs_4_
  47.1 0.3 shard_map.127.refs_0_
  47.4 0.9 %collective-permute-start.19 = (bf16[48,1280]{1,0:T(8,128)(2,1)S(1)}, bf16[48,1280]{1,0:T(8,128)(2,1)S(1)}, u32[]{:S(2)}, u32[]{:S(2)}) collective-permute-start(bf16[48,1280]{1,0:T(8,128)(2,1)S(1)} %shard_map.127.refs_0_), channel_id=1, source_target_pairs={{0,24},{8,16},{16,8},{24,0},{1,25},{9,17},{17,9},{25,1},{2,26},{10... | collective-permute-start | bytes 368648 | tf_op jit(solution)/shard_map/ppermute | solution.py:255
  48.3 1.7 %collective-permute-start.18 = (bf16[48,1280]{1,0:T(8,128)(2,1)S(1)}, bf16[48,1280]{1,0:T(8,128)(2,1)S(1)}, u32[]{:S(2)}, u32[]{:S(2)}) collective-permute-start(bf16[48,1280]{1,0:T(8,128)(2,1)S(1)} %shard_map.127.refs_0_), channel_id=1, source_target_pairs={{0,16},{8,24},{16,0},{24,8},{1,17},{9,25},{17,1},{25,9},{2,18},{10... | collective-permute-start | bytes 368648 | tf_op jit(solution)/shard_map/ppermute | solution.py:255
  50.0 1.4 %collective-permute-start.17 = (bf16[48,1280]{1,0:T(8,128)(2,1)S(1)}, bf16[48,1280]{1,0:T(8,128)(2,1)S(1)}, u32[]{:S(2)}, u32[]{:S(2)}) collective-permute-start(bf16[48,1280]{1,0:T(8,128)(2,1)S(1)} %shard_map.127.refs_0_), channel_id=1, source_target_pairs={{0,8},{8,0},{16,24},{24,16},{1,9},{9,1},{17,25},{25,17},{2,10},{10... | collective-permute-start | bytes 368648 | tf_op jit(solution)/shard_map/ppermute | solution.py:255
  51.4 1.3 %shard_map.126 = (f32[12,5120]{1,0:T(8,128)}, f32[12,5120]{1,0:T(8,128)}, f32[12,5120]{1,0:T(8,128)}) custom-call(f32[12,5120]{1,0:T(8,128)S(1)} %copy-done, f32[12,5120]{1,0:T(8,128)S(1)} %copy-done.1, f32[12,5120]{1,0:T(8,128)S(1)} %copy-done.2, f32[24,640]{1,0:T(8,128)S(1)} %get-tuple-element.48.refs_3_, f32[24,640]{1,0:T(8,128)S(1)} %collective-permute-done.14.refs_4_, ...), custom_call_target="tpu_custom_call" | custom-call | bytes 1720320 | tf_op jit(solution)/shard_map/pallas_call | solution.py:212
  52.7 0.7 %collective-permute-done.19.refs_3_ = bf16[48,1280]{1,0:T(8,128)(2,1)S(1)} collective-permute-done((bf16[48,1280]{1,0:T(8,128)(2,1)S(1)}, bf16[48,1280]{1,0:T(8,128)(2,1)S(1)}, u32[]{:S(2)}, u32[]{:S(2)}) %collective-permute-start.19) | collective-permute-done | bytes 122912 | tf_op jit(solution)/shard_map/ppermute | solution.py:255
  53.4 1.1 %collective-permute-done.18.refs_2_ = bf16[48,1280]{1,0:T(8,128)(2,1)S(1)} collective-permute-done((bf16[48,1280]{1,0:T(8,128)(2,1)S(1)}, bf16[48,1280]{1,0:T(8,128)(2,1)S(1)}, u32[]{:S(2)}, u32[]{:S(2)}) %collective-permute-start.18) | collective-permute-done | bytes 122912 | tf_op jit(solution)/shard_map/ppermute | solution.py:255
  54.5 1.1 %collective-permute-done.17.refs_1_ = bf16[48,1280]{1,0:T(8,128)(2,1)S(1)} collective-permute-done((bf16[48,1280]{1,0:T(8,128)(2,1)S(1)}, bf16[48,1280]{1,0:T(8,128)(2,1)S(1)}, u32[]{:S(2)}, u32[]{:S(2)}) %collective-permute-start.17) | collective-permute-done | bytes 122912 | tf_op jit(solution)/shard_map/ppermute | solution.py:255
  55.6 1.1 %shard_map.128 = bf16[48,5120]{1,0:T(8,128)(2,1)} custom-call(bf16[48,1280]{1,0:T(8,128)(2,1)S(1)} %shard_map.127.refs_0_, bf16[48,1280]{1,0:T(8,128)(2,1)S(1)} %collective-permute-done.17.refs_1_, bf16[48,1280]{1,0:T(8,128)(2,1)S(1)} %collective-permute-done.18.refs_2_, bf16[48,1280]{1,0:T(8,128)(2,1)S(1)} %collective-permute-done.19.refs_3_), custom_call_target="tpu_custom_call" | custom-call | bytes 983040 | tf_op jit(solution)/shard_map/pallas_call | solution.py:212
  (7 shorter events, 0.1 us)
Async XLA Ops:
  0.6 6.2 %collective-permute-start.1 = (bf16[1024,640]{1,0:T(8,128)(2,1)}, bf16[1024,640]{1,0:T(8,128)(2,1)S(1)}, u32[]{:S(2)}, u32[]{:S(2)}) collective-permute-start(bf16[1024,640]{1,0:T(8,128)(2,1)} %hidden_hbm.1), channel_id=1, source_target_pairs={{0,1},{1,0},{2,3},{3,2},{4,5},{5,4},{6,7},{7,6},{8,9},{9,8},{10,11... | collective-permute-start | bytes 3932168 | tf_op jit(solution)/shard_map/ppermute | solution.py:252
  2.6 4.2 %collective-permute-start = (bf16[24,5632]{1,0:T(8,128)(2,1)S(1)}, bf16[24,5632]{1,0:T(8,128)(2,1)S(1)}, u32[]{:S(2)}, u32[]{:S(2)}) collective-permute-start(bf16[24,5632]{1,0:T(8,128)(2,1)S(1)} %get-tuple-element.29), channel_id=1, source_target_pairs={{0,1},{1,0},{2,3},{3,2},{4,5},{5,4},{6,7},{7,6},{8,9},{9,8},{10,11... | collective-permute-start | bytes 811016 | tf_op jit(solution)/shard_map/ppermute | solution.py:252
  2.7 15.7 %collective-permute-start.3 = (bf16[48,1024]{1,0:T(8,128)(2,1)}, bf16[48,1024]{1,0:T(8,128)(2,1)S(1)}, u32[]{:S(2)}, u32[]{:S(2)}) collective-permute-start(bf16[48,1024]{1,0:T(8,128)(2,1)} %bitcast.9), channel_id=1, source_target_pairs={{0,4},{1,5},{2,6},{3,7},{4,0},{5,1},{6,2},{7,3},{8,12},{9,13},{10,... | collective-permute-start | bytes 294920 | tf_op jit(solution)/shard_map/ppermute | solution.py:252
  6.8 20.3 %collective-permute-start.5 = (bf16[48,1408]{1,0:T(8,128)(2,1)S(1)}, bf16[48,1408]{1,0:T(8,128)(2,1)S(1)}, u32[]{:S(2)}, u32[]{:S(2)}) collective-permute-start(bf16[48,1408]{1,0:T(8,128)(2,1)S(1)} %get-tuple-element.35), channel_id=1, source_target_pairs={{0,6},{1,7},{2,4},{3,5},{4,2},{5,3},{6,0},{7,1},{8,14},{9,15},{10,... | collective-permute-start | bytes 405512 | tf_op jit(solution)/shard_map/ppermute | solution.py:252
  9.3 17.8 %collective-permute-start.6 = (bf16[48,1408]{1,0:T(8,128)(2,1)S(1)}, bf16[48,1408]{1,0:T(8,128)(2,1)S(1)}, u32[]{:S(2)}, u32[]{:S(2)}) collective-permute-start(bf16[48,1408]{1,0:T(8,128)(2,1)S(1)} %get-tuple-element.36), channel_id=1, source_target_pairs={{0,4},{1,5},{2,6},{3,7},{4,0},{5,1},{6,2},{7,3},{8,12},{9,13},{10,... | collective-permute-start | bytes 405512 | tf_op jit(solution)/shard_map/ppermute | solution.py:252
  9.9 17.2 %collective-permute-start.7 = (bf16[48,1408]{1,0:T(8,128)(2,1)S(1)}, bf16[48,1408]{1,0:T(8,128)(2,1)S(1)}, u32[]{:S(2)}, u32[]{:S(2)}) collective-permute-start(bf16[48,1408]{1,0:T(8,128)(2,1)S(1)} %get-tuple-element.37), channel_id=1, source_target_pairs={{0,2},{1,3},{2,0},{3,1},{4,6},{5,7},{6,4},{7,5},{8,10},{9,11},{10,... | collective-permute-start | bytes 405512 | tf_op jit(solution)/shard_map/ppermute | solution.py:252
  11.3 10.0 %collective-permute-start.2 = (bf16[48,1024]{1,0:T(8,128)(2,1)}, bf16[48,1024]{1,0:T(8,128)(2,1)S(1)}, u32[]{:S(2)}, u32[]{:S(2)}) collective-permute-start(bf16[48,1024]{1,0:T(8,128)(2,1)} %bitcast.10), channel_id=1, source_target_pairs={{0,2},{1,3},{2,0},{3,1},{4,6},{5,7},{6,4},{7,5},{8,10},{9,11},{10,... | collective-permute-start | bytes 294920 | tf_op jit(solution)/shard_map/ppermute | solution.py:252
  18.5 6.6 %collective-permute-start.4 = (bf16[48,1024]{1,0:T(8,128)(2,1)S(1)}, bf16[48,1024]{1,0:T(8,128)(2,1)S(1)}, u32[]{:S(2)}, u32[]{:S(2)}) collective-permute-start(bf16[48,1024]{1,0:T(8,128)(2,1)S(1)} %collective-permute-done.3.refs_1_), channel_id=1, source_target_pairs={{0,2},{1,3},{2,0},{3,1},{4,6},{5,7},{6,4},{7,5},{8,10},{9,11},{10,... | collective-permute-start | bytes 294920 | tf_op jit(solution)/shard_map/ppermute | solution.py:252
  27.1 20.0 %copy-start = (f32[12,5120]{1,0:T(8,128)S(1)}, f32[12,5120]{1,0:T(8,128)}, u32[]{:S(2)}) copy-start(f32[12,5120]{1,0:T(8,128)} %refs_0_.3) | copy-start | bytes 737284
  27.1 20.0 %copy-start.1 = (f32[12,5120]{1,0:T(8,128)S(1)}, f32[12,5120]{1,0:T(8,128)}, u32[]{:S(2)}) copy-start(f32[12,5120]{1,0:T(8,128)} %refs_1_.3) | copy-start | bytes 737284
  27.1 20.0 %copy-start.2 = (f32[12,5120]{1,0:T(8,128)S(1)}, f32[12,5120]{1,0:T(8,128)}, u32[]{:S(2)}) copy-start(f32[12,5120]{1,0:T(8,128)} %refs_2_.3) | copy-start | bytes 737284
  27.7 6.6 %collective-permute-start.8 = (f32[24,1280]{1,0:T(8,128)S(1)}, f32[24,1280]{1,0:T(8,128)S(1)}, u32[]{:S(2)}, u32[]{:S(2)}) collective-permute-start(f32[24,1280]{1,0:T(8,128)S(1)} %get-tuple-element.40), channel_id=1, source_target_pairs={{0,8},{8,0},{16,24},{24,16},{1,9},{9,1},{17,25},{25,17},{2,10},{10... | collective-permute-start | bytes 368648 | tf_op jit(solution)/shard_map/ppermute | solution.py:255
  29.3 9.2 %collective-permute-start.9 = (f32[24,1280]{1,0:T(8,128)S(1)}, f32[24,1280]{1,0:T(8,128)S(1)}, u32[]{:S(2)}, u32[]{:S(2)}) collective-permute-start(f32[24,1280]{1,0:T(8,128)S(1)} %get-tuple-element.41), channel_id=1, source_target_pairs={{0,16},{8,24},{16,0},{24,8},{1,17},{9,25},{17,1},{25,9},{2,18},{10... | collective-permute-start | bytes 368648 | tf_op jit(solution)/shard_map/ppermute | solution.py:255
  30.8 7.7 %collective-permute-start.10 = (f32[24,1280]{1,0:T(8,128)S(1)}, f32[24,1280]{1,0:T(8,128)S(1)}, u32[]{:S(2)}, u32[]{:S(2)}) collective-permute-start(f32[24,1280]{1,0:T(8,128)S(1)} %get-tuple-element.42), channel_id=1, source_target_pairs={{0,24},{8,16},{16,8},{24,0},{1,25},{9,17},{17,9},{25,1},{2,26},{10... | collective-permute-start | bytes 368648 | tf_op jit(solution)/shard_map/ppermute | solution.py:255
  31.2 11.0 %collective-permute-start.11 = (f32[24,1280]{1,0:T(8,128)S(1)}, f32[24,1280]{1,0:T(8,128)S(1)}, u32[]{:S(2)}, u32[]{:S(2)}) collective-permute-start(f32[24,1280]{1,0:T(8,128)S(1)} %get-tuple-element.45), channel_id=1, source_target_pairs={{0,8},{8,0},{16,24},{24,16},{1,9},{9,1},{17,25},{25,17},{2,10},{10... | collective-permute-start | bytes 368648 | tf_op jit(solution)/shard_map/ppermute | solution.py:255
  32.8 9.5 %collective-permute-start.12 = (f32[24,1280]{1,0:T(8,128)S(1)}, f32[24,1280]{1,0:T(8,128)S(1)}, u32[]{:S(2)}, u32[]{:S(2)}) collective-permute-start(f32[24,1280]{1,0:T(8,128)S(1)} %get-tuple-element.46), channel_id=1, source_target_pairs={{0,16},{8,24},{16,0},{24,8},{1,17},{9,25},{17,1},{25,9},{2,18},{10... | collective-permute-start | bytes 368648 | tf_op jit(solution)/shard_map/ppermute | solution.py:255
  34.3 8.0 %collective-permute-start.13 = (f32[24,1280]{1,0:T(8,128)S(1)}, f32[24,1280]{1,0:T(8,128)S(1)}, u32[]{:S(2)}, u32[]{:S(2)}) collective-permute-start(f32[24,1280]{1,0:T(8,128)S(1)} %get-tuple-element.47), channel_id=1, source_target_pairs={{0,24},{8,16},{16,8},{24,0},{1,25},{9,17},{17,9},{25,1},{2,26},{10... | collective-permute-start | bytes 368648 | tf_op jit(solution)/shard_map/ppermute | solution.py:255
  38.5 8.5 %collective-permute-start.15 = (f32[24,640]{1,0:T(8,128)S(1)}, f32[24,640]{1,0:T(8,128)S(1)}, u32[]{:S(2)}, u32[]{:S(2)}) collective-permute-start(f32[24,640]{1,0:T(8,128)S(1)} %get-tuple-element.43), channel_id=1, source_target_pairs={{0,4},{1,5},{2,6},{3,7},{4,0},{5,1},{6,2},{7,3},{8,12},{9,13},{10,... | collective-permute-start | bytes 184328 | tf_op jit(solution)/shard_map/ppermute | solution.py:252
  40.3 6.7 %collective-permute-start.16 = (f32[24,640]{1,0:T(8,128)S(1)}, f32[24,640]{1,0:T(8,128)S(1)}, u32[]{:S(2)}, u32[]{:S(2)}) collective-permute-start(f32[24,640]{1,0:T(8,128)S(1)} %get-tuple-element.50), channel_id=1, source_target_pairs={{0,6},{1,7},{2,4},{3,5},{4,2},{5,3},{6,0},{7,1},{8,14},{9,15},{10,... | collective-permute-start | bytes 184328 | tf_op jit(solution)/shard_map/ppermute | solution.py:252
  42.3 4.8 %collective-permute-start.14 = (f32[24,640]{1,0:T(8,128)S(1)}, f32[24,640]{1,0:T(8,128)S(1)}, u32[]{:S(2)}, u32[]{:S(2)}) collective-permute-start(f32[24,640]{1,0:T(8,128)S(1)} %get-tuple-element.49), channel_id=1, source_target_pairs={{0,2},{1,3},{2,0},{3,1},{4,6},{5,7},{6,4},{7,5},{8,10},{9,11},{10,... | collective-permute-start | bytes 184328 | tf_op jit(solution)/shard_map/ppermute | solution.py:252
  47.4 5.9 %collective-permute-start.19 = (bf16[48,1280]{1,0:T(8,128)(2,1)S(1)}, bf16[48,1280]{1,0:T(8,128)(2,1)S(1)}, u32[]{:S(2)}, u32[]{:S(2)}) collective-permute-start(bf16[48,1280]{1,0:T(8,128)(2,1)S(1)} %shard_map.127.refs_0_), channel_id=1, source_target_pairs={{0,24},{8,16},{16,8},{24,0},{1,25},{9,17},{17,9},{25,1},{2,26},{10... | collective-permute-start | bytes 368648 | tf_op jit(solution)/shard_map/ppermute | solution.py:255
  48.3 6.2 %collective-permute-start.18 = (bf16[48,1280]{1,0:T(8,128)(2,1)S(1)}, bf16[48,1280]{1,0:T(8,128)(2,1)S(1)}, u32[]{:S(2)}, u32[]{:S(2)}) collective-permute-start(bf16[48,1280]{1,0:T(8,128)(2,1)S(1)} %shard_map.127.refs_0_), channel_id=1, source_target_pairs={{0,16},{8,24},{16,0},{24,8},{1,17},{9,25},{17,1},{25,9},{2,18},{10... | collective-permute-start | bytes 368648 | tf_op jit(solution)/shard_map/ppermute | solution.py:255
  50.0 5.6 %collective-permute-start.17 = (bf16[48,1280]{1,0:T(8,128)(2,1)S(1)}, bf16[48,1280]{1,0:T(8,128)(2,1)S(1)}, u32[]{:S(2)}, u32[]{:S(2)}) collective-permute-start(bf16[48,1280]{1,0:T(8,128)(2,1)S(1)} %shard_map.127.refs_0_), channel_id=1, source_target_pairs={{0,8},{8,0},{16,24},{24,16},{1,9},{9,1},{17,25},{25,17},{2,10},{10... | collective-permute-start | bytes 368648 | tf_op jit(solution)/shard_map/ppermute | solution.py:255

commit v7 on v6

--- a/solution.py
+++ b/solution.py
@@ -34,7 +34,7 @@
     return jnp.dot(left, right, preferred_element_type=jnp.float32)
 
 
-def slots_kernel(chips, dp, shard, slots_hbm, rows_hbm, counts_hbm, own_out, other_out, slots_ref, rows_ref, counts_ref, sems):
+def slots_kernel(chips, slots_hbm, rows_hbm, counts_hbm, own_out, other_out, slots_ref, rows_ref, counts_ref, sems):
     d, z, core = place()
     copies = [
         pltpu.make_async_copy(rows_hbm, rows_ref, sems.at[0]),
@@ -43,52 +43,60 @@
     ]
     for copy in copies:
         copy.start()
-    for copy in copies:
-        copy.wait()
     cap, owners = rows_ref.shape[0], rows_ref.shape[2]
     count = cap * owners
     group = cap * chips
-    width = slots_ref.shape[1] // chips
-    half = chips // 2
+    part = slots_ref.shape[1] // 2
+    q = iota((count, count), 0)
+    away = jnp.where(q >= group, 1, 0)
+    q = q - away * group
+    s = over(q, cap)
+    wanted = (q - s * cap) * owners + (s ^ z) * CORES + (away ^ core)
+    pick = one_hot(iota((count, count), 1) == wanted)
     own_lane = iota((count, owners), 1) == iota((count, owners), 0) % owners
+    for copy in copies[:2]:
+        copy.wait()
     rows = jnp.broadcast_to(rows_ref[...], (cap, owners, owners)).reshape(count, owners)
     rows = jnp.sum(jnp.where(own_lane, rows, 0), axis=1, keepdims=True)
     live = jnp.broadcast_to(counts_ref[...], (count, owners))
     live = jnp.sum(jnp.where(own_lane, live, 0), axis=1, keepdims=True)
-    block = over(rows, shard)
-    ids = (block ^ d) * shard + rows - block * shard
-    ids = jnp.where(over(iota((count, 1), 0), owners) < live, ids, -1)
+    ids = jnp.where(over(iota((count, 1), 0), owners) < live, rows, -1)
     ids = jnp.broadcast_to(ids, (count, LANES)).astype(jnp.bfloat16)
-    q = iota((CORES * group, count), 0)
-    away = jnp.where(q >= group, 1, 0)
-    q = q - away * group
-    near = jnp.where(q >= group // 2, 1, 0)
-    q = q - near * (group // 2)
-    slot = over(q, half)
-    owner = q - slot * half + (1 - near) * half
-    for s in range(chips):
-        wanted = slot * owners + (owner ^ z ^ s) * CORES + (away ^ core)
-        pick = one_hot(iota((CORES * group, count), 1) == wanted)
-        start = pl.multiple_of((z ^ s) * width, LANES)
-        values = exact(pick, slots_ref[:, pl.ds(start, width)])
-        picked_ids = exact(pick, ids)
-        first = s * (width + LANES)
-        for out_ref, spot in ((own_out, slice(0, group)), (other_out, slice(group, CORES * group))):
-            out_ref[:, first : first + width] = values[spot].astype(jnp.bfloat16)
-            out_ref[:, first + width : first + width + LANES] = picked_ids[spot].astype(jnp.bfloat16)
-
-
-def merge_kernel(chips, own_ref, other_ref, *out_refs):
-    size = own_ref.shape[1] // chips
+    ids = exact(pick, ids)
+    copies[2].wait()
+    outs = ((own_out, slice(0, group)), (other_out, slice(group, count)))
+    for away in range(2):
+        start = pl.multiple_of(((d & 1) ^ away) * part, LANES)
+        values = exact(pick, slots_ref[:, pl.ds(start, part)])
+        for out_ref, spot in outs:
+            out_ref[:, away * part : (away + 1) * part] = values[spot].astype(jnp.bfloat16)
+    for out_ref, spot in outs:
+        out_ref[:, 2 * part :] = ids[spot].astype(jnp.bfloat16)
+
+
+def pair_kernel(own_ref, other_ref, out_ref):
+    part = out_ref.shape[1] - LANES
+    both = [ref[:, part:].astype(jnp.float32) for ref in (own_ref, other_ref)]
+    out_ref[...] = jnp.concatenate(both, axis=0).astype(jnp.bfloat16)
+
+
+def owners_kernel(cap, own_ref, other_ref, pair_ref, *out_refs):
+    part = pair_ref.shape[1] - LANES
+    group = own_ref.shape[0]
+    pair = pair_ref[...].astype(jnp.float32)
+    held = [pair[:group], pair[group:]]
+    for ref in (own_ref, other_ref):
+        values = [ref[:, :part].astype(jnp.float32), ref[:, 2 * part :].astype(jnp.float32)]
+        held.append(jnp.concatenate(values, axis=1))
     for s, out_ref in enumerate(out_refs):
-        parts = [ref[:, s * size : (s + 1) * size].astype(jnp.float32) for ref in (own_ref, other_ref)]
-        out_ref[...] = jnp.concatenate(parts, axis=0).astype(jnp.bfloat16)
+        rows = [block[s * cap : (s + 1) * cap] for block in held]
+        out_ref[...] = jnp.concatenate(rows, axis=0).astype(jnp.bfloat16)
 
 
 def head_kernel(chips, dp, shard, mask_hbm, columns_hbm, hidden_hbm, other_ref, *refs):
     d, z, core = place()
-    parts, out_ref = refs[: chips - 1], refs[chips - 1]
-    mask_ref, columns_ref, own_ref, sems = refs[chips:]
+    parts, outs = refs[: chips - 1], refs[chips - 1 : chips - 1 + dp]
+    mask_ref, columns_ref, own_ref, sems = refs[chips - 1 + dp :]
     copies = [
         pltpu.make_async_copy(mask_hbm, mask_ref, sems.at[0]),
         pltpu.make_async_copy(columns_hbm, columns_ref, sems.at[1]),
@@ -99,60 +107,74 @@
     rows = dp * shard
     total = chips * rows
     cols = other_ref.shape[1]
-    half = chips // 2
+    size = chips * shard
     r = iota((total, total), 0)
-    near = jnp.where(r >= total // 2, 1, 0)
-    r = r - near * (total // 2)
-    t = over(r, half * shard)
-    j = over(r - t * (half * shard), shard)
-    i = r - t * (half * shard) - j * shard
-    order = one_hot(iota((total, total), 1) == (j + (1 - near) * half) * rows + (t ^ d) * shard + i)
+    t = over(r, size)
+    s = over(r - t * size, shard)
+    i = r - t * size - s * shard
+    order = one_hot(iota((total, total), 1) == s * rows + (t ^ d) * shard + i)
     for copy in copies[:2]:
         copy.wait()
     mask = mask_ref[...].astype(jnp.float32).astype(jnp.bfloat16)
     columns = jnp.concatenate([part[...] for part in (columns_ref, *parts)], axis=0) * mask
     columns = exact(order, columns).astype(jnp.bfloat16)
-    out_ref[:, pl.ds(pl.multiple_of((1 - core) * cols, LANES), cols)] = exact(columns, other_ref[...])
-    copies[2].wait()
-    out_ref[:, pl.ds(pl.multiple_of(core * cols, LANES), cols)] = exact(columns, own_ref[...])
-
-
-def embed_kernel(chips, dp, shard, head_ref, *refs):
-    slot_refs, out_refs = refs[: -2 * dp], refs[-2 * dp :]
-    half = chips // 2
-    total, cols = head_ref.shape
-    size = half * shard
+    for at, ref in ((1 - core, other_ref), (core, own_ref)):
+        if ref is own_ref:
+            copies[2].wait()
+        head = exact(columns, ref[...])
+        spot = pl.ds(pl.multiple_of(at * cols, LANES), cols)
+        for t, out_ref in enumerate(outs):
+            out_ref[:, spot] = head[t * size : (t + 1) * size]
+
+
+def stacked(rows):
+    cut = rows.shape[1] // 2
+    return jnp.concatenate([rows[:, :cut], rows[:, cut:]], axis=0)
+
+
+def unstacked(rows):
+    cut = rows.shape[0] // 2
+    return jnp.concatenate([rows[:cut], rows[cut:]], axis=1)
+
+
+def embed_kernel(dp, shard, *refs):
+    d, z, core = place()
+    slot_refs, out_refs = refs[:-dp], refs[-dp:]
+    part = slot_refs[0].shape[1] - LANES
     count = sum(ref.shape[0] for ref in slot_refs)
-    ids = jnp.concatenate([ref[:, cols:] for ref in slot_refs], axis=0)
-    ids = ids.astype(jnp.float32)[:, :1].astype(jnp.int32)
-    values = jnp.concatenate([ref[:, :cols] for ref in slot_refs], axis=0)
+    both = jnp.concatenate([ref[...].astype(jnp.float32) for ref in slot_refs], axis=0)
+    ids = both[:, part : part + 1].astype(jnp.int32)
+    values = both[:, :part].astype(jnp.bfloat16)
     block = over(jnp.maximum(ids, 0), shard)
-    group = slot_refs[0].shape[0] // CORES
-    place_in = iota((count, 1), 0) % group
-    near = jnp.where(place_in >= group // 2, 1, 0)
-    target = near * (total // 2) + (block * half + place_in % half) * shard + ids - block * shard
-    target = jnp.where(ids < 0, -1, target)
-    picked = one_hot(iota((count, total), 1) == target)
+    target = jnp.where(ids < 0, -1, (block ^ d) * shard + ids - block * shard)
+    picked = one_hot(iota((count, dp * shard), 1) == target)
     embed = lax.dot_general(picked, values, (((0,), (0,)), ((), ())), preferred_element_type=jnp.float32)
-    for n, out_ref in enumerate(out_refs):
-        spot = slice(n * size, (n + 1) * size)
-        out_ref[...] = head_ref[spot] + embed[spot]
-
-
-def sum_kernel(half, shard, *refs):
-    dp = len(refs) - half
+    for t, out_ref in enumerate(out_refs):
+        out_ref[...] = stacked(embed[t * shard : (t + 1) * shard])
+
+
+def gather_kernel(*refs):
+    d, z, core = place()
+    parts, out_ref = refs[:-1], refs[-1]
+    part = out_ref.shape[1] // 2
+    for side in range(2):
+        total = parts[side][...]
+        for t in range(side + 2, len(parts), 2):
+            total = total + parts[t][...]
+        out_ref[:, pl.ds(pl.multiple_of(((d & 1) ^ side) * part, LANES), part)] = unstacked(total)
+
+
+def sum_kernel(chips, shard, *refs):
+    dp = len(refs) - chips
     total = refs[0][...]
     for t in range(1, dp):
         total = total + refs[t][...]
-    cut = total.shape[1] // CORES
-    for j, out_ref in enumerate(refs[dp:]):
-        rows = total[j * shard : (j + 1) * shard]
-        out_ref[...] = jnp.concatenate([rows[:, :cut], rows[:, cut:]], axis=0)
-
-
-def step(shard, spot, piece_ref, master_ref, first_ref, second_ref):
-    piece = piece_ref[...]
-    gradient = jnp.concatenate([piece[:shard], piece[shard:]], axis=1)
+    for s, out_ref in enumerate(refs[dp:]):
+        out_ref[...] = stacked(total[s * shard : (s + 1) * shard])
+
+
+def step(spot, piece_ref, embed_ref, master_ref, first_ref, second_ref):
+    gradient = unstacked(piece_ref[...]) + embed_ref[:, spot]
     master = master_ref[:, spot]
     first_new = 0.9 * first_ref[:, spot] + 0.1 * gradient
     second_new = 0.95 * second_ref[:, spot] + 0.05 * gradient * gradient
@@ -163,23 +185,23 @@
 
 
 def chip_spot(z, s, piece_ref):
-    cols = piece_ref.shape[1] * CORES
+    cols = piece_ref.shape[1] * 2
     return pl.ds(pl.multiple_of((z ^ s) * cols, LANES), cols)
 
 
-def rows_kernel(shard, *refs):
-    d, z, core = place()
-    state, pieces, out_ref = refs[:3], refs[3:-1], refs[-1]
-    table = [step(shard, chip_spot(z, s, piece), piece, *state)[0] for s, piece in enumerate(pieces)]
+def rows_kernel(*refs):
+    d, z, core = place()
+    state, pieces, out_ref = refs[:4], refs[4:-1], refs[-1]
+    table = [step(chip_spot(z, s, piece), piece, *state)[0] for s, piece in enumerate(pieces)]
     out_ref[...] = jnp.concatenate(table, axis=0).astype(jnp.bfloat16)
 
 
-def adam_kernel(shard, *refs):
-    d, z, core = place()
-    state, pieces, outs = refs[:3], refs[3:-3], refs[-3:]
+def adam_kernel(*refs):
+    d, z, core = place()
+    state, pieces, outs = refs[:4], refs[4:-3], refs[-3:]
     for s, piece in enumerate(pieces):
         spot = chip_spot(z, s, piece)
-        for out_ref, value in zip(outs, step(shard, spot, piece, *state)):
+        for out_ref, value in zip(outs, step(spot, piece, *state)):
             out_ref[:, spot] = value
 
 
@@ -238,14 +260,12 @@
     vocab = lax.axis_size("vocab")
     dp = lax.axis_size("dp")
     chips = vocab // CORES
-    half = chips // 2
     rows = logit_grad.shape[1]
     shard = master.shape[0]
     cols = hidden.shape[1] * CORES
     owners, cap, width = slot_grads.shape[1:]
-    sizes = (chips, dp, shard)
+    group = cap * chips
     bf16, f32 = jnp.bfloat16, jnp.float32
-    far, near = range(half, chips), range(half)
 
     def send(x, s, away=0):
         move = s * CORES + away
@@ -261,73 +281,51 @@
         slot_counts,
     )
     slots_own, slots_other = run(
-        functools.partial(slots_kernel, *sizes),
-        [shaped((cap * chips, chips * (cols + LANES)), bf16)] * CORES,
+        functools.partial(slots_kernel, chips),
+        [shaped((group, width + LANES), bf16)] * CORES,
         *slots_in,
         hbm=3,
         scratch=local_copies(*slots_in),
     )
     slots_other = send(slots_other, 0, 1)
-    slots_other, hidden_other = lax.optimization_barrier((slots_other, hidden_other))
+    slots_pair = send_dp(run(pair_kernel, shaped((CORES * group, width // 2 + LANES), bf16), slots_own, slots_other), 1)
     messages = run(
-        functools.partial(merge_kernel, chips),
-        [shaped((cap * chips * CORES, cols + LANES), bf16)] * chips,
+        functools.partial(owners_kernel, cap),
+        [shaped((2 * CORES * cap, width // 2 + LANES), bf16)] * chips,
         slots_own,
         slots_other,
+        slots_pair,
     )
     columns = [logit_grad.T]
     for s in range(1, chips):
-        if s % 2 and s > 1:
-            late = columns[s - 1]
-            late, _ = lax.optimization_barrier((late, messages[0]))
-            columns.append(send(late, 1))
-        else:
-            columns.append(send(columns[0], s))
+        columns.append(send(columns[s - 1], 1) if s % 2 else send(columns[0], s))
     head_in = (predict_mask[None, :], columns[0], hidden)
     head = run(
-        functools.partial(head_kernel, *sizes),
-        shaped((chips * rows, cols), f32),
+        functools.partial(head_kernel, chips, dp, shard),
+        [shaped((chips * shard, cols), f32)] * dp,
         *head_in,
         hidden_other,
         *columns[1:],
-        cost=0,
         hbm=3,
         scratch=local_copies(*head_in),
     )
-    state = (master, first_moment, second_moment)
-    parts = run(
-        functools.partial(embed_kernel, *sizes),
-        [shaped((half * shard, cols), f32)] * (2 * dp),
-        head,
+    embed = run(
+        functools.partial(embed_kernel, dp, shard),
+        [shaped((2 * shard, width // 4), f32)] * dp,
         *[send(messages[s], s) for s in reversed(range(chips))],
     )
-    pieces = {}
-    for h, members in enumerate((far, near)):
-        heard = [send_dp(parts[h * dp + t], t) for t in range(dp)]
-        if h:
-            heard[0], _ = lax.optimization_barrier((heard[0], sums[0]))
-        sums = run(
-            functools.partial(sum_kernel, half, shard),
-            [shaped((CORES * shard, cols // CORES), f32)] * half,
-            *heard,
-        )
-        for s, total in zip(members, sums):
-            pieces[s] = send(total, s)
-    pieces = [pieces[s] for s in range(chips)]
+    sums = run(
+        functools.partial(sum_kernel, chips, shard),
+        [shaped((2 * shard, cols // 2), f32)] * chips,
+        *[send_dp(head[t], t) for t in range(dp)],
+    )
+    pieces = [send(sums[s], s) for s in range(chips)]
+    embed = run(gather_kernel, shaped((shard, width), f32), *[send_dp(embed[t], t) for t in range(dp)])
+    state = (embed, master, first_moment, second_moment)
+    table = run(rows_kernel, shaped((chips * shard, cols), bf16), *state, *pieces)
+    master_new, first_new, second_new = run(adam_kernel, [shaped(master.shape, f32)] * 3, *state, *pieces)
     table = run(
-        functools.partial(rows_kernel, shard),
-        shaped((chips * shard, cols), bf16),
-        *state,
-        *pieces,
-    )
-    master_new, first_new, second_new = run(
-        functools.partial(adam_kernel, shard),
-        [shaped(master.shape, f32)] * 3,
-        *state,
-        *pieces,
-    )
-    table = run(
-        functools.partial(table_kernel, *sizes),
+        functools.partial(table_kernel, chips, dp, shard),
         shaped((rows, width), bf16),
         *[send_dp(table, t) for t in range(dp)],
     )
@@ -425,7 +423,7 @@
 def local(hidden, logit_grad, predict_mask, slot_grads, *rest):
     vocab = lax.axis_size("vocab")
     fits = hidden.shape[1] % LANES == 0 and logit_grad.shape[1] % 16 == 0
-    fits = fits and (vocab // CORES * slot_grads.shape[2]) % 8 == 0
+    fits = fits and (vocab // CORES * slot_grads.shape[2]) % 8 == 0 and lax.axis_size("dp") % 2 == 0
     step = aligned if fits else plain
     return step(hidden, logit_grad, predict_mask, slot_grads, *rest)
 

time: 56.9 us -> 58.8 us (1.033)
  starting transfers between devices: 27.2 us -> 30.4 us
  waiting for transfers between devices: 22 us -> 20.7 us
    ppermute x11, waiting for transfers between devices: 16.9 us -> 11.3 us  [send(): lax.ppermute(x, 'vocab', [(v, v ^ move) for v in range(vocab)])]
    ppermute x9 -> x10, waiting for transfers between devices: 5.07 us -> 9.37 us  [send_dp(): return lax.ppermute(x, 'dp', [(i, i ^ t) for i in range(dp)]) if t else x]
    ppermute x11, starting transfers between devices: 14.5 us -> 17 us  [send(): lax.ppermute(x, 'vocab', [(v, v ^ move) for v in range(vocab)])]
    ppermute x9 -> x10, starting transfers between devices: 12.6 us -> 13.3 us  [send_dp(): return lax.ppermute(x, 'dp', [(i, i ^ t) for i in range(dp)]) if t else x]
    pallas_call x9 -> x10, Pallas kernels: 6.82 us -> 6.74 us  [run(): pl.pallas_call(kernel, out_shape=outs, in_specs=[pl.BlockSpec(memory_spac...]
  transfers between devices with their start and end apart: 20 -> 21, of which waited for: 9 -> 11; matrix products, arithmetic and copies ran while one was open for 0% -> 0% of each run, Pallas kernels for 9% -> 9%
where the time goes in v7:
time: 58.8 us; the launch traced here: 58.6 us
  starting transfers between devices  30.4 us (52%)
  waiting for transfers between devices  20.7 us (35%)
  Pallas kernels  6.74 us (11%)
  between operations  0.73 us (1%)
    ppermute x11, starting transfers between devices, send(): lax.ppermute(x, 'vocab', [(v, v ^ move) for v in range(vocab)])  17 us
    ppermute x10, starting transfers between devices, send_dp(): return lax.ppermute(x, 'dp', [(i, i ^ t) for i in range(dp)]) if t else x  13.3 us
    ppermute x11, waiting for transfers between devices, send(): lax.ppermute(x, 'vocab', [(v, v ^ move) for v in range(vocab)])  11.3 us
    ppermute x10, waiting for transfers between devices, send_dp(): return lax.ppermute(x, 'dp', [(i, i ^ t) for i in range(dp)]) if t else x  9.37 us
    pallas_call x10, Pallas kernels, run(): pl.pallas_call(kernel, out_shape=outs, in_specs=[pl.BlockSpec(memory_spac...  6.74 us
  transfers between devices with their start and end apart: 21, of which 11 were waited for; matrix products, arithmetic and copies ran while one was open for 0% of the time, Pallas kernels for 9%

profile of v7, /device:TPU:0, one launch (start us, length us, event | category | flops | bytes accessed | tf_op | source)
XLA Modules:
  0.0 58.6 jit_solution(7321573450489933399)
XLA Ops:
  0.6 0.5 collective-permute-start.8
  1.1 1.4 %shard_map.120 = (bf16[24,5248]{1,0:T(8,128)(2,1)S(1)}, bf16[24,5248]{1,0:T(8,128)(2,1)S(1)}) custom-call(bf16[48,5120]{1,0:T(8,128)(2,1)} %bitcast.8, s32[6,1,8]{2,1,0:T(1,128)} %bitcast.13, s32[1,8]{1,0:T(1,128)} %counts_hbm.1), custom_call_target="tpu_custom_call" | custom-call | bytes 995552 | tf_op jit(solution)/shard_map/pallas_call | solution.py:234
  2.5 0.1 collective-permute-start
  2.7 1.5 %collective-permute-done.other_ref = bf16[24,5248]{1,0:T(8,128)(2,1)S(1)} collective-permute-done((bf16[24,5248]{1,0:T(8,128)(2,1)S(1)}, bf16[24,5248]{1,0:T(8,128)(2,1)S(1)}, u32[]{:S(2)}, u32[]{:S(2)}) %collective-permute-start) | collective-permute-done | bytes 251936 | tf_op jit(solution)/shard_map/ppermute | solution.py:272
  4.2 2.9 %collective-permute-start.1 = (bf16[48,2688]{1,0:T(8,128)(2,1)S(1)}, bf16[48,2688]{1,0:T(8,128)(2,1)S(1)}, u32[]{:S(2)}, u32[]{:S(2)}) collective-permute-start(bf16[48,2688]{1,0:T(8,128)(2,1)S(1)} %shard_map.121), channel_id=1, source_target_pairs={{0,8},{8,0},{16,24},{24,16},{1,9},{9,1},{17,25},{25,17},{2,10},{10... | collective-permute-start | bytes 774152 | tf_op jit(solution)/shard_map/ppermute | solution.py:275
  7.1 2.6 %collective-permute-start.10 = (bf16[48,1024]{1,0:T(8,128)(2,1)}, bf16[48,1024]{1,0:T(8,128)(2,1)S(1)}, u32[]{:S(2)}, u32[]{:S(2)}) collective-permute-start(bf16[48,1024]{1,0:T(8,128)(2,1)} %bitcast.9), channel_id=1, source_target_pairs={{0,4},{1,5},{2,6},{3,7},{4,0},{5,1},{6,2},{7,3},{8,12},{9,13},{10,... | collective-permute-start | bytes 294920 | tf_op jit(solution)/shard_map/ppermute | solution.py:272
  9.7 1.6 %collective-permute-start.9 = (bf16[48,1024]{1,0:T(8,128)(2,1)}, bf16[48,1024]{1,0:T(8,128)(2,1)S(1)}, u32[]{:S(2)}, u32[]{:S(2)}) collective-permute-start(bf16[48,1024]{1,0:T(8,128)(2,1)} %bitcast.10), channel_id=1, source_target_pairs={{0,2},{1,3},{2,0},{3,1},{4,6},{5,7},{6,4},{7,5},{8,10},{9,11},{10,... | collective-permute-start | bytes 294920 | tf_op jit(solution)/shard_map/ppermute | solution.py:272
  11.3 3.7 %collective-permute-done.10.refs_1_ = bf16[48,1024]{1,0:T(8,128)(2,1)S(1)} collective-permute-done((bf16[48,1024]{1,0:T(8,128)(2,1)}, bf16[48,1024]{1,0:T(8,128)(2,1)S(1)}, u32[]{:S(2)}, u32[]{:S(2)}) %collective-permute-start.10) | collective-permute-done | bytes 98336 | tf_op jit(solution)/shard_map/ppermute | solution.py:272
  15.0 0.7 %collective-permute-start.11 = (bf16[48,1024]{1,0:T(8,128)(2,1)S(1)}, bf16[48,1024]{1,0:T(8,128)(2,1)S(1)}, u32[]{:S(2)}, u32[]{:S(2)}) collective-permute-start(bf16[48,1024]{1,0:T(8,128)(2,1)S(1)} %collective-permute-done.10.refs_1_), channel_id=1, source_target_pairs={{0,2},{1,3},{2,0},{3,1},{4,6},{5,7},{6,4},{7,5},{8,10},{9,11},{10,... | collective-permute-start | bytes 294920 | tf_op jit(solution)/shard_map/ppermute | solution.py:272
  15.7 0.2 shard_map.122
  15.9 2.8 %collective-permute-start.2 = (bf16[24,2688]{1,0:T(8,128)(2,1)S(1)}, bf16[24,2688]{1,0:T(8,128)(2,1)S(1)}, u32[]{:S(2)}, u32[]{:S(2)}) collective-permute-start(bf16[24,2688]{1,0:T(8,128)(2,1)S(1)} %get-tuple-element.27), channel_id=1, source_target_pairs={{0,6},{1,7},{2,4},{3,5},{4,2},{5,3},{6,0},{7,1},{8,14},{9,15},{10,... | collective-permute-start | bytes 387080 | tf_op jit(solution)/shard_map/ppermute | solution.py:272
  18.6 1.0 %collective-permute-done.11.refs_2_ = bf16[48,1024]{1,0:T(8,128)(2,1)S(1)} collective-permute-done((bf16[48,1024]{1,0:T(8,128)(2,1)S(1)}, bf16[48,1024]{1,0:T(8,128)(2,1)S(1)}, u32[]{:S(2)}, u32[]{:S(2)}) %collective-permute-start.11) | collective-permute-done | bytes 98336 | tf_op jit(solution)/shard_map/ppermute | solution.py:272
  19.6 0.0 collective-permute-done.8.other_ref
  19.6 2.0 %shard_map.125 = (f32[48,1280]{1,0:T(8,128)S(1)}, f32[48,1280]{1,0:T(8,128)S(1)}, f32[48,1280]{1,0:T(8,128)S(1)}, f32[48,1280]{1,0:T(8,128)S(1)}) custom-call(s32[1,1024]{1,0:T(1,128)} %bitcast.12, bf16[48,1024]{1,0:T(8,128)(2,1)} %bitcast.11, bf16[1024,640]{1,0:T(8,128)(2,1)} %hidden_hbm.1, bf16[1024,640]{1,0:T(8,128)(2,1)S(1)} %collective-permute-done.8.other_ref, ...), custom_call_target="tpu_custom_call" | custom-call | bytes 4001792 | tf_op jit(solution)/shard_map/pallas_call | solution.py:234
  21.7 0.0 copy-start
  21.7 0.0 copy-start.1
  21.7 0.0 copy-start.2
  21.7 0.4 collective-permute-start.12
  22.0 3.2 %collective-permute-start.3 = (bf16[24,2688]{1,0:T(8,128)(2,1)S(1)}, bf16[24,2688]{1,0:T(8,128)(2,1)S(1)}, u32[]{:S(2)}, u32[]{:S(2)}) collective-permute-start(bf16[24,2688]{1,0:T(8,128)(2,1)S(1)} %get-tuple-element.28), channel_id=1, source_target_pairs={{0,4},{1,5},{2,6},{3,7},{4,0},{5,1},{6,2},{7,3},{8,12},{9,13},{10,... | collective-permute-start | bytes 387080 | tf_op jit(solution)/shard_map/ppermute | solution.py:272
  25.2 1.1 %collective-permute-start.4 = (bf16[24,2688]{1,0:T(8,128)(2,1)S(1)}, bf16[24,2688]{1,0:T(8,128)(2,1)S(1)}, u32[]{:S(2)}, u32[]{:S(2)}) collective-permute-start(bf16[24,2688]{1,0:T(8,128)(2,1)S(1)} %get-tuple-element.29), channel_id=1, source_target_pairs={{0,2},{1,3},{2,0},{3,1},{4,6},{5,7},{6,4},{7,5},{8,10},{9,11},{10,... | collective-permute-start | bytes 387080 | tf_op jit(solution)/shard_map/ppermute | solution.py:272
  26.3 1.5 %collective-permute-start.13 = (f32[48,1280]{1,0:T(8,128)S(1)}, f32[48,1280]{1,0:T(8,128)S(1)}, u32[]{:S(2)}, u32[]{:S(2)}) collective-permute-start(f32[48,1280]{1,0:T(8,128)S(1)} %get-tuple-element.37), channel_id=1, source_target_pairs={{0,16},{8,24},{16,0},{24,8},{1,17},{9,25},{17,1},{25,9},{2,18},{10... | collective-permute-start | bytes 737288 | tf_op jit(solution)/shard_map/ppermute | solution.py:275
  27.9 0.0 collective-permute-done.2.refs_0_
  27.9 1.4 %collective-permute-start.14 = (f32[48,1280]{1,0:T(8,128)S(1)}, f32[48,1280]{1,0:T(8,128)S(1)}, u32[]{:S(2)}, u32[]{:S(2)}) collective-permute-start(f32[48,1280]{1,0:T(8,128)S(1)} %get-tuple-element.38), channel_id=1, source_target_pairs={{0,24},{8,16},{16,8},{24,0},{1,25},{9,17},{17,9},{25,1},{2,26},{10... | collective-permute-start | bytes 737288 | tf_op jit(solution)/shard_map/ppermute | solution.py:275
  29.3 1.7 %collective-permute-done.3.refs_1_ = bf16[24,2688]{1,0:T(8,128)(2,1)S(1)} collective-permute-done((bf16[24,2688]{1,0:T(8,128)(2,1)S(1)}, bf16[24,2688]{1,0:T(8,128)(2,1)S(1)}, u32[]{:S(2)}, u32[]{:S(2)}) %collective-permute-start.3) | collective-permute-done | bytes 129056 | tf_op jit(solution)/shard_map/ppermute | solution.py:272
  31.0 0.6 %collective-permute-done.4.refs_2_ = bf16[24,2688]{1,0:T(8,128)(2,1)S(1)} collective-permute-done((bf16[24,2688]{1,0:T(8,128)(2,1)S(1)}, bf16[24,2688]{1,0:T(8,128)(2,1)S(1)}, u32[]{:S(2)}, u32[]{:S(2)}) %collective-permute-start.4) | collective-permute-done | bytes 129056 | tf_op jit(solution)/shard_map/ppermute | solution.py:272
  31.5 0.3 shard_map.123
  31.9 0.9 %collective-permute-start.5 = (f32[24,1280]{1,0:T(8,128)S(1)}, f32[24,1280]{1,0:T(8,128)S(1)}, u32[]{:S(2)}, u32[]{:S(2)}) collective-permute-start(f32[24,1280]{1,0:T(8,128)S(1)} %get-tuple-element.32), channel_id=1, source_target_pairs={{0,8},{8,0},{16,24},{24,16},{1,9},{9,1},{17,25},{25,17},{2,10},{10... | collective-permute-start | bytes 368648 | tf_op jit(solution)/shard_map/ppermute | solution.py:275
  32.8 1.5 %collective-permute-start.6 = (f32[24,1280]{1,0:T(8,128)S(1)}, f32[24,1280]{1,0:T(8,128)S(1)}, u32[]{:S(2)}, u32[]{:S(2)}) collective-permute-start(f32[24,1280]{1,0:T(8,128)S(1)} %get-tuple-element.33), channel_id=1, source_target_pairs={{0,16},{8,24},{16,0},{24,8},{1,17},{9,25},{17,1},{25,9},{2,18},{10... | collective-permute-start | bytes 368648 | tf_op jit(solution)/shard_map/ppermute | solution.py:275
  34.3 0.0 collective-permute-done.12.refs_1_
  34.3 1.2 %collective-permute-start.7 = (f32[24,1280]{1,0:T(8,128)S(1)}, f32[24,1280]{1,0:T(8,128)S(1)}, u32[]{:S(2)}, u32[]{:S(2)}) collective-permute-start(f32[24,1280]{1,0:T(8,128)S(1)} %get-tuple-element.34), channel_id=1, source_target_pairs={{0,24},{8,16},{16,8},{24,0},{1,25},{9,17},{17,9},{25,1},{2,26},{10... | collective-permute-start | bytes 368648 | tf_op jit(solution)/shard_map/ppermute | solution.py:275
  35.5 6.3 %collective-permute-done.13.refs_2_ = f32[48,1280]{1,0:T(8,128)S(1)} collective-permute-done((f32[48,1280]{1,0:T(8,128)S(1)}, f32[48,1280]{1,0:T(8,128)S(1)}, u32[]{:S(2)}, u32[]{:S(2)}) %collective-permute-start.13) | collective-permute-done | bytes 245792 | tf_op jit(solution)/shard_map/ppermute | solution.py:275
  41.7 0.0 collective-permute-done.14.refs_3_
  41.7 0.1 shard_map.126
  41.8 0.7 %collective-permute-start.15 = (f32[24,640]{1,0:T(8,128)S(1)}, f32[24,640]{1,0:T(8,128)S(1)}, u32[]{:S(2)}, u32[]{:S(2)}) collective-permute-start(f32[24,640]{1,0:T(8,128)S(1)} %get-tuple-element.40), channel_id=1, source_target_pairs={{0,2},{1,3},{2,0},{3,1},{4,6},{5,7},{6,4},{7,5},{8,10},{9,11},{10,... | collective-permute-start | bytes 184328 | tf_op jit(solution)/shard_map/ppermute | solution.py:272
  42.5 0.0 collective-permute-start.16
  42.5 0.0 collective-permute-done.5.refs_1_
  42.5 3.8 %collective-permute-start.17 = (f32[24,640]{1,0:T(8,128)S(1)}, f32[24,640]{1,0:T(8,128)S(1)}, u32[]{:S(2)}, u32[]{:S(2)}) collective-permute-start(f32[24,640]{1,0:T(8,128)S(1)} %get-tuple-element.42), channel_id=1, source_target_pairs={{0,6},{1,7},{2,4},{3,5},{4,2},{5,3},{6,0},{7,1},{8,14},{9,15},{10,... | collective-permute-start | bytes 184328 | tf_op jit(solution)/shard_map/ppermute | solution.py:272
  46.3 1.3 %collective-permute-done.16.refs_6_ = f32[24,640]{1,0:T(8,128)S(1)} collective-permute-done((f32[24,640]{1,0:T(8,128)S(1)}, f32[24,640]{1,0:T(8,128)S(1)}, u32[]{:S(2)}, u32[]{:S(2)}) %collective-permute-start.16) | collective-permute-done | bytes 61472 | tf_op jit(solution)/shard_map/ppermute | solution.py:272
  47.6 1.6 %collective-permute-done.17.refs_7_ = f32[24,640]{1,0:T(8,128)S(1)} collective-permute-done((f32[24,640]{1,0:T(8,128)S(1)}, f32[24,640]{1,0:T(8,128)S(1)}, u32[]{:S(2)}, u32[]{:S(2)}) %collective-permute-start.17) | collective-permute-done | bytes 61472 | tf_op jit(solution)/shard_map/ppermute | solution.py:272
  49.2 0.3 shard_map.128.refs_0_
  49.6 2.5 %collective-permute-start.20 = (bf16[48,1280]{1,0:T(8,128)(2,1)S(1)}, bf16[48,1280]{1,0:T(8,128)(2,1)S(1)}, u32[]{:S(2)}, u32[]{:S(2)}) collective-permute-start(bf16[48,1280]{1,0:T(8,128)(2,1)S(1)} %shard_map.128.refs_0_), channel_id=1, source_target_pairs={{0,24},{8,16},{16,8},{24,0},{1,25},{9,17},{17,9},{25,1},{2,26},{10... | collective-permute-start | bytes 368648 | tf_op jit(solution)/shard_map/ppermute | solution.py:275
  52.0 0.5 collective-permute-start.19
  52.6 0.5 collective-permute-start.18
  53.1 1.3 %shard_map.127 = (f32[12,5120]{1,0:T(8,128)}, f32[12,5120]{1,0:T(8,128)}, f32[12,5120]{1,0:T(8,128)}) custom-call(f32[12,5120]{1,0:T(8,128)S(1)} %shard_map.124.refs_0_, f32[12,5120]{1,0:T(8,128)S(1)} %copy-done, f32[12,5120]{1,0:T(8,128)S(1)} %copy-done.1, f32[12,5120]{1,0:T(8,128)S(1)} %copy-done.2, f32[24,640]{1,0:T(8,128)S(1)} %get-tuple-element.39.refs_4_, ...), custom_call_target="tpu_custom_call" | custom-call | bytes 1966080 | tf_op jit(solution)/shard_map/pallas_call | solution.py:234
  54.4 1.0 %collective-permute-done.20.refs_3_ = bf16[48,1280]{1,0:T(8,128)(2,1)S(1)} collective-permute-done((bf16[48,1280]{1,0:T(8,128)(2,1)S(1)}, bf16[48,1280]{1,0:T(8,128)(2,1)S(1)}, u32[]{:S(2)}, u32[]{:S(2)}) %collective-permute-start.20) | collective-permute-done | bytes 122912 | tf_op jit(solution)/shard_map/ppermute | solution.py:275
  55.4 1.5 %collective-permute-done.19.refs_2_ = bf16[48,1280]{1,0:T(8,128)(2,1)S(1)} collective-permute-done((bf16[48,1280]{1,0:T(8,128)(2,1)S(1)}, bf16[48,1280]{1,0:T(8,128)(2,1)S(1)}, u32[]{:S(2)}, u32[]{:S(2)}) %collective-permute-start.19) | collective-permute-done | bytes 122912 | tf_op jit(solution)/shard_map/ppermute | solution.py:275
  56.9 0.5 collective-permute-done.18.refs_1_
  57.5 1.1 %shard_map.129 = bf16[48,5120]{1,0:T(8,128)(2,1)} custom-call(bf16[48,1280]{1,0:T(8,128)(2,1)S(1)} %shard_map.128.refs_0_, bf16[48,1280]{1,0:T(8,128)(2,1)S(1)} %collective-permute-done.18.refs_1_, bf16[48,1280]{1,0:T(8,128)(2,1)S(1)} %collective-permute-done.19.refs_2_, bf16[48,1280]{1,0:T(8,128)(2,1)S(1)} %collective-permute-done.20.refs_3_), custom_call_target="tpu_custom_call" | custom-call | bytes 983040 | tf_op jit(solution)/shard_map/pallas_call | solution.py:234
  (10 shorter events, 0.1 us)
Async XLA Ops:
  0.6 19.0 %collective-permute-start.8 = (bf16[1024,640]{1,0:T(8,128)(2,1)}, bf16[1024,640]{1,0:T(8,128)(2,1)S(1)}, u32[]{:S(2)}, u32[]{:S(2)}) collective-permute-start(bf16[1024,640]{1,0:T(8,128)(2,1)} %hidden_hbm.1), channel_id=1, source_target_pairs={{0,1},{1,0},{2,3},{3,2},{4,5},{5,4},{6,7},{7,6},{8,9},{9,8},{10,11... | collective-permute-start | bytes 3932168 | tf_op jit(solution)/shard_map/ppermute | solution.py:272
  2.5 1.7 %collective-permute-start = (bf16[24,5248]{1,0:T(8,128)(2,1)S(1)}, bf16[24,5248]{1,0:T(8,128)(2,1)S(1)}, u32[]{:S(2)}, u32[]{:S(2)}) collective-permute-start(bf16[24,5248]{1,0:T(8,128)(2,1)S(1)} %get-tuple-element.26), channel_id=1, source_target_pairs={{0,1},{1,0},{2,3},{3,2},{4,5},{5,4},{6,7},{7,6},{8,9},{9,8},{10,11... | collective-permute-start | bytes 755720 | tf_op jit(solution)/shard_map/ppermute | solution.py:272
  4.2 11.5 %collective-permute-start.1 = (bf16[48,2688]{1,0:T(8,128)(2,1)S(1)}, bf16[48,2688]{1,0:T(8,128)(2,1)S(1)}, u32[]{:S(2)}, u32[]{:S(2)}) collective-permute-start(bf16[48,2688]{1,0:T(8,128)(2,1)S(1)} %shard_map.121), channel_id=1, source_target_pairs={{0,8},{8,0},{16,24},{24,16},{1,9},{9,1},{17,25},{25,17},{2,10},{10... | collective-permute-start | bytes 774152 | tf_op jit(solution)/shard_map/ppermute | solution.py:275
  7.1 7.9 %collective-permute-start.10 = (bf16[48,1024]{1,0:T(8,128)(2,1)}, bf16[48,1024]{1,0:T(8,128)(2,1)S(1)}, u32[]{:S(2)}, u32[]{:S(2)}) collective-permute-start(bf16[48,1024]{1,0:T(8,128)(2,1)} %bitcast.9), channel_id=1, source_target_pairs={{0,4},{1,5},{2,6},{3,7},{4,0},{5,1},{6,2},{7,3},{8,12},{9,13},{10,... | collective-permute-start | bytes 294920 | tf_op jit(solution)/shard_map/ppermute | solution.py:272
  9.7 8.9 %collective-permute-start.9 = (bf16[48,1024]{1,0:T(8,128)(2,1)}, bf16[48,1024]{1,0:T(8,128)(2,1)S(1)}, u32[]{:S(2)}, u32[]{:S(2)}) collective-permute-start(bf16[48,1024]{1,0:T(8,128)(2,1)} %bitcast.10), channel_id=1, source_target_pairs={{0,2},{1,3},{2,0},{3,1},{4,6},{5,7},{6,4},{7,5},{8,10},{9,11},{10,... | collective-permute-start | bytes 294920 | tf_op jit(solution)/shard_map/ppermute | solution.py:272
  15.0 4.6 %collective-permute-start.11 = (bf16[48,1024]{1,0:T(8,128)(2,1)S(1)}, bf16[48,1024]{1,0:T(8,128)(2,1)S(1)}, u32[]{:S(2)}, u32[]{:S(2)}) collective-permute-start(bf16[48,1024]{1,0:T(8,128)(2,1)S(1)} %collective-permute-done.10.refs_1_), channel_id=1, source_target_pairs={{0,2},{1,3},{2,0},{3,1},{4,6},{5,7},{6,4},{7,5},{8,10},{9,11},{10,... | collective-permute-start | bytes 294920 | tf_op jit(solution)/shard_map/ppermute | solution.py:272
  15.9 12.0 %collective-permute-start.2 = (bf16[24,2688]{1,0:T(8,128)(2,1)S(1)}, bf16[24,2688]{1,0:T(8,128)(2,1)S(1)}, u32[]{:S(2)}, u32[]{:S(2)}) collective-permute-start(bf16[24,2688]{1,0:T(8,128)(2,1)S(1)} %get-tuple-element.27), channel_id=1, source_target_pairs={{0,6},{1,7},{2,4},{3,5},{4,2},{5,3},{6,0},{7,1},{8,14},{9,15},{10,... | collective-permute-start | bytes 387080 | tf_op jit(solution)/shard_map/ppermute | solution.py:272
  21.7 27.6 %copy-start = (f32[12,5120]{1,0:T(8,128)S(1)}, f32[12,5120]{1,0:T(8,128)}, u32[]{:S(2)}) copy-start(f32[12,5120]{1,0:T(8,128)} %refs_1_.3) | copy-start | bytes 737284
  21.7 27.6 %copy-start.1 = (f32[12,5120]{1,0:T(8,128)S(1)}, f32[12,5120]{1,0:T(8,128)}, u32[]{:S(2)}) copy-start(f32[12,5120]{1,0:T(8,128)} %refs_2_.3) | copy-start | bytes 737284
  21.7 27.6 %copy-start.2 = (f32[12,5120]{1,0:T(8,128)S(1)}, f32[12,5120]{1,0:T(8,128)}, u32[]{:S(2)}) copy-start(f32[12,5120]{1,0:T(8,128)} %refs_3_.3) | copy-start | bytes 737284
  21.7 12.6 %collective-permute-start.12 = (f32[48,1280]{1,0:T(8,128)S(1)}, f32[48,1280]{1,0:T(8,128)S(1)}, u32[]{:S(2)}, u32[]{:S(2)}) collective-permute-start(f32[48,1280]{1,0:T(8,128)S(1)} %get-tuple-element.36), channel_id=1, source_target_pairs={{0,8},{8,0},{16,24},{24,16},{1,9},{9,1},{17,25},{25,17},{2,10},{10... | collective-permute-start | bytes 737288 | tf_op jit(solution)/shard_map/ppermute | solution.py:275
  22.0 8.9 %collective-permute-start.3 = (bf16[24,2688]{1,0:T(8,128)(2,1)S(1)}, bf16[24,2688]{1,0:T(8,128)(2,1)S(1)}, u32[]{:S(2)}, u32[]{:S(2)}) collective-permute-start(bf16[24,2688]{1,0:T(8,128)(2,1)S(1)} %get-tuple-element.28), channel_id=1, source_target_pairs={{0,4},{1,5},{2,6},{3,7},{4,0},{5,1},{6,2},{7,3},{8,12},{9,13},{10,... | collective-permute-start | bytes 387080 | tf_op jit(solution)/shard_map/ppermute | solution.py:272
  25.2 6.3 %collective-permute-start.4 = (bf16[24,2688]{1,0:T(8,128)(2,1)S(1)}, bf16[24,2688]{1,0:T(8,128)(2,1)S(1)}, u32[]{:S(2)}, u32[]{:S(2)}) collective-permute-start(bf16[24,2688]{1,0:T(8,128)(2,1)S(1)} %get-tuple-element.29), channel_id=1, source_target_pairs={{0,2},{1,3},{2,0},{3,1},{4,6},{5,7},{6,4},{7,5},{8,10},{9,11},{10,... | collective-permute-start | bytes 387080 | tf_op jit(solution)/shard_map/ppermute | solution.py:272
  26.3 15.4 %collective-permute-start.13 = (f32[48,1280]{1,0:T(8,128)S(1)}, f32[48,1280]{1,0:T(8,128)S(1)}, u32[]{:S(2)}, u32[]{:S(2)}) collective-permute-start(f32[48,1280]{1,0:T(8,128)S(1)} %get-tuple-element.37), channel_id=1, source_target_pairs={{0,16},{8,24},{16,0},{24,8},{1,17},{9,25},{17,1},{25,9},{2,18},{10... | collective-permute-start | bytes 737288 | tf_op jit(solution)/shard_map/ppermute | solution.py:275
  27.9 13.9 %collective-permute-start.14 = (f32[48,1280]{1,0:T(8,128)S(1)}, f32[48,1280]{1,0:T(8,128)S(1)}, u32[]{:S(2)}, u32[]{:S(2)}) collective-permute-start(f32[48,1280]{1,0:T(8,128)S(1)} %get-tuple-element.38), channel_id=1, source_target_pairs={{0,24},{8,16},{16,8},{24,0},{1,25},{9,17},{17,9},{25,1},{2,26},{10... | collective-permute-start | bytes 737288 | tf_op jit(solution)/shard_map/ppermute | solution.py:275
  31.9 10.6 %collective-permute-start.5 = (f32[24,1280]{1,0:T(8,128)S(1)}, f32[24,1280]{1,0:T(8,128)S(1)}, u32[]{:S(2)}, u32[]{:S(2)}) collective-permute-start(f32[24,1280]{1,0:T(8,128)S(1)} %get-tuple-element.32), channel_id=1, source_target_pairs={{0,8},{8,0},{16,24},{24,16},{1,9},{9,1},{17,25},{25,17},{2,10},{10... | collective-permute-start | bytes 368648 | tf_op jit(solution)/shard_map/ppermute | solution.py:275
  32.8 13.5 %collective-permute-start.6 = (f32[24,1280]{1,0:T(8,128)S(1)}, f32[24,1280]{1,0:T(8,128)S(1)}, u32[]{:S(2)}, u32[]{:S(2)}) collective-permute-start(f32[24,1280]{1,0:T(8,128)S(1)} %get-tuple-element.33), channel_id=1, source_target_pairs={{0,16},{8,24},{16,0},{24,8},{1,17},{9,25},{17,1},{25,9},{2,18},{10... | collective-permute-start | bytes 368648 | tf_op jit(solution)/shard_map/ppermute | solution.py:275
  34.3 12.0 %collective-permute-start.7 = (f32[24,1280]{1,0:T(8,128)S(1)}, f32[24,1280]{1,0:T(8,128)S(1)}, u32[]{:S(2)}, u32[]{:S(2)}) collective-permute-start(f32[24,1280]{1,0:T(8,128)S(1)} %get-tuple-element.34), channel_id=1, source_target_pairs={{0,24},{8,16},{16,8},{24,0},{1,25},{9,17},{17,9},{25,1},{2,26},{10... | collective-permute-start | bytes 368648 | tf_op jit(solution)/shard_map/ppermute | solution.py:275
  41.8 4.5 %collective-permute-start.15 = (f32[24,640]{1,0:T(8,128)S(1)}, f32[24,640]{1,0:T(8,128)S(1)}, u32[]{:S(2)}, u32[]{:S(2)}) collective-permute-start(f32[24,640]{1,0:T(8,128)S(1)} %get-tuple-element.40), channel_id=1, source_target_pairs={{0,2},{1,3},{2,0},{3,1},{4,6},{5,7},{6,4},{7,5},{8,10},{9,11},{10,... | collective-permute-start | bytes 184328 | tf_op jit(solution)/shard_map/ppermute | solution.py:272
  42.5 5.1 %collective-permute-start.16 = (f32[24,640]{1,0:T(8,128)S(1)}, f32[24,640]{1,0:T(8,128)S(1)}, u32[]{:S(2)}, u32[]{:S(2)}) collective-permute-start(f32[24,640]{1,0:T(8,128)S(1)} %get-tuple-element.41), channel_id=1, source_target_pairs={{0,4},{1,5},{2,6},{3,7},{4,0},{5,1},{6,2},{7,3},{8,12},{9,13},{10,... | collective-permute-start | bytes 184328 | tf_op jit(solution)/shard_map/ppermute | solution.py:272
  42.5 6.7 %collective-permute-start.17 = (f32[24,640]{1,0:T(8,128)S(1)}, f32[24,640]{1,0:T(8,128)S(1)}, u32[]{:S(2)}, u32[]{:S(2)}) collective-permute-start(f32[24,640]{1,0:T(8,128)S(1)} %get-tuple-element.42), channel_id=1, source_target_pairs={{0,6},{1,7},{2,4},{3,5},{4,2},{5,3},{6,0},{7,1},{8,14},{9,15},{10,... | collective-permute-start | bytes 184328 | tf_op jit(solution)/shard_map/ppermute | solution.py:272
  49.6 5.8 %collective-permute-start.20 = (bf16[48,1280]{1,0:T(8,128)(2,1)S(1)}, bf16[48,1280]{1,0:T(8,128)(2,1)S(1)}, u32[]{:S(2)}, u32[]{:S(2)}) collective-permute-start(bf16[48,1280]{1,0:T(8,128)(2,1)S(1)} %shard_map.128.refs_0_), channel_id=1, source_target_pairs={{0,24},{8,16},{16,8},{24,0},{1,25},{9,17},{17,9},{25,1},{2,26},{10... | collective-permute-start | bytes 368648 | tf_op jit(solution)/shard_map/ppermute | solution.py:275
  52.0 4.9 %collective-permute-start.19 = (bf16[48,1280]{1,0:T(8,128)(2,1)S(1)}, bf16[48,1280]{1,0:T(8,128)(2,1)S(1)}, u32[]{:S(2)}, u32[]{:S(2)}) collective-permute-start(bf16[48,1280]{1,0:T(8,128)(2,1)S(1)} %shard_map.128.refs_0_), channel_id=1, source_target_pairs={{0,16},{8,24},{16,0},{24,8},{1,17},{9,25},{17,1},{25,9},{2,18},{10... | collective-permute-start | bytes 368648 | tf_op jit(solution)/shard_map/ppermute | solution.py:275
  52.6 4.9 %collective-permute-start.18 = (bf16[48,1280]{1,0:T(8,128)(2,1)S(1)}, bf16[48,1280]{1,0:T(8,128)(2,1)S(1)}, u32[]{:S(2)}, u32[]{:S(2)}) collective-permute-start(bf16[48,1280]{1,0:T(8,128)(2,1)S(1)} %shard_map.128.refs_0_), channel_id=1, source_target_pairs={{0,8},{8,0},{16,24},{24,16},{1,9},{9,1},{17,25},{25,17},{2,10},{10... | collective-permute-start | bytes 368648 | tf_op jit(solution)/shard_map/ppermute | solution.py:275

commit v8 on v6

--- a/solution.py
+++ b/solution.py
@@ -10,6 +10,7 @@
 STEP = 8
 CORES = 2
 LANES = 128
+ID_ROWS = 16
 VMEM_LIMIT = 24 * 1024 * 1024
 
 
@@ -43,14 +44,25 @@
     ]
     for copy in copies:
         copy.start()
-    for copy in copies:
-        copy.wait()
     cap, owners = rows_ref.shape[0], rows_ref.shape[2]
     count = cap * owners
     group = cap * chips
     width = slots_ref.shape[1] // chips
     half = chips // 2
+    q = iota((count, count), 0)
+    away = jnp.where(q >= group, 1, 0)
+    q = q - away * group
+    near = jnp.where(q >= group // 2, 1, 0)
+    q = q - near * (group // 2)
+    slot = over(q, half)
+    owner = q - slot * half + (1 - near) * half
+    picks = [
+        one_hot(iota((count, count), 1) == slot * owners + (owner ^ z ^ s) * CORES + (away ^ core))
+        for s in range(chips)
+    ]
     own_lane = iota((count, owners), 1) == iota((count, owners), 0) % owners
+    for copy in copies[:2]:
+        copy.wait()
     rows = jnp.broadcast_to(rows_ref[...], (cap, owners, owners)).reshape(count, owners)
     rows = jnp.sum(jnp.where(own_lane, rows, 0), axis=1, keepdims=True)
     live = jnp.broadcast_to(counts_ref[...], (count, owners))
@@ -59,47 +71,45 @@
     ids = (block ^ d) * shard + rows - block * shard
     ids = jnp.where(over(iota((count, 1), 0), owners) < live, ids, -1)
     ids = jnp.broadcast_to(ids, (count, LANES)).astype(jnp.bfloat16)
-    q = iota((CORES * group, count), 0)
-    away = jnp.where(q >= group, 1, 0)
-    q = q - away * group
-    near = jnp.where(q >= group // 2, 1, 0)
-    q = q - near * (group // 2)
-    slot = over(q, half)
-    owner = q - slot * half + (1 - near) * half
-    for s in range(chips):
-        wanted = slot * owners + (owner ^ z ^ s) * CORES + (away ^ core)
-        pick = one_hot(iota((CORES * group, count), 1) == wanted)
+    copies[2].wait()
+    for s, pick in enumerate(picks):
         start = pl.multiple_of((z ^ s) * width, LANES)
         values = exact(pick, slots_ref[:, pl.ds(start, width)])
         picked_ids = exact(pick, ids)
         first = s * (width + LANES)
-        for out_ref, spot in ((own_out, slice(0, group)), (other_out, slice(group, CORES * group))):
+        for out_ref, spot in ((own_out, slice(0, group)), (other_out, slice(group, count))):
             out_ref[:, first : first + width] = values[spot].astype(jnp.bfloat16)
             out_ref[:, first + width : first + width + LANES] = picked_ids[spot].astype(jnp.bfloat16)
 
 
-def merge_kernel(chips, own_ref, other_ref, *out_refs):
+def diagonal(values, axis):
+    return jnp.sum(jnp.where(iota(values.shape, 0) == iota(values.shape, 1), values, 0.0), axis=axis, keepdims=True)
+
+
+def merge_kernel(chips, hidden_hbm, own_ref, other_ref, *refs):
+    out_refs, hidden_ref, sems = refs[:chips], refs[chips], refs[-1]
+    copy = pltpu.make_async_copy(hidden_hbm, hidden_ref, sems.at[0])
+    copy.start()
     size = own_ref.shape[1] // chips
+    width = size - LANES
     for s, out_ref in enumerate(out_refs):
         parts = [ref[:, s * size : (s + 1) * size].astype(jnp.float32) for ref in (own_ref, other_ref)]
-        out_ref[...] = jnp.concatenate(parts, axis=0).astype(jnp.bfloat16)
-
-
-def head_kernel(chips, dp, shard, mask_hbm, columns_hbm, hidden_hbm, other_ref, *refs):
+        both = jnp.concatenate(parts, axis=0)
+        ids = jnp.broadcast_to(diagonal(both[:, width:], 0), (ID_ROWS, LANES))
+        blocks = [both[:, c : c + LANES] for c in range(0, width, LANES)]
+        out_ref[...] = jnp.concatenate([*blocks, ids], axis=0).astype(jnp.bfloat16)
+    copy.wait()
+
+
+def head_kernel(chips, dp, shard, mask_ref, own_ref, other_ref, *refs):
     d, z, core = place()
-    parts, out_ref = refs[: chips - 1], refs[chips - 1]
-    mask_ref, columns_ref, own_ref, sems = refs[chips:]
-    copies = [
-        pltpu.make_async_copy(mask_hbm, mask_ref, sems.at[0]),
-        pltpu.make_async_copy(columns_hbm, columns_ref, sems.at[1]),
-        pltpu.make_async_copy(hidden_hbm, own_ref, sems.at[2]),
-    ]
-    for copy in copies:
-        copy.start()
+    parts, out_ref = refs[:-1], refs[-1]
     rows = dp * shard
     total = chips * rows
-    cols = other_ref.shape[1]
+    cols = own_ref.shape[1]
     half = chips // 2
+    mask = mask_ref[...].astype(jnp.float32).astype(jnp.bfloat16)
+    columns = jnp.concatenate([part[...] for part in parts], axis=0) * mask
     r = iota((total, total), 0)
     near = jnp.where(r >= total // 2, 1, 0)
     r = r - near * (total // 2)
@@ -107,14 +117,9 @@
     j = over(r - t * (half * shard), shard)
     i = r - t * (half * shard) - j * shard
     order = one_hot(iota((total, total), 1) == (j + (1 - near) * half) * rows + (t ^ d) * shard + i)
-    for copy in copies[:2]:
-        copy.wait()
-    mask = mask_ref[...].astype(jnp.float32).astype(jnp.bfloat16)
-    columns = jnp.concatenate([part[...] for part in (columns_ref, *parts)], axis=0) * mask
     columns = exact(order, columns).astype(jnp.bfloat16)
-    out_ref[:, pl.ds(pl.multiple_of((1 - core) * cols, LANES), cols)] = exact(columns, other_ref[...])
-    copies[2].wait()
-    out_ref[:, pl.ds(pl.multiple_of(core * cols, LANES), cols)] = exact(columns, own_ref[...])
+    for at, ref in ((core, own_ref), (1 - core, other_ref)):
+        out_ref[:, pl.ds(pl.multiple_of(at * cols, LANES), cols)] = exact(columns, ref[...])
 
 
 def embed_kernel(chips, dp, shard, head_ref, *refs):
@@ -122,14 +127,19 @@
     half = chips // 2
     total, cols = head_ref.shape
     size = half * shard
-    count = sum(ref.shape[0] for ref in slot_refs)
-    ids = jnp.concatenate([ref[:, cols:] for ref in slot_refs], axis=0)
-    ids = ids.astype(jnp.float32)[:, :1].astype(jnp.int32)
-    values = jnp.concatenate([ref[:, :cols] for ref in slot_refs], axis=0)
+    group = (slot_refs[0].shape[0] - ID_ROWS) // (cols // LANES)
+    count = len(slot_refs) * group
+    ids, values = [], []
+    for ref in slot_refs:
+        row = ref[cols // LANES * group :, :].astype(jnp.float32)[:1]
+        ids.append(diagonal(jnp.broadcast_to(row, (group, LANES)), 1))
+        blocks = [ref[c * group : (c + 1) * group, :] for c in range(cols // LANES)]
+        values.append(jnp.concatenate(blocks, axis=1))
+    ids = jnp.concatenate(ids, axis=0).astype(jnp.int32)
+    values = jnp.concatenate(values, axis=0)
     block = over(jnp.maximum(ids, 0), shard)
-    group = slot_refs[0].shape[0] // CORES
-    place_in = iota((count, 1), 0) % group
-    near = jnp.where(place_in >= group // 2, 1, 0)
+    place_in = iota((count, 1), 0) % (group // CORES)
+    near = jnp.where(place_in >= group // (2 * CORES), 1, 0)
     target = near * (total // 2) + (block * half + place_in % half) * shard + ids - block * shard
     target = jnp.where(ids < 0, -1, target)
     picked = one_hot(iota((count, total), 1) == target)
@@ -269,11 +279,15 @@
     )
     slots_other = send(slots_other, 0, 1)
     slots_other, hidden_other = lax.optimization_barrier((slots_other, hidden_other))
-    messages = run(
+    slots = cap * chips * CORES
+    *messages, held = run(
         functools.partial(merge_kernel, chips),
-        [shaped((cap * chips * CORES, cols + LANES), bf16)] * chips,
+        [shaped((slots * cols // LANES + ID_ROWS, LANES), bf16)] * chips + [shaped(hidden.shape, bf16)],
+        hidden,
         slots_own,
         slots_other,
+        hbm=1,
+        scratch=[pltpu.SemaphoreType.DMA((1,))],
     )
     columns = [logit_grad.T]
     for s in range(1, chips):
@@ -283,16 +297,14 @@
             columns.append(send(late, 1))
         else:
             columns.append(send(columns[0], s))
-    head_in = (predict_mask[None, :], columns[0], hidden)
     head = run(
         functools.partial(head_kernel, *sizes),
         shaped((chips * rows, cols), f32),
-        *head_in,
+        predict_mask[None, :],
+        held,
         hidden_other,
-        *columns[1:],
+        *columns,
         cost=0,
-        hbm=3,
-        scratch=local_copies(*head_in),
     )
     state = (master, first_moment, second_moment)
     parts = run(
@@ -425,7 +437,8 @@
 def local(hidden, logit_grad, predict_mask, slot_grads, *rest):
     vocab = lax.axis_size("vocab")
     fits = hidden.shape[1] % LANES == 0 and logit_grad.shape[1] % 16 == 0
-    fits = fits and (vocab // CORES * slot_grads.shape[2]) % 8 == 0
+    slots = vocab * slot_grads.shape[2]
+    fits = fits and slots % 16 == 0 and slots <= LANES
     step = aligned if fits else plain
     return step(hidden, logit_grad, predict_mask, slot_grads, *rest)
 

time: 56.9 us -> 54.3 us (0.954)
  waiting for transfers between devices: 22 us -> 19.1 us
    ppermute x11, waiting for transfers between devices: 16.9 us -> 14.2 us  [send(): lax.ppermute(x, 'vocab', [(v, v ^ move) for v in range(vocab)])]
  transfers between devices with their start and end apart: 20 -> 20, of which waited for: 9 -> 11; matrix products, arithmetic and copies ran while one was open for 0% -> 0% of each run, Pallas kernels for 9% -> 9%
where the time goes in v8:
time: 54.3 us; the launch traced here: 54.2 us
  starting transfers between devices  27.3 us (50%)
  waiting for transfers between devices  19.1 us (35%)
  Pallas kernels  7.01 us (13%)
  between operations  0.76 us (1%)
    ppermute x11, starting transfers between devices, send(): lax.ppermute(x, 'vocab', [(v, v ^ move) for v in range(vocab)])  15.1 us
    ppermute x11, waiting for transfers between devices, send(): lax.ppermute(x, 'vocab', [(v, v ^ move) for v in range(vocab)])  14.2 us
    ppermute x9, starting transfers between devices, send_dp(): return lax.ppermute(x, 'dp', [(i, i ^ t) for i in range(dp)]) if t else x  12.2 us
    pallas_call x9, Pallas kernels, run(): pl.pallas_call(kernel, out_shape=outs, in_specs=[pl.BlockSpec(memory_spac...  7.01 us
    ppermute x9, waiting for transfers between devices, send_dp(): return lax.ppermute(x, 'dp', [(i, i ^ t) for i in range(dp)]) if t else x  4.87 us
  transfers between devices with their start and end apart: 20, of which 11 were waited for; matrix products, arithmetic and copies ran while one was open for 0% of the time, Pallas kernels for 9%

profile of v8, /device:TPU:0, one launch (start us, length us, event | category | flops | bytes accessed | tf_op | source)
XLA Modules:
  0.0 54.2 jit_solution(11067797350170113606)
XLA Ops:
  0.6 0.0 copy-start.3
  0.7 0.5 collective-permute-start.1
  1.2 1.4 %shard_map.120 = (bf16[24,5632]{1,0:T(8,128)(2,1)S(1)}, bf16[24,5632]{1,0:T(8,128)(2,1)S(1)}) custom-call(bf16[48,5120]{1,0:T(8,128)(2,1)} %bitcast.12, s32[6,1,8]{2,1,0:T(1,128)} %bitcast.13, s32[1,8]{1,0:T(1,128)} %counts_hbm.1), custom_call_target="tpu_custom_call" | custom-call | bytes 1032416 | tf_op jit(solution)/shard_map/pallas_call | solution.py:222
  2.6 0.1 collective-permute-start
  2.7 4.0 %collective-permute-start.3 = (bf16[48,1024]{1,0:T(8,128)(2,1)}, bf16[48,1024]{1,0:T(8,128)(2,1)S(1)}, u32[]{:S(2)}, u32[]{:S(2)}) collective-permute-start(bf16[48,1024]{1,0:T(8,128)(2,1)} %bitcast.8), channel_id=1, source_target_pairs={{0,4},{1,5},{2,6},{3,7},{4,0},{5,1},{6,2},{7,3},{8,12},{9,13},{10,... | collective-permute-start | bytes 294920 | tf_op jit(solution)/shard_map/ppermute | solution.py:262
  6.7 0.0 collective-permute-done.other_ref
  6.7 0.0 collective-permute-done.1.other_ref
  6.7 1.3 %shard_map.121 = (bf16[496,128]{1,0:T(8,128)(2,1)S(1)}, bf16[496,128]{1,0:T(8,128)(2,1)S(1)}, bf16[496,128]{1,0:T(8,128)(2,1)S(1)}, bf16[496,128]{1,0:T(8,128)(2,1)S(1)}, bf16[1024,640]{1,0:T(8,128)(2,1)S(1)}) custom-call(bf16[1024,640]{1,0:T(8,128)(2,1)} %hidden_hbm.1, bf16[24,5632]{1,0:T(8,128)(2,1)S(1)} %get-tuple-element.30.own_ref, ...), custom_call_target="tpu_custom_call" | custom-call | bytes 3670016 | tf_op jit(solution)/shard_map/pallas_call | solution.py:222
  8.1 2.5 %collective-permute-start.5 = (bf16[496,128]{1,0:T(8,128)(2,1)S(1)}, bf16[496,128]{1,0:T(8,128)(2,1)S(1)}, u32[]{:S(2)}, u32[]{:S(2)}) collective-permute-start(bf16[496,128]{1,0:T(8,128)(2,1)S(1)} %get-tuple-element.37), channel_id=1, source_target_pairs={{0,6},{1,7},{2,4},{3,5},{4,2},{5,3},{6,0},{7,1},{8,14},{9,15},{10,... | collective-permute-start | bytes 380936 | tf_op jit(solution)/shard_map/ppermute | solution.py:262
  10.6 0.6 %collective-permute-start.6 = (bf16[496,128]{1,0:T(8,128)(2,1)S(1)}, bf16[496,128]{1,0:T(8,128)(2,1)S(1)}, u32[]{:S(2)}, u32[]{:S(2)}) collective-permute-start(bf16[496,128]{1,0:T(8,128)(2,1)S(1)} %get-tuple-element.38), channel_id=1, source_target_pairs={{0,4},{1,5},{2,6},{3,7},{4,0},{5,1},{6,2},{7,3},{8,12},{9,13},{10,... | collective-permute-start | bytes 380936 | tf_op jit(solution)/shard_map/ppermute | solution.py:262
  11.2 1.3 %collective-permute-start.7 = (bf16[496,128]{1,0:T(8,128)(2,1)S(1)}, bf16[496,128]{1,0:T(8,128)(2,1)S(1)}, u32[]{:S(2)}, u32[]{:S(2)}) collective-permute-start(bf16[496,128]{1,0:T(8,128)(2,1)S(1)} %get-tuple-element.39), channel_id=1, source_target_pairs={{0,2},{1,3},{2,0},{3,1},{4,6},{5,7},{6,4},{7,5},{8,10},{9,11},{10,... | collective-permute-start | bytes 380936 | tf_op jit(solution)/shard_map/ppermute | solution.py:262
  12.5 0.7 %collective-permute-start.2 = (bf16[48,1024]{1,0:T(8,128)(2,1)S(1)}, bf16[48,1024]{1,0:T(8,128)(2,1)S(1)}, u32[]{:S(2)}, u32[]{:S(2)}) collective-permute-start(bf16[48,1024]{1,0:T(8,128)(2,1)S(1)} %bitcast.9), channel_id=1, source_target_pairs={{0,2},{1,3},{2,0},{3,1},{4,6},{5,7},{6,4},{7,5},{8,10},{9,11},{10,... | collective-permute-start | bytes 294920 | tf_op jit(solution)/shard_map/ppermute | solution.py:262
  13.2 3.8 %collective-permute-done.3.refs_2_ = bf16[48,1024]{1,0:T(8,128)(2,1)S(1)} collective-permute-done((bf16[48,1024]{1,0:T(8,128)(2,1)}, bf16[48,1024]{1,0:T(8,128)(2,1)S(1)}, u32[]{:S(2)}, u32[]{:S(2)}) %collective-permute-start.3) | collective-permute-done | bytes 98336 | tf_op jit(solution)/shard_map/ppermute | solution.py:262
  17.0 0.8 %collective-permute-start.4 = (bf16[48,1024]{1,0:T(8,128)(2,1)S(1)}, bf16[48,1024]{1,0:T(8,128)(2,1)S(1)}, u32[]{:S(2)}, u32[]{:S(2)}) collective-permute-start(bf16[48,1024]{1,0:T(8,128)(2,1)S(1)} %collective-permute-done.3.refs_2_), channel_id=1, source_target_pairs={{0,2},{1,3},{2,0},{3,1},{4,6},{5,7},{6,4},{7,5},{8,10},{9,11},{10,... | collective-permute-start | bytes 294920 | tf_op jit(solution)/shard_map/ppermute | solution.py:262
  17.9 5.3 %collective-permute-done.2.refs_1_ = bf16[48,1024]{1,0:T(8,128)(2,1)S(1)} collective-permute-done((bf16[48,1024]{1,0:T(8,128)(2,1)S(1)}, bf16[48,1024]{1,0:T(8,128)(2,1)S(1)}, u32[]{:S(2)}, u32[]{:S(2)}) %collective-permute-start.2) | collective-permute-done | bytes 98336 | tf_op jit(solution)/shard_map/ppermute | solution.py:262
  23.2 1.7 %collective-permute-done.4.refs_3_ = bf16[48,1024]{1,0:T(8,128)(2,1)S(1)} collective-permute-done((bf16[48,1024]{1,0:T(8,128)(2,1)S(1)}, bf16[48,1024]{1,0:T(8,128)(2,1)S(1)}, u32[]{:S(2)}, u32[]{:S(2)}) %collective-permute-start.4) | collective-permute-done | bytes 98336 | tf_op jit(solution)/shard_map/ppermute | solution.py:262
  24.9 1.0 %shard_map.122.head_ref = f32[192,1280]{1,0:T(8,128)S(1)} custom-call(s32[1,1024]{1,0:T(1,128)S(1)} %bitcast.11, bf16[1024,640]{1,0:T(8,128)(2,1)S(1)} %get-tuple-element.33.own_ref, bf16[1024,640]{1,0:T(8,128)(2,1)S(1)} %collective-permute-done.1.other_ref, bf16[48,1024]{1,0:T(8,128)(2,1)S(1)} %bitcast.10, ...), custom_call_target="tpu_custom_call" | custom-call | tf_op jit(solution)/shard_map/pallas_call | solution.py:222
  25.9 0.0 copy-start
  25.9 0.0 copy-start.1
  25.9 0.0 copy-start.2
  25.9 0.0 collective-permute-done.6.refs_1_
  25.9 0.0 collective-permute-done.7.refs_2_
  25.9 0.6 %shard_map.123 = (f32[24,1280]{1,0:T(8,128)S(1)}, f32[24,1280]{1,0:T(8,128)S(1)}, f32[24,1280]{1,0:T(8,128)S(1)}, f32[24,1280]{1,0:T(8,128)S(1)}, f32[24,1280]{1...) custom-call(f32[192,1280]{1,0:T(8,128)S(1)} %shard_map.122.head_ref, ...), custom_call_target="tpu_custom_call" | custom-call | bytes 2473984 | tf_op jit(solution)/shard_map/pallas_call | solution.py:222
  26.5 1.6 %collective-permute-start.8 = (f32[24,1280]{1,0:T(8,128)S(1)}, f32[24,1280]{1,0:T(8,128)S(1)}, u32[]{:S(2)}, u32[]{:S(2)}) collective-permute-start(f32[24,1280]{1,0:T(8,128)S(1)} %get-tuple-element.42), channel_id=1, source_target_pairs={{0,8},{8,0},{16,24},{24,16},{1,9},{9,1},{17,25},{25,17},{2,10},{10... | collective-permute-start | bytes 368648 | tf_op jit(solution)/shard_map/ppermute | solution.py:265
  28.1 1.5 %collective-permute-start.9 = (f32[24,1280]{1,0:T(8,128)S(1)}, f32[24,1280]{1,0:T(8,128)S(1)}, u32[]{:S(2)}, u32[]{:S(2)}) collective-permute-start(f32[24,1280]{1,0:T(8,128)S(1)} %get-tuple-element.43), channel_id=1, source_target_pairs={{0,16},{8,24},{16,0},{24,8},{1,17},{9,25},{17,1},{25,9},{2,18},{10... | collective-permute-start | bytes 368648 | tf_op jit(solution)/shard_map/ppermute | solution.py:265
  29.6 0.4 collective-permute-start.10
  30.0 1.5 %collective-permute-start.11 = (f32[24,1280]{1,0:T(8,128)S(1)}, f32[24,1280]{1,0:T(8,128)S(1)}, u32[]{:S(2)}, u32[]{:S(2)}) collective-permute-start(f32[24,1280]{1,0:T(8,128)S(1)} %get-tuple-element.47), channel_id=1, source_target_pairs={{0,8},{8,0},{16,24},{24,16},{1,9},{9,1},{17,25},{25,17},{2,10},{10... | collective-permute-start | bytes 368648 | tf_op jit(solution)/shard_map/ppermute | solution.py:265
  31.6 1.5 %collective-permute-start.12 = (f32[24,1280]{1,0:T(8,128)S(1)}, f32[24,1280]{1,0:T(8,128)S(1)}, u32[]{:S(2)}, u32[]{:S(2)}) collective-permute-start(f32[24,1280]{1,0:T(8,128)S(1)} %get-tuple-element.48), channel_id=1, source_target_pairs={{0,16},{8,24},{16,0},{24,8},{1,17},{9,25},{17,1},{25,9},{2,18},{10... | collective-permute-start | bytes 368648 | tf_op jit(solution)/shard_map/ppermute | solution.py:265
  33.1 2.0 %collective-permute-start.13 = (f32[24,1280]{1,0:T(8,128)S(1)}, f32[24,1280]{1,0:T(8,128)S(1)}, u32[]{:S(2)}, u32[]{:S(2)}) collective-permute-start(f32[24,1280]{1,0:T(8,128)S(1)} %get-tuple-element.49), channel_id=1, source_target_pairs={{0,24},{8,16},{16,8},{24,0},{1,25},{9,17},{17,9},{25,1},{2,26},{10... | collective-permute-start | bytes 368648 | tf_op jit(solution)/shard_map/ppermute | solution.py:265
  35.1 1.6 %collective-permute-done.9.refs_2_ = f32[24,1280]{1,0:T(8,128)S(1)} collective-permute-done((f32[24,1280]{1,0:T(8,128)S(1)}, f32[24,1280]{1,0:T(8,128)S(1)}, u32[]{:S(2)}, u32[]{:S(2)}) %collective-permute-start.9) | collective-permute-done | bytes 122912 | tf_op jit(solution)/shard_map/ppermute | solution.py:265
  36.7 0.1 collective-permute-done.10.refs_3_
  36.8 1.5 %collective-permute-start.15 = (f32[24,640]{1,0:T(8,128)S(1)}, f32[24,640]{1,0:T(8,128)S(1)}, u32[]{:S(2)}, u32[]{:S(2)}) collective-permute-start(f32[24,640]{1,0:T(8,128)S(1)} %get-tuple-element.45), channel_id=1, source_target_pairs={{0,4},{1,5},{2,6},{3,7},{4,0},{5,1},{6,2},{7,3},{8,12},{9,13},{10,... | collective-permute-start | bytes 184328 | tf_op jit(solution)/shard_map/ppermute | solution.py:262
  38.4 2.0 %collective-permute-start.16 = (f32[24,640]{1,0:T(8,128)S(1)}, f32[24,640]{1,0:T(8,128)S(1)}, u32[]{:S(2)}, u32[]{:S(2)}) collective-permute-start(f32[24,640]{1,0:T(8,128)S(1)} %get-tuple-element.52), channel_id=1, source_target_pairs={{0,6},{1,7},{2,4},{3,5},{4,2},{5,3},{6,0},{7,1},{8,14},{9,15},{10,... | collective-permute-start | bytes 184328 | tf_op jit(solution)/shard_map/ppermute | solution.py:262
  40.4 0.5 collective-permute-done.12.refs_2_
  40.9 0.0 collective-permute-done.13.refs_3_
  40.9 0.9 %collective-permute-start.14 = (f32[24,640]{1,0:T(8,128)S(1)}, f32[24,640]{1,0:T(8,128)S(1)}, u32[]{:S(2)}, u32[]{:S(2)}) collective-permute-start(f32[24,640]{1,0:T(8,128)S(1)} %get-tuple-element.51), channel_id=1, source_target_pairs={{0,2},{1,3},{2,0},{3,1},{4,6},{5,7},{6,4},{7,5},{8,10},{9,11},{10,... | collective-permute-start | bytes 184328 | tf_op jit(solution)/shard_map/ppermute | solution.py:262
  41.8 2.7 %collective-permute-done.16.refs_6_ = f32[24,640]{1,0:T(8,128)S(1)} collective-permute-done((f32[24,640]{1,0:T(8,128)S(1)}, f32[24,640]{1,0:T(8,128)S(1)}, u32[]{:S(2)}, u32[]{:S(2)}) %collective-permute-start.16) | collective-permute-done | bytes 61472 | tf_op jit(solution)/shard_map/ppermute | solution.py:262
  44.5 0.0 collective-permute-done.15.refs_5_
  44.5 0.7 %collective-permute-done.14.refs_4_ = f32[24,640]{1,0:T(8,128)S(1)} collective-permute-done((f32[24,640]{1,0:T(8,128)S(1)}, f32[24,640]{1,0:T(8,128)S(1)}, u32[]{:S(2)}, u32[]{:S(2)}) %collective-permute-start.14) | collective-permute-done | bytes 61472 | tf_op jit(solution)/shard_map/ppermute | solution.py:262
  45.2 0.3 shard_map.127.refs_0_
  45.5 1.3 %collective-permute-start.19 = (bf16[48,1280]{1,0:T(8,128)(2,1)S(1)}, bf16[48,1280]{1,0:T(8,128)(2,1)S(1)}, u32[]{:S(2)}, u32[]{:S(2)}) collective-permute-start(bf16[48,1280]{1,0:T(8,128)(2,1)S(1)} %shard_map.127.refs_0_), channel_id=1, source_target_pairs={{0,24},{8,16},{16,8},{24,0},{1,25},{9,17},{17,9},{25,1},{2,26},{10... | collective-permute-start | bytes 368648 | tf_op jit(solution)/shard_map/ppermute | solution.py:265
  46.8 1.3 %collective-permute-start.18 = (bf16[48,1280]{1,0:T(8,128)(2,1)S(1)}, bf16[48,1280]{1,0:T(8,128)(2,1)S(1)}, u32[]{:S(2)}, u32[]{:S(2)}) collective-permute-start(bf16[48,1280]{1,0:T(8,128)(2,1)S(1)} %shard_map.127.refs_0_), channel_id=1, source_target_pairs={{0,16},{8,24},{16,0},{24,8},{1,17},{9,25},{17,1},{25,9},{2,18},{10... | collective-permute-start | bytes 368648 | tf_op jit(solution)/shard_map/ppermute | solution.py:265
  48.1 1.0 %collective-permute-start.17 = (bf16[48,1280]{1,0:T(8,128)(2,1)S(1)}, bf16[48,1280]{1,0:T(8,128)(2,1)S(1)}, u32[]{:S(2)}, u32[]{:S(2)}) collective-permute-start(bf16[48,1280]{1,0:T(8,128)(2,1)S(1)} %shard_map.127.refs_0_), channel_id=1, source_target_pairs={{0,8},{8,0},{16,24},{24,16},{1,9},{9,1},{17,25},{25,17},{2,10},{10... | collective-permute-start | bytes 368648 | tf_op jit(solution)/shard_map/ppermute | solution.py:265
  49.1 1.3 %shard_map.126 = (f32[12,5120]{1,0:T(8,128)}, f32[12,5120]{1,0:T(8,128)}, f32[12,5120]{1,0:T(8,128)}) custom-call(f32[12,5120]{1,0:T(8,128)S(1)} %copy-done, f32[12,5120]{1,0:T(8,128)S(1)} %copy-done.1, f32[12,5120]{1,0:T(8,128)S(1)} %copy-done.2, f32[24,640]{1,0:T(8,128)S(1)} %get-tuple-element.50.refs_3_, f32[24,640]{1,0:T(8,128)S(1)} %collective-permute-done.14.refs_4_, ...), custom_call_target="tpu_custom_call" | custom-call | bytes 1720320 | tf_op jit(solution)/shard_map/pallas_call | solution.py:222
  50.4 1.1 %collective-permute-done.19.refs_3_ = bf16[48,1280]{1,0:T(8,128)(2,1)S(1)} collective-permute-done((bf16[48,1280]{1,0:T(8,128)(2,1)S(1)}, bf16[48,1280]{1,0:T(8,128)(2,1)S(1)}, u32[]{:S(2)}, u32[]{:S(2)}) %collective-permute-start.19) | collective-permute-done | bytes 122912 | tf_op jit(solution)/shard_map/ppermute | solution.py:265
  51.5 1.2 %collective-permute-done.18.refs_2_ = bf16[48,1280]{1,0:T(8,128)(2,1)S(1)} collective-permute-done((bf16[48,1280]{1,0:T(8,128)(2,1)S(1)}, bf16[48,1280]{1,0:T(8,128)(2,1)S(1)}, u32[]{:S(2)}, u32[]{:S(2)}) %collective-permute-start.18) | collective-permute-done | bytes 122912 | tf_op jit(solution)/shard_map/ppermute | solution.py:265
  52.7 0.4 collective-permute-done.17.refs_1_
  53.1 1.1 %shard_map.128 = bf16[48,5120]{1,0:T(8,128)(2,1)} custom-call(bf16[48,1280]{1,0:T(8,128)(2,1)S(1)} %shard_map.127.refs_0_, bf16[48,1280]{1,0:T(8,128)(2,1)S(1)} %collective-permute-done.17.refs_1_, bf16[48,1280]{1,0:T(8,128)(2,1)S(1)} %collective-permute-done.18.refs_2_, bf16[48,1280]{1,0:T(8,128)(2,1)S(1)} %collective-permute-done.19.refs_3_), custom_call_target="tpu_custom_call" | custom-call | bytes 983040 | tf_op jit(solution)/shard_map/pallas_call | solution.py:222
  (11 shorter events, 0.1 us)
Async XLA Ops:
  0.6 11.9 %copy-start.3 = (bf16[1024,48]{0,1:T(8,128)(2,1)S(1)}, bf16[1024,48]{0,1:T(8,128)(2,1)}, u32[]{:S(2)}) copy-start(bf16[1024,48]{0,1:T(8,128)(2,1)} %param.10) | copy-start | bytes 294916
  0.6 24.2 %copy-start.4 = (s32[1024]{0:T(1024)S(1)}, s32[1024]{0:T(1024)}, u32[]{:S(2)}) copy-start(s32[1024]{0:T(1024)} %param.11) | copy-start | bytes 12292
  0.7 6.1 %collective-permute-start.1 = (bf16[1024,640]{1,0:T(8,128)(2,1)}, bf16[1024,640]{1,0:T(8,128)(2,1)S(1)}, u32[]{:S(2)}, u32[]{:S(2)}) collective-permute-start(bf16[1024,640]{1,0:T(8,128)(2,1)} %hidden_hbm.1), channel_id=1, source_target_pairs={{0,1},{1,0},{2,3},{3,2},{4,5},{5,4},{6,7},{7,6},{8,9},{9,8},{10,11... | collective-permute-start | bytes 3932168 | tf_op jit(solution)/shard_map/ppermute | solution.py:262
  2.6 4.2 %collective-permute-start = (bf16[24,5632]{1,0:T(8,128)(2,1)S(1)}, bf16[24,5632]{1,0:T(8,128)(2,1)S(1)}, u32[]{:S(2)}, u32[]{:S(2)}) collective-permute-start(bf16[24,5632]{1,0:T(8,128)(2,1)S(1)} %get-tuple-element.31), channel_id=1, source_target_pairs={{0,1},{1,0},{2,3},{3,2},{4,5},{5,4},{6,7},{7,6},{8,9},{9,8},{10,11... | collective-permute-start | bytes 811016 | tf_op jit(solution)/shard_map/ppermute | solution.py:262
  2.7 14.4 %collective-permute-start.3 = (bf16[48,1024]{1,0:T(8,128)(2,1)}, bf16[48,1024]{1,0:T(8,128)(2,1)S(1)}, u32[]{:S(2)}, u32[]{:S(2)}) collective-permute-start(bf16[48,1024]{1,0:T(8,128)(2,1)} %bitcast.8), channel_id=1, source_target_pairs={{0,4},{1,5},{2,6},{3,7},{4,0},{5,1},{6,2},{7,3},{8,12},{9,13},{10,... | collective-permute-start | bytes 294920 | tf_op jit(solution)/shard_map/ppermute | solution.py:262
  8.1 17.8 %collective-permute-start.5 = (bf16[496,128]{1,0:T(8,128)(2,1)S(1)}, bf16[496,128]{1,0:T(8,128)(2,1)S(1)}, u32[]{:S(2)}, u32[]{:S(2)}) collective-permute-start(bf16[496,128]{1,0:T(8,128)(2,1)S(1)} %get-tuple-element.37), channel_id=1, source_target_pairs={{0,6},{1,7},{2,4},{3,5},{4,2},{5,3},{6,0},{7,1},{8,14},{9,15},{10,... | collective-permute-start | bytes 380936 | tf_op jit(solution)/shard_map/ppermute | solution.py:262
  10.6 15.3 %collective-permute-start.6 = (bf16[496,128]{1,0:T(8,128)(2,1)S(1)}, bf16[496,128]{1,0:T(8,128)(2,1)S(1)}, u32[]{:S(2)}, u32[]{:S(2)}) collective-permute-start(bf16[496,128]{1,0:T(8,128)(2,1)S(1)} %get-tuple-element.38), channel_id=1, source_target_pairs={{0,4},{1,5},{2,6},{3,7},{4,0},{5,1},{6,2},{7,3},{8,12},{9,13},{10,... | collective-permute-start | bytes 380936 | tf_op jit(solution)/shard_map/ppermute | solution.py:262
  11.2 14.7 %collective-permute-start.7 = (bf16[496,128]{1,0:T(8,128)(2,1)S(1)}, bf16[496,128]{1,0:T(8,128)(2,1)S(1)}, u32[]{:S(2)}, u32[]{:S(2)}) collective-permute-start(bf16[496,128]{1,0:T(8,128)(2,1)S(1)} %get-tuple-element.39), channel_id=1, source_target_pairs={{0,2},{1,3},{2,0},{3,1},{4,6},{5,7},{6,4},{7,5},{8,10},{9,11},{10,... | collective-permute-start | bytes 380936 | tf_op jit(solution)/shard_map/ppermute | solution.py:262
  12.5 10.7 %collective-permute-start.2 = (bf16[48,1024]{1,0:T(8,128)(2,1)S(1)}, bf16[48,1024]{1,0:T(8,128)(2,1)S(1)}, u32[]{:S(2)}, u32[]{:S(2)}) collective-permute-start(bf16[48,1024]{1,0:T(8,128)(2,1)S(1)} %bitcast.9), channel_id=1, source_target_pairs={{0,2},{1,3},{2,0},{3,1},{4,6},{5,7},{6,4},{7,5},{8,10},{9,11},{10,... | collective-permute-start | bytes 294920 | tf_op jit(solution)/shard_map/ppermute | solution.py:262
  17.0 7.8 %collective-permute-start.4 = (bf16[48,1024]{1,0:T(8,128)(2,1)S(1)}, bf16[48,1024]{1,0:T(8,128)(2,1)S(1)}, u32[]{:S(2)}, u32[]{:S(2)}) collective-permute-start(bf16[48,1024]{1,0:T(8,128)(2,1)S(1)} %collective-permute-done.3.refs_2_), channel_id=1, source_target_pairs={{0,2},{1,3},{2,0},{3,1},{4,6},{5,7},{6,4},{7,5},{8,10},{9,11},{10,... | collective-permute-start | bytes 294920 | tf_op jit(solution)/shard_map/ppermute | solution.py:262
  25.9 19.3 %copy-start = (f32[12,5120]{1,0:T(8,128)S(1)}, f32[12,5120]{1,0:T(8,128)}, u32[]{:S(2)}) copy-start(f32[12,5120]{1,0:T(8,128)} %refs_0_.3) | copy-start | bytes 737284
  25.9 19.3 %copy-start.1 = (f32[12,5120]{1,0:T(8,128)S(1)}, f32[12,5120]{1,0:T(8,128)}, u32[]{:S(2)}) copy-start(f32[12,5120]{1,0:T(8,128)} %refs_1_.3) | copy-start | bytes 737284
  25.9 19.3 %copy-start.2 = (f32[12,5120]{1,0:T(8,128)S(1)}, f32[12,5120]{1,0:T(8,128)}, u32[]{:S(2)}) copy-start(f32[12,5120]{1,0:T(8,128)} %refs_2_.3) | copy-start | bytes 737284
  26.5 6.6 %collective-permute-start.8 = (f32[24,1280]{1,0:T(8,128)S(1)}, f32[24,1280]{1,0:T(8,128)S(1)}, u32[]{:S(2)}, u32[]{:S(2)}) collective-permute-start(f32[24,1280]{1,0:T(8,128)S(1)} %get-tuple-element.42), channel_id=1, source_target_pairs={{0,8},{8,0},{16,24},{24,16},{1,9},{9,1},{17,25},{25,17},{2,10},{10... | collective-permute-start | bytes 368648 | tf_op jit(solution)/shard_map/ppermute | solution.py:265
  28.1 8.6 %collective-permute-start.9 = (f32[24,1280]{1,0:T(8,128)S(1)}, f32[24,1280]{1,0:T(8,128)S(1)}, u32[]{:S(2)}, u32[]{:S(2)}) collective-permute-start(f32[24,1280]{1,0:T(8,128)S(1)} %get-tuple-element.43), channel_id=1, source_target_pairs={{0,16},{8,24},{16,0},{24,8},{1,17},{9,25},{17,1},{25,9},{2,18},{10... | collective-permute-start | bytes 368648 | tf_op jit(solution)/shard_map/ppermute | solution.py:265
  29.6 7.2 %collective-permute-start.10 = (f32[24,1280]{1,0:T(8,128)S(1)}, f32[24,1280]{1,0:T(8,128)S(1)}, u32[]{:S(2)}, u32[]{:S(2)}) collective-permute-start(f32[24,1280]{1,0:T(8,128)S(1)} %get-tuple-element.44), channel_id=1, source_target_pairs={{0,24},{8,16},{16,8},{24,0},{1,25},{9,17},{17,9},{25,1},{2,26},{10... | collective-permute-start | bytes 368648 | tf_op jit(solution)/shard_map/ppermute | solution.py:265
  30.0 10.4 %collective-permute-start.11 = (f32[24,1280]{1,0:T(8,128)S(1)}, f32[24,1280]{1,0:T(8,128)S(1)}, u32[]{:S(2)}, u32[]{:S(2)}) collective-permute-start(f32[24,1280]{1,0:T(8,128)S(1)} %get-tuple-element.47), channel_id=1, source_target_pairs={{0,8},{8,0},{16,24},{24,16},{1,9},{9,1},{17,25},{25,17},{2,10},{10... | collective-permute-start | bytes 368648 | tf_op jit(solution)/shard_map/ppermute | solution.py:265
  31.6 9.3 %collective-permute-start.12 = (f32[24,1280]{1,0:T(8,128)S(1)}, f32[24,1280]{1,0:T(8,128)S(1)}, u32[]{:S(2)}, u32[]{:S(2)}) collective-permute-start(f32[24,1280]{1,0:T(8,128)S(1)} %get-tuple-element.48), channel_id=1, source_target_pairs={{0,16},{8,24},{16,0},{24,8},{1,17},{9,25},{17,1},{25,9},{2,18},{10... | collective-permute-start | bytes 368648 | tf_op jit(solution)/shard_map/ppermute | solution.py:265
  33.1 7.8 %collective-permute-start.13 = (f32[24,1280]{1,0:T(8,128)S(1)}, f32[24,1280]{1,0:T(8,128)S(1)}, u32[]{:S(2)}, u32[]{:S(2)}) collective-permute-start(f32[24,1280]{1,0:T(8,128)S(1)} %get-tuple-element.49), channel_id=1, source_target_pairs={{0,24},{8,16},{16,8},{24,0},{1,25},{9,17},{17,9},{25,1},{2,26},{10... | collective-permute-start | bytes 368648 | tf_op jit(solution)/shard_map/ppermute | solution.py:265
  36.8 7.7 %collective-permute-start.15 = (f32[24,640]{1,0:T(8,128)S(1)}, f32[24,640]{1,0:T(8,128)S(1)}, u32[]{:S(2)}, u32[]{:S(2)}) collective-permute-start(f32[24,640]{1,0:T(8,128)S(1)} %get-tuple-element.45), channel_id=1, source_target_pairs={{0,4},{1,5},{2,6},{3,7},{4,0},{5,1},{6,2},{7,3},{8,12},{9,13},{10,... | collective-permute-start | bytes 184328 | tf_op jit(solution)/shard_map/ppermute | solution.py:262
  38.4 6.1 %collective-permute-start.16 = (f32[24,640]{1,0:T(8,128)S(1)}, f32[24,640]{1,0:T(8,128)S(1)}, u32[]{:S(2)}, u32[]{:S(2)}) collective-permute-start(f32[24,640]{1,0:T(8,128)S(1)} %get-tuple-element.52), channel_id=1, source_target_pairs={{0,6},{1,7},{2,4},{3,5},{4,2},{5,3},{6,0},{7,1},{8,14},{9,15},{10,... | collective-permute-start | bytes 184328 | tf_op jit(solution)/shard_map/ppermute | solution.py:262
  40.9 4.3 %collective-permute-start.14 = (f32[24,640]{1,0:T(8,128)S(1)}, f32[24,640]{1,0:T(8,128)S(1)}, u32[]{:S(2)}, u32[]{:S(2)}) collective-permute-start(f32[24,640]{1,0:T(8,128)S(1)} %get-tuple-element.51), channel_id=1, source_target_pairs={{0,2},{1,3},{2,0},{3,1},{4,6},{5,7},{6,4},{7,5},{8,10},{9,11},{10,... | collective-permute-start | bytes 184328 | tf_op jit(solution)/shard_map/ppermute | solution.py:262
  45.5 5.9 %collective-permute-start.19 = (bf16[48,1280]{1,0:T(8,128)(2,1)S(1)}, bf16[48,1280]{1,0:T(8,128)(2,1)S(1)}, u32[]{:S(2)}, u32[]{:S(2)}) collective-permute-start(bf16[48,1280]{1,0:T(8,128)(2,1)S(1)} %shard_map.127.refs_0_), channel_id=1, source_target_pairs={{0,24},{8,16},{16,8},{24,0},{1,25},{9,17},{17,9},{25,1},{2,26},{10... | collective-permute-start | bytes 368648 | tf_op jit(solution)/shard_map/ppermute | solution.py:265
  46.8 5.9 %collective-permute-start.18 = (bf16[48,1280]{1,0:T(8,128)(2,1)S(1)}, bf16[48,1280]{1,0:T(8,128)(2,1)S(1)}, u32[]{:S(2)}, u32[]{:S(2)}) collective-permute-start(bf16[48,1280]{1,0:T(8,128)(2,1)S(1)} %shard_map.127.refs_0_), channel_id=1, source_target_pairs={{0,16},{8,24},{16,0},{24,8},{1,17},{9,25},{17,1},{25,9},{2,18},{10... | collective-permute-start | bytes 368648 | tf_op jit(solution)/shard_map/ppermute | solution.py:265
  48.1 5.0 %collective-permute-start.17 = (bf16[48,1280]{1,0:T(8,128)(2,1)S(1)}, bf16[48,1280]{1,0:T(8,128)(2,1)S(1)}, u32[]{:S(2)}, u32[]{:S(2)}) collective-permute-start(bf16[48,1280]{1,0:T(8,128)(2,1)S(1)} %shard_map.127.refs_0_), channel_id=1, source_target_pairs={{0,8},{8,0},{16,24},{24,16},{1,9},{9,1},{17,25},{25,17},{2,10},{10... | collective-permute-start | bytes 368648 | tf_op jit(solution)/shard_map/ppermute | solution.py:265

commit v9 on v7

--- a/solution.py
+++ b/solution.py
@@ -10,6 +10,7 @@
 STEP = 8
 CORES = 2
 LANES = 128
+ID_ROWS = 16
 VMEM_LIMIT = 24 * 1024 * 1024
 
 
@@ -34,7 +35,7 @@
     return jnp.dot(left, right, preferred_element_type=jnp.float32)
 
 
-def slots_kernel(chips, slots_hbm, rows_hbm, counts_hbm, own_out, other_out, slots_ref, rows_ref, counts_ref, sems):
+def slots_kernel(chips, dp, slots_hbm, rows_hbm, counts_hbm, own_out, other_out, slots_ref, rows_ref, counts_ref, sems):
     d, z, core = place()
     copies = [
         pltpu.make_async_copy(rows_hbm, rows_ref, sems.at[0]),
@@ -46,7 +47,7 @@
     cap, owners = rows_ref.shape[0], rows_ref.shape[2]
     count = cap * owners
     group = cap * chips
-    part = slots_ref.shape[1] // 2
+    part = slots_ref.shape[1] // dp
     q = iota((count, count), 0)
     away = jnp.where(q >= group, 1, 0)
     q = q - away * group
@@ -65,62 +66,75 @@
     ids = exact(pick, ids)
     copies[2].wait()
     outs = ((own_out, slice(0, group)), (other_out, slice(group, count)))
-    for away in range(2):
-        start = pl.multiple_of(((d & 1) ^ away) * part, LANES)
-        values = exact(pick, slots_ref[:, pl.ds(start, part)])
+    for t in range(dp):
+        values = exact(pick, slots_ref[:, pl.ds(pl.multiple_of((d ^ t) * part, LANES), part)])
         for out_ref, spot in outs:
-            out_ref[:, away * part : (away + 1) * part] = values[spot].astype(jnp.bfloat16)
+            out_ref[:, t * part : (t + 1) * part] = values[spot].astype(jnp.bfloat16)
     for out_ref, spot in outs:
-        out_ref[:, 2 * part :] = ids[spot].astype(jnp.bfloat16)
-
-
-def pair_kernel(own_ref, other_ref, out_ref):
-    part = out_ref.shape[1] - LANES
-    both = [ref[:, part:].astype(jnp.float32) for ref in (own_ref, other_ref)]
-    out_ref[...] = jnp.concatenate(both, axis=0).astype(jnp.bfloat16)
-
-
-def owners_kernel(cap, own_ref, other_ref, pair_ref, *out_refs):
-    part = pair_ref.shape[1] - LANES
-    group = own_ref.shape[0]
-    pair = pair_ref[...].astype(jnp.float32)
-    held = [pair[:group], pair[group:]]
-    for ref in (own_ref, other_ref):
-        values = [ref[:, :part].astype(jnp.float32), ref[:, 2 * part :].astype(jnp.float32)]
-        held.append(jnp.concatenate(values, axis=1))
+        out_ref[:, dp * part :] = ids[spot].astype(jnp.bfloat16)
+
+
+def diagonal(values, axis):
+    return jnp.sum(jnp.where(iota(values.shape, 0) == iota(values.shape, 1), values, 0.0), axis=axis, keepdims=True)
+
+
+def packed(values, ids):
+    ids = jnp.broadcast_to(ids, (ids.shape[0], LANES))
+    ids = jnp.broadcast_to(diagonal(ids, 0), (ID_ROWS, LANES))
+    blocks = [values[:, c : c + LANES] for c in range(0, values.shape[1], LANES)]
+    return jnp.concatenate([*blocks, ids], axis=0).astype(jnp.bfloat16)
+
+
+def unpacked(ref, cols):
+    group = (ref.shape[0] - ID_ROWS) // (cols // LANES)
+    row = ref[cols // LANES * group :, :].astype(jnp.float32)[:1]
+    ids = diagonal(jnp.broadcast_to(row, (group, LANES)), 1)
+    values = [ref[c * group : (c + 1) * group, :] for c in range(cols // LANES)]
+    return jnp.concatenate(values, axis=1).astype(jnp.float32), ids
+
+
+def peers_kernel(dp, own_ref, other_ref, *out_refs):
+    part = (own_ref.shape[1] - LANES) // dp
+    ids = [ref[:, dp * part :].astype(jnp.float32) for ref in (own_ref, other_ref)]
+    ids = jnp.concatenate(ids, axis=0)[:, :1]
+    for t, out_ref in enumerate(out_refs):
+        values = [ref[:, t * part : (t + 1) * part].astype(jnp.float32) for ref in (own_ref, other_ref)]
+        out_ref[...] = packed(jnp.concatenate(values, axis=0), ids)
+
+
+def owners_kernel(chips, cap, cols, *refs):
+    in_refs, out_refs = refs[:-chips], refs[-chips:]
+    held = [unpacked(ref, cols) for ref in in_refs]
+    group = cap * chips
     for s, out_ref in enumerate(out_refs):
-        rows = [block[s * cap : (s + 1) * cap] for block in held]
-        out_ref[...] = jnp.concatenate(rows, axis=0).astype(jnp.bfloat16)
-
-
-def head_kernel(chips, dp, shard, mask_hbm, columns_hbm, hidden_hbm, other_ref, *refs):
-    d, z, core = place()
-    parts, outs = refs[: chips - 1], refs[chips - 1 : chips - 1 + dp]
-    mask_ref, columns_ref, own_ref, sems = refs[chips - 1 + dp :]
-    copies = [
-        pltpu.make_async_copy(mask_hbm, mask_ref, sems.at[0]),
-        pltpu.make_async_copy(columns_hbm, columns_ref, sems.at[1]),
-        pltpu.make_async_copy(hidden_hbm, own_ref, sems.at[2]),
-    ]
-    for copy in copies:
-        copy.start()
+        spots = [slice(core * group + s * cap, core * group + (s + 1) * cap) for core in range(CORES)]
+        rows = [[block[spot] for block in both for spot in spots] for both in zip(*held)]
+        values, ids = [jnp.concatenate(blocks, axis=0) for blocks in rows]
+        out_ref[...] = packed(values, ids)
+
+
+def fetch_kernel(hidden_hbm, hidden_ref, sem):
+    copy = pltpu.make_async_copy(hidden_hbm, hidden_ref, sem)
+    copy.start()
+    copy.wait()
+
+
+def head_kernel(chips, dp, shard, mask_ref, own_ref, other_ref, *refs):
+    d, z, core = place()
+    parts, outs = refs[:chips], refs[chips:]
     rows = dp * shard
     total = chips * rows
-    cols = other_ref.shape[1]
+    cols = own_ref.shape[1]
     size = chips * shard
     r = iota((total, total), 0)
     t = over(r, size)
     s = over(r - t * size, shard)
     i = r - t * size - s * shard
     order = one_hot(iota((total, total), 1) == s * rows + (t ^ d) * shard + i)
-    for copy in copies[:2]:
-        copy.wait()
     mask = mask_ref[...].astype(jnp.float32).astype(jnp.bfloat16)
-    columns = jnp.concatenate([part[...] for part in (columns_ref, *parts)], axis=0) * mask
+    columns = jnp.concatenate([part[...] for part in parts], axis=0) * mask
     columns = exact(order, columns).astype(jnp.bfloat16)
-    for at, ref in ((1 - core, other_ref), (core, own_ref)):
-        if ref is own_ref:
-            copies[2].wait()
+    for at, ref in ((core, own_ref), (1 - core, other_ref)):
         head = exact(columns, ref[...])
         spot = pl.ds(pl.multiple_of(at * cols, LANES), cols)
         for t, out_ref in enumerate(outs):
@@ -137,14 +151,13 @@
     return jnp.concatenate([rows[:cut], rows[cut:]], axis=1)
 
 
-def embed_kernel(dp, shard, *refs):
+def embed_kernel(dp, shard, cols, *refs):
     d, z, core = place()
     slot_refs, out_refs = refs[:-dp], refs[-dp:]
-    part = slot_refs[0].shape[1] - LANES
-    count = sum(ref.shape[0] for ref in slot_refs)
-    both = jnp.concatenate([ref[...].astype(jnp.float32) for ref in slot_refs], axis=0)
-    ids = both[:, part : part + 1].astype(jnp.int32)
-    values = both[:, :part].astype(jnp.bfloat16)
+    held = [unpacked(ref, cols) for ref in slot_refs]
+    values, ids = [jnp.concatenate(blocks, axis=0) for blocks in zip(*held)]
+    values, ids = values.astype(jnp.bfloat16), ids.astype(jnp.int32)
+    count = values.shape[0]
     block = over(jnp.maximum(ids, 0), shard)
     target = jnp.where(ids < 0, -1, (block ^ d) * shard + ids - block * shard)
     picked = one_hot(iota((count, dp * shard), 1) == target)
@@ -156,12 +169,9 @@
 def gather_kernel(*refs):
     d, z, core = place()
     parts, out_ref = refs[:-1], refs[-1]
-    part = out_ref.shape[1] // 2
-    for side in range(2):
-        total = parts[side][...]
-        for t in range(side + 2, len(parts), 2):
-            total = total + parts[t][...]
-        out_ref[:, pl.ds(pl.multiple_of(((d & 1) ^ side) * part, LANES), part)] = unstacked(total)
+    cols = out_ref.shape[1] // len(parts)
+    for t, part in enumerate(parts):
+        out_ref[:, pl.ds(pl.multiple_of((d ^ t) * cols, LANES), cols)] = unstacked(part[...])
 
 
 def sum_kernel(chips, shard, *refs):
@@ -281,37 +291,37 @@
         slot_counts,
     )
     slots_own, slots_other = run(
-        functools.partial(slots_kernel, chips),
+        functools.partial(slots_kernel, chips, dp),
         [shaped((group, width + LANES), bf16)] * CORES,
         *slots_in,
         hbm=3,
         scratch=local_copies(*slots_in),
     )
     slots_other = send(slots_other, 0, 1)
-    slots_pair = send_dp(run(pair_kernel, shaped((CORES * group, width // 2 + LANES), bf16), slots_own, slots_other), 1)
+    slots_other, hidden_other = lax.optimization_barrier((slots_other, hidden_other))
+    quarter = width // dp
+    packets = [shaped((vocab * cap * quarter // LANES + ID_ROWS, LANES), bf16)]
+    quarters = run(functools.partial(peers_kernel, dp), packets * dp, slots_own, slots_other)
     messages = run(
-        functools.partial(owners_kernel, cap),
-        [shaped((2 * CORES * cap, width // 2 + LANES), bf16)] * chips,
-        slots_own,
-        slots_other,
-        slots_pair,
+        functools.partial(owners_kernel, chips, cap, quarter),
+        packets * chips,
+        *[send_dp(quarters[t], t) for t in range(dp)],
     )
     columns = [logit_grad.T]
     for s in range(1, chips):
         columns.append(send(columns[s - 1], 1) if s % 2 else send(columns[0], s))
-    head_in = (predict_mask[None, :], columns[0], hidden)
+    held = run(fetch_kernel, shaped(hidden.shape, bf16), hidden, hbm=1, scratch=[pltpu.SemaphoreType.DMA])
     head = run(
         functools.partial(head_kernel, chips, dp, shard),
         [shaped((chips * shard, cols), f32)] * dp,
-        *head_in,
+        predict_mask[None, :],
+        held,
         hidden_other,
-        *columns[1:],
-        hbm=3,
-        scratch=local_copies(*head_in),
+        *columns,
     )
     embed = run(
-        functools.partial(embed_kernel, dp, shard),
-        [shaped((2 * shard, width // 4), f32)] * dp,
+        functools.partial(embed_kernel, dp, shard, quarter),
+        [shaped((2 * shard, quarter // 2), f32)] * dp,
         *[send(messages[s], s) for s in reversed(range(chips))],
     )
     sums = run(
@@ -423,7 +433,9 @@
 def local(hidden, logit_grad, predict_mask, slot_grads, *rest):
     vocab = lax.axis_size("vocab")
     fits = hidden.shape[1] % LANES == 0 and logit_grad.shape[1] % 16 == 0
-    fits = fits and (vocab // CORES * slot_grads.shape[2]) % 8 == 0 and lax.axis_size("dp") % 2 == 0
+    slots = vocab * slot_grads.shape[2]
+    fits = fits and slots % 16 == 0 and slots <= LANES and lax.axis_size("dp") == vocab // CORES
+    fits = fits and slot_grads.shape[3] // lax.axis_size("dp") % (2 * LANES) == 0
     step = aligned if fits else plain
     return step(hidden, logit_grad, predict_mask, slot_grads, *rest)
 

time: 58.8 us -> 54.2 us (0.922)
  waiting for transfers between devices: 20.7 us -> 15.7 us
    ppermute x11, waiting for transfers between devices: 11.3 us -> 8 us  [send(): lax.ppermute(x, 'vocab', [(v, v ^ move) for v in range(vocab)])]
    ppermute x10 -> x12, waiting for transfers between devices: 9.37 us -> 7.66 us  [send_dp(): return lax.ppermute(x, 'dp', [(i, i ^ t) for i in range(dp)]) if t else x]
    ppermute x11, starting transfers between devices: 17 us -> 15.9 us  [send(): lax.ppermute(x, 'vocab', [(v, v ^ move) for v in range(vocab)])]
    ppermute x10 -> x12, starting transfers between devices: 13.3 us -> 14.3 us  [send_dp(): return lax.ppermute(x, 'dp', [(i, i ^ t) for i in range(dp)]) if t else x]
    pallas_call x10 -> x11, Pallas kernels: 6.74 us -> 7.31 us  [run(): pl.pallas_call(kernel, out_shape=outs, in_specs=[pl.BlockSpec(memory_spac...]
  transfers between devices with their start and end apart: 21 -> 23, of which waited for: 11 -> 9; matrix products, arithmetic and copies ran while one was open for 0% -> 0% of each run, Pallas kernels for 9% -> 11%
where the time goes in v9:
time: 54.2 us; the launch traced here: 54 us
  starting transfers between devices  30.2 us (56%)
  waiting for transfers between devices  15.7 us (29%)
  Pallas kernels  7.31 us (13%)
  between operations  0.79 us (1%)
    ppermute x11, starting transfers between devices, send(): lax.ppermute(x, 'vocab', [(v, v ^ move) for v in range(vocab)])  15.9 us
    ppermute x12, starting transfers between devices, send_dp(): return lax.ppermute(x, 'dp', [(i, i ^ t) for i in range(dp)]) if t else x  14.3 us
    ppermute x11, waiting for transfers between devices, send(): lax.ppermute(x, 'vocab', [(v, v ^ move) for v in range(vocab)])  8 us
    ppermute x12, waiting for transfers between devices, send_dp(): return lax.ppermute(x, 'dp', [(i, i ^ t) for i in range(dp)]) if t else x  7.66 us
    pallas_call x11, Pallas kernels, run(): pl.pallas_call(kernel, out_shape=outs, in_specs=[pl.BlockSpec(memory_spac...  7.31 us
  transfers between devices with their start and end apart: 23, of which 9 were waited for; matrix products, arithmetic and copies ran while one was open for 0% of the time, Pallas kernels for 11%

profile of v9, /device:TPU:0, one launch (start us, length us, event | category | flops | bytes accessed | tf_op | source)
XLA Modules:
  0.0 54.0 jit_solution(17161371779395062764)
XLA Ops:
  0.6 0.5 collective-permute-start.1
  1.1 1.4 %shard_map.120 = (bf16[24,5248]{1,0:T(8,128)(2,1)S(1)}, bf16[24,5248]{1,0:T(8,128)(2,1)S(1)}) custom-call(bf16[48,5120]{1,0:T(8,128)(2,1)} %bitcast.12, s32[6,1,8]{2,1,0:T(1,128)} %bitcast.13, s32[1,8]{1,0:T(1,128)} %counts_hbm.1), custom_call_target="tpu_custom_call" | custom-call | bytes 995552 | tf_op jit(solution)/shard_map/pallas_call | solution.py:244
  2.5 0.1 collective-permute-start
  2.6 4.0 %collective-permute-start.12 = (bf16[48,1024]{1,0:T(8,128)(2,1)}, bf16[48,1024]{1,0:T(8,128)(2,1)S(1)}, u32[]{:S(2)}, u32[]{:S(2)}) collective-permute-start(bf16[48,1024]{1,0:T(8,128)(2,1)} %bitcast.8), channel_id=1, source_target_pairs={{0,4},{1,5},{2,6},{3,7},{4,0},{5,1},{6,2},{7,3},{8,12},{9,13},{10,... | collective-permute-start | bytes 294920 | tf_op jit(solution)/shard_map/ppermute | solution.py:282
  6.7 0.1 shard_map.121
  6.8 1.6 %collective-permute-start.2 = (bf16[496,128]{1,0:T(8,128)(2,1)S(1)}, bf16[496,128]{1,0:T(8,128)(2,1)S(1)}, u32[]{:S(2)}, u32[]{:S(2)}) collective-permute-start(bf16[496,128]{1,0:T(8,128)(2,1)S(1)} %get-tuple-element.35), channel_id=1, source_target_pairs={{0,8},{8,0},{16,24},{24,16},{1,9},{9,1},{17,25},{25,17},{2,10},{10... | collective-permute-start | bytes 380936 | tf_op jit(solution)/shard_map/ppermute | solution.py:285
  8.3 1.5 %collective-permute-start.3 = (bf16[496,128]{1,0:T(8,128)(2,1)S(1)}, bf16[496,128]{1,0:T(8,128)(2,1)S(1)}, u32[]{:S(2)}, u32[]{:S(2)}) collective-permute-start(bf16[496,128]{1,0:T(8,128)(2,1)S(1)} %get-tuple-element.36), channel_id=1, source_target_pairs={{0,16},{8,24},{16,0},{24,8},{1,17},{9,25},{17,1},{25,9},{2,18},{10... | collective-permute-start | bytes 380936 | tf_op jit(solution)/shard_map/ppermute | solution.py:285
  9.9 0.5 collective-permute-start.4
  10.3 1.6 %collective-permute-start.11 = (bf16[48,1024]{1,0:T(8,128)(2,1)}, bf16[48,1024]{1,0:T(8,128)(2,1)S(1)}, u32[]{:S(2)}, u32[]{:S(2)}) collective-permute-start(bf16[48,1024]{1,0:T(8,128)(2,1)} %bitcast.9), channel_id=1, source_target_pairs={{0,2},{1,3},{2,0},{3,1},{4,6},{5,7},{6,4},{7,5},{8,10},{9,11},{10,... | collective-permute-start | bytes 294920 | tf_op jit(solution)/shard_map/ppermute | solution.py:282
  11.9 0.1 collective-permute-done.12.refs_2_
  12.0 0.8 %collective-permute-start.13 = (bf16[48,1024]{1,0:T(8,128)(2,1)S(1)}, bf16[48,1024]{1,0:T(8,128)(2,1)S(1)}, u32[]{:S(2)}, u32[]{:S(2)}) collective-permute-start(bf16[48,1024]{1,0:T(8,128)(2,1)S(1)} %collective-permute-done.12.refs_2_), channel_id=1, source_target_pairs={{0,2},{1,3},{2,0},{3,1},{4,6},{5,7},{6,4},{7,5},{8,10},{9,11},{10,... | collective-permute-start | bytes 294920 | tf_op jit(solution)/shard_map/ppermute | solution.py:282
  12.9 3.1 %collective-permute-done.3.refs_2_ = bf16[496,128]{1,0:T(8,128)(2,1)S(1)} collective-permute-done((bf16[496,128]{1,0:T(8,128)(2,1)S(1)}, bf16[496,128]{1,0:T(8,128)(2,1)S(1)}, u32[]{:S(2)}, u32[]{:S(2)}) %collective-permute-start.3) | collective-permute-done | bytes 127008 | tf_op jit(solution)/shard_map/ppermute | solution.py:285
  16.0 0.4 shard_map.122
  16.3 0.0 copy-start.3
  16.4 0.0 copy-start.4
  16.4 2.8 %collective-permute-start.5 = (bf16[496,128]{1,0:T(8,128)(2,1)S(1)}, bf16[496,128]{1,0:T(8,128)(2,1)S(1)}, u32[]{:S(2)}, u32[]{:S(2)}) collective-permute-start(bf16[496,128]{1,0:T(8,128)(2,1)S(1)} %get-tuple-element.38), channel_id=1, source_target_pairs={{0,6},{1,7},{2,4},{3,5},{4,2},{5,3},{6,0},{7,1},{8,14},{9,15},{10,... | collective-permute-start | bytes 380936 | tf_op jit(solution)/shard_map/ppermute | solution.py:282
  19.1 1.3 %shard_map.125.own_ref = bf16[1024,640]{1,0:T(8,128)(2,1)S(1)} custom-call(bf16[1024,640]{1,0:T(8,128)(2,1)} %hidden_hbm.1), custom_call_target="tpu_custom_call" | custom-call | bytes 2621440 | tf_op jit(solution)/shard_map/pallas_call | solution.py:244
  20.5 0.9 %shard_map.126 = (f32[48,1280]{1,0:T(8,128)S(1)}, f32[48,1280]{1,0:T(8,128)S(1)}, f32[48,1280]{1,0:T(8,128)S(1)}, f32[48,1280]{1,0:T(8,128)S(1)}) custom-call(s32[1,1024]{1,0:T(1,128)S(1)} %bitcast.11, bf16[1024,640]{1,0:T(8,128)(2,1)S(1)} %shard_map.125.own_ref, bf16[1024,640]{1,0:T(8,128)(2,1)S(1)} %collective-permute-done.1.other_ref, ...), custom_call_target="tpu_custom_call" | custom-call | bytes 4001792 | tf_op jit(solution)/shard_map/pallas_call | solution.py:244
  21.5 0.0 copy-start
  21.5 0.0 copy-start.1
  21.5 0.0 copy-start.2
  21.5 1.3 %collective-permute-start.14 = (f32[48,1280]{1,0:T(8,128)S(1)}, f32[48,1280]{1,0:T(8,128)S(1)}, u32[]{:S(2)}, u32[]{:S(2)}) collective-permute-start(f32[48,1280]{1,0:T(8,128)S(1)} %get-tuple-element.48), channel_id=1, source_target_pairs={{0,8},{8,0},{16,24},{24,16},{1,9},{9,1},{17,25},{25,17},{2,10},{10... | collective-permute-start | bytes 737288 | tf_op jit(solution)/shard_map/ppermute | solution.py:285
  22.8 0.8 %collective-permute-start.15 = (f32[48,1280]{1,0:T(8,128)S(1)}, f32[48,1280]{1,0:T(8,128)S(1)}, u32[]{:S(2)}, u32[]{:S(2)}) collective-permute-start(f32[48,1280]{1,0:T(8,128)S(1)} %get-tuple-element.49), channel_id=1, source_target_pairs={{0,16},{8,24},{16,0},{24,8},{1,17},{9,25},{17,1},{25,9},{2,18},{10... | collective-permute-start | bytes 737288 | tf_op jit(solution)/shard_map/ppermute | solution.py:285
  23.6 1.4 %collective-permute-start.16 = (f32[48,1280]{1,0:T(8,128)S(1)}, f32[48,1280]{1,0:T(8,128)S(1)}, u32[]{:S(2)}, u32[]{:S(2)}) collective-permute-start(f32[48,1280]{1,0:T(8,128)S(1)} %get-tuple-element.50), channel_id=1, source_target_pairs={{0,24},{8,16},{16,8},{24,0},{1,25},{9,17},{17,9},{25,1},{2,26},{10... | collective-permute-start | bytes 737288 | tf_op jit(solution)/shard_map/ppermute | solution.py:285
  25.0 0.3 collective-permute-start.6
  25.4 1.3 %collective-permute-start.7 = (bf16[496,128]{1,0:T(8,128)(2,1)S(1)}, bf16[496,128]{1,0:T(8,128)(2,1)S(1)}, u32[]{:S(2)}, u32[]{:S(2)}) collective-permute-start(bf16[496,128]{1,0:T(8,128)(2,1)S(1)} %get-tuple-element.40), channel_id=1, source_target_pairs={{0,2},{1,3},{2,0},{3,1},{4,6},{5,7},{6,4},{7,5},{8,10},{9,11},{10,... | collective-permute-start | bytes 380936 | tf_op jit(solution)/shard_map/ppermute | solution.py:282
  26.7 4.9 %collective-permute-done.6.refs_1_ = bf16[496,128]{1,0:T(8,128)(2,1)S(1)} collective-permute-done((bf16[496,128]{1,0:T(8,128)(2,1)S(1)}, bf16[496,128]{1,0:T(8,128)(2,1)S(1)}, u32[]{:S(2)}, u32[]{:S(2)}) %collective-permute-start.6) | collective-permute-done | bytes 127008 | tf_op jit(solution)/shard_map/ppermute | solution.py:282
  31.7 0.0 collective-permute-done.7.refs_2_
  31.7 0.5 shard_map.123
  32.1 1.6 %collective-permute-start.10 = (f32[24,640]{1,0:T(8,128)S(1)}, f32[24,640]{1,0:T(8,128)S(1)}, u32[]{:S(2)}, u32[]{:S(2)}) collective-permute-start(f32[24,640]{1,0:T(8,128)S(1)} %get-tuple-element.45), channel_id=1, source_target_pairs={{0,24},{8,16},{16,8},{24,0},{1,25},{9,17},{17,9},{25,1},{2,26},{10... | collective-permute-start | bytes 184328 | tf_op jit(solution)/shard_map/ppermute | solution.py:285
  33.7 1.6 %collective-permute-done.15.refs_2_ = f32[48,1280]{1,0:T(8,128)S(1)} collective-permute-done((f32[48,1280]{1,0:T(8,128)S(1)}, f32[48,1280]{1,0:T(8,128)S(1)}, u32[]{:S(2)}, u32[]{:S(2)}) %collective-permute-start.15) | collective-permute-done | bytes 245792 | tf_op jit(solution)/shard_map/ppermute | solution.py:285
  35.3 0.1 shard_map.127
  35.4 0.1 collective-permute-start.17
  35.5 0.4 collective-permute-start.8
  35.9 1.6 %collective-permute-start.9 = (f32[24,640]{1,0:T(8,128)S(1)}, f32[24,640]{1,0:T(8,128)S(1)}, u32[]{:S(2)}, u32[]{:S(2)}) collective-permute-start(f32[24,640]{1,0:T(8,128)S(1)} %get-tuple-element.44), channel_id=1, source_target_pairs={{0,16},{8,24},{16,0},{24,8},{1,17},{9,25},{17,1},{25,9},{2,18},{10... | collective-permute-start | bytes 184328 | tf_op jit(solution)/shard_map/ppermute | solution.py:285
  37.5 1.3 %collective-permute-start.18 = (f32[24,640]{1,0:T(8,128)S(1)}, f32[24,640]{1,0:T(8,128)S(1)}, u32[]{:S(2)}, u32[]{:S(2)}) collective-permute-start(f32[24,640]{1,0:T(8,128)S(1)} %get-tuple-element.53), channel_id=1, source_target_pairs={{0,4},{1,5},{2,6},{3,7},{4,0},{5,1},{6,2},{7,3},{8,12},{9,13},{10,... | collective-permute-start | bytes 184328 | tf_op jit(solution)/shard_map/ppermute | solution.py:282
  38.8 3.0 %collective-permute-start.19 = (f32[24,640]{1,0:T(8,128)S(1)}, f32[24,640]{1,0:T(8,128)S(1)}, u32[]{:S(2)}, u32[]{:S(2)}) collective-permute-start(f32[24,640]{1,0:T(8,128)S(1)} %get-tuple-element.54), channel_id=1, source_target_pairs={{0,6},{1,7},{2,4},{3,5},{4,2},{5,3},{6,0},{7,1},{8,14},{9,15},{10,... | collective-permute-start | bytes 184328 | tf_op jit(solution)/shard_map/ppermute | solution.py:282
  41.9 0.8 %collective-permute-done.18.refs_6_ = f32[24,640]{1,0:T(8,128)S(1)} collective-permute-done((f32[24,640]{1,0:T(8,128)S(1)}, f32[24,640]{1,0:T(8,128)S(1)}, u32[]{:S(2)}, u32[]{:S(2)}) %collective-permute-start.18) | collective-permute-done | bytes 61472 | tf_op jit(solution)/shard_map/ppermute | solution.py:282
  42.6 2.2 %collective-permute-done.19.refs_7_ = f32[24,640]{1,0:T(8,128)S(1)} collective-permute-done((f32[24,640]{1,0:T(8,128)S(1)}, f32[24,640]{1,0:T(8,128)S(1)}, u32[]{:S(2)}, u32[]{:S(2)}) %collective-permute-start.19) | collective-permute-done | bytes 61472 | tf_op jit(solution)/shard_map/ppermute | solution.py:282
  44.8 0.3 shard_map.129.refs_0_
  45.1 1.0 %collective-permute-start.20 = (bf16[48,1280]{1,0:T(8,128)(2,1)S(1)}, bf16[48,1280]{1,0:T(8,128)(2,1)S(1)}, u32[]{:S(2)}, u32[]{:S(2)}) collective-permute-start(bf16[48,1280]{1,0:T(8,128)(2,1)S(1)} %shard_map.129.refs_0_), channel_id=1, source_target_pairs={{0,8},{8,0},{16,24},{24,16},{1,9},{9,1},{17,25},{25,17},{2,10},{10... | collective-permute-start | bytes 368648 | tf_op jit(solution)/shard_map/ppermute | solution.py:285
  46.1 1.0 %collective-permute-start.21 = (bf16[48,1280]{1,0:T(8,128)(2,1)S(1)}, bf16[48,1280]{1,0:T(8,128)(2,1)S(1)}, u32[]{:S(2)}, u32[]{:S(2)}) collective-permute-start(bf16[48,1280]{1,0:T(8,128)(2,1)S(1)} %shard_map.129.refs_0_), channel_id=1, source_target_pairs={{0,16},{8,24},{16,0},{24,8},{1,17},{9,25},{17,1},{25,9},{2,18},{10... | collective-permute-start | bytes 368648 | tf_op jit(solution)/shard_map/ppermute | solution.py:285
  47.1 1.6 %collective-permute-start.22 = (bf16[48,1280]{1,0:T(8,128)(2,1)S(1)}, bf16[48,1280]{1,0:T(8,128)(2,1)S(1)}, u32[]{:S(2)}, u32[]{:S(2)}) collective-permute-start(bf16[48,1280]{1,0:T(8,128)(2,1)S(1)} %shard_map.129.refs_0_), channel_id=1, source_target_pairs={{0,24},{8,16},{16,8},{24,0},{1,25},{9,17},{17,9},{25,1},{2,26},{10... | collective-permute-start | bytes 368648 | tf_op jit(solution)/shard_map/ppermute | solution.py:285
  48.7 1.3 %shard_map.128 = (f32[12,5120]{1,0:T(8,128)}, f32[12,5120]{1,0:T(8,128)}, f32[12,5120]{1,0:T(8,128)}) custom-call(f32[12,5120]{1,0:T(8,128)S(1)} %shard_map.124.refs_0_, f32[12,5120]{1,0:T(8,128)S(1)} %copy-done, f32[12,5120]{1,0:T(8,128)S(1)} %copy-done.1, f32[12,5120]{1,0:T(8,128)S(1)} %copy-done.2, f32[24,640]{1,0:T(8,128)S(1)} %get-tuple-element.51.refs_4_, ...), custom_call_target="tpu_custom_call" | custom-call | bytes 1966080 | tf_op jit(solution)/shard_map/pallas_call | solution.py:244
  50.0 0.1 collective-permute-done.20.refs_1_
  50.1 0.9 %collective-permute-done.21.refs_2_ = bf16[48,1280]{1,0:T(8,128)(2,1)S(1)} collective-permute-done((bf16[48,1280]{1,0:T(8,128)(2,1)S(1)}, bf16[48,1280]{1,0:T(8,128)(2,1)S(1)}, u32[]{:S(2)}, u32[]{:S(2)}) %collective-permute-start.21) | collective-permute-done | bytes 122912 | tf_op jit(solution)/shard_map/ppermute | solution.py:285
  51.0 1.9 %collective-permute-done.22.refs_3_ = bf16[48,1280]{1,0:T(8,128)(2,1)S(1)} collective-permute-done((bf16[48,1280]{1,0:T(8,128)(2,1)S(1)}, bf16[48,1280]{1,0:T(8,128)(2,1)S(1)}, u32[]{:S(2)}, u32[]{:S(2)}) %collective-permute-start.22) | collective-permute-done | bytes 122912 | tf_op jit(solution)/shard_map/ppermute | solution.py:285
  52.9 1.1 %shard_map.130 = bf16[48,5120]{1,0:T(8,128)(2,1)} custom-call(bf16[48,1280]{1,0:T(8,128)(2,1)S(1)} %shard_map.129.refs_0_, bf16[48,1280]{1,0:T(8,128)(2,1)S(1)} %collective-permute-done.20.refs_1_, bf16[48,1280]{1,0:T(8,128)(2,1)S(1)} %collective-permute-done.21.refs_2_, bf16[48,1280]{1,0:T(8,128)(2,1)S(1)} %collective-permute-done.22.refs_3_), custom_call_target="tpu_custom_call" | custom-call | bytes 983040 | tf_op jit(solution)/shard_map/pallas_call | solution.py:244
  (19 shorter events, 0.1 us)
Async XLA Ops:
  0.6 6.1 %collective-permute-start.1 = (bf16[1024,640]{1,0:T(8,128)(2,1)}, bf16[1024,640]{1,0:T(8,128)(2,1)S(1)}, u32[]{:S(2)}, u32[]{:S(2)}) collective-permute-start(bf16[1024,640]{1,0:T(8,128)(2,1)} %hidden_hbm.1), channel_id=1, source_target_pairs={{0,1},{1,0},{2,3},{3,2},{4,5},{5,4},{6,7},{7,6},{8,9},{9,8},{10,11... | collective-permute-start | bytes 3932168 | tf_op jit(solution)/shard_map/ppermute | solution.py:282
  2.5 4.2 %collective-permute-start = (bf16[24,5248]{1,0:T(8,128)(2,1)S(1)}, bf16[24,5248]{1,0:T(8,128)(2,1)S(1)}, u32[]{:S(2)}, u32[]{:S(2)}) collective-permute-start(bf16[24,5248]{1,0:T(8,128)(2,1)S(1)} %get-tuple-element.32), channel_id=1, source_target_pairs={{0,1},{1,0},{2,3},{3,2},{4,5},{5,4},{6,7},{7,6},{8,9},{9,8},{10,11... | collective-permute-start | bytes 755720 | tf_op jit(solution)/shard_map/ppermute | solution.py:282
  2.6 9.4 %collective-permute-start.12 = (bf16[48,1024]{1,0:T(8,128)(2,1)}, bf16[48,1024]{1,0:T(8,128)(2,1)S(1)}, u32[]{:S(2)}, u32[]{:S(2)}) collective-permute-start(bf16[48,1024]{1,0:T(8,128)(2,1)} %bitcast.8), channel_id=1, source_target_pairs={{0,4},{1,5},{2,6},{3,7},{4,0},{5,1},{6,2},{7,3},{8,12},{9,13},{10,... | collective-permute-start | bytes 294920 | tf_op jit(solution)/shard_map/ppermute | solution.py:282
  6.8 6.1 %collective-permute-start.2 = (bf16[496,128]{1,0:T(8,128)(2,1)S(1)}, bf16[496,128]{1,0:T(8,128)(2,1)S(1)}, u32[]{:S(2)}, u32[]{:S(2)}) collective-permute-start(bf16[496,128]{1,0:T(8,128)(2,1)S(1)} %get-tuple-element.35), channel_id=1, source_target_pairs={{0,8},{8,0},{16,24},{24,16},{1,9},{9,1},{17,25},{25,17},{2,10},{10... | collective-permute-start | bytes 380936 | tf_op jit(solution)/shard_map/ppermute | solution.py:285
  8.3 7.6 %collective-permute-start.3 = (bf16[496,128]{1,0:T(8,128)(2,1)S(1)}, bf16[496,128]{1,0:T(8,128)(2,1)S(1)}, u32[]{:S(2)}, u32[]{:S(2)}) collective-permute-start(bf16[496,128]{1,0:T(8,128)(2,1)S(1)} %get-tuple-element.36), channel_id=1, source_target_pairs={{0,16},{8,24},{16,0},{24,8},{1,17},{9,25},{17,1},{25,9},{2,18},{10... | collective-permute-start | bytes 380936 | tf_op jit(solution)/shard_map/ppermute | solution.py:285
  9.9 6.1 %collective-permute-start.4 = (bf16[496,128]{1,0:T(8,128)(2,1)S(1)}, bf16[496,128]{1,0:T(8,128)(2,1)S(1)}, u32[]{:S(2)}, u32[]{:S(2)}) collective-permute-start(bf16[496,128]{1,0:T(8,128)(2,1)S(1)} %get-tuple-element.37), channel_id=1, source_target_pairs={{0,24},{8,16},{16,8},{24,0},{1,25},{9,17},{17,9},{25,1},{2,26},{10... | collective-permute-start | bytes 380936 | tf_op jit(solution)/shard_map/ppermute | solution.py:285
  10.3 10.1 %collective-permute-start.11 = (bf16[48,1024]{1,0:T(8,128)(2,1)}, bf16[48,1024]{1,0:T(8,128)(2,1)S(1)}, u32[]{:S(2)}, u32[]{:S(2)}) collective-permute-start(bf16[48,1024]{1,0:T(8,128)(2,1)} %bitcast.9), channel_id=1, source_target_pairs={{0,2},{1,3},{2,0},{3,1},{4,6},{5,7},{6,4},{7,5},{8,10},{9,11},{10,... | collective-permute-start | bytes 294920 | tf_op jit(solution)/shard_map/ppermute | solution.py:282
  12.0 8.4 %collective-permute-start.13 = (bf16[48,1024]{1,0:T(8,128)(2,1)S(1)}, bf16[48,1024]{1,0:T(8,128)(2,1)S(1)}, u32[]{:S(2)}, u32[]{:S(2)}) collective-permute-start(bf16[48,1024]{1,0:T(8,128)(2,1)S(1)} %collective-permute-done.12.refs_2_), channel_id=1, source_target_pairs={{0,2},{1,3},{2,0},{3,1},{4,6},{5,7},{6,4},{7,5},{8,10},{9,11},{10,... | collective-permute-start | bytes 294920 | tf_op jit(solution)/shard_map/ppermute | solution.py:282
  16.3 4.1 %copy-start.3 = (bf16[1024,48]{0,1:T(8,128)(2,1)S(1)}, bf16[1024,48]{0,1:T(8,128)(2,1)}, u32[]{:S(2)}) copy-start(bf16[1024,48]{0,1:T(8,128)(2,1)} %param.10) | copy-start | bytes 294916
  16.4 4.1 %copy-start.4 = (s32[1024]{0:T(1024)S(1)}, s32[1024]{0:T(1024)}, u32[]{:S(2)}) copy-start(s32[1024]{0:T(1024)} %param.11) | copy-start | bytes 12292
  16.4 9.0 %collective-permute-start.5 = (bf16[496,128]{1,0:T(8,128)(2,1)S(1)}, bf16[496,128]{1,0:T(8,128)(2,1)S(1)}, u32[]{:S(2)}, u32[]{:S(2)}) collective-permute-start(bf16[496,128]{1,0:T(8,128)(2,1)S(1)} %get-tuple-element.38), channel_id=1, source_target_pairs={{0,6},{1,7},{2,4},{3,5},{4,2},{5,3},{6,0},{7,1},{8,14},{9,15},{10,... | collective-permute-start | bytes 380936 | tf_op jit(solution)/shard_map/ppermute | solution.py:282
  21.5 23.4 %copy-start = (f32[12,5120]{1,0:T(8,128)S(1)}, f32[12,5120]{1,0:T(8,128)}, u32[]{:S(2)}) copy-start(f32[12,5120]{1,0:T(8,128)} %refs_1_.3) | copy-start | bytes 737284
  21.5 23.4 %copy-start.1 = (f32[12,5120]{1,0:T(8,128)S(1)}, f32[12,5120]{1,0:T(8,128)}, u32[]{:S(2)}) copy-start(f32[12,5120]{1,0:T(8,128)} %refs_2_.3) | copy-start | bytes 737284
  21.5 23.3 %copy-start.2 = (f32[12,5120]{1,0:T(8,128)S(1)}, f32[12,5120]{1,0:T(8,128)}, u32[]{:S(2)}) copy-start(f32[12,5120]{1,0:T(8,128)} %refs_3_.3) | copy-start | bytes 737284
  21.5 12.2 %collective-permute-start.14 = (f32[48,1280]{1,0:T(8,128)S(1)}, f32[48,1280]{1,0:T(8,128)S(1)}, u32[]{:S(2)}, u32[]{:S(2)}) collective-permute-start(f32[48,1280]{1,0:T(8,128)S(1)} %get-tuple-element.48), channel_id=1, source_target_pairs={{0,8},{8,0},{16,24},{24,16},{1,9},{9,1},{17,25},{25,17},{2,10},{10... | collective-permute-start | bytes 737288 | tf_op jit(solution)/shard_map/ppermute | solution.py:285
  22.8 12.5 %collective-permute-start.15 = (f32[48,1280]{1,0:T(8,128)S(1)}, f32[48,1280]{1,0:T(8,128)S(1)}, u32[]{:S(2)}, u32[]{:S(2)}) collective-permute-start(f32[48,1280]{1,0:T(8,128)S(1)} %get-tuple-element.49), channel_id=1, source_target_pairs={{0,16},{8,24},{16,0},{24,8},{1,17},{9,25},{17,1},{25,9},{2,18},{10... | collective-permute-start | bytes 737288 | tf_op jit(solution)/shard_map/ppermute | solution.py:285
  23.6 11.7 %collective-permute-start.16 = (f32[48,1280]{1,0:T(8,128)S(1)}, f32[48,1280]{1,0:T(8,128)S(1)}, u32[]{:S(2)}, u32[]{:S(2)}) collective-permute-start(f32[48,1280]{1,0:T(8,128)S(1)} %get-tuple-element.50), channel_id=1, source_target_pairs={{0,24},{8,16},{16,8},{24,0},{1,25},{9,17},{17,9},{25,1},{2,26},{10... | collective-permute-start | bytes 737288 | tf_op jit(solution)/shard_map/ppermute | solution.py:285
  25.0 6.6 %collective-permute-start.6 = (bf16[496,128]{1,0:T(8,128)(2,1)S(1)}, bf16[496,128]{1,0:T(8,128)(2,1)S(1)}, u32[]{:S(2)}, u32[]{:S(2)}) collective-permute-start(bf16[496,128]{1,0:T(8,128)(2,1)S(1)} %get-tuple-element.39), channel_id=1, source_target_pairs={{0,4},{1,5},{2,6},{3,7},{4,0},{5,1},{6,2},{7,3},{8,12},{9,13},{10,... | collective-permute-start | bytes 380936 | tf_op jit(solution)/shard_map/ppermute | solution.py:282
  25.4 6.3 %collective-permute-start.7 = (bf16[496,128]{1,0:T(8,128)(2,1)S(1)}, bf16[496,128]{1,0:T(8,128)(2,1)S(1)}, u32[]{:S(2)}, u32[]{:S(2)}) collective-permute-start(bf16[496,128]{1,0:T(8,128)(2,1)S(1)} %get-tuple-element.40), channel_id=1, source_target_pairs={{0,2},{1,3},{2,0},{3,1},{4,6},{5,7},{6,4},{7,5},{8,10},{9,11},{10,... | collective-permute-start | bytes 380936 | tf_op jit(solution)/shard_map/ppermute | solution.py:282
  32.1 6.7 %collective-permute-start.10 = (f32[24,640]{1,0:T(8,128)S(1)}, f32[24,640]{1,0:T(8,128)S(1)}, u32[]{:S(2)}, u32[]{:S(2)}) collective-permute-start(f32[24,640]{1,0:T(8,128)S(1)} %get-tuple-element.45), channel_id=1, source_target_pairs={{0,24},{8,16},{16,8},{24,0},{1,25},{9,17},{17,9},{25,1},{2,26},{10... | collective-permute-start | bytes 184328 | tf_op jit(solution)/shard_map/ppermute | solution.py:285
  35.4 6.5 %collective-permute-start.17 = (f32[24,640]{1,0:T(8,128)S(1)}, f32[24,640]{1,0:T(8,128)S(1)}, u32[]{:S(2)}, u32[]{:S(2)}) collective-permute-start(f32[24,640]{1,0:T(8,128)S(1)} %get-tuple-element.52), channel_id=1, source_target_pairs={{0,2},{1,3},{2,0},{3,1},{4,6},{5,7},{6,4},{7,5},{8,10},{9,11},{10,... | collective-permute-start | bytes 184328 | tf_op jit(solution)/shard_map/ppermute | solution.py:282
  35.5 6.4 %collective-permute-start.8 = (f32[24,640]{1,0:T(8,128)S(1)}, f32[24,640]{1,0:T(8,128)S(1)}, u32[]{:S(2)}, u32[]{:S(2)}) collective-permute-start(f32[24,640]{1,0:T(8,128)S(1)} %get-tuple-element.43), channel_id=1, source_target_pairs={{0,8},{8,0},{16,24},{24,16},{1,9},{9,1},{17,25},{25,17},{2,10},{10... | collective-permute-start | bytes 184328 | tf_op jit(solution)/shard_map/ppermute | solution.py:285
  35.9 5.9 %collective-permute-start.9 = (f32[24,640]{1,0:T(8,128)S(1)}, f32[24,640]{1,0:T(8,128)S(1)}, u32[]{:S(2)}, u32[]{:S(2)}) collective-permute-start(f32[24,640]{1,0:T(8,128)S(1)} %get-tuple-element.44), channel_id=1, source_target_pairs={{0,16},{8,24},{16,0},{24,8},{1,17},{9,25},{17,1},{25,9},{2,18},{10... | collective-permute-start | bytes 184328 | tf_op jit(solution)/shard_map/ppermute | solution.py:285
  37.5 5.1 %collective-permute-start.18 = (f32[24,640]{1,0:T(8,128)S(1)}, f32[24,640]{1,0:T(8,128)S(1)}, u32[]{:S(2)}, u32[]{:S(2)}) collective-permute-start(f32[24,640]{1,0:T(8,128)S(1)} %get-tuple-element.53), channel_id=1, source_target_pairs={{0,4},{1,5},{2,6},{3,7},{4,0},{5,1},{6,2},{7,3},{8,12},{9,13},{10,... | collective-permute-start | bytes 184328 | tf_op jit(solution)/shard_map/ppermute | solution.py:282
  38.8 6.0 %collective-permute-start.19 = (f32[24,640]{1,0:T(8,128)S(1)}, f32[24,640]{1,0:T(8,128)S(1)}, u32[]{:S(2)}, u32[]{:S(2)}) collective-permute-start(f32[24,640]{1,0:T(8,128)S(1)} %get-tuple-element.54), channel_id=1, source_target_pairs={{0,6},{1,7},{2,4},{3,5},{4,2},{5,3},{6,0},{7,1},{8,14},{9,15},{10,... | collective-permute-start | bytes 184328 | tf_op jit(solution)/shard_map/ppermute | solution.py:282
  45.1 4.9 %collective-permute-start.20 = (bf16[48,1280]{1,0:T(8,128)(2,1)S(1)}, bf16[48,1280]{1,0:T(8,128)(2,1)S(1)}, u32[]{:S(2)}, u32[]{:S(2)}) collective-permute-start(bf16[48,1280]{1,0:T(8,128)(2,1)S(1)} %shard_map.129.refs_0_), channel_id=1, source_target_pairs={{0,8},{8,0},{16,24},{24,16},{1,9},{9,1},{17,25},{25,17},{2,10},{10... | collective-permute-start | bytes 368648 | tf_op jit(solution)/shard_map/ppermute | solution.py:285
  46.1 4.9 %collective-permute-start.21 = (bf16[48,1280]{1,0:T(8,128)(2,1)S(1)}, bf16[48,1280]{1,0:T(8,128)(2,1)S(1)}, u32[]{:S(2)}, u32[]{:S(2)}) collective-permute-start(bf16[48,1280]{1,0:T(8,128)(2,1)S(1)} %shard_map.129.refs_0_), channel_id=1, source_target_pairs={{0,16},{8,24},{16,0},{24,8},{1,17},{9,25},{17,1},{25,9},{2,18},{10... | collective-permute-start | bytes 368648 | tf_op jit(solution)/shard_map/ppermute | solution.py:285
  47.1 5.8 %collective-permute-start.22 = (bf16[48,1280]{1,0:T(8,128)(2,1)S(1)}, bf16[48,1280]{1,0:T(8,128)(2,1)S(1)}, u32[]{:S(2)}, u32[]{:S(2)}) collective-permute-start(bf16[48,1280]{1,0:T(8,128)(2,1)S(1)} %shard_map.129.refs_0_), channel_id=1, source_target_pairs={{0,24},{8,16},{16,8},{24,0},{1,25},{9,17},{17,9},{25,1},{2,26},{10... | collective-permute-start | bytes 368648 | tf_op jit(solution)/shard_map/ppermute | solution.py:285

commit v10 on v9

--- a/solution.py
+++ b/solution.py
@@ -202,14 +202,14 @@
 def rows_kernel(*refs):
     d, z, core = place()
     state, pieces, out_ref = refs[:4], refs[4:-1], refs[-1]
-    table = [step(chip_spot(z, s, piece), piece, *state)[0] for s, piece in enumerate(pieces)]
+    table = [step(chip_spot(z, s, piece), piece, *state)[0] for s, piece in enumerate(reversed(pieces))]
     out_ref[...] = jnp.concatenate(table, axis=0).astype(jnp.bfloat16)
 
 
 def adam_kernel(*refs):
     d, z, core = place()
     state, pieces, outs = refs[:4], refs[4:-3], refs[-3:]
-    for s, piece in enumerate(pieces):
+    for s, piece in enumerate(reversed(pieces)):
         spot = chip_spot(z, s, piece)
         for out_ref, value in zip(outs, step(spot, piece, *state)):
             out_ref[:, spot] = value
@@ -302,15 +302,13 @@
     quarter = width // dp
     packets = [shaped((vocab * cap * quarter // LANES + ID_ROWS, LANES), bf16)]
     quarters = run(functools.partial(peers_kernel, dp), packets * dp, slots_own, slots_other)
-    messages = run(
-        functools.partial(owners_kernel, chips, cap, quarter),
-        packets * chips,
-        *[send_dp(quarters[t], t) for t in range(dp)],
-    )
+    held = run(fetch_kernel, shaped(hidden.shape, bf16), hidden, hbm=1, scratch=[pltpu.SemaphoreType.DMA])
+    quarters = [send_dp(quarters[t], t) for t in range(dp)]
+    quarters[0], held = lax.optimization_barrier((quarters[0], held))
+    messages = run(functools.partial(owners_kernel, chips, cap, quarter), packets * chips, *quarters)
     columns = [logit_grad.T]
     for s in range(1, chips):
         columns.append(send(columns[s - 1], 1) if s % 2 else send(columns[0], s))
-    held = run(fetch_kernel, shaped(hidden.shape, bf16), hidden, hbm=1, scratch=[pltpu.SemaphoreType.DMA])
     head = run(
         functools.partial(head_kernel, chips, dp, shard),
         [shaped((chips * shard, cols), f32)] * dp,
@@ -329,7 +327,7 @@
         [shaped((2 * shard, cols // 2), f32)] * chips,
         *[send_dp(head[t], t) for t in range(dp)],
     )
-    pieces = [send(sums[s], s) for s in range(chips)]
+    pieces = [send(sums[s], s) for s in reversed(range(chips))]
     embed = run(gather_kernel, shaped((shard, width), f32), *[send_dp(embed[t], t) for t in range(dp)])
     state = (embed, master, first_moment, second_moment)
     table = run(rows_kernel, shaped((chips * shard, cols), bf16), *state, *pieces)

time: 54.2 us -> 52.8 us (0.974)
  waiting for transfers between devices: 15.7 us -> 13.5 us
  starting transfers between devices: 30.2 us -> 31 us
    ppermute x12, waiting for transfers between devices: 7.66 us -> 6.16 us  [send_dp(): return lax.ppermute(x, 'dp', [(i, i ^ t) for i in range(dp)]) if t else x]
    ppermute x11, starting transfers between devices: 15.9 us -> 16.7 us  [send(): lax.ppermute(x, 'vocab', [(v, v ^ move) for v in range(vocab)])]
    ppermute x11, waiting for transfers between devices: 8 us -> 7.38 us  [send(): lax.ppermute(x, 'vocab', [(v, v ^ move) for v in range(vocab)])]
  transfers between devices with their start and end apart: 23 -> 23, of which waited for: 9 -> 10; matrix products, arithmetic and copies ran while one was open for 0% -> 0% of each run, Pallas kernels for 11% -> 11%
where the time goes in v10:
time: 52.8 us; the launch traced here: 52.6 us
  starting transfers between devices  31 us (59%)
  waiting for transfers between devices  13.5 us (26%)
  Pallas kernels  7.31 us (14%)
  between operations  0.75 us (1%)
    ppermute x11, starting transfers between devices, send(): lax.ppermute(x, 'vocab', [(v, v ^ move) for v in range(vocab)])  16.7 us
    ppermute x12, starting transfers between devices, send_dp(): return lax.ppermute(x, 'dp', [(i, i ^ t) for i in range(dp)]) if t else x  14.3 us
    ppermute x11, waiting for transfers between devices, send(): lax.ppermute(x, 'vocab', [(v, v ^ move) for v in range(vocab)])  7.38 us
    pallas_call x11, Pallas kernels, run(): pl.pallas_call(kernel, out_shape=outs, in_specs=[pl.BlockSpec(memory_spac...  7.31 us
    ppermute x12, waiting for transfers between devices, send_dp(): return lax.ppermute(x, 'dp', [(i, i ^ t) for i in range(dp)]) if t else x  6.16 us
  transfers between devices with their start and end apart: 23, of which 10 were waited for; matrix products, arithmetic and copies ran while one was open for 0% of the time, Pallas kernels for 11%

profile of v10, /device:TPU:0, one launch (start us, length us, event | category | flops | bytes accessed | tf_op | source)
XLA Modules:
  0.0 52.6 jit_solution(14514993889595721016)
XLA Ops:
  0.6 0.5 collective-permute-start.1
  1.1 1.4 %shard_map.120 = (bf16[24,5248]{1,0:T(8,128)(2,1)S(1)}, bf16[24,5248]{1,0:T(8,128)(2,1)S(1)}) custom-call(bf16[48,5120]{1,0:T(8,128)(2,1)} %bitcast.12, s32[6,1,8]{2,1,0:T(1,128)} %bitcast.13, s32[1,8]{1,0:T(1,128)} %counts_hbm.1), custom_call_target="tpu_custom_call" | custom-call | bytes 995552 | tf_op jit(solution)/shard_map/pallas_call | solution.py:244
  2.5 0.1 collective-permute-start
  2.6 4.0 %collective-permute-start.12 = (bf16[48,1024]{1,0:T(8,128)(2,1)}, bf16[48,1024]{1,0:T(8,128)(2,1)S(1)}, u32[]{:S(2)}, u32[]{:S(2)}) collective-permute-start(bf16[48,1024]{1,0:T(8,128)(2,1)} %bitcast.8), channel_id=1, source_target_pairs={{0,4},{1,5},{2,6},{3,7},{4,0},{5,1},{6,2},{7,3},{8,12},{9,13},{10,... | collective-permute-start | bytes 294920 | tf_op jit(solution)/shard_map/ppermute | solution.py:282
  6.7 0.0 collective-permute-done.other_ref
  6.7 0.1 shard_map.121
  6.8 1.6 %collective-permute-start.2 = (bf16[496,128]{1,0:T(8,128)(2,1)S(1)}, bf16[496,128]{1,0:T(8,128)(2,1)S(1)}, u32[]{:S(2)}, u32[]{:S(2)}) collective-permute-start(bf16[496,128]{1,0:T(8,128)(2,1)S(1)} %get-tuple-element.38), channel_id=1, source_target_pairs={{0,8},{8,0},{16,24},{24,16},{1,9},{9,1},{17,25},{25,17},{2,10},{10... | collective-permute-start | bytes 380936 | tf_op jit(solution)/shard_map/ppermute | solution.py:285
  8.3 1.5 %collective-permute-start.3 = (bf16[496,128]{1,0:T(8,128)(2,1)S(1)}, bf16[496,128]{1,0:T(8,128)(2,1)S(1)}, u32[]{:S(2)}, u32[]{:S(2)}) collective-permute-start(bf16[496,128]{1,0:T(8,128)(2,1)S(1)} %get-tuple-element.39), channel_id=1, source_target_pairs={{0,16},{8,24},{16,0},{24,8},{1,17},{9,25},{17,1},{25,9},{2,18},{10... | collective-permute-start | bytes 380936 | tf_op jit(solution)/shard_map/ppermute | solution.py:285
  9.9 0.5 collective-permute-start.4
  10.3 1.6 %collective-permute-start.11 = (bf16[48,1024]{1,0:T(8,128)(2,1)}, bf16[48,1024]{1,0:T(8,128)(2,1)S(1)}, u32[]{:S(2)}, u32[]{:S(2)}) collective-permute-start(bf16[48,1024]{1,0:T(8,128)(2,1)} %bitcast.9), channel_id=1, source_target_pairs={{0,2},{1,3},{2,0},{3,1},{4,6},{5,7},{6,4},{7,5},{8,10},{9,11},{10,... | collective-permute-start | bytes 294920 | tf_op jit(solution)/shard_map/ppermute | solution.py:282
  11.9 0.1 collective-permute-done.12.refs_2_
  12.0 0.8 %collective-permute-start.13 = (bf16[48,1024]{1,0:T(8,128)(2,1)S(1)}, bf16[48,1024]{1,0:T(8,128)(2,1)S(1)}, u32[]{:S(2)}, u32[]{:S(2)}) collective-permute-start(bf16[48,1024]{1,0:T(8,128)(2,1)S(1)} %collective-permute-done.12.refs_2_), channel_id=1, source_target_pairs={{0,2},{1,3},{2,0},{3,1},{4,6},{5,7},{6,4},{7,5},{8,10},{9,11},{10,... | collective-permute-start | bytes 294920 | tf_op jit(solution)/shard_map/ppermute | solution.py:282
  12.9 1.3 %shard_map.122.own_ref = bf16[1024,640]{1,0:T(8,128)(2,1)S(1)} custom-call(bf16[1024,640]{1,0:T(8,128)(2,1)} %hidden_hbm.1), custom_call_target="tpu_custom_call" | custom-call | bytes 2621440 | tf_op jit(solution)/shard_map/pallas_call | solution.py:244
  14.2 1.8 %collective-permute-done.3.refs_2_ = bf16[496,128]{1,0:T(8,128)(2,1)S(1)} collective-permute-done((bf16[496,128]{1,0:T(8,128)(2,1)S(1)}, bf16[496,128]{1,0:T(8,128)(2,1)S(1)}, u32[]{:S(2)}, u32[]{:S(2)}) %collective-permute-start.3) | collective-permute-done | bytes 127008 | tf_op jit(solution)/shard_map/ppermute | solution.py:285
  16.0 0.4 shard_map.123
  16.3 2.8 %collective-permute-start.5 = (bf16[496,128]{1,0:T(8,128)(2,1)S(1)}, bf16[496,128]{1,0:T(8,128)(2,1)S(1)}, u32[]{:S(2)}, u32[]{:S(2)}) collective-permute-start(bf16[496,128]{1,0:T(8,128)(2,1)S(1)} %get-tuple-element.41), channel_id=1, source_target_pairs={{0,6},{1,7},{2,4},{3,5},{4,2},{5,3},{6,0},{7,1},{8,14},{9,15},{10,... | collective-permute-start | bytes 380936 | tf_op jit(solution)/shard_map/ppermute | solution.py:282
  19.1 0.9 %shard_map.126 = (f32[48,1280]{1,0:T(8,128)S(1)}, f32[48,1280]{1,0:T(8,128)S(1)}, f32[48,1280]{1,0:T(8,128)S(1)}, f32[48,1280]{1,0:T(8,128)S(1)}) custom-call(s32[1,1024]{1,0:T(1,128)S(1)} %bitcast.11, bf16[1024,640]{1,0:T(8,128)(2,1)S(1)} %shard_map.122.own_ref, bf16[1024,640]{1,0:T(8,128)(2,1)S(1)} %collective-permute-done.1.other_ref, ...), custom_call_target="tpu_custom_call" | custom-call | bytes 4001792 | tf_op jit(solution)/shard_map/pallas_call | solution.py:244
  20.1 0.0 copy-start
  20.1 0.0 copy-start.1
  20.1 0.0 copy-start.2
  20.1 1.3 %collective-permute-start.14 = (f32[48,1280]{1,0:T(8,128)S(1)}, f32[48,1280]{1,0:T(8,128)S(1)}, u32[]{:S(2)}, u32[]{:S(2)}) collective-permute-start(f32[48,1280]{1,0:T(8,128)S(1)} %get-tuple-element.52), channel_id=1, source_target_pairs={{0,8},{8,0},{16,24},{24,16},{1,9},{9,1},{17,25},{25,17},{2,10},{10... | collective-permute-start | bytes 737288 | tf_op jit(solution)/shard_map/ppermute | solution.py:285
  21.4 0.8 %collective-permute-start.15 = (f32[48,1280]{1,0:T(8,128)S(1)}, f32[48,1280]{1,0:T(8,128)S(1)}, u32[]{:S(2)}, u32[]{:S(2)}) collective-permute-start(f32[48,1280]{1,0:T(8,128)S(1)} %get-tuple-element.53), channel_id=1, source_target_pairs={{0,16},{8,24},{16,0},{24,8},{1,17},{9,25},{17,1},{25,9},{2,18},{10... | collective-permute-start | bytes 737288 | tf_op jit(solution)/shard_map/ppermute | solution.py:285
  22.2 1.4 %collective-permute-start.16 = (f32[48,1280]{1,0:T(8,128)S(1)}, f32[48,1280]{1,0:T(8,128)S(1)}, u32[]{:S(2)}, u32[]{:S(2)}) collective-permute-start(f32[48,1280]{1,0:T(8,128)S(1)} %get-tuple-element.54), channel_id=1, source_target_pairs={{0,24},{8,16},{16,8},{24,0},{1,25},{9,17},{17,9},{25,1},{2,26},{10... | collective-permute-start | bytes 737288 | tf_op jit(solution)/shard_map/ppermute | solution.py:285
  23.7 0.3 collective-permute-start.6
  24.0 1.4 %collective-permute-start.7 = (bf16[496,128]{1,0:T(8,128)(2,1)S(1)}, bf16[496,128]{1,0:T(8,128)(2,1)S(1)}, u32[]{:S(2)}, u32[]{:S(2)}) collective-permute-start(bf16[496,128]{1,0:T(8,128)(2,1)S(1)} %get-tuple-element.43), channel_id=1, source_target_pairs={{0,2},{1,3},{2,0},{3,1},{4,6},{5,7},{6,4},{7,5},{8,10},{9,11},{10,... | collective-permute-start | bytes 380936 | tf_op jit(solution)/shard_map/ppermute | solution.py:282
  25.4 4.9 %collective-permute-done.6.refs_1_ = bf16[496,128]{1,0:T(8,128)(2,1)S(1)} collective-permute-done((bf16[496,128]{1,0:T(8,128)(2,1)S(1)}, bf16[496,128]{1,0:T(8,128)(2,1)S(1)}, u32[]{:S(2)}, u32[]{:S(2)}) %collective-permute-start.6) | collective-permute-done | bytes 127008 | tf_op jit(solution)/shard_map/ppermute | solution.py:282
  30.3 0.0 collective-permute-done.7.refs_2_
  30.3 0.5 shard_map.124
  30.8 2.3 %collective-permute-start.10 = (f32[24,640]{1,0:T(8,128)S(1)}, f32[24,640]{1,0:T(8,128)S(1)}, u32[]{:S(2)}, u32[]{:S(2)}) collective-permute-start(f32[24,640]{1,0:T(8,128)S(1)} %get-tuple-element.48), channel_id=1, source_target_pairs={{0,24},{8,16},{16,8},{24,0},{1,25},{9,17},{17,9},{25,1},{2,26},{10... | collective-permute-start | bytes 184328 | tf_op jit(solution)/shard_map/ppermute | solution.py:285
  33.1 0.8 %collective-permute-done.15.refs_2_ = f32[48,1280]{1,0:T(8,128)S(1)} collective-permute-done((f32[48,1280]{1,0:T(8,128)S(1)}, f32[48,1280]{1,0:T(8,128)S(1)}, u32[]{:S(2)}, u32[]{:S(2)}) %collective-permute-start.15) | collective-permute-done | bytes 245792 | tf_op jit(solution)/shard_map/ppermute | solution.py:285
  34.0 0.1 shard_map.127
  34.0 1.8 %collective-permute-start.17 = (f32[24,640]{1,0:T(8,128)S(1)}, f32[24,640]{1,0:T(8,128)S(1)}, u32[]{:S(2)}, u32[]{:S(2)}) collective-permute-start(f32[24,640]{1,0:T(8,128)S(1)} %get-tuple-element.55), channel_id=1, source_target_pairs={{0,6},{1,7},{2,4},{3,5},{4,2},{5,3},{6,0},{7,1},{8,14},{9,15},{10,... | collective-permute-start | bytes 184328 | tf_op jit(solution)/shard_map/ppermute | solution.py:282
  35.8 0.9 %collective-permute-start.8 = (f32[24,640]{1,0:T(8,128)S(1)}, f32[24,640]{1,0:T(8,128)S(1)}, u32[]{:S(2)}, u32[]{:S(2)}) collective-permute-start(f32[24,640]{1,0:T(8,128)S(1)} %get-tuple-element.46), channel_id=1, source_target_pairs={{0,8},{8,0},{16,24},{24,16},{1,9},{9,1},{17,25},{25,17},{2,10},{10... | collective-permute-start | bytes 184328 | tf_op jit(solution)/shard_map/ppermute | solution.py:285
  36.7 0.5 collective-permute-start.9
  37.1 0.0 collective-permute-start.18
  37.1 3.3 %collective-permute-start.19 = (f32[24,640]{1,0:T(8,128)S(1)}, f32[24,640]{1,0:T(8,128)S(1)}, u32[]{:S(2)}, u32[]{:S(2)}) collective-permute-start(f32[24,640]{1,0:T(8,128)S(1)} %get-tuple-element.57), channel_id=1, source_target_pairs={{0,2},{1,3},{2,0},{3,1},{4,6},{5,7},{6,4},{7,5},{8,10},{9,11},{10,... | collective-permute-start | bytes 184328 | tf_op jit(solution)/shard_map/ppermute | solution.py:282
  40.5 0.4 collective-permute-done.9.refs_2_
  40.9 1.9 %collective-permute-done.18.refs_5_ = f32[24,640]{1,0:T(8,128)S(1)} collective-permute-done((f32[24,640]{1,0:T(8,128)S(1)}, f32[24,640]{1,0:T(8,128)S(1)}, u32[]{:S(2)}, u32[]{:S(2)}) %collective-permute-start.18) | collective-permute-done | bytes 61472 | tf_op jit(solution)/shard_map/ppermute | solution.py:282
  42.9 0.4 collective-permute-done.19.refs_6_
  43.3 0.3 shard_map.129.refs_0_
  43.6 1.1 %collective-permute-start.20 = (bf16[48,1280]{1,0:T(8,128)(2,1)S(1)}, bf16[48,1280]{1,0:T(8,128)(2,1)S(1)}, u32[]{:S(2)}, u32[]{:S(2)}) collective-permute-start(bf16[48,1280]{1,0:T(8,128)(2,1)S(1)} %shard_map.129.refs_0_), channel_id=1, source_target_pairs={{0,8},{8,0},{16,24},{24,16},{1,9},{9,1},{17,25},{25,17},{2,10},{10... | collective-permute-start | bytes 368648 | tf_op jit(solution)/shard_map/ppermute | solution.py:285
  44.6 1.1 %collective-permute-start.21 = (bf16[48,1280]{1,0:T(8,128)(2,1)S(1)}, bf16[48,1280]{1,0:T(8,128)(2,1)S(1)}, u32[]{:S(2)}, u32[]{:S(2)}) collective-permute-start(bf16[48,1280]{1,0:T(8,128)(2,1)S(1)} %shard_map.129.refs_0_), channel_id=1, source_target_pairs={{0,16},{8,24},{16,0},{24,8},{1,17},{9,25},{17,1},{25,9},{2,18},{10... | collective-permute-start | bytes 368648 | tf_op jit(solution)/shard_map/ppermute | solution.py:285
  45.8 1.4 %collective-permute-start.22 = (bf16[48,1280]{1,0:T(8,128)(2,1)S(1)}, bf16[48,1280]{1,0:T(8,128)(2,1)S(1)}, u32[]{:S(2)}, u32[]{:S(2)}) collective-permute-start(bf16[48,1280]{1,0:T(8,128)(2,1)S(1)} %shard_map.129.refs_0_), channel_id=1, source_target_pairs={{0,24},{8,16},{16,8},{24,0},{1,25},{9,17},{17,9},{25,1},{2,26},{10... | collective-permute-start | bytes 368648 | tf_op jit(solution)/shard_map/ppermute | solution.py:285
  47.2 1.3 %shard_map.128 = (f32[12,5120]{1,0:T(8,128)}, f32[12,5120]{1,0:T(8,128)}, f32[12,5120]{1,0:T(8,128)}) custom-call(f32[12,5120]{1,0:T(8,128)S(1)} %shard_map.125.refs_0_, f32[12,5120]{1,0:T(8,128)S(1)} %copy-done, f32[12,5120]{1,0:T(8,128)S(1)} %copy-done.1, f32[12,5120]{1,0:T(8,128)S(1)} %copy-done.2, f32[24,640]{1,0:T(8,128)S(1)} %collective-permute-done.17.refs_4_, ...), custom_call_target="tpu_custom_call" | custom-call | bytes 1966080 | tf_op jit(solution)/shard_map/pallas_call | solution.py:244
  48.4 0.1 collective-permute-done.20.refs_1_
  48.5 1.0 %collective-permute-done.21.refs_2_ = bf16[48,1280]{1,0:T(8,128)(2,1)S(1)} collective-permute-done((bf16[48,1280]{1,0:T(8,128)(2,1)S(1)}, bf16[48,1280]{1,0:T(8,128)(2,1)S(1)}, u32[]{:S(2)}, u32[]{:S(2)}) %collective-permute-start.21) | collective-permute-done | bytes 122912 | tf_op jit(solution)/shard_map/ppermute | solution.py:285
  49.5 2.0 %collective-permute-done.22.refs_3_ = bf16[48,1280]{1,0:T(8,128)(2,1)S(1)} collective-permute-done((bf16[48,1280]{1,0:T(8,128)(2,1)S(1)}, bf16[48,1280]{1,0:T(8,128)(2,1)S(1)}, u32[]{:S(2)}, u32[]{:S(2)}) %collective-permute-start.22) | collective-permute-done | bytes 122912 | tf_op jit(solution)/shard_map/ppermute | solution.py:285
  51.5 1.1 %shard_map.130 = bf16[48,5120]{1,0:T(8,128)(2,1)} custom-call(bf16[48,1280]{1,0:T(8,128)(2,1)S(1)} %shard_map.129.refs_0_, bf16[48,1280]{1,0:T(8,128)(2,1)S(1)} %collective-permute-done.20.refs_1_, bf16[48,1280]{1,0:T(8,128)(2,1)S(1)} %collective-permute-done.21.refs_2_, bf16[48,1280]{1,0:T(8,128)(2,1)S(1)} %collective-permute-done.22.refs_3_), custom_call_target="tpu_custom_call" | custom-call | bytes 983040 | tf_op jit(solution)/shard_map/pallas_call | solution.py:244
  (19 shorter events, 0.1 us)
Async XLA Ops:
  0.6 6.1 %collective-permute-start.1 = (bf16[1024,640]{1,0:T(8,128)(2,1)}, bf16[1024,640]{1,0:T(8,128)(2,1)S(1)}, u32[]{:S(2)}, u32[]{:S(2)}) collective-permute-start(bf16[1024,640]{1,0:T(8,128)(2,1)} %hidden_hbm.1), channel_id=1, source_target_pairs={{0,1},{1,0},{2,3},{3,2},{4,5},{5,4},{6,7},{7,6},{8,9},{9,8},{10,11... | collective-permute-start | bytes 3932168 | tf_op jit(solution)/shard_map/ppermute | solution.py:282
  2.5 4.2 %collective-permute-start = (bf16[24,5248]{1,0:T(8,128)(2,1)S(1)}, bf16[24,5248]{1,0:T(8,128)(2,1)S(1)}, u32[]{:S(2)}, u32[]{:S(2)}) collective-permute-start(bf16[24,5248]{1,0:T(8,128)(2,1)S(1)} %get-tuple-element.34), channel_id=1, source_target_pairs={{0,1},{1,0},{2,3},{3,2},{4,5},{5,4},{6,7},{7,6},{8,9},{9,8},{10,11... | collective-permute-start | bytes 755720 | tf_op jit(solution)/shard_map/ppermute | solution.py:282
  2.6 9.4 %collective-permute-start.12 = (bf16[48,1024]{1,0:T(8,128)(2,1)}, bf16[48,1024]{1,0:T(8,128)(2,1)S(1)}, u32[]{:S(2)}, u32[]{:S(2)}) collective-permute-start(bf16[48,1024]{1,0:T(8,128)(2,1)} %bitcast.8), channel_id=1, source_target_pairs={{0,4},{1,5},{2,6},{3,7},{4,0},{5,1},{6,2},{7,3},{8,12},{9,13},{10,... | collective-permute-start | bytes 294920 | tf_op jit(solution)/shard_map/ppermute | solution.py:282
  6.8 7.4 %collective-permute-start.2 = (bf16[496,128]{1,0:T(8,128)(2,1)S(1)}, bf16[496,128]{1,0:T(8,128)(2,1)S(1)}, u32[]{:S(2)}, u32[]{:S(2)}) collective-permute-start(bf16[496,128]{1,0:T(8,128)(2,1)S(1)} %get-tuple-element.38), channel_id=1, source_target_pairs={{0,8},{8,0},{16,24},{24,16},{1,9},{9,1},{17,25},{25,17},{2,10},{10... | collective-permute-start | bytes 380936 | tf_op jit(solution)/shard_map/ppermute | solution.py:285
  8.3 7.6 %collective-permute-start.3 = (bf16[496,128]{1,0:T(8,128)(2,1)S(1)}, bf16[496,128]{1,0:T(8,128)(2,1)S(1)}, u32[]{:S(2)}, u32[]{:S(2)}) collective-permute-start(bf16[496,128]{1,0:T(8,128)(2,1)S(1)} %get-tuple-element.39), channel_id=1, source_target_pairs={{0,16},{8,24},{16,0},{24,8},{1,17},{9,25},{17,1},{25,9},{2,18},{10... | collective-permute-start | bytes 380936 | tf_op jit(solution)/shard_map/ppermute | solution.py:285
  9.9 9.3 %copy-start.3 = (bf16[1024,48]{0,1:T(8,128)(2,1)S(1)}, bf16[1024,48]{0,1:T(8,128)(2,1)}, u32[]{:S(2)}) copy-start(bf16[1024,48]{0,1:T(8,128)(2,1)} %param.10) | copy-start | bytes 294916
  9.9 9.3 %copy-start.4 = (s32[1024]{0:T(1024)S(1)}, s32[1024]{0:T(1024)}, u32[]{:S(2)}) copy-start(s32[1024]{0:T(1024)} %param.11) | copy-start | bytes 12292
  9.9 6.1 %collective-permute-start.4 = (bf16[496,128]{1,0:T(8,128)(2,1)S(1)}, bf16[496,128]{1,0:T(8,128)(2,1)S(1)}, u32[]{:S(2)}, u32[]{:S(2)}) collective-permute-start(bf16[496,128]{1,0:T(8,128)(2,1)S(1)} %get-tuple-element.40), channel_id=1, source_target_pairs={{0,24},{8,16},{16,8},{24,0},{1,25},{9,17},{17,9},{25,1},{2,26},{10... | collective-permute-start | bytes 380936 | tf_op jit(solution)/shard_map/ppermute | solution.py:285
  10.3 8.8 %collective-permute-start.11 = (bf16[48,1024]{1,0:T(8,128)(2,1)}, bf16[48,1024]{1,0:T(8,128)(2,1)S(1)}, u32[]{:S(2)}, u32[]{:S(2)}) collective-permute-start(bf16[48,1024]{1,0:T(8,128)(2,1)} %bitcast.9), channel_id=1, source_target_pairs={{0,2},{1,3},{2,0},{3,1},{4,6},{5,7},{6,4},{7,5},{8,10},{9,11},{10,... | collective-permute-start | bytes 294920 | tf_op jit(solution)/shard_map/ppermute | solution.py:282
  12.0 7.1 %collective-permute-start.13 = (bf16[48,1024]{1,0:T(8,128)(2,1)S(1)}, bf16[48,1024]{1,0:T(8,128)(2,1)S(1)}, u32[]{:S(2)}, u32[]{:S(2)}) collective-permute-start(bf16[48,1024]{1,0:T(8,128)(2,1)S(1)} %collective-permute-done.12.refs_2_), channel_id=1, source_target_pairs={{0,2},{1,3},{2,0},{3,1},{4,6},{5,7},{6,4},{7,5},{8,10},{9,11},{10,... | collective-permute-start | bytes 294920 | tf_op jit(solution)/shard_map/ppermute | solution.py:282
  16.3 7.7 %collective-permute-start.5 = (bf16[496,128]{1,0:T(8,128)(2,1)S(1)}, bf16[496,128]{1,0:T(8,128)(2,1)S(1)}, u32[]{:S(2)}, u32[]{:S(2)}) collective-permute-start(bf16[496,128]{1,0:T(8,128)(2,1)S(1)} %get-tuple-element.41), channel_id=1, source_target_pairs={{0,6},{1,7},{2,4},{3,5},{4,2},{5,3},{6,0},{7,1},{8,14},{9,15},{10,... | collective-permute-start | bytes 380936 | tf_op jit(solution)/shard_map/ppermute | solution.py:282
  20.1 23.2 %copy-start = (f32[12,5120]{1,0:T(8,128)S(1)}, f32[12,5120]{1,0:T(8,128)}, u32[]{:S(2)}) copy-start(f32[12,5120]{1,0:T(8,128)} %refs_1_.3) | copy-start | bytes 737284
  20.1 23.2 %copy-start.1 = (f32[12,5120]{1,0:T(8,128)S(1)}, f32[12,5120]{1,0:T(8,128)}, u32[]{:S(2)}) copy-start(f32[12,5120]{1,0:T(8,128)} %refs_2_.3) | copy-start | bytes 737284
  20.1 23.2 %copy-start.2 = (f32[12,5120]{1,0:T(8,128)S(1)}, f32[12,5120]{1,0:T(8,128)}, u32[]{:S(2)}) copy-start(f32[12,5120]{1,0:T(8,128)} %refs_3_.3) | copy-start | bytes 737284
  20.1 13.0 %collective-permute-start.14 = (f32[48,1280]{1,0:T(8,128)S(1)}, f32[48,1280]{1,0:T(8,128)S(1)}, u32[]{:S(2)}, u32[]{:S(2)}) collective-permute-start(f32[48,1280]{1,0:T(8,128)S(1)} %get-tuple-element.52), channel_id=1, source_target_pairs={{0,8},{8,0},{16,24},{24,16},{1,9},{9,1},{17,25},{25,17},{2,10},{10... | collective-permute-start | bytes 737288 | tf_op jit(solution)/shard_map/ppermute | solution.py:285
  21.4 12.5 %collective-permute-start.15 = (f32[48,1280]{1,0:T(8,128)S(1)}, f32[48,1280]{1,0:T(8,128)S(1)}, u32[]{:S(2)}, u32[]{:S(2)}) collective-permute-start(f32[48,1280]{1,0:T(8,128)S(1)} %get-tuple-element.53), channel_id=1, source_target_pairs={{0,16},{8,24},{16,0},{24,8},{1,17},{9,25},{17,1},{25,9},{2,18},{10... | collective-permute-start | bytes 737288 | tf_op jit(solution)/shard_map/ppermute | solution.py:285
  22.2 11.7 %collective-permute-start.16 = (f32[48,1280]{1,0:T(8,128)S(1)}, f32[48,1280]{1,0:T(8,128)S(1)}, u32[]{:S(2)}, u32[]{:S(2)}) collective-permute-start(f32[48,1280]{1,0:T(8,128)S(1)} %get-tuple-element.54), channel_id=1, source_target_pairs={{0,24},{8,16},{16,8},{24,0},{1,25},{9,17},{17,9},{25,1},{2,26},{10... | collective-permute-start | bytes 737288 | tf_op jit(solution)/shard_map/ppermute | solution.py:285
  23.7 6.6 %collective-permute-start.6 = (bf16[496,128]{1,0:T(8,128)(2,1)S(1)}, bf16[496,128]{1,0:T(8,128)(2,1)S(1)}, u32[]{:S(2)}, u32[]{:S(2)}) collective-permute-start(bf16[496,128]{1,0:T(8,128)(2,1)S(1)} %get-tuple-element.42), channel_id=1, source_target_pairs={{0,4},{1,5},{2,6},{3,7},{4,0},{5,1},{6,2},{7,3},{8,12},{9,13},{10,... | collective-permute-start | bytes 380936 | tf_op jit(solution)/shard_map/ppermute | solution.py:282
  24.0 6.3 %collective-permute-start.7 = (bf16[496,128]{1,0:T(8,128)(2,1)S(1)}, bf16[496,128]{1,0:T(8,128)(2,1)S(1)}, u32[]{:S(2)}, u32[]{:S(2)}) collective-permute-start(bf16[496,128]{1,0:T(8,128)(2,1)S(1)} %get-tuple-element.43), channel_id=1, source_target_pairs={{0,2},{1,3},{2,0},{3,1},{4,6},{5,7},{6,4},{7,5},{8,10},{9,11},{10,... | collective-permute-start | bytes 380936 | tf_op jit(solution)/shard_map/ppermute | solution.py:282
  30.8 6.4 %collective-permute-start.10 = (f32[24,640]{1,0:T(8,128)S(1)}, f32[24,640]{1,0:T(8,128)S(1)}, u32[]{:S(2)}, u32[]{:S(2)}) collective-permute-start(f32[24,640]{1,0:T(8,128)S(1)} %get-tuple-element.48), channel_id=1, source_target_pairs={{0,24},{8,16},{16,8},{24,0},{1,25},{9,17},{17,9},{25,1},{2,26},{10... | collective-permute-start | bytes 184328 | tf_op jit(solution)/shard_map/ppermute | solution.py:285
  34.0 6.9 %collective-permute-start.17 = (f32[24,640]{1,0:T(8,128)S(1)}, f32[24,640]{1,0:T(8,128)S(1)}, u32[]{:S(2)}, u32[]{:S(2)}) collective-permute-start(f32[24,640]{1,0:T(8,128)S(1)} %get-tuple-element.55), channel_id=1, source_target_pairs={{0,6},{1,7},{2,4},{3,5},{4,2},{5,3},{6,0},{7,1},{8,14},{9,15},{10,... | collective-permute-start | bytes 184328 | tf_op jit(solution)/shard_map/ppermute | solution.py:282
  35.8 4.7 %collective-permute-start.8 = (f32[24,640]{1,0:T(8,128)S(1)}, f32[24,640]{1,0:T(8,128)S(1)}, u32[]{:S(2)}, u32[]{:S(2)}) collective-permute-start(f32[24,640]{1,0:T(8,128)S(1)} %get-tuple-element.46), channel_id=1, source_target_pairs={{0,8},{8,0},{16,24},{24,16},{1,9},{9,1},{17,25},{25,17},{2,10},{10... | collective-permute-start | bytes 184328 | tf_op jit(solution)/shard_map/ppermute | solution.py:285
  36.7 4.2 %collective-permute-start.9 = (f32[24,640]{1,0:T(8,128)S(1)}, f32[24,640]{1,0:T(8,128)S(1)}, u32[]{:S(2)}, u32[]{:S(2)}) collective-permute-start(f32[24,640]{1,0:T(8,128)S(1)} %get-tuple-element.47), channel_id=1, source_target_pairs={{0,16},{8,24},{16,0},{24,8},{1,17},{9,25},{17,1},{25,9},{2,18},{10... | collective-permute-start | bytes 184328 | tf_op jit(solution)/shard_map/ppermute | solution.py:285
  37.1 5.7 %collective-permute-start.18 = (f32[24,640]{1,0:T(8,128)S(1)}, f32[24,640]{1,0:T(8,128)S(1)}, u32[]{:S(2)}, u32[]{:S(2)}) collective-permute-start(f32[24,640]{1,0:T(8,128)S(1)} %get-tuple-element.56), channel_id=1, source_target_pairs={{0,4},{1,5},{2,6},{3,7},{4,0},{5,1},{6,2},{7,3},{8,12},{9,13},{10,... | collective-permute-start | bytes 184328 | tf_op jit(solution)/shard_map/ppermute | solution.py:282
  37.1 6.1 %collective-permute-start.19 = (f32[24,640]{1,0:T(8,128)S(1)}, f32[24,640]{1,0:T(8,128)S(1)}, u32[]{:S(2)}, u32[]{:S(2)}) collective-permute-start(f32[24,640]{1,0:T(8,128)S(1)} %get-tuple-element.57), channel_id=1, source_target_pairs={{0,2},{1,3},{2,0},{3,1},{4,6},{5,7},{6,4},{7,5},{8,10},{9,11},{10,... | collective-permute-start | bytes 184328 | tf_op jit(solution)/shard_map/ppermute | solution.py:282
  43.6 4.9 %collective-permute-start.20 = (bf16[48,1280]{1,0:T(8,128)(2,1)S(1)}, bf16[48,1280]{1,0:T(8,128)(2,1)S(1)}, u32[]{:S(2)}, u32[]{:S(2)}) collective-permute-start(bf16[48,1280]{1,0:T(8,128)(2,1)S(1)} %shard_map.129.refs_0_), channel_id=1, source_target_pairs={{0,8},{8,0},{16,24},{24,16},{1,9},{9,1},{17,25},{25,17},{2,10},{10... | collective-permute-start | bytes 368648 | tf_op jit(solution)/shard_map/ppermute | solution.py:285
  44.6 4.9 %collective-permute-start.21 = (bf16[48,1280]{1,0:T(8,128)(2,1)S(1)}, bf16[48,1280]{1,0:T(8,128)(2,1)S(1)}, u32[]{:S(2)}, u32[]{:S(2)}) collective-permute-start(bf16[48,1280]{1,0:T(8,128)(2,1)S(1)} %shard_map.129.refs_0_), channel_id=1, source_target_pairs={{0,16},{8,24},{16,0},{24,8},{1,17},{9,25},{17,1},{25,9},{2,18},{10... | collective-permute-start | bytes 368648 | tf_op jit(solution)/shard_map/ppermute | solution.py:285
  45.8 5.8 %collective-permute-start.22 = (bf16[48,1280]{1,0:T(8,128)(2,1)S(1)}, bf16[48,1280]{1,0:T(8,128)(2,1)S(1)}, u32[]{:S(2)}, u32[]{:S(2)}) collective-permute-start(bf16[48,1280]{1,0:T(8,128)(2,1)S(1)} %shard_map.129.refs_0_), channel_id=1, source_target_pairs={{0,24},{8,16},{16,8},{24,0},{1,25},{9,17},{17,9},{25,1},{2,26},{10... | collective-permute-start | bytes 368648 | tf_op jit(solution)/shard_map/ppermute | solution.py:285

commit v11 on v10

--- a/solution.py
+++ b/solution.py
@@ -206,38 +206,44 @@
     out_ref[...] = jnp.concatenate(table, axis=0).astype(jnp.bfloat16)
 
 
-def adam_kernel(*refs):
-    d, z, core = place()
-    state, pieces, outs = refs[:4], refs[4:-3], refs[-3:]
+def adam_kernel(chips, dp, shard, *refs):
+    d, z, core = place()
+    state, pieces, outs, order_ref = refs[:4], refs[4:-4], refs[-4:-1], refs[-1]
+    rows = dp * shard
+    total = chips * rows
+    r = iota((total, total), 0)
+    s = over(r, rows)
+    e = over(r - s * rows, shard)
+    i = r - s * rows - e * shard
+    order_ref[...] = one_hot(iota((total, total), 1) == ((e ^ d) * chips + s) * shard + i)
     for s, piece in enumerate(reversed(pieces)):
         spot = chip_spot(z, s, piece)
         for out_ref, value in zip(outs, step(spot, piece, *state)):
             out_ref[:, spot] = value
 
 
-def table_kernel(chips, dp, shard, *refs):
-    d, z, core = place()
-    parts, out_ref = refs[:-1], refs[-1]
+def table_kernel(chips, dp, shard, order_ref, *refs):
+    d, z, core = place()
+    parts, (out_hbm, out_ref, sems) = refs[-4::-1], refs[-3:]
     cols = parts[0].shape[1]
     rows = dp * shard
-    total = chips * rows
     values = jnp.concatenate([part[...] for part in parts], axis=0)
-    r = iota((total, total), 0)
-    s = over(r, rows)
-    e = over(r - s * rows, shard)
-    i = r - s * rows - e * shard
-    order = one_hot(iota((total, total), 1) == ((e ^ d) * chips + s) * shard + i)
-    values = exact(order, values).astype(jnp.bfloat16)
+    values = exact(order_ref[...], values).astype(jnp.bfloat16)
+    copies = []
     for s in range(chips):
+        out_ref[s] = values[s * rows : (s + 1) * rows]
         spot = pl.ds(pl.multiple_of((z ^ s) * cols, LANES), cols)
-        out_ref[:, spot] = values[s * rows : (s + 1) * rows]
+        copies.append(pltpu.make_async_copy(out_ref.at[s], out_hbm.at[:, spot], sems.at[s]))
+        copies[-1].start()
+    for copy in copies:
+        copy.wait()
 
 
 def shaped(shape, kind):
     return jax.ShapeDtypeStruct(shape, kind)
 
 
-def run(kernel, outs, *args, cost=1, hbm=0, scratch=()):
+def run(kernel, outs, *args, cost=1, hbm=0, out_hbm=False, scratch=()):
     moved = sum(x.size * x.dtype.itemsize for x in (*args, *jax.tree.leaves(outs)))
     vmem = pl.BlockSpec(memory_space=pltpu.VMEM)
     args = [pltpu.with_memory_space_constraint(x, pltpu.HBM) if n < hbm else x for n, x in enumerate(args)]
@@ -245,7 +251,7 @@
         kernel,
         out_shape=outs,
         in_specs=[pl.BlockSpec(memory_space=pltpu.HBM)] * hbm + [vmem] * (len(args) - hbm),
-        out_specs=jax.tree.map(lambda _: vmem, outs),
+        out_specs=jax.tree.map(lambda _: pl.BlockSpec(memory_space=pltpu.HBM) if out_hbm else vmem, outs),
         scratch_shapes=list(scratch),
         cost_estimate=pl.CostEstimate(flops=0, bytes_accessed=moved * cost, transcendentals=0),
         compiler_params=pltpu.CompilerParams(vmem_limit_bytes=VMEM_LIMIT),
@@ -303,8 +309,8 @@
     packets = [shaped((vocab * cap * quarter // LANES + ID_ROWS, LANES), bf16)]
     quarters = run(functools.partial(peers_kernel, dp), packets * dp, slots_own, slots_other)
     held = run(fetch_kernel, shaped(hidden.shape, bf16), hidden, hbm=1, scratch=[pltpu.SemaphoreType.DMA])
-    quarters = [send_dp(quarters[t], t) for t in range(dp)]
-    quarters[0], held = lax.optimization_barrier((quarters[0], held))
+    quarters = [send_dp(quarters[t], t) for t in reversed(range(dp))]
+    quarters[-1], held = lax.optimization_barrier((quarters[-1], held))
     messages = run(functools.partial(owners_kernel, chips, cap, quarter), packets * chips, *quarters)
     columns = [logit_grad.T]
     for s in range(1, chips):
@@ -325,17 +331,25 @@
     sums = run(
         functools.partial(sum_kernel, chips, shard),
         [shaped((2 * shard, cols // 2), f32)] * chips,
-        *[send_dp(head[t], t) for t in range(dp)],
+        *[send_dp(head[t], t) for t in reversed(range(dp))],
     )
     pieces = [send(sums[s], s) for s in reversed(range(chips))]
     embed = run(gather_kernel, shaped((shard, width), f32), *[send_dp(embed[t], t) for t in range(dp)])
     state = (embed, master, first_moment, second_moment)
     table = run(rows_kernel, shaped((chips * shard, cols), bf16), *state, *pieces)
-    master_new, first_new, second_new = run(adam_kernel, [shaped(master.shape, f32)] * 3, *state, *pieces)
+    master_new, first_new, second_new, order = run(
+        functools.partial(adam_kernel, chips, dp, shard),
+        [shaped(master.shape, f32)] * 3 + [shaped((chips * rows, chips * rows), bf16)],
+        *state,
+        *pieces,
+    )
     table = run(
         functools.partial(table_kernel, chips, dp, shard),
         shaped((rows, width), bf16),
-        *[send_dp(table, t) for t in range(dp)],
+        order,
+        *[send_dp(table, t) for t in reversed(range(dp))],
+        out_hbm=True,
+        scratch=[pltpu.VMEM((chips, rows, cols), bf16), pltpu.SemaphoreType.DMA((chips,))],
     )
     return (master_new, first_new, second_new, table)
 

time: 52.8 us -> 52.7 us (level)
  waiting for transfers between devices: 13.5 us -> 12.2 us
  starting transfers between devices: 31 us -> 32.3 us
    ppermute x11, starting transfers between devices: 16.7 us -> 18.9 us  [send(): lax.ppermute(x, 'vocab', [(v, v ^ move) for v in range(vocab)])]
    ppermute x12, starting transfers between devices: 14.3 us -> 13.4 us  [send_dp(): return lax.ppermute(x, 'dp', [(i, i ^ t) for i in range(dp)]) if t else x]
    ppermute x12, waiting for transfers between devices: 6.16 us -> 5.41 us  [send_dp(): return lax.ppermute(x, 'dp', [(i, i ^ t) for i in range(dp)]) if t else x]
    ppermute x11, waiting for transfers between devices: 7.38 us -> 6.75 us  [send(): lax.ppermute(x, 'vocab', [(v, v ^ move) for v in range(vocab)])]
  transfers between devices with their start and end apart: 23 -> 23, of which waited for: 10 -> 13; matrix products, arithmetic and copies ran while one was open for 0% -> 0% of each run, Pallas kernels for 11% -> 11%
where the time goes in v11:
time: 52.7 us; the launch traced here: 52.5 us
  starting transfers between devices  32.3 us (61%)
  waiting for transfers between devices  12.2 us (23%)
  Pallas kernels  7.3 us (14%)
  between operations  0.74 us (1%)
    ppermute x11, starting transfers between devices, send(): lax.ppermute(x, 'vocab', [(v, v ^ move) for v in range(vocab)])  18.9 us
    ppermute x12, starting transfers between devices, send_dp(): return lax.ppermute(x, 'dp', [(i, i ^ t) for i in range(dp)]) if t else x  13.4 us
    pallas_call x11, Pallas kernels, run(): pl.pallas_call(kernel, out_shape=outs, in_specs=[pl.BlockSpec(memory_spac...  7.3 us
    ppermute x11, waiting for transfers between devices, send(): lax.ppermute(x, 'vocab', [(v, v ^ move) for v in range(vocab)])  6.75 us
    ppermute x12, waiting for transfers between devices, send_dp(): return lax.ppermute(x, 'dp', [(i, i ^ t) for i in range(dp)]) if t else x  5.41 us
  transfers between devices with their start and end apart: 23, of which 13 were waited for; matrix products, arithmetic and copies ran while one was open for 0% of the time, Pallas kernels for 11%

profile of v11, /device:TPU:0, one launch (start us, length us, event | category | flops | bytes accessed | tf_op | source)
XLA Modules:
  0.0 52.5 jit_solution(16003224868531418954)
XLA Ops:
  0.6 0.5 collective-permute-start.1
  1.1 1.4 %shard_map.120 = (bf16[24,5248]{1,0:T(8,128)(2,1)S(1)}, bf16[24,5248]{1,0:T(8,128)(2,1)S(1)}) custom-call(bf16[48,5120]{1,0:T(8,128)(2,1)} %bitcast.12, s32[6,1,8]{2,1,0:T(1,128)} %bitcast.13, s32[1,8]{1,0:T(1,128)} %counts_hbm.1), custom_call_target="tpu_custom_call" | custom-call | bytes 995552 | tf_op jit(solution)/shard_map/pallas_call | solution.py:250
  2.5 0.1 collective-permute-start
  2.6 4.0 %collective-permute-start.12 = (bf16[48,1024]{1,0:T(8,128)(2,1)}, bf16[48,1024]{1,0:T(8,128)(2,1)S(1)}, u32[]{:S(2)}, u32[]{:S(2)}) collective-permute-start(bf16[48,1024]{1,0:T(8,128)(2,1)} %bitcast.8), channel_id=1, source_target_pairs={{0,4},{1,5},{2,6},{3,7},{4,0},{5,1},{6,2},{7,3},{8,12},{9,13},{10,... | collective-permute-start | bytes 294920 | tf_op jit(solution)/shard_map/ppermute | solution.py:288
  6.7 0.1 shard_map.121
  6.8 2.5 %collective-permute-start.2 = (bf16[496,128]{1,0:T(8,128)(2,1)S(1)}, bf16[496,128]{1,0:T(8,128)(2,1)S(1)}, u32[]{:S(2)}, u32[]{:S(2)}) collective-permute-start(bf16[496,128]{1,0:T(8,128)(2,1)S(1)} %get-tuple-element.37), channel_id=1, source_target_pairs={{0,24},{8,16},{16,8},{24,0},{1,25},{9,17},{17,9},{25,1},{2,26},{10... | collective-permute-start | bytes 380936 | tf_op jit(solution)/shard_map/ppermute | solution.py:291
  9.3 0.5 collective-permute-start.3
  9.8 0.5 %collective-permute-start.4 = (bf16[496,128]{1,0:T(8,128)(2,1)S(1)}, bf16[496,128]{1,0:T(8,128)(2,1)S(1)}, u32[]{:S(2)}, u32[]{:S(2)}) collective-permute-start(bf16[496,128]{1,0:T(8,128)(2,1)S(1)} %get-tuple-element.39), channel_id=1, source_target_pairs={{0,8},{8,0},{16,24},{24,16},{1,9},{9,1},{17,25},{25,17},{2,10},{10... | collective-permute-start | bytes 380936 | tf_op jit(solution)/shard_map/ppermute | solution.py:291
  10.3 1.6 %collective-permute-start.11 = (bf16[48,1024]{1,0:T(8,128)(2,1)}, bf16[48,1024]{1,0:T(8,128)(2,1)S(1)}, u32[]{:S(2)}, u32[]{:S(2)}) collective-permute-start(bf16[48,1024]{1,0:T(8,128)(2,1)} %bitcast.9), channel_id=1, source_target_pairs={{0,2},{1,3},{2,0},{3,1},{4,6},{5,7},{6,4},{7,5},{8,10},{9,11},{10,... | collective-permute-start | bytes 294920 | tf_op jit(solution)/shard_map/ppermute | solution.py:288
  11.9 0.1 collective-permute-done.12.refs_2_
  12.0 0.8 %collective-permute-start.13 = (bf16[48,1024]{1,0:T(8,128)(2,1)S(1)}, bf16[48,1024]{1,0:T(8,128)(2,1)S(1)}, u32[]{:S(2)}, u32[]{:S(2)}) collective-permute-start(bf16[48,1024]{1,0:T(8,128)(2,1)S(1)} %collective-permute-done.12.refs_2_), channel_id=1, source_target_pairs={{0,2},{1,3},{2,0},{3,1},{4,6},{5,7},{6,4},{7,5},{8,10},{9,11},{10,... | collective-permute-start | bytes 294920 | tf_op jit(solution)/shard_map/ppermute | solution.py:288
  12.9 1.3 %shard_map.122.own_ref = bf16[1024,640]{1,0:T(8,128)(2,1)S(1)} custom-call(bf16[1024,640]{1,0:T(8,128)(2,1)} %hidden_hbm.1), custom_call_target="tpu_custom_call" | custom-call | bytes 2621440 | tf_op jit(solution)/shard_map/pallas_call | solution.py:250
  14.2 1.4 %collective-permute-done.3.refs_1_ = bf16[496,128]{1,0:T(8,128)(2,1)S(1)} collective-permute-done((bf16[496,128]{1,0:T(8,128)(2,1)S(1)}, bf16[496,128]{1,0:T(8,128)(2,1)S(1)}, u32[]{:S(2)}, u32[]{:S(2)}) %collective-permute-start.3) | collective-permute-done | bytes 127008 | tf_op jit(solution)/shard_map/ppermute | solution.py:291
  15.6 0.1 collective-permute-done.4.refs_2_
  15.6 0.4 shard_map.123
  16.0 2.9 %collective-permute-start.5 = (bf16[496,128]{1,0:T(8,128)(2,1)S(1)}, bf16[496,128]{1,0:T(8,128)(2,1)S(1)}, u32[]{:S(2)}, u32[]{:S(2)}) collective-permute-start(bf16[496,128]{1,0:T(8,128)(2,1)S(1)} %get-tuple-element.42), channel_id=1, source_target_pairs={{0,6},{1,7},{2,4},{3,5},{4,2},{5,3},{6,0},{7,1},{8,14},{9,15},{10,... | collective-permute-start | bytes 380936 | tf_op jit(solution)/shard_map/ppermute | solution.py:288
  18.9 0.9 %shard_map.126 = (f32[48,1280]{1,0:T(8,128)S(1)}, f32[48,1280]{1,0:T(8,128)S(1)}, f32[48,1280]{1,0:T(8,128)S(1)}, f32[48,1280]{1,0:T(8,128)S(1)}) custom-call(s32[1,1024]{1,0:T(1,128)S(1)} %bitcast.11, bf16[1024,640]{1,0:T(8,128)(2,1)S(1)} %shard_map.122.own_ref, bf16[1024,640]{1,0:T(8,128)(2,1)S(1)} %collective-permute-done.1.other_ref, ...), custom_call_target="tpu_custom_call" | custom-call | bytes 4001792 | tf_op jit(solution)/shard_map/pallas_call | solution.py:250
  19.8 0.0 copy-start
  19.9 0.0 copy-start.2
  19.9 1.7 %collective-permute-start.14 = (f32[48,1280]{1,0:T(8,128)S(1)}, f32[48,1280]{1,0:T(8,128)S(1)}, u32[]{:S(2)}, u32[]{:S(2)}) collective-permute-start(f32[48,1280]{1,0:T(8,128)S(1)} %get-tuple-element.52), channel_id=1, source_target_pairs={{0,24},{8,16},{16,8},{24,0},{1,25},{9,17},{17,9},{25,1},{2,26},{10... | collective-permute-start | bytes 737288 | tf_op jit(solution)/shard_map/ppermute | solution.py:291
  21.6 1.3 %collective-permute-start.15 = (f32[48,1280]{1,0:T(8,128)S(1)}, f32[48,1280]{1,0:T(8,128)S(1)}, u32[]{:S(2)}, u32[]{:S(2)}) collective-permute-start(f32[48,1280]{1,0:T(8,128)S(1)} %get-tuple-element.53), channel_id=1, source_target_pairs={{0,16},{8,24},{16,0},{24,8},{1,17},{9,25},{17,1},{25,9},{2,18},{10... | collective-permute-start | bytes 737288 | tf_op jit(solution)/shard_map/ppermute | solution.py:291
  22.9 0.5 collective-permute-start.16
  23.4 0.2 collective-permute-start.6
  23.7 3.5 %collective-permute-start.7 = (bf16[496,128]{1,0:T(8,128)(2,1)S(1)}, bf16[496,128]{1,0:T(8,128)(2,1)S(1)}, u32[]{:S(2)}, u32[]{:S(2)}) collective-permute-start(bf16[496,128]{1,0:T(8,128)(2,1)S(1)} %get-tuple-element.44), channel_id=1, source_target_pairs={{0,2},{1,3},{2,0},{3,1},{4,6},{5,7},{6,4},{7,5},{8,10},{9,11},{10,... | collective-permute-start | bytes 380936 | tf_op jit(solution)/shard_map/ppermute | solution.py:288
  27.1 3.4 %collective-permute-done.6.refs_1_ = bf16[496,128]{1,0:T(8,128)(2,1)S(1)} collective-permute-done((bf16[496,128]{1,0:T(8,128)(2,1)S(1)}, bf16[496,128]{1,0:T(8,128)(2,1)S(1)}, u32[]{:S(2)}, u32[]{:S(2)}) %collective-permute-start.6) | collective-permute-done | bytes 127008 | tf_op jit(solution)/shard_map/ppermute | solution.py:288
  30.6 0.7 %collective-permute-done.7.refs_2_ = bf16[496,128]{1,0:T(8,128)(2,1)S(1)} collective-permute-done((bf16[496,128]{1,0:T(8,128)(2,1)S(1)}, bf16[496,128]{1,0:T(8,128)(2,1)S(1)}, u32[]{:S(2)}, u32[]{:S(2)}) %collective-permute-start.7) | collective-permute-done | bytes 127008 | tf_op jit(solution)/shard_map/ppermute | solution.py:288
  31.3 0.5 shard_map.124
  31.8 1.5 %collective-permute-start.10 = (f32[24,640]{1,0:T(8,128)S(1)}, f32[24,640]{1,0:T(8,128)S(1)}, u32[]{:S(2)}, u32[]{:S(2)}) collective-permute-start(f32[24,640]{1,0:T(8,128)S(1)} %get-tuple-element.49), channel_id=1, source_target_pairs={{0,24},{8,16},{16,8},{24,0},{1,25},{9,17},{17,9},{25,1},{2,26},{10... | collective-permute-start | bytes 184328 | tf_op jit(solution)/shard_map/ppermute | solution.py:291
  33.2 0.9 %collective-permute-done.15.refs_1_ = f32[48,1280]{1,0:T(8,128)S(1)} collective-permute-done((f32[48,1280]{1,0:T(8,128)S(1)}, f32[48,1280]{1,0:T(8,128)S(1)}, u32[]{:S(2)}, u32[]{:S(2)}) %collective-permute-start.15) | collective-permute-done | bytes 245792 | tf_op jit(solution)/shard_map/ppermute | solution.py:291
  34.2 0.1 collective-permute-done.16.refs_2_
  34.3 0.1 shard_map.127
  34.3 1.5 %collective-permute-start.17 = (f32[24,640]{1,0:T(8,128)S(1)}, f32[24,640]{1,0:T(8,128)S(1)}, u32[]{:S(2)}, u32[]{:S(2)}) collective-permute-start(f32[24,640]{1,0:T(8,128)S(1)} %get-tuple-element.56), channel_id=1, source_target_pairs={{0,6},{1,7},{2,4},{3,5},{4,2},{5,3},{6,0},{7,1},{8,14},{9,15},{10,... | collective-permute-start | bytes 184328 | tf_op jit(solution)/shard_map/ppermute | solution.py:288
  35.8 0.8 %collective-permute-start.8 = (f32[24,640]{1,0:T(8,128)S(1)}, f32[24,640]{1,0:T(8,128)S(1)}, u32[]{:S(2)}, u32[]{:S(2)}) collective-permute-start(f32[24,640]{1,0:T(8,128)S(1)} %get-tuple-element.47), channel_id=1, source_target_pairs={{0,8},{8,0},{16,24},{24,16},{1,9},{9,1},{17,25},{25,17},{2,10},{10... | collective-permute-start | bytes 184328 | tf_op jit(solution)/shard_map/ppermute | solution.py:291
  36.6 0.5 %collective-permute-start.9 = (f32[24,640]{1,0:T(8,128)S(1)}, f32[24,640]{1,0:T(8,128)S(1)}, u32[]{:S(2)}, u32[]{:S(2)}) collective-permute-start(f32[24,640]{1,0:T(8,128)S(1)} %get-tuple-element.48), channel_id=1, source_target_pairs={{0,16},{8,24},{16,0},{24,8},{1,17},{9,25},{17,1},{25,9},{2,18},{10... | collective-permute-start | bytes 184328 | tf_op jit(solution)/shard_map/ppermute | solution.py:291
  37.1 0.6 %collective-permute-start.18 = (f32[24,640]{1,0:T(8,128)S(1)}, f32[24,640]{1,0:T(8,128)S(1)}, u32[]{:S(2)}, u32[]{:S(2)}) collective-permute-start(f32[24,640]{1,0:T(8,128)S(1)} %get-tuple-element.57), channel_id=1, source_target_pairs={{0,4},{1,5},{2,6},{3,7},{4,0},{5,1},{6,2},{7,3},{8,12},{9,13},{10,... | collective-permute-start | bytes 184328 | tf_op jit(solution)/shard_map/ppermute | solution.py:288
  37.7 3.2 %collective-permute-start.19 = (f32[24,640]{1,0:T(8,128)S(1)}, f32[24,640]{1,0:T(8,128)S(1)}, u32[]{:S(2)}, u32[]{:S(2)}) collective-permute-start(f32[24,640]{1,0:T(8,128)S(1)} %get-tuple-element.58), channel_id=1, source_target_pairs={{0,2},{1,3},{2,0},{3,1},{4,6},{5,7},{6,4},{7,5},{8,10},{9,11},{10,... | collective-permute-start | bytes 184328 | tf_op jit(solution)/shard_map/ppermute | solution.py:288
  40.9 0.2 collective-permute-done.17.refs_4_
  41.1 1.9 %collective-permute-done.18.refs_5_ = f32[24,640]{1,0:T(8,128)S(1)} collective-permute-done((f32[24,640]{1,0:T(8,128)S(1)}, f32[24,640]{1,0:T(8,128)S(1)}, u32[]{:S(2)}, u32[]{:S(2)}) %collective-permute-start.18) | collective-permute-done | bytes 61472 | tf_op jit(solution)/shard_map/ppermute | solution.py:288
  43.0 0.4 collective-permute-done.19.refs_6_
  43.4 0.3 shard_map.129.refs_3_
  43.7 1.8 %collective-permute-start.20 = (bf16[48,1280]{1,0:T(8,128)(2,1)S(1)}, bf16[48,1280]{1,0:T(8,128)(2,1)S(1)}, u32[]{:S(2)}, u32[]{:S(2)}) collective-permute-start(bf16[48,1280]{1,0:T(8,128)(2,1)S(1)} %shard_map.129.refs_3_), channel_id=1, source_target_pairs={{0,24},{8,16},{16,8},{24,0},{1,25},{9,17},{17,9},{25,1},{2,26},{10... | collective-permute-start | bytes 368648 | tf_op jit(solution)/shard_map/ppermute | solution.py:291
  45.5 1.1 %collective-permute-start.21 = (bf16[48,1280]{1,0:T(8,128)(2,1)S(1)}, bf16[48,1280]{1,0:T(8,128)(2,1)S(1)}, u32[]{:S(2)}, u32[]{:S(2)}) collective-permute-start(bf16[48,1280]{1,0:T(8,128)(2,1)S(1)} %shard_map.129.refs_3_), channel_id=1, source_target_pairs={{0,16},{8,24},{16,0},{24,8},{1,17},{9,25},{17,1},{25,9},{2,18},{10... | collective-permute-start | bytes 368648 | tf_op jit(solution)/shard_map/ppermute | solution.py:291
  46.6 0.6 %collective-permute-start.22 = (bf16[48,1280]{1,0:T(8,128)(2,1)S(1)}, bf16[48,1280]{1,0:T(8,128)(2,1)S(1)}, u32[]{:S(2)}, u32[]{:S(2)}) collective-permute-start(bf16[48,1280]{1,0:T(8,128)(2,1)S(1)} %shard_map.129.refs_3_), channel_id=1, source_target_pairs={{0,8},{8,0},{16,24},{24,16},{1,9},{9,1},{17,25},{25,17},{2,10},{10... | collective-permute-start | bytes 368648 | tf_op jit(solution)/shard_map/ppermute | solution.py:291
  47.2 1.3 %shard_map.128 = (f32[12,5120]{1,0:T(8,128)}, f32[12,5120]{1,0:T(8,128)}, f32[12,5120]{1,0:T(8,128)}, bf16[192,192]{1,0:T(8,128)(2,1)S(1)}) custom-call(f32[12,5120]{1,0:T(8,128)S(1)} %shard_map.125.refs_0_, f32[12,5120]{1,0:T(8,128)S(1)} %copy-done, f32[12,5120]{1,0:T(8,128)S(1)} %copy-done.1, f32[12,5120]{1,0:T(8,128)S(1)} %copy-done.2, ...), custom_call_target="tpu_custom_call" | custom-call | bytes 2039808 | tf_op jit(solution)/shard_map/pallas_call | solution.py:250
  48.5 1.3 %collective-permute-done.20.refs_0_ = bf16[48,1280]{1,0:T(8,128)(2,1)S(1)} collective-permute-done((bf16[48,1280]{1,0:T(8,128)(2,1)S(1)}, bf16[48,1280]{1,0:T(8,128)(2,1)S(1)}, u32[]{:S(2)}, u32[]{:S(2)}) %collective-permute-start.20) | collective-permute-done | bytes 122912 | tf_op jit(solution)/shard_map/ppermute | solution.py:291
  49.8 1.2 %collective-permute-done.21.refs_1_ = bf16[48,1280]{1,0:T(8,128)(2,1)S(1)} collective-permute-done((bf16[48,1280]{1,0:T(8,128)(2,1)S(1)}, bf16[48,1280]{1,0:T(8,128)(2,1)S(1)}, u32[]{:S(2)}, u32[]{:S(2)}) %collective-permute-start.21) | collective-permute-done | bytes 122912 | tf_op jit(solution)/shard_map/ppermute | solution.py:291
  51.1 0.4 collective-permute-done.22.refs_2_
  51.5 1.1 %shard_map.130 = bf16[48,5120]{1,0:T(8,128)(2,1)} custom-call(bf16[192,192]{1,0:T(8,128)(2,1)S(1)} %get-tuple-element.63.order_ref, bf16[48,1280]{1,0:T(8,128)(2,1)S(1)} %collective-permute-done.20.refs_0_, bf16[48,1280]{1,0:T(8,128)(2,1)S(1)} %collective-permute-done.21.refs_1_, bf16[48,1280]{1,0:T(8,128)(2,1)S(1)} %collective-permute-done.22.refs_2_, ...), custom_call_target="tpu_custom_call" | custom-call | bytes 1056768 | tf_op jit(solution)/shard_map/pallas_call | solution.py:250
  (19 shorter events, 0.1 us)
Async XLA Ops:
  0.6 6.1 %collective-permute-start.1 = (bf16[1024,640]{1,0:T(8,128)(2,1)}, bf16[1024,640]{1,0:T(8,128)(2,1)S(1)}, u32[]{:S(2)}, u32[]{:S(2)}) collective-permute-start(bf16[1024,640]{1,0:T(8,128)(2,1)} %hidden_hbm.1), channel_id=1, source_target_pairs={{0,1},{1,0},{2,3},{3,2},{4,5},{5,4},{6,7},{7,6},{8,9},{9,8},{10,11... | collective-permute-start | bytes 3932168 | tf_op jit(solution)/shard_map/ppermute | solution.py:288
  2.5 4.2 %collective-permute-start = (bf16[24,5248]{1,0:T(8,128)(2,1)S(1)}, bf16[24,5248]{1,0:T(8,128)(2,1)S(1)}, u32[]{:S(2)}, u32[]{:S(2)}) collective-permute-start(bf16[24,5248]{1,0:T(8,128)(2,1)S(1)} %get-tuple-element.35), channel_id=1, source_target_pairs={{0,1},{1,0},{2,3},{3,2},{4,5},{5,4},{6,7},{7,6},{8,9},{9,8},{10,11... | collective-permute-start | bytes 755720 | tf_op jit(solution)/shard_map/ppermute | solution.py:288
  2.6 9.4 %collective-permute-start.12 = (bf16[48,1024]{1,0:T(8,128)(2,1)}, bf16[48,1024]{1,0:T(8,128)(2,1)S(1)}, u32[]{:S(2)}, u32[]{:S(2)}) collective-permute-start(bf16[48,1024]{1,0:T(8,128)(2,1)} %bitcast.8), channel_id=1, source_target_pairs={{0,4},{1,5},{2,6},{3,7},{4,0},{5,1},{6,2},{7,3},{8,12},{9,13},{10,... | collective-permute-start | bytes 294920 | tf_op jit(solution)/shard_map/ppermute | solution.py:288
  6.8 7.4 %collective-permute-start.2 = (bf16[496,128]{1,0:T(8,128)(2,1)S(1)}, bf16[496,128]{1,0:T(8,128)(2,1)S(1)}, u32[]{:S(2)}, u32[]{:S(2)}) collective-permute-start(bf16[496,128]{1,0:T(8,128)(2,1)S(1)} %get-tuple-element.37), channel_id=1, source_target_pairs={{0,24},{8,16},{16,8},{24,0},{1,25},{9,17},{17,9},{25,1},{2,26},{10... | collective-permute-start | bytes 380936 | tf_op jit(solution)/shard_map/ppermute | solution.py:291
  9.3 6.3 %collective-permute-start.3 = (bf16[496,128]{1,0:T(8,128)(2,1)S(1)}, bf16[496,128]{1,0:T(8,128)(2,1)S(1)}, u32[]{:S(2)}, u32[]{:S(2)}) collective-permute-start(bf16[496,128]{1,0:T(8,128)(2,1)S(1)} %get-tuple-element.38), channel_id=1, source_target_pairs={{0,16},{8,24},{16,0},{24,8},{1,17},{9,25},{17,1},{25,9},{2,18},{10... | collective-permute-start | bytes 380936 | tf_op jit(solution)/shard_map/ppermute | solution.py:291
  9.8 9.1 %copy-start.3 = (bf16[1024,48]{0,1:T(8,128)(2,1)S(1)}, bf16[1024,48]{0,1:T(8,128)(2,1)}, u32[]{:S(2)}) copy-start(bf16[1024,48]{0,1:T(8,128)(2,1)} %param.10) | copy-start | bytes 294916
  9.8 9.1 %copy-start.4 = (s32[1024]{0:T(1024)S(1)}, s32[1024]{0:T(1024)}, u32[]{:S(2)}) copy-start(s32[1024]{0:T(1024)} %param.11) | copy-start | bytes 12292
  9.8 5.8 %collective-permute-start.4 = (bf16[496,128]{1,0:T(8,128)(2,1)S(1)}, bf16[496,128]{1,0:T(8,128)(2,1)S(1)}, u32[]{:S(2)}, u32[]{:S(2)}) collective-permute-start(bf16[496,128]{1,0:T(8,128)(2,1)S(1)} %get-tuple-element.39), channel_id=1, source_target_pairs={{0,8},{8,0},{16,24},{24,16},{1,9},{9,1},{17,25},{25,17},{2,10},{10... | collective-permute-start | bytes 380936 | tf_op jit(solution)/shard_map/ppermute | solution.py:291
  10.3 8.5 %collective-permute-start.11 = (bf16[48,1024]{1,0:T(8,128)(2,1)}, bf16[48,1024]{1,0:T(8,128)(2,1)S(1)}, u32[]{:S(2)}, u32[]{:S(2)}) collective-permute-start(bf16[48,1024]{1,0:T(8,128)(2,1)} %bitcast.9), channel_id=1, source_target_pairs={{0,2},{1,3},{2,0},{3,1},{4,6},{5,7},{6,4},{7,5},{8,10},{9,11},{10,... | collective-permute-start | bytes 294920 | tf_op jit(solution)/shard_map/ppermute | solution.py:288
  12.0 6.8 %collective-permute-start.13 = (bf16[48,1024]{1,0:T(8,128)(2,1)S(1)}, bf16[48,1024]{1,0:T(8,128)(2,1)S(1)}, u32[]{:S(2)}, u32[]{:S(2)}) collective-permute-start(bf16[48,1024]{1,0:T(8,128)(2,1)S(1)} %collective-permute-done.12.refs_2_), channel_id=1, source_target_pairs={{0,2},{1,3},{2,0},{3,1},{4,6},{5,7},{6,4},{7,5},{8,10},{9,11},{10,... | collective-permute-start | bytes 294920 | tf_op jit(solution)/shard_map/ppermute | solution.py:288
  16.0 7.7 %collective-permute-start.5 = (bf16[496,128]{1,0:T(8,128)(2,1)S(1)}, bf16[496,128]{1,0:T(8,128)(2,1)S(1)}, u32[]{:S(2)}, u32[]{:S(2)}) collective-permute-start(bf16[496,128]{1,0:T(8,128)(2,1)S(1)} %get-tuple-element.42), channel_id=1, source_target_pairs={{0,6},{1,7},{2,4},{3,5},{4,2},{5,3},{6,0},{7,1},{8,14},{9,15},{10,... | collective-permute-start | bytes 380936 | tf_op jit(solution)/shard_map/ppermute | solution.py:288
  19.8 23.5 %copy-start = (f32[12,5120]{1,0:T(8,128)S(1)}, f32[12,5120]{1,0:T(8,128)}, u32[]{:S(2)}) copy-start(f32[12,5120]{1,0:T(8,128)} %refs_1_.3) | copy-start | bytes 737284
  19.9 23.5 %copy-start.1 = (f32[12,5120]{1,0:T(8,128)S(1)}, f32[12,5120]{1,0:T(8,128)}, u32[]{:S(2)}) copy-start(f32[12,5120]{1,0:T(8,128)} %refs_2_.3) | copy-start | bytes 737284
  19.9 23.5 %copy-start.2 = (f32[12,5120]{1,0:T(8,128)S(1)}, f32[12,5120]{1,0:T(8,128)}, u32[]{:S(2)}) copy-start(f32[12,5120]{1,0:T(8,128)} %refs_3_.3) | copy-start | bytes 737284
  19.9 13.3 %collective-permute-start.14 = (f32[48,1280]{1,0:T(8,128)S(1)}, f32[48,1280]{1,0:T(8,128)S(1)}, u32[]{:S(2)}, u32[]{:S(2)}) collective-permute-start(f32[48,1280]{1,0:T(8,128)S(1)} %get-tuple-element.52), channel_id=1, source_target_pairs={{0,24},{8,16},{16,8},{24,0},{1,25},{9,17},{17,9},{25,1},{2,26},{10... | collective-permute-start | bytes 737288 | tf_op jit(solution)/shard_map/ppermute | solution.py:291
  21.6 12.5 %collective-permute-start.15 = (f32[48,1280]{1,0:T(8,128)S(1)}, f32[48,1280]{1,0:T(8,128)S(1)}, u32[]{:S(2)}, u32[]{:S(2)}) collective-permute-start(f32[48,1280]{1,0:T(8,128)S(1)} %get-tuple-element.53), channel_id=1, source_target_pairs={{0,16},{8,24},{16,0},{24,8},{1,17},{9,25},{17,1},{25,9},{2,18},{10... | collective-permute-start | bytes 737288 | tf_op jit(solution)/shard_map/ppermute | solution.py:291
  22.9 11.3 %collective-permute-start.16 = (f32[48,1280]{1,0:T(8,128)S(1)}, f32[48,1280]{1,0:T(8,128)S(1)}, u32[]{:S(2)}, u32[]{:S(2)}) collective-permute-start(f32[48,1280]{1,0:T(8,128)S(1)} %get-tuple-element.54), channel_id=1, source_target_pairs={{0,8},{8,0},{16,24},{24,16},{1,9},{9,1},{17,25},{25,17},{2,10},{10... | collective-permute-start | bytes 737288 | tf_op jit(solution)/shard_map/ppermute | solution.py:291
  23.4 7.1 %collective-permute-start.6 = (bf16[496,128]{1,0:T(8,128)(2,1)S(1)}, bf16[496,128]{1,0:T(8,128)(2,1)S(1)}, u32[]{:S(2)}, u32[]{:S(2)}) collective-permute-start(bf16[496,128]{1,0:T(8,128)(2,1)S(1)} %get-tuple-element.43), channel_id=1, source_target_pairs={{0,4},{1,5},{2,6},{3,7},{4,0},{5,1},{6,2},{7,3},{8,12},{9,13},{10,... | collective-permute-start | bytes 380936 | tf_op jit(solution)/shard_map/ppermute | solution.py:288
  23.7 7.6 %collective-permute-start.7 = (bf16[496,128]{1,0:T(8,128)(2,1)S(1)}, bf16[496,128]{1,0:T(8,128)(2,1)S(1)}, u32[]{:S(2)}, u32[]{:S(2)}) collective-permute-start(bf16[496,128]{1,0:T(8,128)(2,1)S(1)} %get-tuple-element.44), channel_id=1, source_target_pairs={{0,2},{1,3},{2,0},{3,1},{4,6},{5,7},{6,4},{7,5},{8,10},{9,11},{10,... | collective-permute-start | bytes 380936 | tf_op jit(solution)/shard_map/ppermute | solution.py:288
  31.8 5.9 %collective-permute-start.10 = (f32[24,640]{1,0:T(8,128)S(1)}, f32[24,640]{1,0:T(8,128)S(1)}, u32[]{:S(2)}, u32[]{:S(2)}) collective-permute-start(f32[24,640]{1,0:T(8,128)S(1)} %get-tuple-element.49), channel_id=1, source_target_pairs={{0,24},{8,16},{16,8},{24,0},{1,25},{9,17},{17,9},{25,1},{2,26},{10... | collective-permute-start | bytes 184328 | tf_op jit(solution)/shard_map/ppermute | solution.py:291
  34.3 6.8 %collective-permute-start.17 = (f32[24,640]{1,0:T(8,128)S(1)}, f32[24,640]{1,0:T(8,128)S(1)}, u32[]{:S(2)}, u32[]{:S(2)}) collective-permute-start(f32[24,640]{1,0:T(8,128)S(1)} %get-tuple-element.56), channel_id=1, source_target_pairs={{0,6},{1,7},{2,4},{3,5},{4,2},{5,3},{6,0},{7,1},{8,14},{9,15},{10,... | collective-permute-start | bytes 184328 | tf_op jit(solution)/shard_map/ppermute | solution.py:288
  35.8 5.0 %collective-permute-start.8 = (f32[24,640]{1,0:T(8,128)S(1)}, f32[24,640]{1,0:T(8,128)S(1)}, u32[]{:S(2)}, u32[]{:S(2)}) collective-permute-start(f32[24,640]{1,0:T(8,128)S(1)} %get-tuple-element.47), channel_id=1, source_target_pairs={{0,8},{8,0},{16,24},{24,16},{1,9},{9,1},{17,25},{25,17},{2,10},{10... | collective-permute-start | bytes 184328 | tf_op jit(solution)/shard_map/ppermute | solution.py:291
  36.6 4.3 %collective-permute-start.9 = (f32[24,640]{1,0:T(8,128)S(1)}, f32[24,640]{1,0:T(8,128)S(1)}, u32[]{:S(2)}, u32[]{:S(2)}) collective-permute-start(f32[24,640]{1,0:T(8,128)S(1)} %get-tuple-element.48), channel_id=1, source_target_pairs={{0,16},{8,24},{16,0},{24,8},{1,17},{9,25},{17,1},{25,9},{2,18},{10... | collective-permute-start | bytes 184328 | tf_op jit(solution)/shard_map/ppermute | solution.py:291
  37.1 5.9 %collective-permute-start.18 = (f32[24,640]{1,0:T(8,128)S(1)}, f32[24,640]{1,0:T(8,128)S(1)}, u32[]{:S(2)}, u32[]{:S(2)}) collective-permute-start(f32[24,640]{1,0:T(8,128)S(1)} %get-tuple-element.57), channel_id=1, source_target_pairs={{0,4},{1,5},{2,6},{3,7},{4,0},{5,1},{6,2},{7,3},{8,12},{9,13},{10,... | collective-permute-start | bytes 184328 | tf_op jit(solution)/shard_map/ppermute | solution.py:288
  37.7 5.7 %collective-permute-start.19 = (f32[24,640]{1,0:T(8,128)S(1)}, f32[24,640]{1,0:T(8,128)S(1)}, u32[]{:S(2)}, u32[]{:S(2)}) collective-permute-start(f32[24,640]{1,0:T(8,128)S(1)} %get-tuple-element.58), channel_id=1, source_target_pairs={{0,2},{1,3},{2,0},{3,1},{4,6},{5,7},{6,4},{7,5},{8,10},{9,11},{10,... | collective-permute-start | bytes 184328 | tf_op jit(solution)/shard_map/ppermute | solution.py:288
  43.7 6.2 %collective-permute-start.20 = (bf16[48,1280]{1,0:T(8,128)(2,1)S(1)}, bf16[48,1280]{1,0:T(8,128)(2,1)S(1)}, u32[]{:S(2)}, u32[]{:S(2)}) collective-permute-start(bf16[48,1280]{1,0:T(8,128)(2,1)S(1)} %shard_map.129.refs_3_), channel_id=1, source_target_pairs={{0,24},{8,16},{16,8},{24,0},{1,25},{9,17},{17,9},{25,1},{2,26},{10... | collective-permute-start | bytes 368648 | tf_op jit(solution)/shard_map/ppermute | solution.py:291
  45.5 5.6 %collective-permute-start.21 = (bf16[48,1280]{1,0:T(8,128)(2,1)S(1)}, bf16[48,1280]{1,0:T(8,128)(2,1)S(1)}, u32[]{:S(2)}, u32[]{:S(2)}) collective-permute-start(bf16[48,1280]{1,0:T(8,128)(2,1)S(1)} %shard_map.129.refs_3_), channel_id=1, source_target_pairs={{0,16},{8,24},{16,0},{24,8},{1,17},{9,25},{17,1},{25,9},{2,18},{10... | collective-permute-start | bytes 368648 | tf_op jit(solution)/shard_map/ppermute | solution.py:291
  46.6 4.9 %collective-permute-start.22 = (bf16[48,1280]{1,0:T(8,128)(2,1)S(1)}, bf16[48,1280]{1,0:T(8,128)(2,1)S(1)}, u32[]{:S(2)}, u32[]{:S(2)}) collective-permute-start(bf16[48,1280]{1,0:T(8,128)(2,1)S(1)} %shard_map.129.refs_3_), channel_id=1, source_target_pairs={{0,8},{8,0},{16,24},{24,16},{1,9},{9,1},{17,25},{25,17},{2,10},{10... | collective-permute-start | bytes 368648 | tf_op jit(solution)/shard_map/ppermute | solution.py:291

commit v12 on v11

--- a/solution.py
+++ b/solution.py
@@ -125,11 +125,15 @@
     rows = dp * shard
     total = chips * rows
     cols = own_ref.shape[1]
-    size = chips * shard
+    half = chips // 2
+    size = half * shard
     r = iota((total, total), 0)
+    near = jnp.where(r >= total // 2, 1, 0)
+    r = r - near * (total // 2)
     t = over(r, size)
     s = over(r - t * size, shard)
     i = r - t * size - s * shard
+    s = s + (1 - near) * half
     order = one_hot(iota((total, total), 1) == s * rows + (t ^ d) * shard + i)
     mask = mask_ref[...].astype(jnp.float32).astype(jnp.bfloat16)
     columns = jnp.concatenate([part[...] for part in parts], axis=0) * mask
@@ -137,8 +141,8 @@
     for at, ref in ((core, own_ref), (1 - core, other_ref)):
         head = exact(columns, ref[...])
         spot = pl.ds(pl.multiple_of(at * cols, LANES), cols)
-        for t, out_ref in enumerate(outs):
-            out_ref[:, spot] = head[t * size : (t + 1) * size]
+        for n, out_ref in enumerate(outs):
+            out_ref[:, spot] = head[n * size : (n + 1) * size]
 
 
 def stacked(rows):
@@ -174,8 +178,8 @@
         out_ref[:, pl.ds(pl.multiple_of((d ^ t) * cols, LANES), cols)] = unstacked(part[...])
 
 
-def sum_kernel(chips, shard, *refs):
-    dp = len(refs) - chips
+def sum_kernel(half, shard, *refs):
+    dp = len(refs) - half
     total = refs[0][...]
     for t in range(1, dp):
         total = total + refs[t][...]
@@ -281,6 +285,7 @@
     cols = hidden.shape[1] * CORES
     owners, cap, width = slot_grads.shape[1:]
     group = cap * chips
+    half = chips // 2
     bf16, f32 = jnp.bfloat16, jnp.float32
 
     def send(x, s, away=0):
@@ -317,7 +322,7 @@
         columns.append(send(columns[s - 1], 1) if s % 2 else send(columns[0], s))
     head = run(
         functools.partial(head_kernel, chips, dp, shard),
-        [shaped((chips * shard, cols), f32)] * dp,
+        [shaped((half * shard, cols), f32)] * (2 * dp),
         predict_mask[None, :],
         held,
         hidden_other,
@@ -328,12 +333,19 @@
         [shaped((2 * shard, quarter // 2), f32)] * dp,
         *[send(messages[s], s) for s in reversed(range(chips))],
     )
-    sums = run(
-        functools.partial(sum_kernel, chips, shard),
-        [shaped((2 * shard, cols // 2), f32)] * chips,
-        *[send_dp(head[t], t) for t in reversed(range(dp))],
-    )
-    pieces = [send(sums[s], s) for s in reversed(range(chips))]
+    pieces = {}
+    for h, members in enumerate((range(half, chips), range(half))):
+        heard = [send_dp(head[h * dp + t], t) for t in reversed(range(dp))]
+        if h:
+            heard[-1], _ = lax.optimization_barrier((heard[-1], sums[0]))
+        sums = run(
+            functools.partial(sum_kernel, half, shard),
+            [shaped((2 * shard, cols // 2), f32)] * half,
+            *heard,
+        )
+        for s, total in zip(members, sums):
+            pieces[s] = send(total, s)
+    pieces = [pieces[s] for s in reversed(range(chips))]
     embed = run(gather_kernel, shaped((shard, width), f32), *[send_dp(embed[t], t) for t in range(dp)])
     state = (embed, master, first_moment, second_moment)
     table = run(rows_kernel, shaped((chips * shard, cols), bf16), *state, *pieces)

time: 52.7 us -> 55.1 us (1.046)
  starting transfers between devices: 32.3 us -> 34.1 us
    ppermute x12 -> x15, waiting for transfers between devices: 5.41 us -> 11.6 us  [send_dp(): return lax.ppermute(x, 'dp', [(i, i ^ t) for i in range(dp)]) if t else x]
    ppermute x11, waiting for transfers between devices: 6.75 us -> 1.14 us  [send(): lax.ppermute(x, 'vocab', [(v, v ^ move) for v in range(vocab)])]
    ppermute x12 -> x15, starting transfers between devices: 13.4 us -> 18.5 us  [send_dp(): return lax.ppermute(x, 'dp', [(i, i ^ t) for i in range(dp)]) if t else x]
    ppermute x11, starting transfers between devices: 18.9 us -> 15.6 us  [send(): lax.ppermute(x, 'vocab', [(v, v ^ move) for v in range(vocab)])]
    pallas_call x11 -> x12, Pallas kernels: 7.3 us -> 7.33 us  [run(): pl.pallas_call(kernel, out_shape=outs, in_specs=[pl.BlockSpec(memory_spac...]
  transfers between devices with their start and end apart: 23 -> 26, of which waited for: 13 -> 12; matrix products, arithmetic and copies ran while one was open for 0% -> 0% of each run, Pallas kernels for 11% -> 11%
where the time goes in v12:
time: 55.1 us; the launch traced here: 54.9 us
  starting transfers between devices  34.1 us (62%)
  waiting for transfers between devices  12.7 us (23%)
  Pallas kernels  7.33 us (13%)
  between operations  0.77 us (1%)
    ppermute x15, starting transfers between devices, send_dp(): return lax.ppermute(x, 'dp', [(i, i ^ t) for i in range(dp)]) if t else x  18.5 us
    ppermute x11, starting transfers between devices, send(): lax.ppermute(x, 'vocab', [(v, v ^ move) for v in range(vocab)])  15.6 us
    ppermute x15, waiting for transfers between devices, send_dp(): return lax.ppermute(x, 'dp', [(i, i ^ t) for i in range(dp)]) if t else x  11.6 us
    pallas_call x12, Pallas kernels, run(): pl.pallas_call(kernel, out_shape=outs, in_specs=[pl.BlockSpec(memory_spac...  7.33 us
    ppermute x11, waiting for transfers between devices, send(): lax.ppermute(x, 'vocab', [(v, v ^ move) for v in range(vocab)])  1.14 us
  transfers between devices with their start and end apart: 26, of which 12 were waited for; matrix products, arithmetic and copies ran while one was open for 0% of the time, Pallas kernels for 11%

profile of v12, /device:TPU:0, one launch (start us, length us, event | category | flops | bytes accessed | tf_op | source)
XLA Modules:
  0.0 54.9 jit_solution(13835737895276494680)
XLA Ops:
  0.6 0.5 collective-permute-start.1
  1.1 1.4 %shard_map.120 = (bf16[24,5248]{1,0:T(8,128)(2,1)S(1)}, bf16[24,5248]{1,0:T(8,128)(2,1)S(1)}) custom-call(bf16[48,5120]{1,0:T(8,128)(2,1)} %bitcast.12, s32[6,1,8]{2,1,0:T(1,128)} %bitcast.13, s32[1,8]{1,0:T(1,128)} %counts_hbm.1), custom_call_target="tpu_custom_call" | custom-call | bytes 995552 | tf_op jit(solution)/shard_map/pallas_call | solution.py:254
  2.5 0.1 collective-permute-start
  2.6 4.0 %collective-permute-start.12 = (bf16[48,1024]{1,0:T(8,128)(2,1)}, bf16[48,1024]{1,0:T(8,128)(2,1)S(1)}, u32[]{:S(2)}, u32[]{:S(2)}) collective-permute-start(bf16[48,1024]{1,0:T(8,128)(2,1)} %bitcast.8), channel_id=1, source_target_pairs={{0,4},{1,5},{2,6},{3,7},{4,0},{5,1},{6,2},{7,3},{8,12},{9,13},{10,... | collective-permute-start | bytes 294920 | tf_op jit(solution)/shard_map/ppermute | solution.py:293
  6.7 0.1 shard_map.121
  6.8 2.5 %collective-permute-start.2 = (bf16[496,128]{1,0:T(8,128)(2,1)S(1)}, bf16[496,128]{1,0:T(8,128)(2,1)S(1)}, u32[]{:S(2)}, u32[]{:S(2)}) collective-permute-start(bf16[496,128]{1,0:T(8,128)(2,1)S(1)} %get-tuple-element.42), channel_id=1, source_target_pairs={{0,24},{8,16},{16,8},{24,0},{1,25},{9,17},{17,9},{25,1},{2,26},{10... | collective-permute-start | bytes 380936 | tf_op jit(solution)/shard_map/ppermute | solution.py:296
  9.3 0.5 collective-permute-start.3
  9.8 0.5 collective-permute-start.4
  10.3 1.6 %collective-permute-start.11 = (bf16[48,1024]{1,0:T(8,128)(2,1)}, bf16[48,1024]{1,0:T(8,128)(2,1)S(1)}, u32[]{:S(2)}, u32[]{:S(2)}) collective-permute-start(bf16[48,1024]{1,0:T(8,128)(2,1)} %bitcast.9), channel_id=1, source_target_pairs={{0,2},{1,3},{2,0},{3,1},{4,6},{5,7},{6,4},{7,5},{8,10},{9,11},{10,... | collective-permute-start | bytes 294920 | tf_op jit(solution)/shard_map/ppermute | solution.py:293
  11.9 0.1 collective-permute-done.12.refs_2_
  12.0 0.8 %collective-permute-start.13 = (bf16[48,1024]{1,0:T(8,128)(2,1)S(1)}, bf16[48,1024]{1,0:T(8,128)(2,1)S(1)}, u32[]{:S(2)}, u32[]{:S(2)}) collective-permute-start(bf16[48,1024]{1,0:T(8,128)(2,1)S(1)} %collective-permute-done.12.refs_2_), channel_id=1, source_target_pairs={{0,2},{1,3},{2,0},{3,1},{4,6},{5,7},{6,4},{7,5},{8,10},{9,11},{10,... | collective-permute-start | bytes 294920 | tf_op jit(solution)/shard_map/ppermute | solution.py:293
  12.9 1.3 %shard_map.122.own_ref = bf16[1024,640]{1,0:T(8,128)(2,1)S(1)} custom-call(bf16[1024,640]{1,0:T(8,128)(2,1)} %hidden_hbm.1), custom_call_target="tpu_custom_call" | custom-call | bytes 2621440 | tf_op jit(solution)/shard_map/pallas_call | solution.py:254
  14.2 1.4 %collective-permute-done.3.refs_1_ = bf16[496,128]{1,0:T(8,128)(2,1)S(1)} collective-permute-done((bf16[496,128]{1,0:T(8,128)(2,1)S(1)}, bf16[496,128]{1,0:T(8,128)(2,1)S(1)}, u32[]{:S(2)}, u32[]{:S(2)}) %collective-permute-start.3) | collective-permute-done | bytes 127008 | tf_op jit(solution)/shard_map/ppermute | solution.py:296
  15.6 0.1 collective-permute-done.4.refs_2_
  15.6 0.4 shard_map.123
  16.0 2.9 %collective-permute-start.5 = (bf16[496,128]{1,0:T(8,128)(2,1)S(1)}, bf16[496,128]{1,0:T(8,128)(2,1)S(1)}, u32[]{:S(2)}, u32[]{:S(2)}) collective-permute-start(bf16[496,128]{1,0:T(8,128)(2,1)S(1)} %get-tuple-element.47), channel_id=1, source_target_pairs={{0,6},{1,7},{2,4},{3,5},{4,2},{5,3},{6,0},{7,1},{8,14},{9,15},{10,... | collective-permute-start | bytes 380936 | tf_op jit(solution)/shard_map/ppermute | solution.py:293
  18.9 0.2 collective-permute-start.6
  19.1 1.4 %collective-permute-start.7 = (bf16[496,128]{1,0:T(8,128)(2,1)S(1)}, bf16[496,128]{1,0:T(8,128)(2,1)S(1)}, u32[]{:S(2)}, u32[]{:S(2)}) collective-permute-start(bf16[496,128]{1,0:T(8,128)(2,1)S(1)} %get-tuple-element.49), channel_id=1, source_target_pairs={{0,2},{1,3},{2,0},{3,1},{4,6},{5,7},{6,4},{7,5},{8,10},{9,11},{10,... | collective-permute-start | bytes 380936 | tf_op jit(solution)/shard_map/ppermute | solution.py:293
  20.5 1.0 %shard_map.126 = (f32[24,1280]{1,0:T(8,128)S(1)}, f32[24,1280]{1,0:T(8,128)S(1)}, f32[24,1280]{1,0:T(8,128)S(1)}, f32[24,1280]{1,0:T(8,128)S(1)}, f32[24,1280]{1...) custom-call(s32[1,1024]{1,0:T(1,128)S(1)} %bitcast.11, ...), custom_call_target="tpu_custom_call" | custom-call | bytes 4001792 | tf_op jit(solution)/shard_map/pallas_call | solution.py:254
  21.4 0.0 copy-start
  21.5 1.7 %collective-permute-start.14 = (f32[24,1280]{1,0:T(8,128)S(1)}, f32[24,1280]{1,0:T(8,128)S(1)}, u32[]{:S(2)}, u32[]{:S(2)}) collective-permute-start(f32[24,1280]{1,0:T(8,128)S(1)} %get-tuple-element.57), channel_id=1, source_target_pairs={{0,24},{8,16},{16,8},{24,0},{1,25},{9,17},{17,9},{25,1},{2,26},{10... | collective-permute-start | bytes 368648 | tf_op jit(solution)/shard_map/ppermute | solution.py:296
  23.2 1.3 %collective-permute-start.15 = (f32[24,1280]{1,0:T(8,128)S(1)}, f32[24,1280]{1,0:T(8,128)S(1)}, u32[]{:S(2)}, u32[]{:S(2)}) collective-permute-start(f32[24,1280]{1,0:T(8,128)S(1)} %get-tuple-element.58), channel_id=1, source_target_pairs={{0,16},{8,24},{16,0},{24,8},{1,17},{9,25},{17,1},{25,9},{2,18},{10... | collective-permute-start | bytes 368648 | tf_op jit(solution)/shard_map/ppermute | solution.py:296
  24.5 2.9 %collective-permute-done.14.refs_0_ = f32[24,1280]{1,0:T(8,128)S(1)} collective-permute-done((f32[24,1280]{1,0:T(8,128)S(1)}, f32[24,1280]{1,0:T(8,128)S(1)}, u32[]{:S(2)}, u32[]{:S(2)}) %collective-permute-start.14) | collective-permute-done | bytes 122912 | tf_op jit(solution)/shard_map/ppermute | solution.py:296
  27.4 1.5 %collective-permute-start.16 = (f32[24,1280]{1,0:T(8,128)S(1)}, f32[24,1280]{1,0:T(8,128)S(1)}, u32[]{:S(2)}, u32[]{:S(2)}) collective-permute-start(f32[24,1280]{1,0:T(8,128)S(1)} %get-tuple-element.59), channel_id=1, source_target_pairs={{0,8},{8,0},{16,24},{24,16},{1,9},{9,1},{17,25},{25,17},{2,10},{10... | collective-permute-start | bytes 368648 | tf_op jit(solution)/shard_map/ppermute | solution.py:296
  29.0 1.3 %collective-permute-start.19 = (f32[24,1280]{1,0:T(8,128)S(1)}, f32[24,1280]{1,0:T(8,128)S(1)}, u32[]{:S(2)}, u32[]{:S(2)}) collective-permute-start(f32[24,1280]{1,0:T(8,128)S(1)} %get-tuple-element.63), channel_id=1, source_target_pairs={{0,24},{8,16},{16,8},{24,0},{1,25},{9,17},{17,9},{25,1},{2,26},{10... | collective-permute-start | bytes 368648 | tf_op jit(solution)/shard_map/ppermute | solution.py:296
  30.3 0.2 collective-permute-done.6.refs_1_
  30.5 1.5 %collective-permute-start.20 = (f32[24,1280]{1,0:T(8,128)S(1)}, f32[24,1280]{1,0:T(8,128)S(1)}, u32[]{:S(2)}, u32[]{:S(2)}) collective-permute-start(f32[24,1280]{1,0:T(8,128)S(1)} %get-tuple-element.64), channel_id=1, source_target_pairs={{0,16},{8,24},{16,0},{24,8},{1,17},{9,25},{17,1},{25,9},{2,18},{10... | collective-permute-start | bytes 368648 | tf_op jit(solution)/shard_map/ppermute | solution.py:296
  32.0 0.4 collective-permute-start.21
  32.5 0.5 shard_map.124
  32.9 1.7 %collective-permute-start.8 = (f32[24,640]{1,0:T(8,128)S(1)}, f32[24,640]{1,0:T(8,128)S(1)}, u32[]{:S(2)}, u32[]{:S(2)}) collective-permute-start(f32[24,640]{1,0:T(8,128)S(1)} %get-tuple-element.52), channel_id=1, source_target_pairs={{0,8},{8,0},{16,24},{24,16},{1,9},{9,1},{17,25},{25,17},{2,10},{10... | collective-permute-start | bytes 184328 | tf_op jit(solution)/shard_map/ppermute | solution.py:296
  34.6 0.6 %collective-permute-start.18 = (f32[24,640]{1,0:T(8,128)S(1)}, f32[24,640]{1,0:T(8,128)S(1)}, u32[]{:S(2)}, u32[]{:S(2)}) collective-permute-start(f32[24,640]{1,0:T(8,128)S(1)} %get-tuple-element.62), channel_id=1, source_target_pairs={{0,4},{1,5},{2,6},{3,7},{4,0},{5,1},{6,2},{7,3},{8,12},{9,13},{10,... | collective-permute-start | bytes 184328 | tf_op jit(solution)/shard_map/ppermute | solution.py:293
  35.2 0.7 %collective-permute-done.19.refs_0_ = f32[24,1280]{1,0:T(8,128)S(1)} collective-permute-done((f32[24,1280]{1,0:T(8,128)S(1)}, f32[24,1280]{1,0:T(8,128)S(1)}, u32[]{:S(2)}, u32[]{:S(2)}) %collective-permute-start.19) | collective-permute-done | bytes 122912 | tf_op jit(solution)/shard_map/ppermute | solution.py:296
  36.0 3.3 %collective-permute-start.17 = (f32[24,640]{1,0:T(8,128)S(1)}, f32[24,640]{1,0:T(8,128)S(1)}, u32[]{:S(2)}, u32[]{:S(2)}) collective-permute-start(f32[24,640]{1,0:T(8,128)S(1)} %get-tuple-element.61), channel_id=1, source_target_pairs={{0,6},{1,7},{2,4},{3,5},{4,2},{5,3},{6,0},{7,1},{8,14},{9,15},{10,... | collective-permute-start | bytes 184328 | tf_op jit(solution)/shard_map/ppermute | solution.py:293
  39.3 0.2 collective-permute-start.9
  39.5 1.7 %collective-permute-start.10 = (f32[24,640]{1,0:T(8,128)S(1)}, f32[24,640]{1,0:T(8,128)S(1)}, u32[]{:S(2)}, u32[]{:S(2)}) collective-permute-start(f32[24,640]{1,0:T(8,128)S(1)} %get-tuple-element.54), channel_id=1, source_target_pairs={{0,24},{8,16},{16,8},{24,0},{1,25},{9,17},{17,9},{25,1},{2,26},{10... | collective-permute-start | bytes 184328 | tf_op jit(solution)/shard_map/ppermute | solution.py:296
  41.2 0.1 collective-permute-start.22
  41.3 2.2 %collective-permute-done.9.refs_2_ = f32[24,640]{1,0:T(8,128)S(1)} collective-permute-done((f32[24,640]{1,0:T(8,128)S(1)}, f32[24,640]{1,0:T(8,128)S(1)}, u32[]{:S(2)}, u32[]{:S(2)}) %collective-permute-start.9) | collective-permute-done | bytes 61472 | tf_op jit(solution)/shard_map/ppermute | solution.py:296
  43.5 1.1 %collective-permute-done.10.refs_3_ = f32[24,640]{1,0:T(8,128)S(1)} collective-permute-done((f32[24,640]{1,0:T(8,128)S(1)}, f32[24,640]{1,0:T(8,128)S(1)}, u32[]{:S(2)}, u32[]{:S(2)}) %collective-permute-start.10) | collective-permute-done | bytes 61472 | tf_op jit(solution)/shard_map/ppermute | solution.py:296
  44.7 0.8 %collective-permute-done.22.refs_6_ = f32[24,640]{1,0:T(8,128)S(1)} collective-permute-done((f32[24,640]{1,0:T(8,128)S(1)}, f32[24,640]{1,0:T(8,128)S(1)}, u32[]{:S(2)}, u32[]{:S(2)}) %collective-permute-start.22) | collective-permute-done | bytes 61472 | tf_op jit(solution)/shard_map/ppermute | solution.py:293
  45.5 0.3 shard_map.130.refs_3_
  45.8 1.3 %collective-permute-start.23 = (bf16[48,1280]{1,0:T(8,128)(2,1)S(1)}, bf16[48,1280]{1,0:T(8,128)(2,1)S(1)}, u32[]{:S(2)}, u32[]{:S(2)}) collective-permute-start(bf16[48,1280]{1,0:T(8,128)(2,1)S(1)} %shard_map.130.refs_3_), channel_id=1, source_target_pairs={{0,24},{8,16},{16,8},{24,0},{1,25},{9,17},{17,9},{25,1},{2,26},{10... | collective-permute-start | bytes 368648 | tf_op jit(solution)/shard_map/ppermute | solution.py:296
  47.1 1.8 %collective-permute-start.24 = (bf16[48,1280]{1,0:T(8,128)(2,1)S(1)}, bf16[48,1280]{1,0:T(8,128)(2,1)S(1)}, u32[]{:S(2)}, u32[]{:S(2)}) collective-permute-start(bf16[48,1280]{1,0:T(8,128)(2,1)S(1)} %shard_map.130.refs_3_), channel_id=1, source_target_pairs={{0,16},{8,24},{16,0},{24,8},{1,17},{9,25},{17,1},{25,9},{2,18},{10... | collective-permute-start | bytes 368648 | tf_op jit(solution)/shard_map/ppermute | solution.py:296
  49.0 0.4 collective-permute-start.25
  49.3 1.3 %shard_map.129 = (f32[12,5120]{1,0:T(8,128)}, f32[12,5120]{1,0:T(8,128)}, f32[12,5120]{1,0:T(8,128)}, bf16[192,192]{1,0:T(8,128)(2,1)S(1)}) custom-call(f32[12,5120]{1,0:T(8,128)S(1)} %shard_map.125.refs_0_, f32[12,5120]{1,0:T(8,128)S(1)} %copy-done, f32[12,5120]{1,0:T(8,128)S(1)} %copy-done.1, f32[12,5120]{1,0:T(8,128)S(1)} %copy-done.2, ...), custom_call_target="tpu_custom_call" | custom-call | bytes 2039808 | tf_op jit(solution)/shard_map/pallas_call | solution.py:254
  50.6 1.1 %collective-permute-done.23.refs_0_ = bf16[48,1280]{1,0:T(8,128)(2,1)S(1)} collective-permute-done((bf16[48,1280]{1,0:T(8,128)(2,1)S(1)}, bf16[48,1280]{1,0:T(8,128)(2,1)S(1)}, u32[]{:S(2)}, u32[]{:S(2)}) %collective-permute-start.23) | collective-permute-done | bytes 122912 | tf_op jit(solution)/shard_map/ppermute | solution.py:296
  51.7 1.2 %collective-permute-done.24.refs_1_ = bf16[48,1280]{1,0:T(8,128)(2,1)S(1)} collective-permute-done((bf16[48,1280]{1,0:T(8,128)(2,1)S(1)}, bf16[48,1280]{1,0:T(8,128)(2,1)S(1)}, u32[]{:S(2)}, u32[]{:S(2)}) %collective-permute-start.24) | collective-permute-done | bytes 122912 | tf_op jit(solution)/shard_map/ppermute | solution.py:296
  52.9 0.9 %collective-permute-done.25.refs_2_ = bf16[48,1280]{1,0:T(8,128)(2,1)S(1)} collective-permute-done((bf16[48,1280]{1,0:T(8,128)(2,1)S(1)}, bf16[48,1280]{1,0:T(8,128)(2,1)S(1)}, u32[]{:S(2)}, u32[]{:S(2)}) %collective-permute-start.25) | collective-permute-done | bytes 122912 | tf_op jit(solution)/shard_map/ppermute | solution.py:296
  53.9 1.1 %shard_map.131 = bf16[48,5120]{1,0:T(8,128)(2,1)} custom-call(bf16[192,192]{1,0:T(8,128)(2,1)S(1)} %get-tuple-element.73.order_ref, bf16[48,1280]{1,0:T(8,128)(2,1)S(1)} %collective-permute-done.23.refs_0_, bf16[48,1280]{1,0:T(8,128)(2,1)S(1)} %collective-permute-done.24.refs_1_, bf16[48,1280]{1,0:T(8,128)(2,1)S(1)} %collective-permute-done.25.refs_2_, ...), custom_call_target="tpu_custom_call" | custom-call | bytes 1056768 | tf_op jit(solution)/shard_map/pallas_call | solution.py:254
  (26 shorter events, 0.2 us)
Async XLA Ops:
  0.6 6.1 %collective-permute-start.1 = (bf16[1024,640]{1,0:T(8,128)(2,1)}, bf16[1024,640]{1,0:T(8,128)(2,1)S(1)}, u32[]{:S(2)}, u32[]{:S(2)}) collective-permute-start(bf16[1024,640]{1,0:T(8,128)(2,1)} %hidden_hbm.1), channel_id=1, source_target_pairs={{0,1},{1,0},{2,3},{3,2},{4,5},{5,4},{6,7},{7,6},{8,9},{9,8},{10,11... | collective-permute-start | bytes 3932168 | tf_op jit(solution)/shard_map/ppermute | solution.py:293
  2.5 4.2 %collective-permute-start = (bf16[24,5248]{1,0:T(8,128)(2,1)S(1)}, bf16[24,5248]{1,0:T(8,128)(2,1)S(1)}, u32[]{:S(2)}, u32[]{:S(2)}) collective-permute-start(bf16[24,5248]{1,0:T(8,128)(2,1)S(1)} %get-tuple-element.40), channel_id=1, source_target_pairs={{0,1},{1,0},{2,3},{3,2},{4,5},{5,4},{6,7},{7,6},{8,9},{9,8},{10,11... | collective-permute-start | bytes 755720 | tf_op jit(solution)/shard_map/ppermute | solution.py:293
  2.6 9.4 %collective-permute-start.12 = (bf16[48,1024]{1,0:T(8,128)(2,1)}, bf16[48,1024]{1,0:T(8,128)(2,1)S(1)}, u32[]{:S(2)}, u32[]{:S(2)}) collective-permute-start(bf16[48,1024]{1,0:T(8,128)(2,1)} %bitcast.8), channel_id=1, source_target_pairs={{0,4},{1,5},{2,6},{3,7},{4,0},{5,1},{6,2},{7,3},{8,12},{9,13},{10,... | collective-permute-start | bytes 294920 | tf_op jit(solution)/shard_map/ppermute | solution.py:293
  6.8 7.4 %collective-permute-start.2 = (bf16[496,128]{1,0:T(8,128)(2,1)S(1)}, bf16[496,128]{1,0:T(8,128)(2,1)S(1)}, u32[]{:S(2)}, u32[]{:S(2)}) collective-permute-start(bf16[496,128]{1,0:T(8,128)(2,1)S(1)} %get-tuple-element.42), channel_id=1, source_target_pairs={{0,24},{8,16},{16,8},{24,0},{1,25},{9,17},{17,9},{25,1},{2,26},{10... | collective-permute-start | bytes 380936 | tf_op jit(solution)/shard_map/ppermute | solution.py:296
  9.3 6.3 %collective-permute-start.3 = (bf16[496,128]{1,0:T(8,128)(2,1)S(1)}, bf16[496,128]{1,0:T(8,128)(2,1)S(1)}, u32[]{:S(2)}, u32[]{:S(2)}) collective-permute-start(bf16[496,128]{1,0:T(8,128)(2,1)S(1)} %get-tuple-element.43), channel_id=1, source_target_pairs={{0,16},{8,24},{16,0},{24,8},{1,17},{9,25},{17,1},{25,9},{2,18},{10... | collective-permute-start | bytes 380936 | tf_op jit(solution)/shard_map/ppermute | solution.py:296
  9.8 10.7 %copy-start.3 = (bf16[1024,48]{0,1:T(8,128)(2,1)S(1)}, bf16[1024,48]{0,1:T(8,128)(2,1)}, u32[]{:S(2)}) copy-start(bf16[1024,48]{0,1:T(8,128)(2,1)} %param.10) | copy-start | bytes 294916
  9.8 10.7 %copy-start.4 = (s32[1024]{0:T(1024)S(1)}, s32[1024]{0:T(1024)}, u32[]{:S(2)}) copy-start(s32[1024]{0:T(1024)} %param.11) | copy-start | bytes 12292
  9.8 5.8 %collective-permute-start.4 = (bf16[496,128]{1,0:T(8,128)(2,1)S(1)}, bf16[496,128]{1,0:T(8,128)(2,1)S(1)}, u32[]{:S(2)}, u32[]{:S(2)}) collective-permute-start(bf16[496,128]{1,0:T(8,128)(2,1)S(1)} %get-tuple-element.44), channel_id=1, source_target_pairs={{0,8},{8,0},{16,24},{24,16},{1,9},{9,1},{17,25},{25,17},{2,10},{10... | collective-permute-start | bytes 380936 | tf_op jit(solution)/shard_map/ppermute | solution.py:296
  10.3 10.1 %collective-permute-start.11 = (bf16[48,1024]{1,0:T(8,128)(2,1)}, bf16[48,1024]{1,0:T(8,128)(2,1)S(1)}, u32[]{:S(2)}, u32[]{:S(2)}) collective-permute-start(bf16[48,1024]{1,0:T(8,128)(2,1)} %bitcast.9), channel_id=1, source_target_pairs={{0,2},{1,3},{2,0},{3,1},{4,6},{5,7},{6,4},{7,5},{8,10},{9,11},{10,... | collective-permute-start | bytes 294920 | tf_op jit(solution)/shard_map/ppermute | solution.py:293
  12.0 8.4 %collective-permute-start.13 = (bf16[48,1024]{1,0:T(8,128)(2,1)S(1)}, bf16[48,1024]{1,0:T(8,128)(2,1)S(1)}, u32[]{:S(2)}, u32[]{:S(2)}) collective-permute-start(bf16[48,1024]{1,0:T(8,128)(2,1)S(1)} %collective-permute-done.12.refs_2_), channel_id=1, source_target_pairs={{0,2},{1,3},{2,0},{3,1},{4,6},{5,7},{6,4},{7,5},{8,10},{9,11},{10,... | collective-permute-start | bytes 294920 | tf_op jit(solution)/shard_map/ppermute | solution.py:293
  16.0 13.0 %collective-permute-start.5 = (bf16[496,128]{1,0:T(8,128)(2,1)S(1)}, bf16[496,128]{1,0:T(8,128)(2,1)S(1)}, u32[]{:S(2)}, u32[]{:S(2)}) collective-permute-start(bf16[496,128]{1,0:T(8,128)(2,1)S(1)} %get-tuple-element.47), channel_id=1, source_target_pairs={{0,6},{1,7},{2,4},{3,5},{4,2},{5,3},{6,0},{7,1},{8,14},{9,15},{10,... | collective-permute-start | bytes 380936 | tf_op jit(solution)/shard_map/ppermute | solution.py:293
  18.9 11.6 %collective-permute-start.6 = (bf16[496,128]{1,0:T(8,128)(2,1)S(1)}, bf16[496,128]{1,0:T(8,128)(2,1)S(1)}, u32[]{:S(2)}, u32[]{:S(2)}) collective-permute-start(bf16[496,128]{1,0:T(8,128)(2,1)S(1)} %get-tuple-element.48), channel_id=1, source_target_pairs={{0,4},{1,5},{2,6},{3,7},{4,0},{5,1},{6,2},{7,3},{8,12},{9,13},{10,... | collective-permute-start | bytes 380936 | tf_op jit(solution)/shard_map/ppermute | solution.py:293
  19.1 12.9 %collective-permute-start.7 = (bf16[496,128]{1,0:T(8,128)(2,1)S(1)}, bf16[496,128]{1,0:T(8,128)(2,1)S(1)}, u32[]{:S(2)}, u32[]{:S(2)}) collective-permute-start(bf16[496,128]{1,0:T(8,128)(2,1)S(1)} %get-tuple-element.49), channel_id=1, source_target_pairs={{0,2},{1,3},{2,0},{3,1},{4,6},{5,7},{6,4},{7,5},{8,10},{9,11},{10,... | collective-permute-start | bytes 380936 | tf_op jit(solution)/shard_map/ppermute | solution.py:293
  21.4 24.0 %copy-start = (f32[12,5120]{1,0:T(8,128)S(1)}, f32[12,5120]{1,0:T(8,128)}, u32[]{:S(2)}) copy-start(f32[12,5120]{1,0:T(8,128)} %refs_1_.3) | copy-start | bytes 737284
  21.5 24.0 %copy-start.1 = (f32[12,5120]{1,0:T(8,128)S(1)}, f32[12,5120]{1,0:T(8,128)}, u32[]{:S(2)}) copy-start(f32[12,5120]{1,0:T(8,128)} %refs_2_.3) | copy-start | bytes 737284
  21.5 24.0 %copy-start.2 = (f32[12,5120]{1,0:T(8,128)S(1)}, f32[12,5120]{1,0:T(8,128)}, u32[]{:S(2)}) copy-start(f32[12,5120]{1,0:T(8,128)} %refs_3_.3) | copy-start | bytes 737284
  21.5 6.0 %collective-permute-start.14 = (f32[24,1280]{1,0:T(8,128)S(1)}, f32[24,1280]{1,0:T(8,128)S(1)}, u32[]{:S(2)}, u32[]{:S(2)}) collective-permute-start(f32[24,1280]{1,0:T(8,128)S(1)} %get-tuple-element.57), channel_id=1, source_target_pairs={{0,24},{8,16},{16,8},{24,0},{1,25},{9,17},{17,9},{25,1},{2,26},{10... | collective-permute-start | bytes 368648 | tf_op jit(solution)/shard_map/ppermute | solution.py:296
  23.2 9.7 %collective-permute-start.15 = (f32[24,1280]{1,0:T(8,128)S(1)}, f32[24,1280]{1,0:T(8,128)S(1)}, u32[]{:S(2)}, u32[]{:S(2)}) collective-permute-start(f32[24,1280]{1,0:T(8,128)S(1)} %get-tuple-element.58), channel_id=1, source_target_pairs={{0,16},{8,24},{16,0},{24,8},{1,17},{9,25},{17,1},{25,9},{2,18},{10... | collective-permute-start | bytes 368648 | tf_op jit(solution)/shard_map/ppermute | solution.py:296
  27.4 7.2 %collective-permute-start.16 = (f32[24,1280]{1,0:T(8,128)S(1)}, f32[24,1280]{1,0:T(8,128)S(1)}, u32[]{:S(2)}, u32[]{:S(2)}) collective-permute-start(f32[24,1280]{1,0:T(8,128)S(1)} %get-tuple-element.59), channel_id=1, source_target_pairs={{0,8},{8,0},{16,24},{24,16},{1,9},{9,1},{17,25},{25,17},{2,10},{10... | collective-permute-start | bytes 368648 | tf_op jit(solution)/shard_map/ppermute | solution.py:296
  29.0 7.0 %collective-permute-start.19 = (f32[24,1280]{1,0:T(8,128)S(1)}, f32[24,1280]{1,0:T(8,128)S(1)}, u32[]{:S(2)}, u32[]{:S(2)}) collective-permute-start(f32[24,1280]{1,0:T(8,128)S(1)} %get-tuple-element.63), channel_id=1, source_target_pairs={{0,24},{8,16},{16,8},{24,0},{1,25},{9,17},{17,9},{25,1},{2,26},{10... | collective-permute-start | bytes 368648 | tf_op jit(solution)/shard_map/ppermute | solution.py:296
  30.5 8.8 %collective-permute-start.20 = (f32[24,1280]{1,0:T(8,128)S(1)}, f32[24,1280]{1,0:T(8,128)S(1)}, u32[]{:S(2)}, u32[]{:S(2)}) collective-permute-start(f32[24,1280]{1,0:T(8,128)S(1)} %get-tuple-element.64), channel_id=1, source_target_pairs={{0,16},{8,24},{16,0},{24,8},{1,17},{9,25},{17,1},{25,9},{2,18},{10... | collective-permute-start | bytes 368648 | tf_op jit(solution)/shard_map/ppermute | solution.py:296
  32.0 7.5 %collective-permute-start.21 = (f32[24,1280]{1,0:T(8,128)S(1)}, f32[24,1280]{1,0:T(8,128)S(1)}, u32[]{:S(2)}, u32[]{:S(2)}) collective-permute-start(f32[24,1280]{1,0:T(8,128)S(1)} %get-tuple-element.65), channel_id=1, source_target_pairs={{0,8},{8,0},{16,24},{24,16},{1,9},{9,1},{17,25},{25,17},{2,10},{10... | collective-permute-start | bytes 368648 | tf_op jit(solution)/shard_map/ppermute | solution.py:296
  32.9 8.2 %collective-permute-start.8 = (f32[24,640]{1,0:T(8,128)S(1)}, f32[24,640]{1,0:T(8,128)S(1)}, u32[]{:S(2)}, u32[]{:S(2)}) collective-permute-start(f32[24,640]{1,0:T(8,128)S(1)} %get-tuple-element.52), channel_id=1, source_target_pairs={{0,8},{8,0},{16,24},{24,16},{1,9},{9,1},{17,25},{25,17},{2,10},{10... | collective-permute-start | bytes 184328 | tf_op jit(solution)/shard_map/ppermute | solution.py:296
  34.6 10.0 %collective-permute-start.18 = (f32[24,640]{1,0:T(8,128)S(1)}, f32[24,640]{1,0:T(8,128)S(1)}, u32[]{:S(2)}, u32[]{:S(2)}) collective-permute-start(f32[24,640]{1,0:T(8,128)S(1)} %get-tuple-element.62), channel_id=1, source_target_pairs={{0,4},{1,5},{2,6},{3,7},{4,0},{5,1},{6,2},{7,3},{8,12},{9,13},{10,... | collective-permute-start | bytes 184328 | tf_op jit(solution)/shard_map/ppermute | solution.py:293
  36.0 8.7 %collective-permute-start.17 = (f32[24,640]{1,0:T(8,128)S(1)}, f32[24,640]{1,0:T(8,128)S(1)}, u32[]{:S(2)}, u32[]{:S(2)}) collective-permute-start(f32[24,640]{1,0:T(8,128)S(1)} %get-tuple-element.61), channel_id=1, source_target_pairs={{0,6},{1,7},{2,4},{3,5},{4,2},{5,3},{6,0},{7,1},{8,14},{9,15},{10,... | collective-permute-start | bytes 184328 | tf_op jit(solution)/shard_map/ppermute | solution.py:293
  39.3 4.2 %collective-permute-start.9 = (f32[24,640]{1,0:T(8,128)S(1)}, f32[24,640]{1,0:T(8,128)S(1)}, u32[]{:S(2)}, u32[]{:S(2)}) collective-permute-start(f32[24,640]{1,0:T(8,128)S(1)} %get-tuple-element.53), channel_id=1, source_target_pairs={{0,16},{8,24},{16,0},{24,8},{1,17},{9,25},{17,1},{25,9},{2,18},{10... | collective-permute-start | bytes 184328 | tf_op jit(solution)/shard_map/ppermute | solution.py:296
  39.5 5.1 %collective-permute-start.10 = (f32[24,640]{1,0:T(8,128)S(1)}, f32[24,640]{1,0:T(8,128)S(1)}, u32[]{:S(2)}, u32[]{:S(2)}) collective-permute-start(f32[24,640]{1,0:T(8,128)S(1)} %get-tuple-element.54), channel_id=1, source_target_pairs={{0,24},{8,16},{16,8},{24,0},{1,25},{9,17},{17,9},{25,1},{2,26},{10... | collective-permute-start | bytes 184328 | tf_op jit(solution)/shard_map/ppermute | solution.py:296
  41.2 4.3 %collective-permute-start.22 = (f32[24,640]{1,0:T(8,128)S(1)}, f32[24,640]{1,0:T(8,128)S(1)}, u32[]{:S(2)}, u32[]{:S(2)}) collective-permute-start(f32[24,640]{1,0:T(8,128)S(1)} %get-tuple-element.68), channel_id=1, source_target_pairs={{0,2},{1,3},{2,0},{3,1},{4,6},{5,7},{6,4},{7,5},{8,10},{9,11},{10,... | collective-permute-start | bytes 184328 | tf_op jit(solution)/shard_map/ppermute | solution.py:293
  45.8 5.9 %collective-permute-start.23 = (bf16[48,1280]{1,0:T(8,128)(2,1)S(1)}, bf16[48,1280]{1,0:T(8,128)(2,1)S(1)}, u32[]{:S(2)}, u32[]{:S(2)}) collective-permute-start(bf16[48,1280]{1,0:T(8,128)(2,1)S(1)} %shard_map.130.refs_3_), channel_id=1, source_target_pairs={{0,24},{8,16},{16,8},{24,0},{1,25},{9,17},{17,9},{25,1},{2,26},{10... | collective-permute-start | bytes 368648 | tf_op jit(solution)/shard_map/ppermute | solution.py:296
  47.1 5.8 %collective-permute-start.24 = (bf16[48,1280]{1,0:T(8,128)(2,1)S(1)}, bf16[48,1280]{1,0:T(8,128)(2,1)S(1)}, u32[]{:S(2)}, u32[]{:S(2)}) collective-permute-start(bf16[48,1280]{1,0:T(8,128)(2,1)S(1)} %shard_map.130.refs_3_), channel_id=1, source_target_pairs={{0,16},{8,24},{16,0},{24,8},{1,17},{9,25},{17,1},{25,9},{2,18},{10... | collective-permute-start | bytes 368648 | tf_op jit(solution)/shard_map/ppermute | solution.py:296
  49.0 4.9 %collective-permute-start.25 = (bf16[48,1280]{1,0:T(8,128)(2,1)S(1)}, bf16[48,1280]{1,0:T(8,128)(2,1)S(1)}, u32[]{:S(2)}, u32[]{:S(2)}) collective-permute-start(bf16[48,1280]{1,0:T(8,128)(2,1)S(1)} %shard_map.130.refs_3_), channel_id=1, source_target_pairs={{0,8},{8,0},{16,24},{24,16},{1,9},{9,1},{17,25},{25,17},{2,10},{10... | collective-permute-start | bytes 368648 | tf_op jit(solution)/shard_map/ppermute | solution.py:296

commit v13 on v11

--- a/solution.py
+++ b/solution.py
@@ -199,24 +199,25 @@
     return pl.ds(pl.multiple_of((z ^ s) * cols, LANES), cols)
 
 
-def rows_kernel(*refs):
+def rows_kernel(members, *refs):
     d, z, core = place()
     state, pieces, out_ref = refs[:4], refs[4:-1], refs[-1]
-    table = [step(chip_spot(z, s, piece), piece, *state)[0] for s, piece in enumerate(reversed(pieces))]
+    table = [step(chip_spot(z, s, piece), piece, *state)[0] for s, piece in zip(members, pieces)]
+    table = [table[members.index(s)] for s in range(len(members))]
     out_ref[...] = jnp.concatenate(table, axis=0).astype(jnp.bfloat16)
 
 
-def adam_kernel(chips, dp, shard, *refs):
+def adam_kernel(members, dp, shard, *refs):
     d, z, core = place()
     state, pieces, outs, order_ref = refs[:4], refs[4:-4], refs[-4:-1], refs[-1]
     rows = dp * shard
-    total = chips * rows
+    total = len(members) * rows
     r = iota((total, total), 0)
     s = over(r, rows)
     e = over(r - s * rows, shard)
     i = r - s * rows - e * shard
-    order_ref[...] = one_hot(iota((total, total), 1) == ((e ^ d) * chips + s) * shard + i)
-    for s, piece in enumerate(reversed(pieces)):
+    order_ref[...] = one_hot(iota((total, total), 1) == ((e ^ d) * len(members) + s) * shard + i)
+    for s, piece in zip(members, pieces):
         spot = chip_spot(z, s, piece)
         for out_ref, value in zip(outs, step(spot, piece, *state)):
             out_ref[:, spot] = value
@@ -281,6 +282,7 @@
     cols = hidden.shape[1] * CORES
     owners, cap, width = slot_grads.shape[1:]
     group = cap * chips
+    far_first = (*range(chips // 2, chips), *reversed(range(chips // 2)))
     bf16, f32 = jnp.bfloat16, jnp.float32
 
     def send(x, s, away=0):
@@ -326,19 +328,19 @@
     embed = run(
         functools.partial(embed_kernel, dp, shard, quarter),
         [shaped((2 * shard, quarter // 2), f32)] * dp,
-        *[send(messages[s], s) for s in reversed(range(chips))],
+        *[send(messages[s], s) for s in far_first],
     )
     sums = run(
         functools.partial(sum_kernel, chips, shard),
         [shaped((2 * shard, cols // 2), f32)] * chips,
         *[send_dp(head[t], t) for t in reversed(range(dp))],
     )
-    pieces = [send(sums[s], s) for s in reversed(range(chips))]
+    pieces = [send(sums[s], s) for s in far_first]
     embed = run(gather_kernel, shaped((shard, width), f32), *[send_dp(embed[t], t) for t in range(dp)])
     state = (embed, master, first_moment, second_moment)
-    table = run(rows_kernel, shaped((chips * shard, cols), bf16), *state, *pieces)
+    table = run(functools.partial(rows_kernel, far_first), shaped((chips * shard, cols), bf16), *state, *pieces)
     master_new, first_new, second_new, order = run(
-        functools.partial(adam_kernel, chips, dp, shard),
+        functools.partial(adam_kernel, far_first, dp, shard),
         [shaped(master.shape, f32)] * 3 + [shaped((chips * rows, chips * rows), bf16)],
         *state,
         *pieces,

time: 52.7 us -> 52.9 us (level)
  waiting for transfers between devices: 12.2 us -> 15.3 us
  starting transfers between devices: 32.3 us -> 29.4 us
    ppermute x11, starting transfers between devices: 18.9 us -> 14.3 us  [send(): lax.ppermute(x, 'vocab', [(v, v ^ move) for v in range(vocab)])]
    ppermute x11, waiting for transfers between devices: 6.75 us -> 9.48 us  [send(): lax.ppermute(x, 'vocab', [(v, v ^ move) for v in range(vocab)])]
    ppermute x12, starting transfers between devices: 13.4 us -> 15 us  [send_dp(): return lax.ppermute(x, 'dp', [(i, i ^ t) for i in range(dp)]) if t else x]
where the time goes in v13:
time: 52.9 us; the launch traced here: 52.8 us
  starting transfers between devices  29.4 us (56%)
  waiting for transfers between devices  15.3 us (29%)
  Pallas kernels  7.31 us (14%)
  between operations  0.74 us (1%)
    ppermute x12, starting transfers between devices, send_dp(): return lax.ppermute(x, 'dp', [(i, i ^ t) for i in range(dp)]) if t else x  15 us
    ppermute x11, starting transfers between devices, send(): lax.ppermute(x, 'vocab', [(v, v ^ move) for v in range(vocab)])  14.3 us
    ppermute x11, waiting for transfers between devices, send(): lax.ppermute(x, 'vocab', [(v, v ^ move) for v in range(vocab)])  9.48 us
    pallas_call x11, Pallas kernels, run(): pl.pallas_call(kernel, out_shape=outs, in_specs=[pl.BlockSpec(memory_spac...  7.31 us
    ppermute x12, waiting for transfers between devices, send_dp(): return lax.ppermute(x, 'dp', [(i, i ^ t) for i in range(dp)]) if t else x  5.86 us
  transfers between devices with their start and end apart: 23, of which 13 were waited for; matrix products, arithmetic and copies ran while one was open for 0% of the time, Pallas kernels for 11%

profile of v13, /device:TPU:0, one launch (start us, length us, event | category | flops | bytes accessed | tf_op | source)
XLA Modules:
  0.0 52.8 jit_solution(2648893635248086371)
XLA Ops:
  0.6 0.5 collective-permute-start.1
  1.1 1.4 %shard_map.120 = (bf16[24,5248]{1,0:T(8,128)(2,1)S(1)}, bf16[24,5248]{1,0:T(8,128)(2,1)S(1)}) custom-call(bf16[48,5120]{1,0:T(8,128)(2,1)} %bitcast.12, s32[6,1,8]{2,1,0:T(1,128)} %bitcast.13, s32[1,8]{1,0:T(1,128)} %counts_hbm.1), custom_call_target="tpu_custom_call" | custom-call | bytes 995552 | tf_op jit(solution)/shard_map/pallas_call | solution.py:251
  2.5 0.1 collective-permute-start
  2.6 4.0 %collective-permute-start.12 = (bf16[48,1024]{1,0:T(8,128)(2,1)}, bf16[48,1024]{1,0:T(8,128)(2,1)S(1)}, u32[]{:S(2)}, u32[]{:S(2)}) collective-permute-start(bf16[48,1024]{1,0:T(8,128)(2,1)} %bitcast.8), channel_id=1, source_target_pairs={{0,4},{1,5},{2,6},{3,7},{4,0},{5,1},{6,2},{7,3},{8,12},{9,13},{10,... | collective-permute-start | bytes 294920 | tf_op jit(solution)/shard_map/ppermute | solution.py:290
  6.7 0.1 shard_map.121
  6.8 2.5 %collective-permute-start.2 = (bf16[496,128]{1,0:T(8,128)(2,1)S(1)}, bf16[496,128]{1,0:T(8,128)(2,1)S(1)}, u32[]{:S(2)}, u32[]{:S(2)}) collective-permute-start(bf16[496,128]{1,0:T(8,128)(2,1)S(1)} %get-tuple-element.37), channel_id=1, source_target_pairs={{0,24},{8,16},{16,8},{24,0},{1,25},{9,17},{17,9},{25,1},{2,26},{10... | collective-permute-start | bytes 380936 | tf_op jit(solution)/shard_map/ppermute | solution.py:293
  9.3 0.5 collective-permute-start.3
  9.8 0.5 %collective-permute-start.4 = (bf16[496,128]{1,0:T(8,128)(2,1)S(1)}, bf16[496,128]{1,0:T(8,128)(2,1)S(1)}, u32[]{:S(2)}, u32[]{:S(2)}) collective-permute-start(bf16[496,128]{1,0:T(8,128)(2,1)S(1)} %get-tuple-element.39), channel_id=1, source_target_pairs={{0,8},{8,0},{16,24},{24,16},{1,9},{9,1},{17,25},{25,17},{2,10},{10... | collective-permute-start | bytes 380936 | tf_op jit(solution)/shard_map/ppermute | solution.py:293
  10.3 1.6 %collective-permute-start.11 = (bf16[48,1024]{1,0:T(8,128)(2,1)}, bf16[48,1024]{1,0:T(8,128)(2,1)S(1)}, u32[]{:S(2)}, u32[]{:S(2)}) collective-permute-start(bf16[48,1024]{1,0:T(8,128)(2,1)} %bitcast.9), channel_id=1, source_target_pairs={{0,2},{1,3},{2,0},{3,1},{4,6},{5,7},{6,4},{7,5},{8,10},{9,11},{10,... | collective-permute-start | bytes 294920 | tf_op jit(solution)/shard_map/ppermute | solution.py:290
  11.9 0.1 collective-permute-done.12.refs_2_
  12.0 0.8 %collective-permute-start.13 = (bf16[48,1024]{1,0:T(8,128)(2,1)S(1)}, bf16[48,1024]{1,0:T(8,128)(2,1)S(1)}, u32[]{:S(2)}, u32[]{:S(2)}) collective-permute-start(bf16[48,1024]{1,0:T(8,128)(2,1)S(1)} %collective-permute-done.12.refs_2_), channel_id=1, source_target_pairs={{0,2},{1,3},{2,0},{3,1},{4,6},{5,7},{6,4},{7,5},{8,10},{9,11},{10,... | collective-permute-start | bytes 294920 | tf_op jit(solution)/shard_map/ppermute | solution.py:290
  12.9 1.3 %shard_map.122.own_ref = bf16[1024,640]{1,0:T(8,128)(2,1)S(1)} custom-call(bf16[1024,640]{1,0:T(8,128)(2,1)} %hidden_hbm.1), custom_call_target="tpu_custom_call" | custom-call | bytes 2621440 | tf_op jit(solution)/shard_map/pallas_call | solution.py:251
  14.2 1.4 %collective-permute-done.3.refs_1_ = bf16[496,128]{1,0:T(8,128)(2,1)S(1)} collective-permute-done((bf16[496,128]{1,0:T(8,128)(2,1)S(1)}, bf16[496,128]{1,0:T(8,128)(2,1)S(1)}, u32[]{:S(2)}, u32[]{:S(2)}) %collective-permute-start.3) | collective-permute-done | bytes 127008 | tf_op jit(solution)/shard_map/ppermute | solution.py:293
  15.6 0.1 collective-permute-done.4.refs_2_
  15.6 0.4 shard_map.123
  16.0 2.0 %collective-permute-start.5 = (bf16[496,128]{1,0:T(8,128)(2,1)S(1)}, bf16[496,128]{1,0:T(8,128)(2,1)S(1)}, u32[]{:S(2)}, u32[]{:S(2)}) collective-permute-start(bf16[496,128]{1,0:T(8,128)(2,1)S(1)} %get-tuple-element.42), channel_id=1, source_target_pairs={{0,4},{1,5},{2,6},{3,7},{4,0},{5,1},{6,2},{7,3},{8,12},{9,13},{10,... | collective-permute-start | bytes 380936 | tf_op jit(solution)/shard_map/ppermute | solution.py:290
  18.0 0.0 collective-permute-done.11.refs_1_
  18.0 0.9 %shard_map.126 = (f32[48,1280]{1,0:T(8,128)S(1)}, f32[48,1280]{1,0:T(8,128)S(1)}, f32[48,1280]{1,0:T(8,128)S(1)}, f32[48,1280]{1,0:T(8,128)S(1)}) custom-call(s32[1,1024]{1,0:T(1,128)S(1)} %bitcast.11, bf16[1024,640]{1,0:T(8,128)(2,1)S(1)} %shard_map.122.own_ref, bf16[1024,640]{1,0:T(8,128)(2,1)S(1)} %collective-permute-done.1.other_ref, ...), custom_call_target="tpu_custom_call" | custom-call | bytes 4001792 | tf_op jit(solution)/shard_map/pallas_call | solution.py:251
  19.0 0.0 copy-start
  19.0 0.0 copy-start.1
  19.0 0.0 copy-start.2
  19.0 2.5 %collective-permute-start.14 = (f32[48,1280]{1,0:T(8,128)S(1)}, f32[48,1280]{1,0:T(8,128)S(1)}, u32[]{:S(2)}, u32[]{:S(2)}) collective-permute-start(f32[48,1280]{1,0:T(8,128)S(1)} %get-tuple-element.52), channel_id=1, source_target_pairs={{0,24},{8,16},{16,8},{24,0},{1,25},{9,17},{17,9},{25,1},{2,26},{10... | collective-permute-start | bytes 737288 | tf_op jit(solution)/shard_map/ppermute | solution.py:293
  21.5 0.5 collective-permute-start.15
  22.0 0.5 %collective-permute-start.16 = (f32[48,1280]{1,0:T(8,128)S(1)}, f32[48,1280]{1,0:T(8,128)S(1)}, u32[]{:S(2)}, u32[]{:S(2)}) collective-permute-start(f32[48,1280]{1,0:T(8,128)S(1)} %get-tuple-element.54), channel_id=1, source_target_pairs={{0,8},{8,0},{16,24},{24,16},{1,9},{9,1},{17,25},{25,17},{2,10},{10... | collective-permute-start | bytes 737288 | tf_op jit(solution)/shard_map/ppermute | solution.py:293
  22.6 2.3 %collective-permute-start.6 = (bf16[496,128]{1,0:T(8,128)(2,1)S(1)}, bf16[496,128]{1,0:T(8,128)(2,1)S(1)}, u32[]{:S(2)}, u32[]{:S(2)}) collective-permute-start(bf16[496,128]{1,0:T(8,128)(2,1)S(1)} %get-tuple-element.43), channel_id=1, source_target_pairs={{0,6},{1,7},{2,4},{3,5},{4,2},{5,3},{6,0},{7,1},{8,14},{9,15},{10,... | collective-permute-start | bytes 380936 | tf_op jit(solution)/shard_map/ppermute | solution.py:290
  24.8 0.1 collective-permute-done.5.refs_0_
  25.0 5.2 %collective-permute-done.6.refs_1_ = bf16[496,128]{1,0:T(8,128)(2,1)S(1)} collective-permute-done((bf16[496,128]{1,0:T(8,128)(2,1)S(1)}, bf16[496,128]{1,0:T(8,128)(2,1)S(1)}, u32[]{:S(2)}, u32[]{:S(2)}) %collective-permute-start.6) | collective-permute-done | bytes 127008 | tf_op jit(solution)/shard_map/ppermute | solution.py:290
  30.1 1.0 %collective-permute-done.7.refs_2_ = bf16[496,128]{1,0:T(8,128)(2,1)S(1)} collective-permute-done((bf16[496,128]{1,0:T(8,128)(2,1)S(1)}, bf16[496,128]{1,0:T(8,128)(2,1)S(1)}, u32[]{:S(2)}, u32[]{:S(2)}) %collective-permute-start.7) | collective-permute-done | bytes 127008 | tf_op jit(solution)/shard_map/ppermute | solution.py:290
  31.2 0.5 shard_map.124
  31.6 2.3 %collective-permute-start.10 = (f32[24,640]{1,0:T(8,128)S(1)}, f32[24,640]{1,0:T(8,128)S(1)}, u32[]{:S(2)}, u32[]{:S(2)}) collective-permute-start(f32[24,640]{1,0:T(8,128)S(1)} %get-tuple-element.49), channel_id=1, source_target_pairs={{0,24},{8,16},{16,8},{24,0},{1,25},{9,17},{17,9},{25,1},{2,26},{10... | collective-permute-start | bytes 184328 | tf_op jit(solution)/shard_map/ppermute | solution.py:293
  33.9 0.1 shard_map.127
  34.0 0.6 %collective-permute-start.17 = (f32[24,640]{1,0:T(8,128)S(1)}, f32[24,640]{1,0:T(8,128)S(1)}, u32[]{:S(2)}, u32[]{:S(2)}) collective-permute-start(f32[24,640]{1,0:T(8,128)S(1)} %get-tuple-element.56), channel_id=1, source_target_pairs={{0,4},{1,5},{2,6},{3,7},{4,0},{5,1},{6,2},{7,3},{8,12},{9,13},{10,... | collective-permute-start | bytes 184328 | tf_op jit(solution)/shard_map/ppermute | solution.py:290
  34.6 1.6 %collective-permute-start.8 = (f32[24,640]{1,0:T(8,128)S(1)}, f32[24,640]{1,0:T(8,128)S(1)}, u32[]{:S(2)}, u32[]{:S(2)}) collective-permute-start(f32[24,640]{1,0:T(8,128)S(1)} %get-tuple-element.47), channel_id=1, source_target_pairs={{0,8},{8,0},{16,24},{24,16},{1,9},{9,1},{17,25},{25,17},{2,10},{10... | collective-permute-start | bytes 184328 | tf_op jit(solution)/shard_map/ppermute | solution.py:293
  36.2 0.5 collective-permute-start.9
  36.7 2.3 %collective-permute-start.18 = (f32[24,640]{1,0:T(8,128)S(1)}, f32[24,640]{1,0:T(8,128)S(1)}, u32[]{:S(2)}, u32[]{:S(2)}) collective-permute-start(f32[24,640]{1,0:T(8,128)S(1)} %get-tuple-element.57), channel_id=1, source_target_pairs={{0,6},{1,7},{2,4},{3,5},{4,2},{5,3},{6,0},{7,1},{8,14},{9,15},{10,... | collective-permute-start | bytes 184328 | tf_op jit(solution)/shard_map/ppermute | solution.py:290
  39.1 1.4 %collective-permute-done.9.refs_2_ = f32[24,640]{1,0:T(8,128)S(1)} collective-permute-done((f32[24,640]{1,0:T(8,128)S(1)}, f32[24,640]{1,0:T(8,128)S(1)}, u32[]{:S(2)}, u32[]{:S(2)}) %collective-permute-start.9) | collective-permute-done | bytes 61472 | tf_op jit(solution)/shard_map/ppermute | solution.py:293
  40.5 0.3 collective-permute-done.17.refs_4_
  40.8 2.1 %collective-permute-done.18.refs_5_ = f32[24,640]{1,0:T(8,128)S(1)} collective-permute-done((f32[24,640]{1,0:T(8,128)S(1)}, f32[24,640]{1,0:T(8,128)S(1)}, u32[]{:S(2)}, u32[]{:S(2)}) %collective-permute-start.18) | collective-permute-done | bytes 61472 | tf_op jit(solution)/shard_map/ppermute | solution.py:290
  42.9 0.6 %collective-permute-done.19.refs_6_ = f32[24,640]{1,0:T(8,128)S(1)} collective-permute-done((f32[24,640]{1,0:T(8,128)S(1)}, f32[24,640]{1,0:T(8,128)S(1)}, u32[]{:S(2)}, u32[]{:S(2)}) %collective-permute-start.19) | collective-permute-done | bytes 61472 | tf_op jit(solution)/shard_map/ppermute | solution.py:290
  43.5 0.3 shard_map.129.refs_3_
  43.8 1.5 %collective-permute-start.20 = (bf16[48,1280]{1,0:T(8,128)(2,1)S(1)}, bf16[48,1280]{1,0:T(8,128)(2,1)S(1)}, u32[]{:S(2)}, u32[]{:S(2)}) collective-permute-start(bf16[48,1280]{1,0:T(8,128)(2,1)S(1)} %shard_map.129.refs_3_), channel_id=1, source_target_pairs={{0,24},{8,16},{16,8},{24,0},{1,25},{9,17},{17,9},{25,1},{2,26},{10... | collective-permute-start | bytes 368648 | tf_op jit(solution)/shard_map/ppermute | solution.py:293
  45.3 1.6 %collective-permute-start.21 = (bf16[48,1280]{1,0:T(8,128)(2,1)S(1)}, bf16[48,1280]{1,0:T(8,128)(2,1)S(1)}, u32[]{:S(2)}, u32[]{:S(2)}) collective-permute-start(bf16[48,1280]{1,0:T(8,128)(2,1)S(1)} %shard_map.129.refs_3_), channel_id=1, source_target_pairs={{0,16},{8,24},{16,0},{24,8},{1,17},{9,25},{17,1},{25,9},{2,18},{10... | collective-permute-start | bytes 368648 | tf_op jit(solution)/shard_map/ppermute | solution.py:293
  46.8 0.5 %collective-permute-start.22 = (bf16[48,1280]{1,0:T(8,128)(2,1)S(1)}, bf16[48,1280]{1,0:T(8,128)(2,1)S(1)}, u32[]{:S(2)}, u32[]{:S(2)}) collective-permute-start(bf16[48,1280]{1,0:T(8,128)(2,1)S(1)} %shard_map.129.refs_3_), channel_id=1, source_target_pairs={{0,8},{8,0},{16,24},{24,16},{1,9},{9,1},{17,25},{25,17},{2,10},{10... | collective-permute-start | bytes 368648 | tf_op jit(solution)/shard_map/ppermute | solution.py:293
  47.4 1.3 %shard_map.128 = (f32[12,5120]{1,0:T(8,128)}, f32[12,5120]{1,0:T(8,128)}, f32[12,5120]{1,0:T(8,128)}, bf16[192,192]{1,0:T(8,128)(2,1)S(1)}) custom-call(f32[12,5120]{1,0:T(8,128)S(1)} %shard_map.125.refs_0_, f32[12,5120]{1,0:T(8,128)S(1)} %copy-done, f32[12,5120]{1,0:T(8,128)S(1)} %copy-done.1, f32[12,5120]{1,0:T(8,128)S(1)} %copy-done.2, ...), custom_call_target="tpu_custom_call" | custom-call | bytes 2039808 | tf_op jit(solution)/shard_map/pallas_call | solution.py:251
  48.7 1.1 %collective-permute-done.20.refs_0_ = bf16[48,1280]{1,0:T(8,128)(2,1)S(1)} collective-permute-done((bf16[48,1280]{1,0:T(8,128)(2,1)S(1)}, bf16[48,1280]{1,0:T(8,128)(2,1)S(1)}, u32[]{:S(2)}, u32[]{:S(2)}) %collective-permute-start.20) | collective-permute-done | bytes 122912 | tf_op jit(solution)/shard_map/ppermute | solution.py:293
  49.8 1.2 %collective-permute-done.21.refs_1_ = bf16[48,1280]{1,0:T(8,128)(2,1)S(1)} collective-permute-done((bf16[48,1280]{1,0:T(8,128)(2,1)S(1)}, bf16[48,1280]{1,0:T(8,128)(2,1)S(1)}, u32[]{:S(2)}, u32[]{:S(2)}) %collective-permute-start.21) | collective-permute-done | bytes 122912 | tf_op jit(solution)/shard_map/ppermute | solution.py:293
  51.0 0.7 %collective-permute-done.22.refs_2_ = bf16[48,1280]{1,0:T(8,128)(2,1)S(1)} collective-permute-done((bf16[48,1280]{1,0:T(8,128)(2,1)S(1)}, bf16[48,1280]{1,0:T(8,128)(2,1)S(1)}, u32[]{:S(2)}, u32[]{:S(2)}) %collective-permute-start.22) | collective-permute-done | bytes 122912 | tf_op jit(solution)/shard_map/ppermute | solution.py:293
  51.7 1.1 %shard_map.130 = bf16[48,5120]{1,0:T(8,128)(2,1)} custom-call(bf16[192,192]{1,0:T(8,128)(2,1)S(1)} %get-tuple-element.63.order_ref, bf16[48,1280]{1,0:T(8,128)(2,1)S(1)} %collective-permute-done.20.refs_0_, bf16[48,1280]{1,0:T(8,128)(2,1)S(1)} %collective-permute-done.21.refs_1_, bf16[48,1280]{1,0:T(8,128)(2,1)S(1)} %collective-permute-done.22.refs_2_, ...), custom_call_target="tpu_custom_call" | custom-call | bytes 1056768 | tf_op jit(solution)/shard_map/pallas_call | solution.py:251
  (19 shorter events, 0.1 us)
Async XLA Ops:
  0.6 6.1 %collective-permute-start.1 = (bf16[1024,640]{1,0:T(8,128)(2,1)}, bf16[1024,640]{1,0:T(8,128)(2,1)S(1)}, u32[]{:S(2)}, u32[]{:S(2)}) collective-permute-start(bf16[1024,640]{1,0:T(8,128)(2,1)} %hidden_hbm.1), channel_id=1, source_target_pairs={{0,1},{1,0},{2,3},{3,2},{4,5},{5,4},{6,7},{7,6},{8,9},{9,8},{10,11... | collective-permute-start | bytes 3932168 | tf_op jit(solution)/shard_map/ppermute | solution.py:290
  2.5 4.2 %collective-permute-start = (bf16[24,5248]{1,0:T(8,128)(2,1)S(1)}, bf16[24,5248]{1,0:T(8,128)(2,1)S(1)}, u32[]{:S(2)}, u32[]{:S(2)}) collective-permute-start(bf16[24,5248]{1,0:T(8,128)(2,1)S(1)} %get-tuple-element.35), channel_id=1, source_target_pairs={{0,1},{1,0},{2,3},{3,2},{4,5},{5,4},{6,7},{7,6},{8,9},{9,8},{10,11... | collective-permute-start | bytes 755720 | tf_op jit(solution)/shard_map/ppermute | solution.py:290
  2.6 9.4 %collective-permute-start.12 = (bf16[48,1024]{1,0:T(8,128)(2,1)}, bf16[48,1024]{1,0:T(8,128)(2,1)S(1)}, u32[]{:S(2)}, u32[]{:S(2)}) collective-permute-start(bf16[48,1024]{1,0:T(8,128)(2,1)} %bitcast.8), channel_id=1, source_target_pairs={{0,4},{1,5},{2,6},{3,7},{4,0},{5,1},{6,2},{7,3},{8,12},{9,13},{10,... | collective-permute-start | bytes 294920 | tf_op jit(solution)/shard_map/ppermute | solution.py:290
  6.8 7.4 %collective-permute-start.2 = (bf16[496,128]{1,0:T(8,128)(2,1)S(1)}, bf16[496,128]{1,0:T(8,128)(2,1)S(1)}, u32[]{:S(2)}, u32[]{:S(2)}) collective-permute-start(bf16[496,128]{1,0:T(8,128)(2,1)S(1)} %get-tuple-element.37), channel_id=1, source_target_pairs={{0,24},{8,16},{16,8},{24,0},{1,25},{9,17},{17,9},{25,1},{2,26},{10... | collective-permute-start | bytes 380936 | tf_op jit(solution)/shard_map/ppermute | solution.py:293
  9.3 6.3 %collective-permute-start.3 = (bf16[496,128]{1,0:T(8,128)(2,1)S(1)}, bf16[496,128]{1,0:T(8,128)(2,1)S(1)}, u32[]{:S(2)}, u32[]{:S(2)}) collective-permute-start(bf16[496,128]{1,0:T(8,128)(2,1)S(1)} %get-tuple-element.38), channel_id=1, source_target_pairs={{0,16},{8,24},{16,0},{24,8},{1,17},{9,25},{17,1},{25,9},{2,18},{10... | collective-permute-start | bytes 380936 | tf_op jit(solution)/shard_map/ppermute | solution.py:293
  9.8 8.2 %copy-start.3 = (bf16[1024,48]{0,1:T(8,128)(2,1)S(1)}, bf16[1024,48]{0,1:T(8,128)(2,1)}, u32[]{:S(2)}) copy-start(bf16[1024,48]{0,1:T(8,128)(2,1)} %param.10) | copy-start | bytes 294916
  9.8 8.2 %copy-start.4 = (s32[1024]{0:T(1024)S(1)}, s32[1024]{0:T(1024)}, u32[]{:S(2)}) copy-start(s32[1024]{0:T(1024)} %param.11) | copy-start | bytes 12292
  9.8 5.8 %collective-permute-start.4 = (bf16[496,128]{1,0:T(8,128)(2,1)S(1)}, bf16[496,128]{1,0:T(8,128)(2,1)S(1)}, u32[]{:S(2)}, u32[]{:S(2)}) collective-permute-start(bf16[496,128]{1,0:T(8,128)(2,1)S(1)} %get-tuple-element.39), channel_id=1, source_target_pairs={{0,8},{8,0},{16,24},{24,16},{1,9},{9,1},{17,25},{25,17},{2,10},{10... | collective-permute-start | bytes 380936 | tf_op jit(solution)/shard_map/ppermute | solution.py:293
  10.3 7.7 %collective-permute-start.11 = (bf16[48,1024]{1,0:T(8,128)(2,1)}, bf16[48,1024]{1,0:T(8,128)(2,1)S(1)}, u32[]{:S(2)}, u32[]{:S(2)}) collective-permute-start(bf16[48,1024]{1,0:T(8,128)(2,1)} %bitcast.9), channel_id=1, source_target_pairs={{0,2},{1,3},{2,0},{3,1},{4,6},{5,7},{6,4},{7,5},{8,10},{9,11},{10,... | collective-permute-start | bytes 294920 | tf_op jit(solution)/shard_map/ppermute | solution.py:290
  12.0 6.0 %collective-permute-start.13 = (bf16[48,1024]{1,0:T(8,128)(2,1)S(1)}, bf16[48,1024]{1,0:T(8,128)(2,1)S(1)}, u32[]{:S(2)}, u32[]{:S(2)}) collective-permute-start(bf16[48,1024]{1,0:T(8,128)(2,1)S(1)} %collective-permute-done.12.refs_2_), channel_id=1, source_target_pairs={{0,2},{1,3},{2,0},{3,1},{4,6},{5,7},{6,4},{7,5},{8,10},{9,11},{10,... | collective-permute-start | bytes 294920 | tf_op jit(solution)/shard_map/ppermute | solution.py:290
  16.0 9.0 %collective-permute-start.5 = (bf16[496,128]{1,0:T(8,128)(2,1)S(1)}, bf16[496,128]{1,0:T(8,128)(2,1)S(1)}, u32[]{:S(2)}, u32[]{:S(2)}) collective-permute-start(bf16[496,128]{1,0:T(8,128)(2,1)S(1)} %get-tuple-element.42), channel_id=1, source_target_pairs={{0,4},{1,5},{2,6},{3,7},{4,0},{5,1},{6,2},{7,3},{8,12},{9,13},{10,... | collective-permute-start | bytes 380936 | tf_op jit(solution)/shard_map/ppermute | solution.py:290
  19.0 24.5 %copy-start = (f32[12,5120]{1,0:T(8,128)S(1)}, f32[12,5120]{1,0:T(8,128)}, u32[]{:S(2)}) copy-start(f32[12,5120]{1,0:T(8,128)} %refs_1_.3) | copy-start | bytes 737284
  19.0 24.5 %copy-start.1 = (f32[12,5120]{1,0:T(8,128)S(1)}, f32[12,5120]{1,0:T(8,128)}, u32[]{:S(2)}) copy-start(f32[12,5120]{1,0:T(8,128)} %refs_2_.3) | copy-start | bytes 737284
  19.0 24.5 %copy-start.2 = (f32[12,5120]{1,0:T(8,128)S(1)}, f32[12,5120]{1,0:T(8,128)}, u32[]{:S(2)}) copy-start(f32[12,5120]{1,0:T(8,128)} %refs_3_.3) | copy-start | bytes 737284
  19.0 14.9 %collective-permute-start.14 = (f32[48,1280]{1,0:T(8,128)S(1)}, f32[48,1280]{1,0:T(8,128)S(1)}, u32[]{:S(2)}, u32[]{:S(2)}) collective-permute-start(f32[48,1280]{1,0:T(8,128)S(1)} %get-tuple-element.52), channel_id=1, source_target_pairs={{0,24},{8,16},{16,8},{24,0},{1,25},{9,17},{17,9},{25,1},{2,26},{10... | collective-permute-start | bytes 737288 | tf_op jit(solution)/shard_map/ppermute | solution.py:293
  21.5 12.4 %collective-permute-start.15 = (f32[48,1280]{1,0:T(8,128)S(1)}, f32[48,1280]{1,0:T(8,128)S(1)}, u32[]{:S(2)}, u32[]{:S(2)}) collective-permute-start(f32[48,1280]{1,0:T(8,128)S(1)} %get-tuple-element.53), channel_id=1, source_target_pairs={{0,16},{8,24},{16,0},{24,8},{1,17},{9,25},{17,1},{25,9},{2,18},{10... | collective-permute-start | bytes 737288 | tf_op jit(solution)/shard_map/ppermute | solution.py:293
  22.0 11.9 %collective-permute-start.16 = (f32[48,1280]{1,0:T(8,128)S(1)}, f32[48,1280]{1,0:T(8,128)S(1)}, u32[]{:S(2)}, u32[]{:S(2)}) collective-permute-start(f32[48,1280]{1,0:T(8,128)S(1)} %get-tuple-element.54), channel_id=1, source_target_pairs={{0,8},{8,0},{16,24},{24,16},{1,9},{9,1},{17,25},{25,17},{2,10},{10... | collective-permute-start | bytes 737288 | tf_op jit(solution)/shard_map/ppermute | solution.py:293
  22.6 7.6 %collective-permute-start.6 = (bf16[496,128]{1,0:T(8,128)(2,1)S(1)}, bf16[496,128]{1,0:T(8,128)(2,1)S(1)}, u32[]{:S(2)}, u32[]{:S(2)}) collective-permute-start(bf16[496,128]{1,0:T(8,128)(2,1)S(1)} %get-tuple-element.43), channel_id=1, source_target_pairs={{0,6},{1,7},{2,4},{3,5},{4,2},{5,3},{6,0},{7,1},{8,14},{9,15},{10,... | collective-permute-start | bytes 380936 | tf_op jit(solution)/shard_map/ppermute | solution.py:290
  25.0 6.2 %collective-permute-start.7 = (bf16[496,128]{1,0:T(8,128)(2,1)S(1)}, bf16[496,128]{1,0:T(8,128)(2,1)S(1)}, u32[]{:S(2)}, u32[]{:S(2)}) collective-permute-start(bf16[496,128]{1,0:T(8,128)(2,1)S(1)} %get-tuple-element.44), channel_id=1, source_target_pairs={{0,2},{1,3},{2,0},{3,1},{4,6},{5,7},{6,4},{7,5},{8,10},{9,11},{10,... | collective-permute-start | bytes 380936 | tf_op jit(solution)/shard_map/ppermute | solution.py:290
  31.6 7.4 %collective-permute-start.10 = (f32[24,640]{1,0:T(8,128)S(1)}, f32[24,640]{1,0:T(8,128)S(1)}, u32[]{:S(2)}, u32[]{:S(2)}) collective-permute-start(f32[24,640]{1,0:T(8,128)S(1)} %get-tuple-element.49), channel_id=1, source_target_pairs={{0,24},{8,16},{16,8},{24,0},{1,25},{9,17},{17,9},{25,1},{2,26},{10... | collective-permute-start | bytes 184328 | tf_op jit(solution)/shard_map/ppermute | solution.py:293
  34.0 6.8 %collective-permute-start.17 = (f32[24,640]{1,0:T(8,128)S(1)}, f32[24,640]{1,0:T(8,128)S(1)}, u32[]{:S(2)}, u32[]{:S(2)}) collective-permute-start(f32[24,640]{1,0:T(8,128)S(1)} %get-tuple-element.56), channel_id=1, source_target_pairs={{0,4},{1,5},{2,6},{3,7},{4,0},{5,1},{6,2},{7,3},{8,12},{9,13},{10,... | collective-permute-start | bytes 184328 | tf_op jit(solution)/shard_map/ppermute | solution.py:290
  34.6 4.4 %collective-permute-start.8 = (f32[24,640]{1,0:T(8,128)S(1)}, f32[24,640]{1,0:T(8,128)S(1)}, u32[]{:S(2)}, u32[]{:S(2)}) collective-permute-start(f32[24,640]{1,0:T(8,128)S(1)} %get-tuple-element.47), channel_id=1, source_target_pairs={{0,8},{8,0},{16,24},{24,16},{1,9},{9,1},{17,25},{25,17},{2,10},{10... | collective-permute-start | bytes 184328 | tf_op jit(solution)/shard_map/ppermute | solution.py:293
  36.2 4.2 %collective-permute-start.9 = (f32[24,640]{1,0:T(8,128)S(1)}, f32[24,640]{1,0:T(8,128)S(1)}, u32[]{:S(2)}, u32[]{:S(2)}) collective-permute-start(f32[24,640]{1,0:T(8,128)S(1)} %get-tuple-element.48), channel_id=1, source_target_pairs={{0,16},{8,24},{16,0},{24,8},{1,17},{9,25},{17,1},{25,9},{2,18},{10... | collective-permute-start | bytes 184328 | tf_op jit(solution)/shard_map/ppermute | solution.py:293
  36.7 6.1 %collective-permute-start.18 = (f32[24,640]{1,0:T(8,128)S(1)}, f32[24,640]{1,0:T(8,128)S(1)}, u32[]{:S(2)}, u32[]{:S(2)}) collective-permute-start(f32[24,640]{1,0:T(8,128)S(1)} %get-tuple-element.57), channel_id=1, source_target_pairs={{0,6},{1,7},{2,4},{3,5},{4,2},{5,3},{6,0},{7,1},{8,14},{9,15},{10,... | collective-permute-start | bytes 184328 | tf_op jit(solution)/shard_map/ppermute | solution.py:290
  39.1 4.5 %collective-permute-start.19 = (f32[24,640]{1,0:T(8,128)S(1)}, f32[24,640]{1,0:T(8,128)S(1)}, u32[]{:S(2)}, u32[]{:S(2)}) collective-permute-start(f32[24,640]{1,0:T(8,128)S(1)} %get-tuple-element.58), channel_id=1, source_target_pairs={{0,2},{1,3},{2,0},{3,1},{4,6},{5,7},{6,4},{7,5},{8,10},{9,11},{10,... | collective-permute-start | bytes 184328 | tf_op jit(solution)/shard_map/ppermute | solution.py:290
  43.8 5.9 %collective-permute-start.20 = (bf16[48,1280]{1,0:T(8,128)(2,1)S(1)}, bf16[48,1280]{1,0:T(8,128)(2,1)S(1)}, u32[]{:S(2)}, u32[]{:S(2)}) collective-permute-start(bf16[48,1280]{1,0:T(8,128)(2,1)S(1)} %shard_map.129.refs_3_), channel_id=1, source_target_pairs={{0,24},{8,16},{16,8},{24,0},{1,25},{9,17},{17,9},{25,1},{2,26},{10... | collective-permute-start | bytes 368648 | tf_op jit(solution)/shard_map/ppermute | solution.py:293
  45.3 5.7 %collective-permute-start.21 = (bf16[48,1280]{1,0:T(8,128)(2,1)S(1)}, bf16[48,1280]{1,0:T(8,128)(2,1)S(1)}, u32[]{:S(2)}, u32[]{:S(2)}) collective-permute-start(bf16[48,1280]{1,0:T(8,128)(2,1)S(1)} %shard_map.129.refs_3_), channel_id=1, source_target_pairs={{0,16},{8,24},{16,0},{24,8},{1,17},{9,25},{17,1},{25,9},{2,18},{10... | collective-permute-start | bytes 368648 | tf_op jit(solution)/shard_map/ppermute | solution.py:293
  46.8 4.9 %collective-permute-start.22 = (bf16[48,1280]{1,0:T(8,128)(2,1)S(1)}, bf16[48,1280]{1,0:T(8,128)(2,1)S(1)}, u32[]{:S(2)}, u32[]{:S(2)}) collective-permute-start(bf16[48,1280]{1,0:T(8,128)(2,1)S(1)} %shard_map.129.refs_3_), channel_id=1, source_target_pairs={{0,8},{8,0},{16,24},{24,16},{1,9},{9,1},{17,25},{25,17},{2,10},{10... | collective-permute-start | bytes 368648 | tf_op jit(solution)/shard_map/ppermute | solution.py:293

commit v14 on v13

--- a/solution.py
+++ b/solution.py
@@ -335,8 +335,13 @@
         [shaped((2 * shard, cols // 2), f32)] * chips,
         *[send_dp(head[t], t) for t in reversed(range(dp))],
     )
-    pieces = [send(sums[s], s) for s in far_first]
-    embed = run(gather_kernel, shaped((shard, width), f32), *[send_dp(embed[t], t) for t in range(dp)])
+    half = chips // 2
+    pieces = [send(sums[s], s) for s in far_first[:half]]
+    sums, _ = lax.optimization_barrier((list(sums), pieces[0]))
+    pieces += [send(sums[s], s) for s in far_first[half:]]
+    last = send_dp(embed[dp - 1], dp - 1)
+    rest, last = lax.optimization_barrier((list(embed[: dp - 1]), last))
+    embed = run(gather_kernel, shaped((shard, width), f32), *[send_dp(rest[t], t) for t in range(dp - 1)], last)
     state = (embed, master, first_moment, second_moment)
     table = run(functools.partial(rows_kernel, far_first), shaped((chips * shard, cols), bf16), *state, *pieces)
     master_new, first_new, second_new, order = run(

time: 52.9 us -> 54.9 us (1.038)
  waiting for transfers between devices: 15.3 us -> 16.8 us
    ppermute x11, waiting for transfers between devices: 9.48 us -> 10.8 us  [send(): lax.ppermute(x, 'vocab', [(v, v ^ move) for v in range(vocab)])]
  transfers between devices with their start and end apart: 23 -> 23, of which waited for: 13 -> 12; matrix products, arithmetic and copies ran while one was open for 0% -> 0% of each run, Pallas kernels for 11% -> 11%
where the time goes in v14:
time: 54.9 us; the launch traced here: 54.8 us
  starting transfers between devices  29.9 us (54%)
  waiting for transfers between devices  16.8 us (31%)
  Pallas kernels  7.31 us (13%)
  between operations  0.75 us (1%)
    ppermute x12, starting transfers between devices, send_dp(): return lax.ppermute(x, 'dp', [(i, i ^ t) for i in range(dp)]) if t else x  15.5 us
    ppermute x11, starting transfers between devices, send(): lax.ppermute(x, 'vocab', [(v, v ^ move) for v in range(vocab)])  14.4 us
    ppermute x11, waiting for transfers between devices, send(): lax.ppermute(x, 'vocab', [(v, v ^ move) for v in range(vocab)])  10.8 us
    pallas_call x11, Pallas kernels, run(): pl.pallas_call(kernel, out_shape=outs, in_specs=[pl.BlockSpec(memory_spac...  7.31 us
    ppermute x12, waiting for transfers between devices, send_dp(): return lax.ppermute(x, 'dp', [(i, i ^ t) for i in range(dp)]) if t else x  5.95 us
  transfers between devices with their start and end apart: 23, of which 12 were waited for; matrix products, arithmetic and copies ran while one was open for 0% of the time, Pallas kernels for 11%

profile of v14, /device:TPU:0, one launch (start us, length us, event | category | flops | bytes accessed | tf_op | source)
XLA Modules:
  0.0 54.8 jit_solution(14126477532615260051)
XLA Ops:
  0.6 0.5 collective-permute-start.1
  1.1 1.4 %shard_map.120 = (bf16[24,5248]{1,0:T(8,128)(2,1)S(1)}, bf16[24,5248]{1,0:T(8,128)(2,1)S(1)}) custom-call(bf16[48,5120]{1,0:T(8,128)(2,1)} %bitcast.12, s32[6,1,8]{2,1,0:T(1,128)} %bitcast.13, s32[1,8]{1,0:T(1,128)} %counts_hbm.1), custom_call_target="tpu_custom_call" | custom-call | bytes 995552 | tf_op jit(solution)/shard_map/pallas_call | solution.py:251
  2.5 0.1 collective-permute-start
  2.6 4.0 %collective-permute-start.12 = (bf16[48,1024]{1,0:T(8,128)(2,1)}, bf16[48,1024]{1,0:T(8,128)(2,1)S(1)}, u32[]{:S(2)}, u32[]{:S(2)}) collective-permute-start(bf16[48,1024]{1,0:T(8,128)(2,1)} %bitcast.8), channel_id=1, source_target_pairs={{0,4},{1,5},{2,6},{3,7},{4,0},{5,1},{6,2},{7,3},{8,12},{9,13},{10,... | collective-permute-start | bytes 294920 | tf_op jit(solution)/shard_map/ppermute | solution.py:290
  6.7 0.0 collective-permute-done.other_ref
  6.7 0.1 shard_map.121
  6.8 2.5 %collective-permute-start.2 = (bf16[496,128]{1,0:T(8,128)(2,1)S(1)}, bf16[496,128]{1,0:T(8,128)(2,1)S(1)}, u32[]{:S(2)}, u32[]{:S(2)}) collective-permute-start(bf16[496,128]{1,0:T(8,128)(2,1)S(1)} %get-tuple-element.43), channel_id=1, source_target_pairs={{0,24},{8,16},{16,8},{24,0},{1,25},{9,17},{17,9},{25,1},{2,26},{10... | collective-permute-start | bytes 380936 | tf_op jit(solution)/shard_map/ppermute | solution.py:293
  9.3 0.5 collective-permute-start.3
  9.8 0.5 collective-permute-start.4
  10.3 1.6 %collective-permute-start.11 = (bf16[48,1024]{1,0:T(8,128)(2,1)}, bf16[48,1024]{1,0:T(8,128)(2,1)S(1)}, u32[]{:S(2)}, u32[]{:S(2)}) collective-permute-start(bf16[48,1024]{1,0:T(8,128)(2,1)} %bitcast.9), channel_id=1, source_target_pairs={{0,2},{1,3},{2,0},{3,1},{4,6},{5,7},{6,4},{7,5},{8,10},{9,11},{10,... | collective-permute-start | bytes 294920 | tf_op jit(solution)/shard_map/ppermute | solution.py:290
  11.9 0.1 collective-permute-done.12.refs_2_
  12.0 0.8 %collective-permute-start.13 = (bf16[48,1024]{1,0:T(8,128)(2,1)S(1)}, bf16[48,1024]{1,0:T(8,128)(2,1)S(1)}, u32[]{:S(2)}, u32[]{:S(2)}) collective-permute-start(bf16[48,1024]{1,0:T(8,128)(2,1)S(1)} %collective-permute-done.12.refs_2_), channel_id=1, source_target_pairs={{0,2},{1,3},{2,0},{3,1},{4,6},{5,7},{6,4},{7,5},{8,10},{9,11},{10,... | collective-permute-start | bytes 294920 | tf_op jit(solution)/shard_map/ppermute | solution.py:290
  12.9 1.3 %shard_map.122.own_ref = bf16[1024,640]{1,0:T(8,128)(2,1)S(1)} custom-call(bf16[1024,640]{1,0:T(8,128)(2,1)} %hidden_hbm.1), custom_call_target="tpu_custom_call" | custom-call | bytes 2621440 | tf_op jit(solution)/shard_map/pallas_call | solution.py:251
  14.2 1.4 %collective-permute-done.3.refs_1_ = bf16[496,128]{1,0:T(8,128)(2,1)S(1)} collective-permute-done((bf16[496,128]{1,0:T(8,128)(2,1)S(1)}, bf16[496,128]{1,0:T(8,128)(2,1)S(1)}, u32[]{:S(2)}, u32[]{:S(2)}) %collective-permute-start.3) | collective-permute-done | bytes 127008 | tf_op jit(solution)/shard_map/ppermute | solution.py:293
  15.6 0.1 collective-permute-done.4.refs_2_
  15.6 0.4 shard_map.123
  16.0 2.0 %collective-permute-start.5 = (bf16[496,128]{1,0:T(8,128)(2,1)S(1)}, bf16[496,128]{1,0:T(8,128)(2,1)S(1)}, u32[]{:S(2)}, u32[]{:S(2)}) collective-permute-start(bf16[496,128]{1,0:T(8,128)(2,1)S(1)} %get-tuple-element.48), channel_id=1, source_target_pairs={{0,4},{1,5},{2,6},{3,7},{4,0},{5,1},{6,2},{7,3},{8,12},{9,13},{10,... | collective-permute-start | bytes 380936 | tf_op jit(solution)/shard_map/ppermute | solution.py:290
  18.0 0.9 %shard_map.126 = (f32[48,1280]{1,0:T(8,128)S(1)}, f32[48,1280]{1,0:T(8,128)S(1)}, f32[48,1280]{1,0:T(8,128)S(1)}, f32[48,1280]{1,0:T(8,128)S(1)}) custom-call(s32[1,1024]{1,0:T(1,128)S(1)} %bitcast.11, bf16[1024,640]{1,0:T(8,128)(2,1)S(1)} %shard_map.122.own_ref, bf16[1024,640]{1,0:T(8,128)(2,1)S(1)} %collective-permute-done.1.other_ref, ...), custom_call_target="tpu_custom_call" | custom-call | bytes 4001792 | tf_op jit(solution)/shard_map/pallas_call | solution.py:251
  19.0 0.0 copy-start
  19.0 0.0 copy-start.1
  19.0 0.0 copy-start.2
  19.0 2.5 %collective-permute-start.14 = (f32[48,1280]{1,0:T(8,128)S(1)}, f32[48,1280]{1,0:T(8,128)S(1)}, u32[]{:S(2)}, u32[]{:S(2)}) collective-permute-start(f32[48,1280]{1,0:T(8,128)S(1)} %get-tuple-element.62), channel_id=1, source_target_pairs={{0,24},{8,16},{16,8},{24,0},{1,25},{9,17},{17,9},{25,1},{2,26},{10... | collective-permute-start | bytes 737288 | tf_op jit(solution)/shard_map/ppermute | solution.py:293
  21.5 0.5 collective-permute-start.15
  22.0 0.5 collective-permute-start.16
  22.6 2.3 %collective-permute-start.6 = (bf16[496,128]{1,0:T(8,128)(2,1)S(1)}, bf16[496,128]{1,0:T(8,128)(2,1)S(1)}, u32[]{:S(2)}, u32[]{:S(2)}) collective-permute-start(bf16[496,128]{1,0:T(8,128)(2,1)S(1)} %get-tuple-element.49), channel_id=1, source_target_pairs={{0,6},{1,7},{2,4},{3,5},{4,2},{5,3},{6,0},{7,1},{8,14},{9,15},{10,... | collective-permute-start | bytes 380936 | tf_op jit(solution)/shard_map/ppermute | solution.py:290
  24.8 0.1 collective-permute-done.5.refs_0_
  25.0 5.2 %collective-permute-done.6.refs_1_ = bf16[496,128]{1,0:T(8,128)(2,1)S(1)} collective-permute-done((bf16[496,128]{1,0:T(8,128)(2,1)S(1)}, bf16[496,128]{1,0:T(8,128)(2,1)S(1)}, u32[]{:S(2)}, u32[]{:S(2)}) %collective-permute-start.6) | collective-permute-done | bytes 127008 | tf_op jit(solution)/shard_map/ppermute | solution.py:290
  30.1 1.0 %collective-permute-done.7.refs_2_ = bf16[496,128]{1,0:T(8,128)(2,1)S(1)} collective-permute-done((bf16[496,128]{1,0:T(8,128)(2,1)S(1)}, bf16[496,128]{1,0:T(8,128)(2,1)S(1)}, u32[]{:S(2)}, u32[]{:S(2)}) %collective-permute-start.7) | collective-permute-done | bytes 127008 | tf_op jit(solution)/shard_map/ppermute | solution.py:290
  31.2 0.5 shard_map.124
  31.6 2.3 %collective-permute-start.8 = (f32[24,640]{1,0:T(8,128)S(1)}, f32[24,640]{1,0:T(8,128)S(1)}, u32[]{:S(2)}, u32[]{:S(2)}) collective-permute-start(f32[24,640]{1,0:T(8,128)S(1)} %get-tuple-element.55), channel_id=1, source_target_pairs={{0,24},{8,16},{16,8},{24,0},{1,25},{9,17},{17,9},{25,1},{2,26},{10... | collective-permute-start | bytes 184328 | tf_op jit(solution)/shard_map/ppermute | solution.py:293
  33.9 0.1 shard_map.127
  34.0 0.6 %collective-permute-start.17 = (f32[24,640]{1,0:T(8,128)S(1)}, f32[24,640]{1,0:T(8,128)S(1)}, u32[]{:S(2)}, u32[]{:S(2)}) collective-permute-start(f32[24,640]{1,0:T(8,128)S(1)} %get-tuple-element.66), channel_id=1, source_target_pairs={{0,4},{1,5},{2,6},{3,7},{4,0},{5,1},{6,2},{7,3},{8,12},{9,13},{10,... | collective-permute-start | bytes 184328 | tf_op jit(solution)/shard_map/ppermute | solution.py:290
  34.6 2.4 %collective-permute-start.18 = (f32[24,640]{1,0:T(8,128)S(1)}, f32[24,640]{1,0:T(8,128)S(1)}, u32[]{:S(2)}, u32[]{:S(2)}) collective-permute-start(f32[24,640]{1,0:T(8,128)S(1)} %get-tuple-element.67), channel_id=1, source_target_pairs={{0,6},{1,7},{2,4},{3,5},{4,2},{5,3},{6,0},{7,1},{8,14},{9,15},{10,... | collective-permute-start | bytes 184328 | tf_op jit(solution)/shard_map/ppermute | solution.py:290
  37.0 1.4 %collective-permute-start.9 = (f32[24,640]{1,0:T(8,128)S(1)}, f32[24,640]{1,0:T(8,128)S(1)}, u32[]{:S(2)}, u32[]{:S(2)}) collective-permute-start(f32[24,640]{1,0:T(8,128)S(1)} %get-tuple-element.57), channel_id=1, source_target_pairs={{0,8},{8,0},{16,24},{24,16},{1,9},{9,1},{17,25},{25,17},{2,10},{10... | collective-permute-start | bytes 184328 | tf_op jit(solution)/shard_map/ppermute | solution.py:293
  38.4 1.2 %collective-permute-start.10 = (f32[24,640]{1,0:T(8,128)S(1)}, f32[24,640]{1,0:T(8,128)S(1)}, u32[]{:S(2)}, u32[]{:S(2)}) collective-permute-start(f32[24,640]{1,0:T(8,128)S(1)} %get-tuple-element.58), channel_id=1, source_target_pairs={{0,16},{8,24},{16,0},{24,8},{1,17},{9,25},{17,1},{25,9},{2,18},{10... | collective-permute-start | bytes 184328 | tf_op jit(solution)/shard_map/ppermute | solution.py:293
  39.6 1.6 %collective-permute-done.17.refs_4_ = f32[24,640]{1,0:T(8,128)S(1)} collective-permute-done((f32[24,640]{1,0:T(8,128)S(1)}, f32[24,640]{1,0:T(8,128)S(1)}, u32[]{:S(2)}, u32[]{:S(2)}) %collective-permute-start.17) | collective-permute-done | bytes 61472 | tf_op jit(solution)/shard_map/ppermute | solution.py:290
  41.2 0.0 collective-permute-done.9.refs_1_
  41.3 1.4 %collective-permute-done.10.refs_2_ = f32[24,640]{1,0:T(8,128)S(1)} collective-permute-done((f32[24,640]{1,0:T(8,128)S(1)}, f32[24,640]{1,0:T(8,128)S(1)}, u32[]{:S(2)}, u32[]{:S(2)}) %collective-permute-start.10) | collective-permute-done | bytes 61472 | tf_op jit(solution)/shard_map/ppermute | solution.py:293
  42.7 2.8 %collective-permute-done.19.refs_6_ = f32[24,640]{1,0:T(8,128)S(1)} collective-permute-done((f32[24,640]{1,0:T(8,128)S(1)}, f32[24,640]{1,0:T(8,128)S(1)}, u32[]{:S(2)}, u32[]{:S(2)}) %collective-permute-start.19) | collective-permute-done | bytes 61472 | tf_op jit(solution)/shard_map/ppermute | solution.py:290
  45.4 0.3 shard_map.129.refs_3_
  45.8 0.4 collective-permute-start.20
  46.2 2.7 %collective-permute-start.21 = (bf16[48,1280]{1,0:T(8,128)(2,1)S(1)}, bf16[48,1280]{1,0:T(8,128)(2,1)S(1)}, u32[]{:S(2)}, u32[]{:S(2)}) collective-permute-start(bf16[48,1280]{1,0:T(8,128)(2,1)S(1)} %shard_map.129.refs_3_), channel_id=1, source_target_pairs={{0,16},{8,24},{16,0},{24,8},{1,17},{9,25},{17,1},{25,9},{2,18},{10... | collective-permute-start | bytes 368648 | tf_op jit(solution)/shard_map/ppermute | solution.py:293
  48.8 0.5 collective-permute-start.22
  49.3 1.3 %shard_map.128 = (f32[12,5120]{1,0:T(8,128)}, f32[12,5120]{1,0:T(8,128)}, f32[12,5120]{1,0:T(8,128)}, bf16[192,192]{1,0:T(8,128)(2,1)S(1)}) custom-call(f32[12,5120]{1,0:T(8,128)S(1)} %shard_map.125.refs_0_, f32[12,5120]{1,0:T(8,128)S(1)} %copy-done, f32[12,5120]{1,0:T(8,128)S(1)} %copy-done.1, f32[12,5120]{1,0:T(8,128)S(1)} %copy-done.2, ...), custom_call_target="tpu_custom_call" | custom-call | bytes 2039808 | tf_op jit(solution)/shard_map/pallas_call | solution.py:251
  50.6 1.1 %collective-permute-done.20.refs_0_ = bf16[48,1280]{1,0:T(8,128)(2,1)S(1)} collective-permute-done((bf16[48,1280]{1,0:T(8,128)(2,1)S(1)}, bf16[48,1280]{1,0:T(8,128)(2,1)S(1)}, u32[]{:S(2)}, u32[]{:S(2)}) %collective-permute-start.20) | collective-permute-done | bytes 122912 | tf_op jit(solution)/shard_map/ppermute | solution.py:293
  51.7 1.2 %collective-permute-done.21.refs_1_ = bf16[48,1280]{1,0:T(8,128)(2,1)S(1)} collective-permute-done((bf16[48,1280]{1,0:T(8,128)(2,1)S(1)}, bf16[48,1280]{1,0:T(8,128)(2,1)S(1)}, u32[]{:S(2)}, u32[]{:S(2)}) %collective-permute-start.21) | collective-permute-done | bytes 122912 | tf_op jit(solution)/shard_map/ppermute | solution.py:293
  52.9 0.8 %collective-permute-done.22.refs_2_ = bf16[48,1280]{1,0:T(8,128)(2,1)S(1)} collective-permute-done((bf16[48,1280]{1,0:T(8,128)(2,1)S(1)}, bf16[48,1280]{1,0:T(8,128)(2,1)S(1)}, u32[]{:S(2)}, u32[]{:S(2)}) %collective-permute-start.22) | collective-permute-done | bytes 122912 | tf_op jit(solution)/shard_map/ppermute | solution.py:293
  53.7 1.1 %shard_map.130 = bf16[48,5120]{1,0:T(8,128)(2,1)} custom-call(bf16[192,192]{1,0:T(8,128)(2,1)S(1)} %get-tuple-element.75.order_ref, bf16[48,1280]{1,0:T(8,128)(2,1)S(1)} %collective-permute-done.20.refs_0_, bf16[48,1280]{1,0:T(8,128)(2,1)S(1)} %collective-permute-done.21.refs_1_, bf16[48,1280]{1,0:T(8,128)(2,1)S(1)} %collective-permute-done.22.refs_2_, ...), custom_call_target="tpu_custom_call" | custom-call | bytes 1056768 | tf_op jit(solution)/shard_map/pallas_call | solution.py:251
  (19 shorter events, 0.1 us)
Async XLA Ops:
  0.6 6.1 %collective-permute-start.1 = (bf16[1024,640]{1,0:T(8,128)(2,1)}, bf16[1024,640]{1,0:T(8,128)(2,1)S(1)}, u32[]{:S(2)}, u32[]{:S(2)}) collective-permute-start(bf16[1024,640]{1,0:T(8,128)(2,1)} %hidden_hbm.1), channel_id=1, source_target_pairs={{0,1},{1,0},{2,3},{3,2},{4,5},{5,4},{6,7},{7,6},{8,9},{9,8},{10,11... | collective-permute-start | bytes 3932168 | tf_op jit(solution)/shard_map/ppermute | solution.py:290
  2.5 4.2 %collective-permute-start = (bf16[24,5248]{1,0:T(8,128)(2,1)S(1)}, bf16[24,5248]{1,0:T(8,128)(2,1)S(1)}, u32[]{:S(2)}, u32[]{:S(2)}) collective-permute-start(bf16[24,5248]{1,0:T(8,128)(2,1)S(1)} %get-tuple-element.41), channel_id=1, source_target_pairs={{0,1},{1,0},{2,3},{3,2},{4,5},{5,4},{6,7},{7,6},{8,9},{9,8},{10,11... | collective-permute-start | bytes 755720 | tf_op jit(solution)/shard_map/ppermute | solution.py:290
  2.6 9.4 %collective-permute-start.12 = (bf16[48,1024]{1,0:T(8,128)(2,1)}, bf16[48,1024]{1,0:T(8,128)(2,1)S(1)}, u32[]{:S(2)}, u32[]{:S(2)}) collective-permute-start(bf16[48,1024]{1,0:T(8,128)(2,1)} %bitcast.8), channel_id=1, source_target_pairs={{0,4},{1,5},{2,6},{3,7},{4,0},{5,1},{6,2},{7,3},{8,12},{9,13},{10,... | collective-permute-start | bytes 294920 | tf_op jit(solution)/shard_map/ppermute | solution.py:290
  6.8 7.4 %collective-permute-start.2 = (bf16[496,128]{1,0:T(8,128)(2,1)S(1)}, bf16[496,128]{1,0:T(8,128)(2,1)S(1)}, u32[]{:S(2)}, u32[]{:S(2)}) collective-permute-start(bf16[496,128]{1,0:T(8,128)(2,1)S(1)} %get-tuple-element.43), channel_id=1, source_target_pairs={{0,24},{8,16},{16,8},{24,0},{1,25},{9,17},{17,9},{25,1},{2,26},{10... | collective-permute-start | bytes 380936 | tf_op jit(solution)/shard_map/ppermute | solution.py:293
  9.3 6.3 %collective-permute-start.3 = (bf16[496,128]{1,0:T(8,128)(2,1)S(1)}, bf16[496,128]{1,0:T(8,128)(2,1)S(1)}, u32[]{:S(2)}, u32[]{:S(2)}) collective-permute-start(bf16[496,128]{1,0:T(8,128)(2,1)S(1)} %get-tuple-element.44), channel_id=1, source_target_pairs={{0,16},{8,24},{16,0},{24,8},{1,17},{9,25},{17,1},{25,9},{2,18},{10... | collective-permute-start | bytes 380936 | tf_op jit(solution)/shard_map/ppermute | solution.py:293
  9.8 8.2 %copy-start.3 = (bf16[1024,48]{0,1:T(8,128)(2,1)S(1)}, bf16[1024,48]{0,1:T(8,128)(2,1)}, u32[]{:S(2)}) copy-start(bf16[1024,48]{0,1:T(8,128)(2,1)} %param.10) | copy-start | bytes 294916
  9.8 8.2 %copy-start.4 = (s32[1024]{0:T(1024)S(1)}, s32[1024]{0:T(1024)}, u32[]{:S(2)}) copy-start(s32[1024]{0:T(1024)} %param.11) | copy-start | bytes 12292
  9.8 5.8 %collective-permute-start.4 = (bf16[496,128]{1,0:T(8,128)(2,1)S(1)}, bf16[496,128]{1,0:T(8,128)(2,1)S(1)}, u32[]{:S(2)}, u32[]{:S(2)}) collective-permute-start(bf16[496,128]{1,0:T(8,128)(2,1)S(1)} %get-tuple-element.45), channel_id=1, source_target_pairs={{0,8},{8,0},{16,24},{24,16},{1,9},{9,1},{17,25},{25,17},{2,10},{10... | collective-permute-start | bytes 380936 | tf_op jit(solution)/shard_map/ppermute | solution.py:293
  10.3 7.7 %collective-permute-start.11 = (bf16[48,1024]{1,0:T(8,128)(2,1)}, bf16[48,1024]{1,0:T(8,128)(2,1)S(1)}, u32[]{:S(2)}, u32[]{:S(2)}) collective-permute-start(bf16[48,1024]{1,0:T(8,128)(2,1)} %bitcast.9), channel_id=1, source_target_pairs={{0,2},{1,3},{2,0},{3,1},{4,6},{5,7},{6,4},{7,5},{8,10},{9,11},{10,... | collective-permute-start | bytes 294920 | tf_op jit(solution)/shard_map/ppermute | solution.py:290
  12.0 6.0 %collective-permute-start.13 = (bf16[48,1024]{1,0:T(8,128)(2,1)S(1)}, bf16[48,1024]{1,0:T(8,128)(2,1)S(1)}, u32[]{:S(2)}, u32[]{:S(2)}) collective-permute-start(bf16[48,1024]{1,0:T(8,128)(2,1)S(1)} %collective-permute-done.12.refs_2_), channel_id=1, source_target_pairs={{0,2},{1,3},{2,0},{3,1},{4,6},{5,7},{6,4},{7,5},{8,10},{9,11},{10,... | collective-permute-start | bytes 294920 | tf_op jit(solution)/shard_map/ppermute | solution.py:290
  16.0 9.0 %collective-permute-start.5 = (bf16[496,128]{1,0:T(8,128)(2,1)S(1)}, bf16[496,128]{1,0:T(8,128)(2,1)S(1)}, u32[]{:S(2)}, u32[]{:S(2)}) collective-permute-start(bf16[496,128]{1,0:T(8,128)(2,1)S(1)} %get-tuple-element.48), channel_id=1, source_target_pairs={{0,4},{1,5},{2,6},{3,7},{4,0},{5,1},{6,2},{7,3},{8,12},{9,13},{10,... | collective-permute-start | bytes 380936 | tf_op jit(solution)/shard_map/ppermute | solution.py:290
  19.0 26.5 %copy-start = (f32[12,5120]{1,0:T(8,128)S(1)}, f32[12,5120]{1,0:T(8,128)}, u32[]{:S(2)}) copy-start(f32[12,5120]{1,0:T(8,128)} %refs_1_.3) | copy-start | bytes 737284
  19.0 26.5 %copy-start.1 = (f32[12,5120]{1,0:T(8,128)S(1)}, f32[12,5120]{1,0:T(8,128)}, u32[]{:S(2)}) copy-start(f32[12,5120]{1,0:T(8,128)} %refs_2_.3) | copy-start | bytes 737284
  19.0 26.4 %copy-start.2 = (f32[12,5120]{1,0:T(8,128)S(1)}, f32[12,5120]{1,0:T(8,128)}, u32[]{:S(2)}) copy-start(f32[12,5120]{1,0:T(8,128)} %refs_3_.3) | copy-start | bytes 737284
  19.0 14.9 %collective-permute-start.14 = (f32[48,1280]{1,0:T(8,128)S(1)}, f32[48,1280]{1,0:T(8,128)S(1)}, u32[]{:S(2)}, u32[]{:S(2)}) collective-permute-start(f32[48,1280]{1,0:T(8,128)S(1)} %get-tuple-element.62), channel_id=1, source_target_pairs={{0,24},{8,16},{16,8},{24,0},{1,25},{9,17},{17,9},{25,1},{2,26},{10... | collective-permute-start | bytes 737288 | tf_op jit(solution)/shard_map/ppermute | solution.py:293
  21.5 12.4 %collective-permute-start.15 = (f32[48,1280]{1,0:T(8,128)S(1)}, f32[48,1280]{1,0:T(8,128)S(1)}, u32[]{:S(2)}, u32[]{:S(2)}) collective-permute-start(f32[48,1280]{1,0:T(8,128)S(1)} %get-tuple-element.63), channel_id=1, source_target_pairs={{0,16},{8,24},{16,0},{24,8},{1,17},{9,25},{17,1},{25,9},{2,18},{10... | collective-permute-start | bytes 737288 | tf_op jit(solution)/shard_map/ppermute | solution.py:293
  22.0 11.9 %collective-permute-start.16 = (f32[48,1280]{1,0:T(8,128)S(1)}, f32[48,1280]{1,0:T(8,128)S(1)}, u32[]{:S(2)}, u32[]{:S(2)}) collective-permute-start(f32[48,1280]{1,0:T(8,128)S(1)} %get-tuple-element.64), channel_id=1, source_target_pairs={{0,8},{8,0},{16,24},{24,16},{1,9},{9,1},{17,25},{25,17},{2,10},{10... | collective-permute-start | bytes 737288 | tf_op jit(solution)/shard_map/ppermute | solution.py:293
  22.6 7.6 %collective-permute-start.6 = (bf16[496,128]{1,0:T(8,128)(2,1)S(1)}, bf16[496,128]{1,0:T(8,128)(2,1)S(1)}, u32[]{:S(2)}, u32[]{:S(2)}) collective-permute-start(bf16[496,128]{1,0:T(8,128)(2,1)S(1)} %get-tuple-element.49), channel_id=1, source_target_pairs={{0,6},{1,7},{2,4},{3,5},{4,2},{5,3},{6,0},{7,1},{8,14},{9,15},{10,... | collective-permute-start | bytes 380936 | tf_op jit(solution)/shard_map/ppermute | solution.py:290
  25.0 6.2 %collective-permute-start.7 = (bf16[496,128]{1,0:T(8,128)(2,1)S(1)}, bf16[496,128]{1,0:T(8,128)(2,1)S(1)}, u32[]{:S(2)}, u32[]{:S(2)}) collective-permute-start(bf16[496,128]{1,0:T(8,128)(2,1)S(1)} %get-tuple-element.50), channel_id=1, source_target_pairs={{0,2},{1,3},{2,0},{3,1},{4,6},{5,7},{6,4},{7,5},{8,10},{9,11},{10,... | collective-permute-start | bytes 380936 | tf_op jit(solution)/shard_map/ppermute | solution.py:290
  31.6 5.4 %collective-permute-start.8 = (f32[24,640]{1,0:T(8,128)S(1)}, f32[24,640]{1,0:T(8,128)S(1)}, u32[]{:S(2)}, u32[]{:S(2)}) collective-permute-start(f32[24,640]{1,0:T(8,128)S(1)} %get-tuple-element.55), channel_id=1, source_target_pairs={{0,24},{8,16},{16,8},{24,0},{1,25},{9,17},{17,9},{25,1},{2,26},{10... | collective-permute-start | bytes 184328 | tf_op jit(solution)/shard_map/ppermute | solution.py:293
  34.0 7.2 %collective-permute-start.17 = (f32[24,640]{1,0:T(8,128)S(1)}, f32[24,640]{1,0:T(8,128)S(1)}, u32[]{:S(2)}, u32[]{:S(2)}) collective-permute-start(f32[24,640]{1,0:T(8,128)S(1)} %get-tuple-element.66), channel_id=1, source_target_pairs={{0,4},{1,5},{2,6},{3,7},{4,0},{5,1},{6,2},{7,3},{8,12},{9,13},{10,... | collective-permute-start | bytes 184328 | tf_op jit(solution)/shard_map/ppermute | solution.py:290
  34.6 8.0 %collective-permute-start.18 = (f32[24,640]{1,0:T(8,128)S(1)}, f32[24,640]{1,0:T(8,128)S(1)}, u32[]{:S(2)}, u32[]{:S(2)}) collective-permute-start(f32[24,640]{1,0:T(8,128)S(1)} %get-tuple-element.67), channel_id=1, source_target_pairs={{0,6},{1,7},{2,4},{3,5},{4,2},{5,3},{6,0},{7,1},{8,14},{9,15},{10,... | collective-permute-start | bytes 184328 | tf_op jit(solution)/shard_map/ppermute | solution.py:290
  37.0 4.2 %collective-permute-start.9 = (f32[24,640]{1,0:T(8,128)S(1)}, f32[24,640]{1,0:T(8,128)S(1)}, u32[]{:S(2)}, u32[]{:S(2)}) collective-permute-start(f32[24,640]{1,0:T(8,128)S(1)} %get-tuple-element.57), channel_id=1, source_target_pairs={{0,8},{8,0},{16,24},{24,16},{1,9},{9,1},{17,25},{25,17},{2,10},{10... | collective-permute-start | bytes 184328 | tf_op jit(solution)/shard_map/ppermute | solution.py:293
  38.4 4.2 %collective-permute-start.10 = (f32[24,640]{1,0:T(8,128)S(1)}, f32[24,640]{1,0:T(8,128)S(1)}, u32[]{:S(2)}, u32[]{:S(2)}) collective-permute-start(f32[24,640]{1,0:T(8,128)S(1)} %get-tuple-element.58), channel_id=1, source_target_pairs={{0,16},{8,24},{16,0},{24,8},{1,17},{9,25},{17,1},{25,9},{2,18},{10... | collective-permute-start | bytes 184328 | tf_op jit(solution)/shard_map/ppermute | solution.py:293
  41.2 4.2 %collective-permute-start.19 = (f32[24,640]{1,0:T(8,128)S(1)}, f32[24,640]{1,0:T(8,128)S(1)}, u32[]{:S(2)}, u32[]{:S(2)}) collective-permute-start(f32[24,640]{1,0:T(8,128)S(1)} %get-tuple-element.70), channel_id=1, source_target_pairs={{0,2},{1,3},{2,0},{3,1},{4,6},{5,7},{6,4},{7,5},{8,10},{9,11},{10,... | collective-permute-start | bytes 184328 | tf_op jit(solution)/shard_map/ppermute | solution.py:290
  45.8 5.9 %collective-permute-start.20 = (bf16[48,1280]{1,0:T(8,128)(2,1)S(1)}, bf16[48,1280]{1,0:T(8,128)(2,1)S(1)}, u32[]{:S(2)}, u32[]{:S(2)}) collective-permute-start(bf16[48,1280]{1,0:T(8,128)(2,1)S(1)} %shard_map.129.refs_3_), channel_id=1, source_target_pairs={{0,24},{8,16},{16,8},{24,0},{1,25},{9,17},{17,9},{25,1},{2,26},{10... | collective-permute-start | bytes 368648 | tf_op jit(solution)/shard_map/ppermute | solution.py:293
  46.2 6.8 %collective-permute-start.21 = (bf16[48,1280]{1,0:T(8,128)(2,1)S(1)}, bf16[48,1280]{1,0:T(8,128)(2,1)S(1)}, u32[]{:S(2)}, u32[]{:S(2)}) collective-permute-start(bf16[48,1280]{1,0:T(8,128)(2,1)S(1)} %shard_map.129.refs_3_), channel_id=1, source_target_pairs={{0,16},{8,24},{16,0},{24,8},{1,17},{9,25},{17,1},{25,9},{2,18},{10... | collective-permute-start | bytes 368648 | tf_op jit(solution)/shard_map/ppermute | solution.py:293
  48.8 4.9 %collective-permute-start.22 = (bf16[48,1280]{1,0:T(8,128)(2,1)S(1)}, bf16[48,1280]{1,0:T(8,128)(2,1)S(1)}, u32[]{:S(2)}, u32[]{:S(2)}) collective-permute-start(bf16[48,1280]{1,0:T(8,128)(2,1)S(1)} %shard_map.129.refs_3_), channel_id=1, source_target_pairs={{0,8},{8,0},{16,24},{24,16},{1,9},{9,1},{17,25},{25,17},{2,10},{10... | collective-permute-start | bytes 368648 | tf_op jit(solution)/shard_map/ppermute | solution.py:293

commit v15 on v11

--- a/solution.py
+++ b/solution.py
@@ -37,17 +37,19 @@
 
 def slots_kernel(chips, dp, slots_hbm, rows_hbm, counts_hbm, own_out, other_out, slots_ref, rows_ref, counts_ref, sems):
     d, z, core = place()
+    part = slots_ref.shape[2]
     copies = [
         pltpu.make_async_copy(rows_hbm, rows_ref, sems.at[0]),
         pltpu.make_async_copy(counts_hbm, counts_ref, sems.at[1]),
-        pltpu.make_async_copy(slots_hbm, slots_ref, sems.at[2]),
     ]
+    for t in range(dp):
+        spot = pl.ds(pl.multiple_of((d ^ t) * part, LANES), part)
+        copies.append(pltpu.make_async_copy(slots_hbm.at[:, spot], slots_ref.at[t], sems.at[2 + t]))
     for copy in copies:
         copy.start()
     cap, owners = rows_ref.shape[0], rows_ref.shape[2]
     count = cap * owners
     group = cap * chips
-    part = slots_ref.shape[1] // dp
     q = iota((count, count), 0)
     away = jnp.where(q >= group, 1, 0)
     q = q - away * group
@@ -64,10 +66,10 @@
     ids = jnp.where(over(iota((count, 1), 0), owners) < live, rows, -1)
     ids = jnp.broadcast_to(ids, (count, LANES)).astype(jnp.bfloat16)
     ids = exact(pick, ids)
-    copies[2].wait()
     outs = ((own_out, slice(0, group)), (other_out, slice(group, count)))
     for t in range(dp):
-        values = exact(pick, slots_ref[:, pl.ds(pl.multiple_of((d ^ t) * part, LANES), part)])
+        copies[2 + t].wait()
+        values = exact(pick, slots_ref[t])
         for out_ref, spot in outs:
             out_ref[:, t * part : (t + 1) * part] = values[spot].astype(jnp.bfloat16)
     for out_ref, spot in outs:
@@ -113,27 +115,29 @@
         out_ref[...] = packed(values, ids)
 
 
-def fetch_kernel(hidden_hbm, hidden_ref, sem):
+def fetch_kernel(chips, dp, shard, hidden_hbm, hidden_ref, order_ref, sem):
     copy = pltpu.make_async_copy(hidden_hbm, hidden_ref, sem)
     copy.start()
-    copy.wait()
-
-
-def head_kernel(chips, dp, shard, mask_ref, own_ref, other_ref, *refs):
-    d, z, core = place()
-    parts, outs = refs[:chips], refs[chips:]
+    d, z, core = place()
     rows = dp * shard
     total = chips * rows
-    cols = own_ref.shape[1]
     size = chips * shard
     r = iota((total, total), 0)
     t = over(r, size)
     s = over(r - t * size, shard)
     i = r - t * size - s * shard
-    order = one_hot(iota((total, total), 1) == s * rows + (t ^ d) * shard + i)
+    order_ref[...] = one_hot(iota((total, total), 1) == s * rows + (t ^ d) * shard + i)
+    copy.wait()
+
+
+def head_kernel(size, mask_ref, order_ref, own_ref, other_ref, *refs):
+    d, z, core = place()
+    cols = own_ref.shape[1]
+    chips = len(refs) - order_ref.shape[0] // size
+    parts, outs = refs[:chips], refs[chips:]
     mask = mask_ref[...].astype(jnp.float32).astype(jnp.bfloat16)
     columns = jnp.concatenate([part[...] for part in parts], axis=0) * mask
-    columns = exact(order, columns).astype(jnp.bfloat16)
+    columns = exact(order_ref[...], columns).astype(jnp.bfloat16)
     for at, ref in ((core, own_ref), (1 - core, other_ref)):
         head = exact(columns, ref[...])
         spot = pl.ds(pl.multiple_of(at * cols, LANES), cols)
@@ -256,10 +260,6 @@
         cost_estimate=pl.CostEstimate(flops=0, bytes_accessed=moved * cost, transcendentals=0),
         compiler_params=pltpu.CompilerParams(vmem_limit_bytes=VMEM_LIMIT),
     )(*args)
-
-
-def local_copies(*args):
-    return [pltpu.VMEM(x.shape, x.dtype) for x in args] + [pltpu.SemaphoreType.DMA((len(args),))]
 
 
 def aligned(
@@ -301,14 +301,25 @@
         [shaped((group, width + LANES), bf16)] * CORES,
         *slots_in,
         hbm=3,
-        scratch=local_copies(*slots_in),
+        scratch=[
+            pltpu.VMEM((dp, cap * owners, width // dp), bf16),
+            pltpu.VMEM(slots_in[1].shape, jnp.int32),
+            pltpu.VMEM(slots_in[2].shape, jnp.int32),
+            pltpu.SemaphoreType.DMA((2 + dp,)),
+        ],
     )
     slots_other = send(slots_other, 0, 1)
     slots_other, hidden_other = lax.optimization_barrier((slots_other, hidden_other))
     quarter = width // dp
     packets = [shaped((vocab * cap * quarter // LANES + ID_ROWS, LANES), bf16)]
     quarters = run(functools.partial(peers_kernel, dp), packets * dp, slots_own, slots_other)
-    held = run(fetch_kernel, shaped(hidden.shape, bf16), hidden, hbm=1, scratch=[pltpu.SemaphoreType.DMA])
+    held, head_order = run(
+        functools.partial(fetch_kernel, chips, dp, shard),
+        [shaped(hidden.shape, bf16), shaped((chips * rows, chips * rows), bf16)],
+        hidden,
+        hbm=1,
+        scratch=[pltpu.SemaphoreType.DMA],
+    )
     quarters = [send_dp(quarters[t], t) for t in reversed(range(dp))]
     quarters[-1], held = lax.optimization_barrier((quarters[-1], held))
     messages = run(functools.partial(owners_kernel, chips, cap, quarter), packets * chips, *quarters)
@@ -316,9 +327,10 @@
     for s in range(1, chips):
         columns.append(send(columns[s - 1], 1) if s % 2 else send(columns[0], s))
     head = run(
-        functools.partial(head_kernel, chips, dp, shard),
+        functools.partial(head_kernel, chips * shard),
         [shaped((chips * shard, cols), f32)] * dp,
         predict_mask[None, :],
+        head_order,
         held,
         hidden_other,
         *columns,

time: 52.7 us -> 53 us (level)
  transfers between devices with their start and end apart: 23 -> 23, of which waited for: 13 -> 12; matrix products, arithmetic and copies ran while one was open for 0% -> 0% of each run, Pallas kernels for 11% -> 12%
where the time goes in v15:
time: 53 us; the launch traced here: 52.8 us
  starting transfers between devices  32.4 us (61%)
  waiting for transfers between devices  12 us (23%)
  Pallas kernels  7.62 us (14%)
  between operations  0.75 us (1%)
    ppermute x11, starting transfers between devices, send(): lax.ppermute(x, 'vocab', [(v, v ^ move) for v in range(vocab)])  19.2 us
    ppermute x12, starting transfers between devices, send_dp(): return lax.ppermute(x, 'dp', [(i, i ^ t) for i in range(dp)]) if t else x  13.2 us
    pallas_call x11, Pallas kernels, run(): pl.pallas_call(kernel, out_shape=outs, in_specs=[pl.BlockSpec(memory_spac...  7.62 us
    ppermute x11, waiting for transfers between devices, send(): lax.ppermute(x, 'vocab', [(v, v ^ move) for v in range(vocab)])  6.75 us
    ppermute x12, waiting for transfers between devices, send_dp(): return lax.ppermute(x, 'dp', [(i, i ^ t) for i in range(dp)]) if t else x  5.26 us
  transfers between devices with their start and end apart: 23, of which 12 were waited for; matrix products, arithmetic and copies ran while one was open for 0% of the time, Pallas kernels for 12%

profile of v15, /device:TPU:0, one launch (start us, length us, event | category | flops | bytes accessed | tf_op | source)
XLA Modules:
  0.0 52.8 jit_solution(175137554758771758)
XLA Ops:
  0.6 0.5 collective-permute-start.1
  1.2 1.7 %shard_map.120 = (bf16[24,5248]{1,0:T(8,128)(2,1)S(1)}, bf16[24,5248]{1,0:T(8,128)(2,1)S(1)}) custom-call(bf16[48,5120]{1,0:T(8,128)(2,1)} %bitcast.12, s32[6,1,8]{2,1,0:T(1,128)} %bitcast.13, s32[1,8]{1,0:T(1,128)} %counts_hbm.1), custom_call_target="tpu_custom_call" | custom-call | bytes 995552 | tf_op jit(solution)/shard_map/pallas_call | solution.py:254
  2.9 0.1 collective-permute-start
  3.0 4.0 %collective-permute-start.12 = (bf16[48,1024]{1,0:T(8,128)(2,1)}, bf16[48,1024]{1,0:T(8,128)(2,1)S(1)}, u32[]{:S(2)}, u32[]{:S(2)}) collective-permute-start(bf16[48,1024]{1,0:T(8,128)(2,1)} %bitcast.8), channel_id=1, source_target_pairs={{0,4},{1,5},{2,6},{3,7},{4,0},{5,1},{6,2},{7,3},{8,12},{9,13},{10,... | collective-permute-start | bytes 294920 | tf_op jit(solution)/shard_map/ppermute | solution.py:288
  7.0 0.1 shard_map.121
  7.1 2.5 %collective-permute-start.2 = (bf16[496,128]{1,0:T(8,128)(2,1)S(1)}, bf16[496,128]{1,0:T(8,128)(2,1)S(1)}, u32[]{:S(2)}, u32[]{:S(2)}) collective-permute-start(bf16[496,128]{1,0:T(8,128)(2,1)S(1)} %get-tuple-element.39), channel_id=1, source_target_pairs={{0,24},{8,16},{16,8},{24,0},{1,25},{9,17},{17,9},{25,1},{2,26},{10... | collective-permute-start | bytes 380936 | tf_op jit(solution)/shard_map/ppermute | solution.py:291
  9.6 0.5 collective-permute-start.3
  10.1 0.5 %collective-permute-start.4 = (bf16[496,128]{1,0:T(8,128)(2,1)S(1)}, bf16[496,128]{1,0:T(8,128)(2,1)S(1)}, u32[]{:S(2)}, u32[]{:S(2)}) collective-permute-start(bf16[496,128]{1,0:T(8,128)(2,1)S(1)} %get-tuple-element.41), channel_id=1, source_target_pairs={{0,8},{8,0},{16,24},{24,16},{1,9},{9,1},{17,25},{25,17},{2,10},{10... | collective-permute-start | bytes 380936 | tf_op jit(solution)/shard_map/ppermute | solution.py:291
  10.7 1.6 %collective-permute-start.11 = (bf16[48,1024]{1,0:T(8,128)(2,1)}, bf16[48,1024]{1,0:T(8,128)(2,1)S(1)}, u32[]{:S(2)}, u32[]{:S(2)}) collective-permute-start(bf16[48,1024]{1,0:T(8,128)(2,1)} %bitcast.9), channel_id=1, source_target_pairs={{0,2},{1,3},{2,0},{3,1},{4,6},{5,7},{6,4},{7,5},{8,10},{9,11},{10,... | collective-permute-start | bytes 294920 | tf_op jit(solution)/shard_map/ppermute | solution.py:288
  12.2 0.1 collective-permute-done.12.refs_2_
  12.4 0.8 %collective-permute-start.13 = (bf16[48,1024]{1,0:T(8,128)(2,1)S(1)}, bf16[48,1024]{1,0:T(8,128)(2,1)S(1)}, u32[]{:S(2)}, u32[]{:S(2)}) collective-permute-start(bf16[48,1024]{1,0:T(8,128)(2,1)S(1)} %collective-permute-done.12.refs_2_), channel_id=1, source_target_pairs={{0,2},{1,3},{2,0},{3,1},{4,6},{5,7},{6,4},{7,5},{8,10},{9,11},{10,... | collective-permute-start | bytes 294920 | tf_op jit(solution)/shard_map/ppermute | solution.py:288
  13.2 1.3 %shard_map.122 = (bf16[1024,640]{1,0:T(8,128)(2,1)S(1)}, bf16[192,192]{1,0:T(8,128)(2,1)S(1)}) custom-call(bf16[1024,640]{1,0:T(8,128)(2,1)} %hidden_hbm.1), custom_call_target="tpu_custom_call" | custom-call | bytes 2695168 | tf_op jit(solution)/shard_map/pallas_call | solution.py:254
  14.5 1.4 %collective-permute-done.3.refs_1_ = bf16[496,128]{1,0:T(8,128)(2,1)S(1)} collective-permute-done((bf16[496,128]{1,0:T(8,128)(2,1)S(1)}, bf16[496,128]{1,0:T(8,128)(2,1)S(1)}, u32[]{:S(2)}, u32[]{:S(2)}) %collective-permute-start.3) | collective-permute-done | bytes 127008 | tf_op jit(solution)/shard_map/ppermute | solution.py:291
  15.9 0.1 collective-permute-done.4.refs_2_
  16.0 0.4 shard_map.123
  16.3 2.8 %collective-permute-start.5 = (bf16[496,128]{1,0:T(8,128)(2,1)S(1)}, bf16[496,128]{1,0:T(8,128)(2,1)S(1)}, u32[]{:S(2)}, u32[]{:S(2)}) collective-permute-start(bf16[496,128]{1,0:T(8,128)(2,1)S(1)} %get-tuple-element.45), channel_id=1, source_target_pairs={{0,6},{1,7},{2,4},{3,5},{4,2},{5,3},{6,0},{7,1},{8,14},{9,15},{10,... | collective-permute-start | bytes 380936 | tf_op jit(solution)/shard_map/ppermute | solution.py:288
  19.2 0.9 %shard_map.126 = (f32[48,1280]{1,0:T(8,128)S(1)}, f32[48,1280]{1,0:T(8,128)S(1)}, f32[48,1280]{1,0:T(8,128)S(1)}, f32[48,1280]{1,0:T(8,128)S(1)}) custom-call(s32[1,1024]{1,0:T(1,128)S(1)} %bitcast.11, bf16[192,192]{1,0:T(8,128)(2,1)S(1)} %get-tuple-element.53.order_ref, bf16[1024,640]{1,0:T(8,128)(2,1)S(1)} %get-tuple-element.54.own_ref, ...), custom_call_target="tpu_custom_call" | custom-call | bytes 4075520 | tf_op jit(solution)/shard_map/pallas_call | solution.py:254
  20.1 0.0 copy-start
  20.1 0.0 copy-start.1
  20.1 0.0 copy-start.2
  20.2 1.7 %collective-permute-start.14 = (f32[48,1280]{1,0:T(8,128)S(1)}, f32[48,1280]{1,0:T(8,128)S(1)}, u32[]{:S(2)}, u32[]{:S(2)}) collective-permute-start(f32[48,1280]{1,0:T(8,128)S(1)} %get-tuple-element.56), channel_id=1, source_target_pairs={{0,24},{8,16},{16,8},{24,0},{1,25},{9,17},{17,9},{25,1},{2,26},{10... | collective-permute-start | bytes 737288 | tf_op jit(solution)/shard_map/ppermute | solution.py:291
  21.9 1.3 %collective-permute-start.15 = (f32[48,1280]{1,0:T(8,128)S(1)}, f32[48,1280]{1,0:T(8,128)S(1)}, u32[]{:S(2)}, u32[]{:S(2)}) collective-permute-start(f32[48,1280]{1,0:T(8,128)S(1)} %get-tuple-element.57), channel_id=1, source_target_pairs={{0,16},{8,24},{16,0},{24,8},{1,17},{9,25},{17,1},{25,9},{2,18},{10... | collective-permute-start | bytes 737288 | tf_op jit(solution)/shard_map/ppermute | solution.py:291
  23.2 0.5 %collective-permute-start.16 = (f32[48,1280]{1,0:T(8,128)S(1)}, f32[48,1280]{1,0:T(8,128)S(1)}, u32[]{:S(2)}, u32[]{:S(2)}) collective-permute-start(f32[48,1280]{1,0:T(8,128)S(1)} %get-tuple-element.58), channel_id=1, source_target_pairs={{0,8},{8,0},{16,24},{24,16},{1,9},{9,1},{17,25},{25,17},{2,10},{10... | collective-permute-start | bytes 737288 | tf_op jit(solution)/shard_map/ppermute | solution.py:291
  23.7 0.3 collective-permute-start.6
  24.0 3.6 %collective-permute-start.7 = (bf16[496,128]{1,0:T(8,128)(2,1)S(1)}, bf16[496,128]{1,0:T(8,128)(2,1)S(1)}, u32[]{:S(2)}, u32[]{:S(2)}) collective-permute-start(bf16[496,128]{1,0:T(8,128)(2,1)S(1)} %get-tuple-element.47), channel_id=1, source_target_pairs={{0,2},{1,3},{2,0},{3,1},{4,6},{5,7},{6,4},{7,5},{8,10},{9,11},{10,... | collective-permute-start | bytes 380936 | tf_op jit(solution)/shard_map/ppermute | solution.py:288
  27.5 3.3 %collective-permute-done.6.refs_1_ = bf16[496,128]{1,0:T(8,128)(2,1)S(1)} collective-permute-done((bf16[496,128]{1,0:T(8,128)(2,1)S(1)}, bf16[496,128]{1,0:T(8,128)(2,1)S(1)}, u32[]{:S(2)}, u32[]{:S(2)}) %collective-permute-start.6) | collective-permute-done | bytes 127008 | tf_op jit(solution)/shard_map/ppermute | solution.py:288
  30.9 0.8 %collective-permute-done.7.refs_2_ = bf16[496,128]{1,0:T(8,128)(2,1)S(1)} collective-permute-done((bf16[496,128]{1,0:T(8,128)(2,1)S(1)}, bf16[496,128]{1,0:T(8,128)(2,1)S(1)}, u32[]{:S(2)}, u32[]{:S(2)}) %collective-permute-start.7) | collective-permute-done | bytes 127008 | tf_op jit(solution)/shard_map/ppermute | solution.py:288
  31.7 0.5 shard_map.124
  32.1 1.3 %collective-permute-start.10 = (f32[24,640]{1,0:T(8,128)S(1)}, f32[24,640]{1,0:T(8,128)S(1)}, u32[]{:S(2)}, u32[]{:S(2)}) collective-permute-start(f32[24,640]{1,0:T(8,128)S(1)} %get-tuple-element.52), channel_id=1, source_target_pairs={{0,24},{8,16},{16,8},{24,0},{1,25},{9,17},{17,9},{25,1},{2,26},{10... | collective-permute-start | bytes 184328 | tf_op jit(solution)/shard_map/ppermute | solution.py:291
  33.5 0.8 %collective-permute-done.15.refs_1_ = f32[48,1280]{1,0:T(8,128)S(1)} collective-permute-done((f32[48,1280]{1,0:T(8,128)S(1)}, f32[48,1280]{1,0:T(8,128)S(1)}, u32[]{:S(2)}, u32[]{:S(2)}) %collective-permute-start.15) | collective-permute-done | bytes 245792 | tf_op jit(solution)/shard_map/ppermute | solution.py:291
  34.3 0.1 shard_map.127
  34.3 1.9 %collective-permute-start.17 = (f32[24,640]{1,0:T(8,128)S(1)}, f32[24,640]{1,0:T(8,128)S(1)}, u32[]{:S(2)}, u32[]{:S(2)}) collective-permute-start(f32[24,640]{1,0:T(8,128)S(1)} %get-tuple-element.60), channel_id=1, source_target_pairs={{0,6},{1,7},{2,4},{3,5},{4,2},{5,3},{6,0},{7,1},{8,14},{9,15},{10,... | collective-permute-start | bytes 184328 | tf_op jit(solution)/shard_map/ppermute | solution.py:288
  36.2 0.7 %collective-permute-start.8 = (f32[24,640]{1,0:T(8,128)S(1)}, f32[24,640]{1,0:T(8,128)S(1)}, u32[]{:S(2)}, u32[]{:S(2)}) collective-permute-start(f32[24,640]{1,0:T(8,128)S(1)} %get-tuple-element.50), channel_id=1, source_target_pairs={{0,8},{8,0},{16,24},{24,16},{1,9},{9,1},{17,25},{25,17},{2,10},{10... | collective-permute-start | bytes 184328 | tf_op jit(solution)/shard_map/ppermute | solution.py:291
  36.9 0.5 collective-permute-start.9
  37.4 0.7 %collective-permute-start.18 = (f32[24,640]{1,0:T(8,128)S(1)}, f32[24,640]{1,0:T(8,128)S(1)}, u32[]{:S(2)}, u32[]{:S(2)}) collective-permute-start(f32[24,640]{1,0:T(8,128)S(1)} %get-tuple-element.61), channel_id=1, source_target_pairs={{0,4},{1,5},{2,6},{3,7},{4,0},{5,1},{6,2},{7,3},{8,12},{9,13},{10,... | collective-permute-start | bytes 184328 | tf_op jit(solution)/shard_map/ppermute | solution.py:288
  38.1 2.9 %collective-permute-start.19 = (f32[24,640]{1,0:T(8,128)S(1)}, f32[24,640]{1,0:T(8,128)S(1)}, u32[]{:S(2)}, u32[]{:S(2)}) collective-permute-start(f32[24,640]{1,0:T(8,128)S(1)} %get-tuple-element.62), channel_id=1, source_target_pairs={{0,2},{1,3},{2,0},{3,1},{4,6},{5,7},{6,4},{7,5},{8,10},{9,11},{10,... | collective-permute-start | bytes 184328 | tf_op jit(solution)/shard_map/ppermute | solution.py:288
  41.0 0.1 collective-permute-done.9.refs_2_
  41.2 2.1 %collective-permute-done.18.refs_5_ = f32[24,640]{1,0:T(8,128)S(1)} collective-permute-done((f32[24,640]{1,0:T(8,128)S(1)}, f32[24,640]{1,0:T(8,128)S(1)}, u32[]{:S(2)}, u32[]{:S(2)}) %collective-permute-start.18) | collective-permute-done | bytes 61472 | tf_op jit(solution)/shard_map/ppermute | solution.py:288
  43.3 0.4 collective-permute-done.19.refs_6_
  43.7 0.3 shard_map.129.refs_3_
  44.0 1.6 %collective-permute-start.20 = (bf16[48,1280]{1,0:T(8,128)(2,1)S(1)}, bf16[48,1280]{1,0:T(8,128)(2,1)S(1)}, u32[]{:S(2)}, u32[]{:S(2)}) collective-permute-start(bf16[48,1280]{1,0:T(8,128)(2,1)S(1)} %shard_map.129.refs_3_), channel_id=1, source_target_pairs={{0,24},{8,16},{16,8},{24,0},{1,25},{9,17},{17,9},{25,1},{2,26},{10... | collective-permute-start | bytes 368648 | tf_op jit(solution)/shard_map/ppermute | solution.py:291
  45.5 1.3 %collective-permute-start.21 = (bf16[48,1280]{1,0:T(8,128)(2,1)S(1)}, bf16[48,1280]{1,0:T(8,128)(2,1)S(1)}, u32[]{:S(2)}, u32[]{:S(2)}) collective-permute-start(bf16[48,1280]{1,0:T(8,128)(2,1)S(1)} %shard_map.129.refs_3_), channel_id=1, source_target_pairs={{0,16},{8,24},{16,0},{24,8},{1,17},{9,25},{17,1},{25,9},{2,18},{10... | collective-permute-start | bytes 368648 | tf_op jit(solution)/shard_map/ppermute | solution.py:291
  46.9 0.7 %collective-permute-start.22 = (bf16[48,1280]{1,0:T(8,128)(2,1)S(1)}, bf16[48,1280]{1,0:T(8,128)(2,1)S(1)}, u32[]{:S(2)}, u32[]{:S(2)}) collective-permute-start(bf16[48,1280]{1,0:T(8,128)(2,1)S(1)} %shard_map.129.refs_3_), channel_id=1, source_target_pairs={{0,8},{8,0},{16,24},{24,16},{1,9},{9,1},{17,25},{25,17},{2,10},{10... | collective-permute-start | bytes 368648 | tf_op jit(solution)/shard_map/ppermute | solution.py:291
  47.5 1.3 %shard_map.128 = (f32[12,5120]{1,0:T(8,128)}, f32[12,5120]{1,0:T(8,128)}, f32[12,5120]{1,0:T(8,128)}, bf16[192,192]{1,0:T(8,128)(2,1)S(1)}) custom-call(f32[12,5120]{1,0:T(8,128)S(1)} %shard_map.125.refs_0_, f32[12,5120]{1,0:T(8,128)S(1)} %copy-done, f32[12,5120]{1,0:T(8,128)S(1)} %copy-done.1, f32[12,5120]{1,0:T(8,128)S(1)} %copy-done.2, ...), custom_call_target="tpu_custom_call" | custom-call | bytes 2039808 | tf_op jit(solution)/shard_map/pallas_call | solution.py:254
  48.8 1.1 %collective-permute-done.20.refs_0_ = bf16[48,1280]{1,0:T(8,128)(2,1)S(1)} collective-permute-done((bf16[48,1280]{1,0:T(8,128)(2,1)S(1)}, bf16[48,1280]{1,0:T(8,128)(2,1)S(1)}, u32[]{:S(2)}, u32[]{:S(2)}) %collective-permute-start.20) | collective-permute-done | bytes 122912 | tf_op jit(solution)/shard_map/ppermute | solution.py:291
  49.9 1.2 %collective-permute-done.21.refs_1_ = bf16[48,1280]{1,0:T(8,128)(2,1)S(1)} collective-permute-done((bf16[48,1280]{1,0:T(8,128)(2,1)S(1)}, bf16[48,1280]{1,0:T(8,128)(2,1)S(1)}, u32[]{:S(2)}, u32[]{:S(2)}) %collective-permute-start.21) | collective-permute-done | bytes 122912 | tf_op jit(solution)/shard_map/ppermute | solution.py:291
  51.1 0.6 %collective-permute-done.22.refs_2_ = bf16[48,1280]{1,0:T(8,128)(2,1)S(1)} collective-permute-done((bf16[48,1280]{1,0:T(8,128)(2,1)S(1)}, bf16[48,1280]{1,0:T(8,128)(2,1)S(1)}, u32[]{:S(2)}, u32[]{:S(2)}) %collective-permute-start.22) | collective-permute-done | bytes 122912 | tf_op jit(solution)/shard_map/ppermute | solution.py:291
  51.7 1.1 %shard_map.130 = bf16[48,5120]{1,0:T(8,128)(2,1)} custom-call(bf16[192,192]{1,0:T(8,128)(2,1)S(1)} %get-tuple-element.67.order_ref, bf16[48,1280]{1,0:T(8,128)(2,1)S(1)} %collective-permute-done.20.refs_0_, bf16[48,1280]{1,0:T(8,128)(2,1)S(1)} %collective-permute-done.21.refs_1_, bf16[48,1280]{1,0:T(8,128)(2,1)S(1)} %collective-permute-done.22.refs_2_, ...), custom_call_target="tpu_custom_call" | custom-call | bytes 1056768 | tf_op jit(solution)/shard_map/pallas_call | solution.py:254
  (19 shorter events, 0.1 us)
Async XLA Ops:
  0.6 6.4 %collective-permute-start.1 = (bf16[1024,640]{1,0:T(8,128)(2,1)}, bf16[1024,640]{1,0:T(8,128)(2,1)S(1)}, u32[]{:S(2)}, u32[]{:S(2)}) collective-permute-start(bf16[1024,640]{1,0:T(8,128)(2,1)} %hidden_hbm.1), channel_id=1, source_target_pairs={{0,1},{1,0},{2,3},{3,2},{4,5},{5,4},{6,7},{7,6},{8,9},{9,8},{10,11... | collective-permute-start | bytes 3932168 | tf_op jit(solution)/shard_map/ppermute | solution.py:288
  1.1 18.0 %copy-start.3 = (bf16[1024,48]{0,1:T(8,128)(2,1)S(1)}, bf16[1024,48]{0,1:T(8,128)(2,1)}, u32[]{:S(2)}) copy-start(bf16[1024,48]{0,1:T(8,128)(2,1)} %param.10) | copy-start | bytes 294916
  1.2 18.0 %copy-start.4 = (s32[1024]{0:T(1024)S(1)}, s32[1024]{0:T(1024)}, u32[]{:S(2)}) copy-start(s32[1024]{0:T(1024)} %param.11) | copy-start | bytes 12292
  2.9 4.2 %collective-permute-start = (bf16[24,5248]{1,0:T(8,128)(2,1)S(1)}, bf16[24,5248]{1,0:T(8,128)(2,1)S(1)}, u32[]{:S(2)}, u32[]{:S(2)}) collective-permute-start(bf16[24,5248]{1,0:T(8,128)(2,1)S(1)} %get-tuple-element.37), channel_id=1, source_target_pairs={{0,1},{1,0},{2,3},{3,2},{4,5},{5,4},{6,7},{7,6},{8,9},{9,8},{10,11... | collective-permute-start | bytes 755720 | tf_op jit(solution)/shard_map/ppermute | solution.py:288
  3.0 9.4 %collective-permute-start.12 = (bf16[48,1024]{1,0:T(8,128)(2,1)}, bf16[48,1024]{1,0:T(8,128)(2,1)S(1)}, u32[]{:S(2)}, u32[]{:S(2)}) collective-permute-start(bf16[48,1024]{1,0:T(8,128)(2,1)} %bitcast.8), channel_id=1, source_target_pairs={{0,4},{1,5},{2,6},{3,7},{4,0},{5,1},{6,2},{7,3},{8,12},{9,13},{10,... | collective-permute-start | bytes 294920 | tf_op jit(solution)/shard_map/ppermute | solution.py:288
  7.1 7.4 %collective-permute-start.2 = (bf16[496,128]{1,0:T(8,128)(2,1)S(1)}, bf16[496,128]{1,0:T(8,128)(2,1)S(1)}, u32[]{:S(2)}, u32[]{:S(2)}) collective-permute-start(bf16[496,128]{1,0:T(8,128)(2,1)S(1)} %get-tuple-element.39), channel_id=1, source_target_pairs={{0,24},{8,16},{16,8},{24,0},{1,25},{9,17},{17,9},{25,1},{2,26},{10... | collective-permute-start | bytes 380936 | tf_op jit(solution)/shard_map/ppermute | solution.py:291
  9.6 6.3 %collective-permute-start.3 = (bf16[496,128]{1,0:T(8,128)(2,1)S(1)}, bf16[496,128]{1,0:T(8,128)(2,1)S(1)}, u32[]{:S(2)}, u32[]{:S(2)}) collective-permute-start(bf16[496,128]{1,0:T(8,128)(2,1)S(1)} %get-tuple-element.40), channel_id=1, source_target_pairs={{0,16},{8,24},{16,0},{24,8},{1,17},{9,25},{17,1},{25,9},{2,18},{10... | collective-permute-start | bytes 380936 | tf_op jit(solution)/shard_map/ppermute | solution.py:291
  10.1 5.8 %collective-permute-start.4 = (bf16[496,128]{1,0:T(8,128)(2,1)S(1)}, bf16[496,128]{1,0:T(8,128)(2,1)S(1)}, u32[]{:S(2)}, u32[]{:S(2)}) collective-permute-start(bf16[496,128]{1,0:T(8,128)(2,1)S(1)} %get-tuple-element.41), channel_id=1, source_target_pairs={{0,8},{8,0},{16,24},{24,16},{1,9},{9,1},{17,25},{25,17},{2,10},{10... | collective-permute-start | bytes 380936 | tf_op jit(solution)/shard_map/ppermute | solution.py:291
  10.7 8.5 %collective-permute-start.11 = (bf16[48,1024]{1,0:T(8,128)(2,1)}, bf16[48,1024]{1,0:T(8,128)(2,1)S(1)}, u32[]{:S(2)}, u32[]{:S(2)}) collective-permute-start(bf16[48,1024]{1,0:T(8,128)(2,1)} %bitcast.9), channel_id=1, source_target_pairs={{0,2},{1,3},{2,0},{3,1},{4,6},{5,7},{6,4},{7,5},{8,10},{9,11},{10,... | collective-permute-start | bytes 294920 | tf_op jit(solution)/shard_map/ppermute | solution.py:288
  12.4 6.8 %collective-permute-start.13 = (bf16[48,1024]{1,0:T(8,128)(2,1)S(1)}, bf16[48,1024]{1,0:T(8,128)(2,1)S(1)}, u32[]{:S(2)}, u32[]{:S(2)}) collective-permute-start(bf16[48,1024]{1,0:T(8,128)(2,1)S(1)} %collective-permute-done.12.refs_2_), channel_id=1, source_target_pairs={{0,2},{1,3},{2,0},{3,1},{4,6},{5,7},{6,4},{7,5},{8,10},{9,11},{10,... | collective-permute-start | bytes 294920 | tf_op jit(solution)/shard_map/ppermute | solution.py:288
  16.3 7.7 %collective-permute-start.5 = (bf16[496,128]{1,0:T(8,128)(2,1)S(1)}, bf16[496,128]{1,0:T(8,128)(2,1)S(1)}, u32[]{:S(2)}, u32[]{:S(2)}) collective-permute-start(bf16[496,128]{1,0:T(8,128)(2,1)S(1)} %get-tuple-element.45), channel_id=1, source_target_pairs={{0,6},{1,7},{2,4},{3,5},{4,2},{5,3},{6,0},{7,1},{8,14},{9,15},{10,... | collective-permute-start | bytes 380936 | tf_op jit(solution)/shard_map/ppermute | solution.py:288
  20.1 23.5 %copy-start = (f32[12,5120]{1,0:T(8,128)S(1)}, f32[12,5120]{1,0:T(8,128)}, u32[]{:S(2)}) copy-start(f32[12,5120]{1,0:T(8,128)} %refs_1_.3) | copy-start | bytes 737284
  20.1 23.5 %copy-start.1 = (f32[12,5120]{1,0:T(8,128)S(1)}, f32[12,5120]{1,0:T(8,128)}, u32[]{:S(2)}) copy-start(f32[12,5120]{1,0:T(8,128)} %refs_2_.3) | copy-start | bytes 737284
  20.1 23.5 %copy-start.2 = (f32[12,5120]{1,0:T(8,128)S(1)}, f32[12,5120]{1,0:T(8,128)}, u32[]{:S(2)}) copy-start(f32[12,5120]{1,0:T(8,128)} %refs_3_.3) | copy-start | bytes 737284
  20.2 13.3 %collective-permute-start.14 = (f32[48,1280]{1,0:T(8,128)S(1)}, f32[48,1280]{1,0:T(8,128)S(1)}, u32[]{:S(2)}, u32[]{:S(2)}) collective-permute-start(f32[48,1280]{1,0:T(8,128)S(1)} %get-tuple-element.56), channel_id=1, source_target_pairs={{0,24},{8,16},{16,8},{24,0},{1,25},{9,17},{17,9},{25,1},{2,26},{10... | collective-permute-start | bytes 737288 | tf_op jit(solution)/shard_map/ppermute | solution.py:291
  21.9 12.4 %collective-permute-start.15 = (f32[48,1280]{1,0:T(8,128)S(1)}, f32[48,1280]{1,0:T(8,128)S(1)}, u32[]{:S(2)}, u32[]{:S(2)}) collective-permute-start(f32[48,1280]{1,0:T(8,128)S(1)} %get-tuple-element.57), channel_id=1, source_target_pairs={{0,16},{8,24},{16,0},{24,8},{1,17},{9,25},{17,1},{25,9},{2,18},{10... | collective-permute-start | bytes 737288 | tf_op jit(solution)/shard_map/ppermute | solution.py:291
  23.2 11.1 %collective-permute-start.16 = (f32[48,1280]{1,0:T(8,128)S(1)}, f32[48,1280]{1,0:T(8,128)S(1)}, u32[]{:S(2)}, u32[]{:S(2)}) collective-permute-start(f32[48,1280]{1,0:T(8,128)S(1)} %get-tuple-element.58), channel_id=1, source_target_pairs={{0,8},{8,0},{16,24},{24,16},{1,9},{9,1},{17,25},{25,17},{2,10},{10... | collective-permute-start | bytes 737288 | tf_op jit(solution)/shard_map/ppermute | solution.py:291
  23.7 7.2 %collective-permute-start.6 = (bf16[496,128]{1,0:T(8,128)(2,1)S(1)}, bf16[496,128]{1,0:T(8,128)(2,1)S(1)}, u32[]{:S(2)}, u32[]{:S(2)}) collective-permute-start(bf16[496,128]{1,0:T(8,128)(2,1)S(1)} %get-tuple-element.46), channel_id=1, source_target_pairs={{0,4},{1,5},{2,6},{3,7},{4,0},{5,1},{6,2},{7,3},{8,12},{9,13},{10,... | collective-permute-start | bytes 380936 | tf_op jit(solution)/shard_map/ppermute | solution.py:288
  24.0 7.7 %collective-permute-start.7 = (bf16[496,128]{1,0:T(8,128)(2,1)S(1)}, bf16[496,128]{1,0:T(8,128)(2,1)S(1)}, u32[]{:S(2)}, u32[]{:S(2)}) collective-permute-start(bf16[496,128]{1,0:T(8,128)(2,1)S(1)} %get-tuple-element.47), channel_id=1, source_target_pairs={{0,2},{1,3},{2,0},{3,1},{4,6},{5,7},{6,4},{7,5},{8,10},{9,11},{10,... | collective-permute-start | bytes 380936 | tf_op jit(solution)/shard_map/ppermute | solution.py:288
  32.1 6.0 %collective-permute-start.10 = (f32[24,640]{1,0:T(8,128)S(1)}, f32[24,640]{1,0:T(8,128)S(1)}, u32[]{:S(2)}, u32[]{:S(2)}) collective-permute-start(f32[24,640]{1,0:T(8,128)S(1)} %get-tuple-element.52), channel_id=1, source_target_pairs={{0,24},{8,16},{16,8},{24,0},{1,25},{9,17},{17,9},{25,1},{2,26},{10... | collective-permute-start | bytes 184328 | tf_op jit(solution)/shard_map/ppermute | solution.py:291
  34.3 6.8 %collective-permute-start.17 = (f32[24,640]{1,0:T(8,128)S(1)}, f32[24,640]{1,0:T(8,128)S(1)}, u32[]{:S(2)}, u32[]{:S(2)}) collective-permute-start(f32[24,640]{1,0:T(8,128)S(1)} %get-tuple-element.60), channel_id=1, source_target_pairs={{0,6},{1,7},{2,4},{3,5},{4,2},{5,3},{6,0},{7,1},{8,14},{9,15},{10,... | collective-permute-start | bytes 184328 | tf_op jit(solution)/shard_map/ppermute | solution.py:288
  36.2 4.8 %collective-permute-start.8 = (f32[24,640]{1,0:T(8,128)S(1)}, f32[24,640]{1,0:T(8,128)S(1)}, u32[]{:S(2)}, u32[]{:S(2)}) collective-permute-start(f32[24,640]{1,0:T(8,128)S(1)} %get-tuple-element.50), channel_id=1, source_target_pairs={{0,8},{8,0},{16,24},{24,16},{1,9},{9,1},{17,25},{25,17},{2,10},{10... | collective-permute-start | bytes 184328 | tf_op jit(solution)/shard_map/ppermute | solution.py:291
  36.9 4.2 %collective-permute-start.9 = (f32[24,640]{1,0:T(8,128)S(1)}, f32[24,640]{1,0:T(8,128)S(1)}, u32[]{:S(2)}, u32[]{:S(2)}) collective-permute-start(f32[24,640]{1,0:T(8,128)S(1)} %get-tuple-element.51), channel_id=1, source_target_pairs={{0,16},{8,24},{16,0},{24,8},{1,17},{9,25},{17,1},{25,9},{2,18},{10... | collective-permute-start | bytes 184328 | tf_op jit(solution)/shard_map/ppermute | solution.py:291
  37.4 5.9 %collective-permute-start.18 = (f32[24,640]{1,0:T(8,128)S(1)}, f32[24,640]{1,0:T(8,128)S(1)}, u32[]{:S(2)}, u32[]{:S(2)}) collective-permute-start(f32[24,640]{1,0:T(8,128)S(1)} %get-tuple-element.61), channel_id=1, source_target_pairs={{0,4},{1,5},{2,6},{3,7},{4,0},{5,1},{6,2},{7,3},{8,12},{9,13},{10,... | collective-permute-start | bytes 184328 | tf_op jit(solution)/shard_map/ppermute | solution.py:288
  38.1 5.6 %collective-permute-start.19 = (f32[24,640]{1,0:T(8,128)S(1)}, f32[24,640]{1,0:T(8,128)S(1)}, u32[]{:S(2)}, u32[]{:S(2)}) collective-permute-start(f32[24,640]{1,0:T(8,128)S(1)} %get-tuple-element.62), channel_id=1, source_target_pairs={{0,2},{1,3},{2,0},{3,1},{4,6},{5,7},{6,4},{7,5},{8,10},{9,11},{10,... | collective-permute-start | bytes 184328 | tf_op jit(solution)/shard_map/ppermute | solution.py:288
  44.0 5.9 %collective-permute-start.20 = (bf16[48,1280]{1,0:T(8,128)(2,1)S(1)}, bf16[48,1280]{1,0:T(8,128)(2,1)S(1)}, u32[]{:S(2)}, u32[]{:S(2)}) collective-permute-start(bf16[48,1280]{1,0:T(8,128)(2,1)S(1)} %shard_map.129.refs_3_), channel_id=1, source_target_pairs={{0,24},{8,16},{16,8},{24,0},{1,25},{9,17},{17,9},{25,1},{2,26},{10... | collective-permute-start | bytes 368648 | tf_op jit(solution)/shard_map/ppermute | solution.py:291
  45.5 5.6 %collective-permute-start.21 = (bf16[48,1280]{1,0:T(8,128)(2,1)S(1)}, bf16[48,1280]{1,0:T(8,128)(2,1)S(1)}, u32[]{:S(2)}, u32[]{:S(2)}) collective-permute-start(bf16[48,1280]{1,0:T(8,128)(2,1)S(1)} %shard_map.129.refs_3_), channel_id=1, source_target_pairs={{0,16},{8,24},{16,0},{24,8},{1,17},{9,25},{17,1},{25,9},{2,18},{10... | collective-permute-start | bytes 368648 | tf_op jit(solution)/shard_map/ppermute | solution.py:291
  46.9 4.9 %collective-permute-start.22 = (bf16[48,1280]{1,0:T(8,128)(2,1)S(1)}, bf16[48,1280]{1,0:T(8,128)(2,1)S(1)}, u32[]{:S(2)}, u32[]{:S(2)}) collective-permute-start(bf16[48,1280]{1,0:T(8,128)(2,1)S(1)} %shard_map.129.refs_3_), channel_id=1, source_target_pairs={{0,8},{8,0},{16,24},{24,16},{1,9},{9,1},{17,25},{25,17},{2,10},{10... | collective-permute-start | bytes 368648 | tf_op jit(solution)/shard_map/ppermute | solution.py:291

commit v16 on v11

--- a/solution.py
+++ b/solution.py
@@ -166,12 +166,15 @@
         out_ref[...] = stacked(embed[t * shard : (t + 1) * shard])
 
 
-def gather_kernel(*refs):
-    d, z, core = place()
-    parts, out_ref = refs[:-1], refs[-1]
-    cols = out_ref.shape[1] // len(parts)
+def gather_kernel(dp, members, *refs):
+    d, z, core = place()
+    parts, pieces, out_ref = refs[:dp], refs[dp:-1], refs[-1]
+    cols = out_ref.shape[1] // dp
     for t, part in enumerate(parts):
         out_ref[:, pl.ds(pl.multiple_of((d ^ t) * cols, LANES), cols)] = unstacked(part[...])
+    for s, piece in zip(members, pieces):
+        spot = chip_spot(z, s, piece)
+        out_ref[:, spot] += unstacked(piece[...])
 
 
 def sum_kernel(chips, shard, *refs):
@@ -183,8 +186,7 @@
         out_ref[...] = stacked(total[s * shard : (s + 1) * shard])
 
 
-def step(spot, piece_ref, embed_ref, master_ref, first_ref, second_ref):
-    gradient = unstacked(piece_ref[...]) + embed_ref[:, spot]
+def step(spot, gradient, master_ref, first_ref, second_ref):
     master = master_ref[:, spot]
     first_new = 0.9 * first_ref[:, spot] + 0.1 * gradient
     second_new = 0.95 * second_ref[:, spot] + 0.05 * gradient * gradient
@@ -199,16 +201,24 @@
     return pl.ds(pl.multiple_of((z ^ s) * cols, LANES), cols)
 
 
-def rows_kernel(*refs):
-    d, z, core = place()
-    state, pieces, out_ref = refs[:4], refs[4:-1], refs[-1]
-    table = [step(chip_spot(z, s, piece), piece, *state)[0] for s, piece in enumerate(reversed(pieces))]
+def gradients(chips, cols, gradient_ref, pieces):
+    d, z, core = place()
+    for s in range(chips):
+        spot = pl.ds(pl.multiple_of((z ^ s) * cols, LANES), cols)
+        gradient = gradient_ref[:, spot]
+        yield spot, gradient + unstacked(pieces[s][...]) if s < len(pieces) else gradient
+
+
+def rows_kernel(chips, *refs):
+    (gradient_ref, *state), pieces, out_ref = refs[:4], refs[4:-1], refs[-1]
+    cols = out_ref.shape[1]
+    table = [step(spot, gradient, *state)[0] for spot, gradient in gradients(chips, cols, gradient_ref, pieces)]
     out_ref[...] = jnp.concatenate(table, axis=0).astype(jnp.bfloat16)
 
 
 def adam_kernel(chips, dp, shard, *refs):
     d, z, core = place()
-    state, pieces, outs, order_ref = refs[:4], refs[4:-4], refs[-4:-1], refs[-1]
+    (gradient_ref, *state), pieces, outs, order_ref = refs[:4], refs[4:-4], refs[-4:-1], refs[-1]
     rows = dp * shard
     total = chips * rows
     r = iota((total, total), 0)
@@ -216,9 +226,9 @@
     e = over(r - s * rows, shard)
     i = r - s * rows - e * shard
     order_ref[...] = one_hot(iota((total, total), 1) == ((e ^ d) * chips + s) * shard + i)
-    for s, piece in enumerate(reversed(pieces)):
-        spot = chip_spot(z, s, piece)
-        for out_ref, value in zip(outs, step(spot, piece, *state)):
+    cols = gradient_ref.shape[1] // chips
+    for spot, gradient in gradients(chips, cols, gradient_ref, pieces):
+        for out_ref, value in zip(outs, step(spot, gradient, *state)):
             out_ref[:, spot] = value
 
 
@@ -315,6 +325,7 @@
     columns = [logit_grad.T]
     for s in range(1, chips):
         columns.append(send(columns[s - 1], 1) if s % 2 else send(columns[0], s))
+    held, _ = lax.optimization_barrier((held, messages[0]))
     head = run(
         functools.partial(head_kernel, chips, dp, shard),
         [shaped((chips * shard, cols), f32)] * dp,
@@ -333,10 +344,18 @@
         [shaped((2 * shard, cols // 2), f32)] * chips,
         *[send_dp(head[t], t) for t in reversed(range(dp))],
     )
-    pieces = [send(sums[s], s) for s in reversed(range(chips))]
-    embed = run(gather_kernel, shaped((shard, width), f32), *[send_dp(embed[t], t) for t in range(dp)])
-    state = (embed, master, first_moment, second_moment)
-    table = run(rows_kernel, shaped((chips * shard, cols), bf16), *state, *pieces)
+    half = chips // 2
+    pieces = [send(sums[s], s) for s in reversed(range(chips))][::-1]
+    embed = [send_dp(embed[t], t) for t in range(dp)]
+    gradient = run(
+        functools.partial(gather_kernel, dp, reversed(range(half, chips))),
+        shaped((shard, width), f32),
+        *embed,
+        *pieces[:half - 1 : -1],
+    )
+    state = (gradient, master, first_moment, second_moment)
+    pieces = pieces[:half]
+    table = run(functools.partial(rows_kernel, chips), shaped((chips * shard, cols), bf16), *state, *pieces)
     master_new, first_new, second_new, order = run(
         functools.partial(adam_kernel, chips, dp, shard),
         [shaped(master.shape, f32)] * 3 + [shaped((chips * rows, chips * rows), bf16)],

time: 52.7 us -> 52.3 us (level)
    ppermute x12, waiting for transfers between devices: 5.41 us -> 4.5 us  [send_dp(): return lax.ppermute(x, 'dp', [(i, i ^ t) for i in range(dp)]) if t else x]
    ppermute x12, starting transfers between devices: 13.4 us -> 14.2 us  [send_dp(): return lax.ppermute(x, 'dp', [(i, i ^ t) for i in range(dp)]) if t else x]
    ppermute x11, starting transfers between devices: 18.9 us -> 18.1 us  [send(): lax.ppermute(x, 'vocab', [(v, v ^ move) for v in range(vocab)])]
  transfers between devices with their start and end apart: 23 -> 23, of which waited for: 13 -> 10; matrix products, arithmetic and copies ran while one was open for 0% -> 0% of each run, Pallas kernels for 11% -> 11%
where the time goes in v16:
time: 52.3 us; the launch traced here: 52.1 us
  starting transfers between devices  32.3 us (62%)
  waiting for transfers between devices  11.7 us (22%)
  Pallas kernels  7.31 us (14%)
  between operations  0.77 us (1%)
    ppermute x11, starting transfers between devices, send(): lax.ppermute(x, 'vocab', [(v, v ^ move) for v in range(vocab)])  18.1 us
    ppermute x12, starting transfers between devices, send_dp(): return lax.ppermute(x, 'dp', [(i, i ^ t) for i in range(dp)]) if t else x  14.2 us
    pallas_call x11, Pallas kernels, run(): pl.pallas_call(kernel, out_shape=outs, in_specs=[pl.BlockSpec(memory_spac...  7.31 us
    ppermute x11, waiting for transfers between devices, send(): lax.ppermute(x, 'vocab', [(v, v ^ move) for v in range(vocab)])  7.23 us
    ppermute x12, waiting for transfers between devices, send_dp(): return lax.ppermute(x, 'dp', [(i, i ^ t) for i in range(dp)]) if t else x  4.5 us
  transfers between devices with their start and end apart: 23, of which 10 were waited for; matrix products, arithmetic and copies ran while one was open for 0% of the time, Pallas kernels for 11%

profile of v16, /device:TPU:0, one launch (start us, length us, event | category | flops | bytes accessed | tf_op | source)
XLA Modules:
  0.0 52.1 jit_solution(12864138953205367458)
XLA Ops:
  0.6 0.5 collective-permute-start.1
  1.1 1.4 %shard_map.120 = (bf16[24,5248]{1,0:T(8,128)(2,1)S(1)}, bf16[24,5248]{1,0:T(8,128)(2,1)S(1)}) custom-call(bf16[48,5120]{1,0:T(8,128)(2,1)} %bitcast.12, s32[6,1,8]{2,1,0:T(1,128)} %bitcast.13, s32[1,8]{1,0:T(1,128)} %counts_hbm.1), custom_call_target="tpu_custom_call" | custom-call | bytes 995552 | tf_op jit(solution)/shard_map/pallas_call | solution.py:260
  2.5 0.1 collective-permute-start
  2.6 4.0 %collective-permute-start.12 = (bf16[48,1024]{1,0:T(8,128)(2,1)}, bf16[48,1024]{1,0:T(8,128)(2,1)S(1)}, u32[]{:S(2)}, u32[]{:S(2)}) collective-permute-start(bf16[48,1024]{1,0:T(8,128)(2,1)} %bitcast.8), channel_id=1, source_target_pairs={{0,4},{1,5},{2,6},{3,7},{4,0},{5,1},{6,2},{7,3},{8,12},{9,13},{10,... | collective-permute-start | bytes 294920 | tf_op jit(solution)/shard_map/ppermute | solution.py:298
  6.7 0.0 collective-permute-done.other_ref
  6.7 0.1 shard_map.121
  6.8 2.5 %collective-permute-start.2 = (bf16[496,128]{1,0:T(8,128)(2,1)S(1)}, bf16[496,128]{1,0:T(8,128)(2,1)S(1)}, u32[]{:S(2)}, u32[]{:S(2)}) collective-permute-start(bf16[496,128]{1,0:T(8,128)(2,1)S(1)} %get-tuple-element.38), channel_id=1, source_target_pairs={{0,24},{8,16},{16,8},{24,0},{1,25},{9,17},{17,9},{25,1},{2,26},{10... | collective-permute-start | bytes 380936 | tf_op jit(solution)/shard_map/ppermute | solution.py:301
  9.3 0.5 collective-permute-start.3
  9.8 0.5 %collective-permute-start.4 = (bf16[496,128]{1,0:T(8,128)(2,1)S(1)}, bf16[496,128]{1,0:T(8,128)(2,1)S(1)}, u32[]{:S(2)}, u32[]{:S(2)}) collective-permute-start(bf16[496,128]{1,0:T(8,128)(2,1)S(1)} %get-tuple-element.40), channel_id=1, source_target_pairs={{0,8},{8,0},{16,24},{24,16},{1,9},{9,1},{17,25},{25,17},{2,10},{10... | collective-permute-start | bytes 380936 | tf_op jit(solution)/shard_map/ppermute | solution.py:301
  10.3 1.6 %collective-permute-start.11 = (bf16[48,1024]{1,0:T(8,128)(2,1)}, bf16[48,1024]{1,0:T(8,128)(2,1)S(1)}, u32[]{:S(2)}, u32[]{:S(2)}) collective-permute-start(bf16[48,1024]{1,0:T(8,128)(2,1)} %bitcast.9), channel_id=1, source_target_pairs={{0,2},{1,3},{2,0},{3,1},{4,6},{5,7},{6,4},{7,5},{8,10},{9,11},{10,... | collective-permute-start | bytes 294920 | tf_op jit(solution)/shard_map/ppermute | solution.py:298
  11.9 0.1 collective-permute-done.12.refs_2_
  12.0 0.8 %collective-permute-start.13 = (bf16[48,1024]{1,0:T(8,128)(2,1)S(1)}, bf16[48,1024]{1,0:T(8,128)(2,1)S(1)}, u32[]{:S(2)}, u32[]{:S(2)}) collective-permute-start(bf16[48,1024]{1,0:T(8,128)(2,1)S(1)} %collective-permute-done.12.refs_2_), channel_id=1, source_target_pairs={{0,2},{1,3},{2,0},{3,1},{4,6},{5,7},{6,4},{7,5},{8,10},{9,11},{10,... | collective-permute-start | bytes 294920 | tf_op jit(solution)/shard_map/ppermute | solution.py:298
  12.9 1.3 %shard_map.122.own_ref = bf16[1024,640]{1,0:T(8,128)(2,1)S(1)} custom-call(bf16[1024,640]{1,0:T(8,128)(2,1)} %hidden_hbm.1), custom_call_target="tpu_custom_call" | custom-call | bytes 2621440 | tf_op jit(solution)/shard_map/pallas_call | solution.py:260
  14.2 1.4 %collective-permute-done.3.refs_1_ = bf16[496,128]{1,0:T(8,128)(2,1)S(1)} collective-permute-done((bf16[496,128]{1,0:T(8,128)(2,1)S(1)}, bf16[496,128]{1,0:T(8,128)(2,1)S(1)}, u32[]{:S(2)}, u32[]{:S(2)}) %collective-permute-start.3) | collective-permute-done | bytes 127008 | tf_op jit(solution)/shard_map/ppermute | solution.py:301
  15.6 0.1 collective-permute-done.4.refs_2_
  15.6 0.4 shard_map.123
  16.0 2.9 %collective-permute-start.5 = (bf16[496,128]{1,0:T(8,128)(2,1)S(1)}, bf16[496,128]{1,0:T(8,128)(2,1)S(1)}, u32[]{:S(2)}, u32[]{:S(2)}) collective-permute-start(bf16[496,128]{1,0:T(8,128)(2,1)S(1)} %get-tuple-element.43), channel_id=1, source_target_pairs={{0,6},{1,7},{2,4},{3,5},{4,2},{5,3},{6,0},{7,1},{8,14},{9,15},{10,... | collective-permute-start | bytes 380936 | tf_op jit(solution)/shard_map/ppermute | solution.py:298
  18.9 0.9 %shard_map.125 = (f32[48,1280]{1,0:T(8,128)S(1)}, f32[48,1280]{1,0:T(8,128)S(1)}, f32[48,1280]{1,0:T(8,128)S(1)}, f32[48,1280]{1,0:T(8,128)S(1)}) custom-call(s32[1,1024]{1,0:T(1,128)S(1)} %bitcast.11, bf16[1024,640]{1,0:T(8,128)(2,1)S(1)} %shard_map.122.own_ref, bf16[1024,640]{1,0:T(8,128)(2,1)S(1)} %collective-permute-done.1.other_ref, ...), custom_call_target="tpu_custom_call" | custom-call | bytes 4001792 | tf_op jit(solution)/shard_map/pallas_call | solution.py:260
  19.8 0.0 copy-start
  19.9 0.0 copy-start.1
  19.9 0.0 copy-start.2
  19.9 1.7 %collective-permute-start.14 = (f32[48,1280]{1,0:T(8,128)S(1)}, f32[48,1280]{1,0:T(8,128)S(1)}, u32[]{:S(2)}, u32[]{:S(2)}) collective-permute-start(f32[48,1280]{1,0:T(8,128)S(1)} %get-tuple-element.54), channel_id=1, source_target_pairs={{0,24},{8,16},{16,8},{24,0},{1,25},{9,17},{17,9},{25,1},{2,26},{10... | collective-permute-start | bytes 737288 | tf_op jit(solution)/shard_map/ppermute | solution.py:301
  21.6 1.3 %collective-permute-start.15 = (f32[48,1280]{1,0:T(8,128)S(1)}, f32[48,1280]{1,0:T(8,128)S(1)}, u32[]{:S(2)}, u32[]{:S(2)}) collective-permute-start(f32[48,1280]{1,0:T(8,128)S(1)} %get-tuple-element.55), channel_id=1, source_target_pairs={{0,16},{8,24},{16,0},{24,8},{1,17},{9,25},{17,1},{25,9},{2,18},{10... | collective-permute-start | bytes 737288 | tf_op jit(solution)/shard_map/ppermute | solution.py:301
  22.9 0.5 collective-permute-start.16
  23.4 0.2 collective-permute-start.6
  23.7 3.5 %collective-permute-start.7 = (bf16[496,128]{1,0:T(8,128)(2,1)S(1)}, bf16[496,128]{1,0:T(8,128)(2,1)S(1)}, u32[]{:S(2)}, u32[]{:S(2)}) collective-permute-start(bf16[496,128]{1,0:T(8,128)(2,1)S(1)} %get-tuple-element.45), channel_id=1, source_target_pairs={{0,2},{1,3},{2,0},{3,1},{4,6},{5,7},{6,4},{7,5},{8,10},{9,11},{10,... | collective-permute-start | bytes 380936 | tf_op jit(solution)/shard_map/ppermute | solution.py:298
  27.1 3.4 %collective-permute-done.6.refs_1_ = bf16[496,128]{1,0:T(8,128)(2,1)S(1)} collective-permute-done((bf16[496,128]{1,0:T(8,128)(2,1)S(1)}, bf16[496,128]{1,0:T(8,128)(2,1)S(1)}, u32[]{:S(2)}, u32[]{:S(2)}) %collective-permute-start.6) | collective-permute-done | bytes 127008 | tf_op jit(solution)/shard_map/ppermute | solution.py:298
  30.6 0.7 %collective-permute-done.7.refs_2_ = bf16[496,128]{1,0:T(8,128)(2,1)S(1)} collective-permute-done((bf16[496,128]{1,0:T(8,128)(2,1)S(1)}, bf16[496,128]{1,0:T(8,128)(2,1)S(1)}, u32[]{:S(2)}, u32[]{:S(2)}) %collective-permute-start.7) | collective-permute-done | bytes 127008 | tf_op jit(solution)/shard_map/ppermute | solution.py:298
  31.3 0.5 shard_map.124
  31.8 1.5 %collective-permute-start.8 = (f32[24,640]{1,0:T(8,128)S(1)}, f32[24,640]{1,0:T(8,128)S(1)}, u32[]{:S(2)}, u32[]{:S(2)}) collective-permute-start(f32[24,640]{1,0:T(8,128)S(1)} %get-tuple-element.48), channel_id=1, source_target_pairs={{0,8},{8,0},{16,24},{24,16},{1,9},{9,1},{17,25},{25,17},{2,10},{10... | collective-permute-start | bytes 184328 | tf_op jit(solution)/shard_map/ppermute | solution.py:301
  33.3 0.5 collective-permute-start.9
  33.8 1.5 %collective-permute-start.10 = (f32[24,640]{1,0:T(8,128)S(1)}, f32[24,640]{1,0:T(8,128)S(1)}, u32[]{:S(2)}, u32[]{:S(2)}) collective-permute-start(f32[24,640]{1,0:T(8,128)S(1)} %get-tuple-element.50), channel_id=1, source_target_pairs={{0,24},{8,16},{16,8},{24,0},{1,25},{9,17},{17,9},{25,1},{2,26},{10... | collective-permute-start | bytes 184328 | tf_op jit(solution)/shard_map/ppermute | solution.py:301
  35.3 0.1 shard_map.126
  35.4 1.6 %collective-permute-start.17 = (f32[24,640]{1,0:T(8,128)S(1)}, f32[24,640]{1,0:T(8,128)S(1)}, u32[]{:S(2)}, u32[]{:S(2)}) collective-permute-start(f32[24,640]{1,0:T(8,128)S(1)} %get-tuple-element.58), channel_id=1, source_target_pairs={{0,6},{1,7},{2,4},{3,5},{4,2},{5,3},{6,0},{7,1},{8,14},{9,15},{10,... | collective-permute-start | bytes 184328 | tf_op jit(solution)/shard_map/ppermute | solution.py:298
  37.0 0.6 %collective-permute-start.18 = (f32[24,640]{1,0:T(8,128)S(1)}, f32[24,640]{1,0:T(8,128)S(1)}, u32[]{:S(2)}, u32[]{:S(2)}) collective-permute-start(f32[24,640]{1,0:T(8,128)S(1)} %get-tuple-element.59), channel_id=1, source_target_pairs={{0,4},{1,5},{2,6},{3,7},{4,0},{5,1},{6,2},{7,3},{8,12},{9,13},{10,... | collective-permute-start | bytes 184328 | tf_op jit(solution)/shard_map/ppermute | solution.py:298
  37.7 2.2 %collective-permute-start.19 = (f32[24,640]{1,0:T(8,128)S(1)}, f32[24,640]{1,0:T(8,128)S(1)}, u32[]{:S(2)}, u32[]{:S(2)}) collective-permute-start(f32[24,640]{1,0:T(8,128)S(1)} %get-tuple-element.61), channel_id=1, source_target_pairs={{0,2},{1,3},{2,0},{3,1},{4,6},{5,7},{6,4},{7,5},{8,10},{9,11},{10,... | collective-permute-start | bytes 184328 | tf_op jit(solution)/shard_map/ppermute | solution.py:298
  39.9 1.6 %collective-permute-done.17.refs_4_ = f32[24,640]{1,0:T(8,128)S(1)} collective-permute-done((f32[24,640]{1,0:T(8,128)S(1)}, f32[24,640]{1,0:T(8,128)S(1)}, u32[]{:S(2)}, u32[]{:S(2)}) %collective-permute-start.17) | collective-permute-done | bytes 61472 | tf_op jit(solution)/shard_map/ppermute | solution.py:298
  41.5 1.3 %collective-permute-done.18.refs_5_ = f32[24,640]{1,0:T(8,128)S(1)} collective-permute-done((f32[24,640]{1,0:T(8,128)S(1)}, f32[24,640]{1,0:T(8,128)S(1)}, u32[]{:S(2)}, u32[]{:S(2)}) %collective-permute-start.18) | collective-permute-done | bytes 61472 | tf_op jit(solution)/shard_map/ppermute | solution.py:298
  42.8 0.1 shard_map.127.refs_0_
  42.9 0.3 shard_map.129.refs_3_
  43.2 1.7 %collective-permute-start.20 = (bf16[48,1280]{1,0:T(8,128)(2,1)S(1)}, bf16[48,1280]{1,0:T(8,128)(2,1)S(1)}, u32[]{:S(2)}, u32[]{:S(2)}) collective-permute-start(bf16[48,1280]{1,0:T(8,128)(2,1)S(1)} %shard_map.129.refs_3_), channel_id=1, source_target_pairs={{0,24},{8,16},{16,8},{24,0},{1,25},{9,17},{17,9},{25,1},{2,26},{10... | collective-permute-start | bytes 368648 | tf_op jit(solution)/shard_map/ppermute | solution.py:301
  44.9 1.3 %collective-permute-start.21 = (bf16[48,1280]{1,0:T(8,128)(2,1)S(1)}, bf16[48,1280]{1,0:T(8,128)(2,1)S(1)}, u32[]{:S(2)}, u32[]{:S(2)}) collective-permute-start(bf16[48,1280]{1,0:T(8,128)(2,1)S(1)} %shard_map.129.refs_3_), channel_id=1, source_target_pairs={{0,16},{8,24},{16,0},{24,8},{1,17},{9,25},{17,1},{25,9},{2,18},{10... | collective-permute-start | bytes 368648 | tf_op jit(solution)/shard_map/ppermute | solution.py:301
  46.2 0.5 %collective-permute-start.22 = (bf16[48,1280]{1,0:T(8,128)(2,1)S(1)}, bf16[48,1280]{1,0:T(8,128)(2,1)S(1)}, u32[]{:S(2)}, u32[]{:S(2)}) collective-permute-start(bf16[48,1280]{1,0:T(8,128)(2,1)S(1)} %shard_map.129.refs_3_), channel_id=1, source_target_pairs={{0,8},{8,0},{16,24},{24,16},{1,9},{9,1},{17,25},{25,17},{2,10},{10... | collective-permute-start | bytes 368648 | tf_op jit(solution)/shard_map/ppermute | solution.py:301
  46.7 1.3 %shard_map.128 = (f32[12,5120]{1,0:T(8,128)}, f32[12,5120]{1,0:T(8,128)}, f32[12,5120]{1,0:T(8,128)}, bf16[192,192]{1,0:T(8,128)(2,1)S(1)}) custom-call(f32[12,5120]{1,0:T(8,128)S(1)} %shard_map.127.refs_0_, f32[12,5120]{1,0:T(8,128)S(1)} %copy-done, f32[12,5120]{1,0:T(8,128)S(1)} %copy-done.1, f32[12,5120]{1,0:T(8,128)S(1)} %copy-done.2, ...), custom_call_target="tpu_custom_call" | custom-call | bytes 1916928 | tf_op jit(solution)/shard_map/pallas_call | solution.py:260
  48.0 1.1 %collective-permute-done.20.refs_0_ = bf16[48,1280]{1,0:T(8,128)(2,1)S(1)} collective-permute-done((bf16[48,1280]{1,0:T(8,128)(2,1)S(1)}, bf16[48,1280]{1,0:T(8,128)(2,1)S(1)}, u32[]{:S(2)}, u32[]{:S(2)}) %collective-permute-start.20) | collective-permute-done | bytes 122912 | tf_op jit(solution)/shard_map/ppermute | solution.py:301
  49.1 1.3 %collective-permute-done.21.refs_1_ = bf16[48,1280]{1,0:T(8,128)(2,1)S(1)} collective-permute-done((bf16[48,1280]{1,0:T(8,128)(2,1)S(1)}, bf16[48,1280]{1,0:T(8,128)(2,1)S(1)}, u32[]{:S(2)}, u32[]{:S(2)}) %collective-permute-start.21) | collective-permute-done | bytes 122912 | tf_op jit(solution)/shard_map/ppermute | solution.py:301
  50.3 0.7 %collective-permute-done.22.refs_2_ = bf16[48,1280]{1,0:T(8,128)(2,1)S(1)} collective-permute-done((bf16[48,1280]{1,0:T(8,128)(2,1)S(1)}, bf16[48,1280]{1,0:T(8,128)(2,1)S(1)}, u32[]{:S(2)}, u32[]{:S(2)}) %collective-permute-start.22) | collective-permute-done | bytes 122912 | tf_op jit(solution)/shard_map/ppermute | solution.py:301
  51.1 1.1 %shard_map.130 = bf16[48,5120]{1,0:T(8,128)(2,1)} custom-call(bf16[192,192]{1,0:T(8,128)(2,1)S(1)} %get-tuple-element.65.order_ref, bf16[48,1280]{1,0:T(8,128)(2,1)S(1)} %collective-permute-done.20.refs_0_, bf16[48,1280]{1,0:T(8,128)(2,1)S(1)} %collective-permute-done.21.refs_1_, bf16[48,1280]{1,0:T(8,128)(2,1)S(1)} %collective-permute-done.22.refs_2_, ...), custom_call_target="tpu_custom_call" | custom-call | bytes 1056768 | tf_op jit(solution)/shard_map/pallas_call | solution.py:260
  (19 shorter events, 0.0 us)
Async XLA Ops:
  0.6 6.1 %collective-permute-start.1 = (bf16[1024,640]{1,0:T(8,128)(2,1)}, bf16[1024,640]{1,0:T(8,128)(2,1)S(1)}, u32[]{:S(2)}, u32[]{:S(2)}) collective-permute-start(bf16[1024,640]{1,0:T(8,128)(2,1)} %hidden_hbm.1), channel_id=1, source_target_pairs={{0,1},{1,0},{2,3},{3,2},{4,5},{5,4},{6,7},{7,6},{8,9},{9,8},{10,11... | collective-permute-start | bytes 3932168 | tf_op jit(solution)/shard_map/ppermute | solution.py:298
  2.5 4.2 %collective-permute-start = (bf16[24,5248]{1,0:T(8,128)(2,1)S(1)}, bf16[24,5248]{1,0:T(8,128)(2,1)S(1)}, u32[]{:S(2)}, u32[]{:S(2)}) collective-permute-start(bf16[24,5248]{1,0:T(8,128)(2,1)S(1)} %get-tuple-element.36), channel_id=1, source_target_pairs={{0,1},{1,0},{2,3},{3,2},{4,5},{5,4},{6,7},{7,6},{8,9},{9,8},{10,11... | collective-permute-start | bytes 755720 | tf_op jit(solution)/shard_map/ppermute | solution.py:298
  2.6 9.4 %collective-permute-start.12 = (bf16[48,1024]{1,0:T(8,128)(2,1)}, bf16[48,1024]{1,0:T(8,128)(2,1)S(1)}, u32[]{:S(2)}, u32[]{:S(2)}) collective-permute-start(bf16[48,1024]{1,0:T(8,128)(2,1)} %bitcast.8), channel_id=1, source_target_pairs={{0,4},{1,5},{2,6},{3,7},{4,0},{5,1},{6,2},{7,3},{8,12},{9,13},{10,... | collective-permute-start | bytes 294920 | tf_op jit(solution)/shard_map/ppermute | solution.py:298
  6.8 7.4 %collective-permute-start.2 = (bf16[496,128]{1,0:T(8,128)(2,1)S(1)}, bf16[496,128]{1,0:T(8,128)(2,1)S(1)}, u32[]{:S(2)}, u32[]{:S(2)}) collective-permute-start(bf16[496,128]{1,0:T(8,128)(2,1)S(1)} %get-tuple-element.38), channel_id=1, source_target_pairs={{0,24},{8,16},{16,8},{24,0},{1,25},{9,17},{17,9},{25,1},{2,26},{10... | collective-permute-start | bytes 380936 | tf_op jit(solution)/shard_map/ppermute | solution.py:301
  9.3 6.3 %collective-permute-start.3 = (bf16[496,128]{1,0:T(8,128)(2,1)S(1)}, bf16[496,128]{1,0:T(8,128)(2,1)S(1)}, u32[]{:S(2)}, u32[]{:S(2)}) collective-permute-start(bf16[496,128]{1,0:T(8,128)(2,1)S(1)} %get-tuple-element.39), channel_id=1, source_target_pairs={{0,16},{8,24},{16,0},{24,8},{1,17},{9,25},{17,1},{25,9},{2,18},{10... | collective-permute-start | bytes 380936 | tf_op jit(solution)/shard_map/ppermute | solution.py:301
  9.8 9.1 %copy-start.3 = (bf16[1024,48]{0,1:T(8,128)(2,1)S(1)}, bf16[1024,48]{0,1:T(8,128)(2,1)}, u32[]{:S(2)}) copy-start(bf16[1024,48]{0,1:T(8,128)(2,1)} %param.10) | copy-start | bytes 294916
  9.8 9.1 %copy-start.4 = (s32[1024]{0:T(1024)S(1)}, s32[1024]{0:T(1024)}, u32[]{:S(2)}) copy-start(s32[1024]{0:T(1024)} %param.11) | copy-start | bytes 12292
  9.8 5.8 %collective-permute-start.4 = (bf16[496,128]{1,0:T(8,128)(2,1)S(1)}, bf16[496,128]{1,0:T(8,128)(2,1)S(1)}, u32[]{:S(2)}, u32[]{:S(2)}) collective-permute-start(bf16[496,128]{1,0:T(8,128)(2,1)S(1)} %get-tuple-element.40), channel_id=1, source_target_pairs={{0,8},{8,0},{16,24},{24,16},{1,9},{9,1},{17,25},{25,17},{2,10},{10... | collective-permute-start | bytes 380936 | tf_op jit(solution)/shard_map/ppermute | solution.py:301
  10.3 8.5 %collective-permute-start.11 = (bf16[48,1024]{1,0:T(8,128)(2,1)}, bf16[48,1024]{1,0:T(8,128)(2,1)S(1)}, u32[]{:S(2)}, u32[]{:S(2)}) collective-permute-start(bf16[48,1024]{1,0:T(8,128)(2,1)} %bitcast.9), channel_id=1, source_target_pairs={{0,2},{1,3},{2,0},{3,1},{4,6},{5,7},{6,4},{7,5},{8,10},{9,11},{10,... | collective-permute-start | bytes 294920 | tf_op jit(solution)/shard_map/ppermute | solution.py:298
  12.0 6.8 %collective-permute-start.13 = (bf16[48,1024]{1,0:T(8,128)(2,1)S(1)}, bf16[48,1024]{1,0:T(8,128)(2,1)S(1)}, u32[]{:S(2)}, u32[]{:S(2)}) collective-permute-start(bf16[48,1024]{1,0:T(8,128)(2,1)S(1)} %collective-permute-done.12.refs_2_), channel_id=1, source_target_pairs={{0,2},{1,3},{2,0},{3,1},{4,6},{5,7},{6,4},{7,5},{8,10},{9,11},{10,... | collective-permute-start | bytes 294920 | tf_op jit(solution)/shard_map/ppermute | solution.py:298
  16.0 7.7 %collective-permute-start.5 = (bf16[496,128]{1,0:T(8,128)(2,1)S(1)}, bf16[496,128]{1,0:T(8,128)(2,1)S(1)}, u32[]{:S(2)}, u32[]{:S(2)}) collective-permute-start(bf16[496,128]{1,0:T(8,128)(2,1)S(1)} %get-tuple-element.43), channel_id=1, source_target_pairs={{0,6},{1,7},{2,4},{3,5},{4,2},{5,3},{6,0},{7,1},{8,14},{9,15},{10,... | collective-permute-start | bytes 380936 | tf_op jit(solution)/shard_map/ppermute | solution.py:298
  19.8 23.0 %copy-start = (f32[12,5120]{1,0:T(8,128)S(1)}, f32[12,5120]{1,0:T(8,128)}, u32[]{:S(2)}) copy-start(f32[12,5120]{1,0:T(8,128)} %refs_1_.3) | copy-start | bytes 737284
  19.9 23.0 %copy-start.1 = (f32[12,5120]{1,0:T(8,128)S(1)}, f32[12,5120]{1,0:T(8,128)}, u32[]{:S(2)}) copy-start(f32[12,5120]{1,0:T(8,128)} %refs_2_.3) | copy-start | bytes 737284
  19.9 23.0 %copy-start.2 = (f32[12,5120]{1,0:T(8,128)S(1)}, f32[12,5120]{1,0:T(8,128)}, u32[]{:S(2)}) copy-start(f32[12,5120]{1,0:T(8,128)} %refs_3_.3) | copy-start | bytes 737284
  19.9 13.9 %collective-permute-start.14 = (f32[48,1280]{1,0:T(8,128)S(1)}, f32[48,1280]{1,0:T(8,128)S(1)}, u32[]{:S(2)}, u32[]{:S(2)}) collective-permute-start(f32[48,1280]{1,0:T(8,128)S(1)} %get-tuple-element.54), channel_id=1, source_target_pairs={{0,24},{8,16},{16,8},{24,0},{1,25},{9,17},{17,9},{25,1},{2,26},{10... | collective-permute-start | bytes 737288 | tf_op jit(solution)/shard_map/ppermute | solution.py:301
  21.6 13.7 %collective-permute-start.15 = (f32[48,1280]{1,0:T(8,128)S(1)}, f32[48,1280]{1,0:T(8,128)S(1)}, u32[]{:S(2)}, u32[]{:S(2)}) collective-permute-start(f32[48,1280]{1,0:T(8,128)S(1)} %get-tuple-element.55), channel_id=1, source_target_pairs={{0,16},{8,24},{16,0},{24,8},{1,17},{9,25},{17,1},{25,9},{2,18},{10... | collective-permute-start | bytes 737288 | tf_op jit(solution)/shard_map/ppermute | solution.py:301
  22.9 12.4 %collective-permute-start.16 = (f32[48,1280]{1,0:T(8,128)S(1)}, f32[48,1280]{1,0:T(8,128)S(1)}, u32[]{:S(2)}, u32[]{:S(2)}) collective-permute-start(f32[48,1280]{1,0:T(8,128)S(1)} %get-tuple-element.56), channel_id=1, source_target_pairs={{0,8},{8,0},{16,24},{24,16},{1,9},{9,1},{17,25},{25,17},{2,10},{10... | collective-permute-start | bytes 737288 | tf_op jit(solution)/shard_map/ppermute | solution.py:301
  23.4 7.1 %collective-permute-start.6 = (bf16[496,128]{1,0:T(8,128)(2,1)S(1)}, bf16[496,128]{1,0:T(8,128)(2,1)S(1)}, u32[]{:S(2)}, u32[]{:S(2)}) collective-permute-start(bf16[496,128]{1,0:T(8,128)(2,1)S(1)} %get-tuple-element.44), channel_id=1, source_target_pairs={{0,4},{1,5},{2,6},{3,7},{4,0},{5,1},{6,2},{7,3},{8,12},{9,13},{10,... | collective-permute-start | bytes 380936 | tf_op jit(solution)/shard_map/ppermute | solution.py:298
  23.7 7.6 %collective-permute-start.7 = (bf16[496,128]{1,0:T(8,128)(2,1)S(1)}, bf16[496,128]{1,0:T(8,128)(2,1)S(1)}, u32[]{:S(2)}, u32[]{:S(2)}) collective-permute-start(bf16[496,128]{1,0:T(8,128)(2,1)S(1)} %get-tuple-element.45), channel_id=1, source_target_pairs={{0,2},{1,3},{2,0},{3,1},{4,6},{5,7},{6,4},{7,5},{8,10},{9,11},{10,... | collective-permute-start | bytes 380936 | tf_op jit(solution)/shard_map/ppermute | solution.py:298
  31.8 5.9 %collective-permute-start.8 = (f32[24,640]{1,0:T(8,128)S(1)}, f32[24,640]{1,0:T(8,128)S(1)}, u32[]{:S(2)}, u32[]{:S(2)}) collective-permute-start(f32[24,640]{1,0:T(8,128)S(1)} %get-tuple-element.48), channel_id=1, source_target_pairs={{0,8},{8,0},{16,24},{24,16},{1,9},{9,1},{17,25},{25,17},{2,10},{10... | collective-permute-start | bytes 184328 | tf_op jit(solution)/shard_map/ppermute | solution.py:301
  33.3 6.5 %collective-permute-start.9 = (f32[24,640]{1,0:T(8,128)S(1)}, f32[24,640]{1,0:T(8,128)S(1)}, u32[]{:S(2)}, u32[]{:S(2)}) collective-permute-start(f32[24,640]{1,0:T(8,128)S(1)} %get-tuple-element.49), channel_id=1, source_target_pairs={{0,16},{8,24},{16,0},{24,8},{1,17},{9,25},{17,1},{25,9},{2,18},{10... | collective-permute-start | bytes 184328 | tf_op jit(solution)/shard_map/ppermute | solution.py:301
  33.8 6.1 %collective-permute-start.10 = (f32[24,640]{1,0:T(8,128)S(1)}, f32[24,640]{1,0:T(8,128)S(1)}, u32[]{:S(2)}, u32[]{:S(2)}) collective-permute-start(f32[24,640]{1,0:T(8,128)S(1)} %get-tuple-element.50), channel_id=1, source_target_pairs={{0,24},{8,16},{16,8},{24,0},{1,25},{9,17},{17,9},{25,1},{2,26},{10... | collective-permute-start | bytes 184328 | tf_op jit(solution)/shard_map/ppermute | solution.py:301
  35.4 6.1 %collective-permute-start.17 = (f32[24,640]{1,0:T(8,128)S(1)}, f32[24,640]{1,0:T(8,128)S(1)}, u32[]{:S(2)}, u32[]{:S(2)}) collective-permute-start(f32[24,640]{1,0:T(8,128)S(1)} %get-tuple-element.58), channel_id=1, source_target_pairs={{0,6},{1,7},{2,4},{3,5},{4,2},{5,3},{6,0},{7,1},{8,14},{9,15},{10,... | collective-permute-start | bytes 184328 | tf_op jit(solution)/shard_map/ppermute | solution.py:298
  37.0 5.8 %collective-permute-start.18 = (f32[24,640]{1,0:T(8,128)S(1)}, f32[24,640]{1,0:T(8,128)S(1)}, u32[]{:S(2)}, u32[]{:S(2)}) collective-permute-start(f32[24,640]{1,0:T(8,128)S(1)} %get-tuple-element.59), channel_id=1, source_target_pairs={{0,4},{1,5},{2,6},{3,7},{4,0},{5,1},{6,2},{7,3},{8,12},{9,13},{10,... | collective-permute-start | bytes 184328 | tf_op jit(solution)/shard_map/ppermute | solution.py:298
  37.7 5.2 %collective-permute-start.19 = (f32[24,640]{1,0:T(8,128)S(1)}, f32[24,640]{1,0:T(8,128)S(1)}, u32[]{:S(2)}, u32[]{:S(2)}) collective-permute-start(f32[24,640]{1,0:T(8,128)S(1)} %get-tuple-element.61), channel_id=1, source_target_pairs={{0,2},{1,3},{2,0},{3,1},{4,6},{5,7},{6,4},{7,5},{8,10},{9,11},{10,... | collective-permute-start | bytes 184328 | tf_op jit(solution)/shard_map/ppermute | solution.py:298
  43.2 5.9 %collective-permute-start.20 = (bf16[48,1280]{1,0:T(8,128)(2,1)S(1)}, bf16[48,1280]{1,0:T(8,128)(2,1)S(1)}, u32[]{:S(2)}, u32[]{:S(2)}) collective-permute-start(bf16[48,1280]{1,0:T(8,128)(2,1)S(1)} %shard_map.129.refs_3_), channel_id=1, source_target_pairs={{0,24},{8,16},{16,8},{24,0},{1,25},{9,17},{17,9},{25,1},{2,26},{10... | collective-permute-start | bytes 368648 | tf_op jit(solution)/shard_map/ppermute | solution.py:301
  44.9 5.5 %collective-permute-start.21 = (bf16[48,1280]{1,0:T(8,128)(2,1)S(1)}, bf16[48,1280]{1,0:T(8,128)(2,1)S(1)}, u32[]{:S(2)}, u32[]{:S(2)}) collective-permute-start(bf16[48,1280]{1,0:T(8,128)(2,1)S(1)} %shard_map.129.refs_3_), channel_id=1, source_target_pairs={{0,16},{8,24},{16,0},{24,8},{1,17},{9,25},{17,1},{25,9},{2,18},{10... | collective-permute-start | bytes 368648 | tf_op jit(solution)/shard_map/ppermute | solution.py:301
  46.2 4.9 %collective-permute-start.22 = (bf16[48,1280]{1,0:T(8,128)(2,1)S(1)}, bf16[48,1280]{1,0:T(8,128)(2,1)S(1)}, u32[]{:S(2)}, u32[]{:S(2)}) collective-permute-start(bf16[48,1280]{1,0:T(8,128)(2,1)S(1)} %shard_map.129.refs_3_), channel_id=1, source_target_pairs={{0,8},{8,0},{16,24},{24,16},{1,9},{9,1},{17,25},{25,17},{2,10},{10... | collective-permute-start | bytes 368648 | tf_op jit(solution)/shard_map/ppermute | solution.py:301
